TPU v7x, 512 devices: a whole 4x4x16 slice. The times are simulated.
512 devices in a mesh: seq: 64 (over x, z), head: 8 (over y, core).
Axes of the slice: x: 4, y: 4, z: 16, core: 2. Of those that a mesh axis runs over, the one named last changes fastest.
Arguments:
- q_raw: bfloat16 [8192, 24, 128], P('seq', 'head'), may hold values from -120 to 120
- k_raw: bfloat16 [8192, 24, 128], P('seq', 'head'), may hold values from -120 to 120
- values: bfloat16 [8192, 24, 128], P('seq', 'head'), may hold values from -6 to 6
- grad_out: bfloat16 [8192, 24, 128], P('seq', 'head'), may hold values from -6 to 6
- q_gain: float32 [24, 128], P('head'), may hold values from 0.5 to 1.5
- k_gain: float32 [24, 128], P('head'), may hold values from 0.5 to 1.5
- key_tiles: int32 [64, 13], replicated, may hold values from -1 to 63, as said below
Outputs:
- attended: bfloat16 [8192, 24, 128], P('seq', 'head')
- grad_q: bfloat16 [8192, 24, 128], P('seq', 'head')
- grad_k: bfloat16 [8192, 24, 128], P('seq', 'head')
- grad_v: bfloat16 [8192, 24, 128], P('seq', 'head')
Inputs may be any that keep to these rules, and one draw needn't show every extreme that they name: `key_tiles`: frame f is the single tile f. Row r (frame f = r) lists tile f in slot 0, tile f - 1 in slot 1 and tile f + 1 in slot 2; then for each level L from 2 to 6 two slots: tile f - 2^(L-1), then tile f + 2^(L-1). An entry is -1 where that frame lies outside the clip.
All inputs are finite; a program needn't handle non-finite values.
Results may differ from a plain program's by a relative error of at most 0.03.
Values may be sent and summed in bfloat16 or wider, within the bound.
No kernel may reach another device: no remote copies, remote signals or barrier semaphores. Data moves between devices by JAX's collectives and lax.ppermute only.
A program may use at most 64 MiB of HBM per device.

v0:
```python
import jax
import jax.numpy as jnp
from jax import lax
from jax.sharding import PartitionSpec as P

TILE = 128


EPS = 1e-06


def passed_along(value, axis, steps):
    count = lax.axis_size(axis)
    leading, last = (max(0, -steps), min(count, count - steps))
    return lax.ppermute(value, axis, [(source, source + steps) for source in range(leading, last)])


def contract(left, right, left_dim, right_dim):
    return lax.dot_general(
        left, right, (((left_dim,), (right_dim,)), ((), ())), preferred_element_type=jnp.float32
    )


def tile_member(own_rows, tile_ids):
    found = jnp.any(own_rows[:, :, None] == tile_ids[None, None, :], axis=1)
    return found & (tile_ids >= 0)[None, :]


def per_device(q_raw, k_raw, values, grad_out, q_gain, k_gain, key_tiles):
    seq_count = lax.axis_size("seq")
    seq_place = lax.axis_index("seq")
    levels_here = seq_count.bit_length() - 1
    rows_dev, head_count, head_width = q_raw.shape
    tiles_dev = rows_dev // TILE
    channels = head_count * head_width * lax.axis_size("head")
    scale = head_width ** (-0.5)
    query_floats = q_raw.astype(jnp.float32)
    key_floats = k_raw.astype(jnp.float32)
    query_total, key_total_sq = lax.psum(
        (
            jnp.sum(query_floats * query_floats, axis=(1, 2)),
            jnp.sum(key_floats * key_floats, axis=(1, 2)),
        ),
        "head",
    )
    query_inverse = lax.rsqrt(query_total / channels + EPS)
    key_inverse = lax.rsqrt(key_total_sq / channels + EPS)
    q_norm = (query_floats * query_inverse[:, None, None] * q_gain[None]).astype(jnp.bfloat16)
    k_norm = (key_floats * key_inverse[:, None, None] * k_gain[None]).astype(jnp.bfloat16)
    own_rows = lax.dynamic_slice_in_dim(key_tiles, seq_place * tiles_dev, tiles_dev, 0)
    local_ids = seq_place * tiles_dev + jnp.arange(tiles_dev, dtype=jnp.int32)
    key_parts = [k_norm]
    value_parts = [values]
    mask_parts = [tile_member(own_rows, local_ids)]
    returns = []
    for degree in range(1, levels_here + 1):
        distance = 2 ** (degree - 1)
        for facing in (-1, 1):
            source = seq_place + facing * distance
            inside = (source >= 0) & (source < seq_count)
            offset = None
            tile_ids = jnp.where(
                inside, source * tiles_dev + jnp.arange(tiles_dev, dtype=jnp.int32), -2
            )
            got_keys, got_values = passed_along((k_norm, values), "seq", -facing * distance)
            key_parts.append(got_keys)
            value_parts.append(got_values)
            mask_parts.append(tile_member(own_rows, tile_ids))
            returns.append((facing * distance, offset, got_keys.shape[0]))
    all_keys = jnp.concatenate(key_parts, axis=0)
    all_values = jnp.concatenate(value_parts, axis=0)
    mask_rows = jnp.repeat(
        jnp.repeat(jnp.concatenate(mask_parts, axis=1), TILE, axis=0), TILE, axis=1
    )
    out_heads = []
    query_grads = []
    key_grads = []
    value_grads = []
    row_maxima = []
    row_totals = []
    row_deltas = []
    for column in range(head_count):
        query_head = q_norm[:, column]
        key_head = all_keys[:, column]
        value_head = all_values[:, column]
        upstream = grad_out[:, column]
        score = contract(query_head, key_head, 1, 1) * scale
        score = jnp.where(mask_rows, score, -1e30)
        top = jnp.max(score, axis=1, keepdims=True)
        weights_raw = jnp.exp(score - top)
        total = jnp.sum(weights_raw, axis=1, keepdims=True)
        prob = weights_raw / total
        prob_b = prob.astype(jnp.bfloat16)
        out_head = contract(prob_b, value_head, 1, 0).astype(jnp.bfloat16)
        delta = jnp.sum(
            upstream.astype(jnp.float32) * out_head.astype(jnp.float32), axis=1, keepdims=True
        )
        dprob = contract(upstream, value_head, 1, 1)
        dscore = (prob * (dprob - delta)).astype(jnp.bfloat16)
        out_heads.append(out_head)
        query_grads.append(contract(dscore, key_head, 1, 0) * scale)
        key_grads.append(contract(dscore, query_head, 0, 0) * scale)
        value_grads.append(contract(prob_b, upstream, 0, 0))
        row_maxima.append(top[:, 0])
        row_totals.append(total[:, 0])
        row_deltas.append(delta[:, 0])
    attended = jnp.stack(out_heads, axis=1)
    dq_norm = jnp.stack(query_grads, axis=1)
    key_all_grad = jnp.stack(key_grads, axis=1)
    value_all_grad = jnp.stack(value_grads, axis=1)
    key_sum = key_all_grad[:rows_dev]
    value_sum = value_all_grad[:rows_dev]
    cursor = rows_dev
    for shift_back, offset, piece_rows in returns:
        piece_keys = key_all_grad[cursor : cursor + piece_rows]
        piece_values = value_all_grad[cursor : cursor + piece_rows]
        back_keys, back_values = passed_along((piece_keys, piece_values), "seq", shift_back)
        key_sum = key_sum + back_keys
        value_sum = value_sum + back_values
        cursor = cursor + piece_rows
    query_scaled = dq_norm * q_gain[None]
    key_scaled = key_sum * k_gain[None]
    query_inner, key_inner = lax.psum(
        (
            jnp.sum(query_floats * query_scaled, axis=(1, 2)),
            jnp.sum(key_floats * key_scaled, axis=(1, 2)),
        ),
        "head",
    )
    grad_q = (
        query_inverse[:, None, None] * query_scaled
        - query_floats * (query_inverse**3 * query_inner / channels)[:, None, None]
    )
    grad_k = (
        key_inverse[:, None, None] * key_scaled
        - key_floats * (key_inverse**3 * key_inner / channels)[:, None, None]
    )
    return (
        attended,
        grad_q.astype(jnp.bfloat16),
        grad_k.astype(jnp.bfloat16),
        value_sum.astype(jnp.bfloat16),
    )


def solution(mesh):
    return jax.shard_map(
        per_device,
        mesh=mesh,
        in_specs=(
            P("seq", "head", None),
            P("seq", "head", None),
            P("seq", "head", None),
            P("seq", "head", None),
            P("head", None),
            P("head", None),
            P(),
        ),
        out_specs=(
            P("seq", "head", None),
            P("seq", "head", None),
            P("seq", "head", None),
            P("seq", "head", None),
        ),
        check_vma=False,
    )
```

profile of v0, /device:TPU:7, one launch (start us, length us, event | category | flops | bytes accessed | tf_op | source)
XLA Modules:
  0.0 439.8 jit_solution(13505699226241353566)
XLA Ops:
  2.1 2.5 collective-permute-start.21
  5.8 18.5 %collective-permute-start.19 = (bf16[128,3,128]{2,0,1:T(8,128)(2,1)}, bf16[128,3,128]{2,0,1:T(8,128)(2,1)S(1)}, u32[]{:S(2)}, u32[]{:S(2)}) collective-permute-start(bf16[128,3,128]{2,0,1:T(8,128)(2,1)} %param.9), channel_id=1, source_target_pairs={{64,0},{72,8},{80,16},{88,24},{96,32},{104,40},{112,48},{120,56},{... | collective-permute-start | bytes 294920 | tf_op jit(solution)/shard_map/ppermute | solution.py:15
  26.5 13.5 %all-reduce.1 = (f32[128]{0:T(128)S(1)}, f32[128]{0:T(128)S(1)}) all-reduce(f32[128]{0:T(128)S(1)} %fusion.36, f32[128]{0:T(128)S(1)} %fusion.30), channel_id=1, replica_groups=mesh['seq'=64,'head'=8] {'head'}, use_global_device_ids=true, to_apply=%region_16.17 | all-reduce | flops 256 | bytes 2048 | tf_op jit(solution)/shard_map/psum | solution.py:39
  40.8 2.6 collective-permute-start
  55.0 4.7 %collective-permute-start.1 = (bf16[128,3,128]{0,2,1:T(8,128)(2,1)S(1)}, bf16[128,3,128]{0,2,1:T(8,128)(2,1)S(1)}, u32[]{:S(2)}, u32[]{:S(2)}) collective-permute-start(bf16[128,3,128]{0,2,1:T(8,128)(2,1)S(1)} %get-tuple-element.28), channel_id=1, source_target_pairs={{8,0},{16,8},{24,16},{32,24},{40,32},{48,40},{56,48},{64,56},{72,6... | collective-permute-start | bytes 294920 | tf_op jit(solution)/shard_map/ppermute | solution.py:15
  63.5 6.3 %collective-permute-done.2 = bf16[128,3,128]{0,2,1:T(8,128)(2,1)S(1)} collective-permute-done((bf16[128,3,128]{0,2,1:T(8,128)(2,1)S(1)}, bf16[128,3,128]{0,2,1:T(8,128)(2,1)S(1)}, u32[]{:S(2)}, u32[]{:S(2)}) %collective-permute-start.2) | collective-permute-done | bytes 98336 | tf_op jit(solution)/shard_map/ppermute | solution.py:15
  71.8 4.4 collective-permute-done.3
  78.4 11.2 %collective-permute-done.4 = bf16[128,3,128]{0,2,1:T(8,128)(2,1)S(1)} collective-permute-done((bf16[128,3,128]{0,2,1:T(8,128)(2,1)S(1)}, bf16[128,3,128]{0,2,1:T(8,128)(2,1)S(1)}, u32[]{:S(2)}, u32[]{:S(2)}) %collective-permute-start.4) | collective-permute-done | bytes 98336 | tf_op jit(solution)/shard_map/ppermute | solution.py:15
  91.5 8.7 %collective-permute-done.5 = bf16[128,3,128]{0,2,1:T(8,128)(2,1)S(1)} collective-permute-done((bf16[128,3,128]{0,2,1:T(8,128)(2,1)S(1)}, bf16[128,3,128]{0,2,1:T(8,128)(2,1)S(1)}, u32[]{:S(2)}, u32[]{:S(2)}) %collective-permute-start.5) | collective-permute-done | bytes 98336 | tf_op jit(solution)/shard_map/ppermute | solution.py:15
  102.2 13.0 %collective-permute-done.6 = bf16[128,3,128]{0,2,1:T(8,128)(2,1)S(1)} collective-permute-done((bf16[128,3,128]{0,2,1:T(8,128)(2,1)S(1)}, bf16[128,3,128]{0,2,1:T(8,128)(2,1)S(1)}, u32[]{:S(2)}, u32[]{:S(2)}) %collective-permute-start.6) | collective-permute-done | bytes 98336 | tf_op jit(solution)/shard_map/ppermute | solution.py:15
  117.1 12.1 %collective-permute-done.7 = bf16[128,3,128]{0,2,1:T(8,128)(2,1)S(1)} collective-permute-done((bf16[128,3,128]{0,2,1:T(8,128)(2,1)S(1)}, bf16[128,3,128]{0,2,1:T(8,128)(2,1)S(1)}, u32[]{:S(2)}, u32[]{:S(2)}) %collective-permute-start.7) | collective-permute-done | bytes 98336 | tf_op jit(solution)/shard_map/ppermute | solution.py:15
  130.6 4.1 collective-permute-done.8
  134.6 3.4 collective-permute-start.9
  140.9 5.5 %collective-permute-done.10 = bf16[128,3,128]{0,2,1:T(8,128)(2,1)S(1)} collective-permute-done((bf16[128,3,128]{0,2,1:T(8,128)(2,1)S(1)}, bf16[128,3,128]{0,2,1:T(8,128)(2,1)S(1)}, u32[]{:S(2)}, u32[]{:S(2)}) %collective-permute-start.10) | collective-permute-done | bytes 98336 | tf_op jit(solution)/shard_map/ppermute | solution.py:15
  149.6 4.5 %collective-permute-start.12 = (bf16[128,3,128]{2,0,1:T(8,128)(2,1)S(1)}, bf16[128,3,128]{2,0,1:T(8,128)(2,1)S(1)}, u32[]{:S(2)}, u32[]{:S(2)}) collective-permute-start(bf16[128,3,128]{2,0,1:T(8,128)(2,1)S(1)} %copy-done.10), channel_id=1, source_target_pairs={{0,8},{8,16},{16,24},{24,32},{32,40},{40,48},{48,56},{56,64},{64,7... | collective-permute-start | bytes 294920 | tf_op jit(solution)/shard_map/ppermute | solution.py:15
  158.5 3.4 collective-permute-start.13
  165.7 6.5 %collective-permute-done.14 = bf16[128,3,128]{2,0,1:T(8,128)(2,1)S(1)} collective-permute-done((bf16[128,3,128]{2,0,1:T(8,128)(2,1)S(1)}, bf16[128,3,128]{2,0,1:T(8,128)(2,1)S(1)}, u32[]{:S(2)}, u32[]{:S(2)}) %collective-permute-start.14) | collective-permute-done | bytes 98336 | tf_op jit(solution)/shard_map/ppermute | solution.py:15
  174.3 4.3 collective-permute-done.15
  178.6 3.3 collective-permute-start.16
  181.9 9.3 %collective-permute-done.16 = bf16[128,3,128]{2,0,1:T(8,128)(2,1)S(1)} collective-permute-done((bf16[128,3,128]{2,0,1:T(8,128)(2,1)S(1)}, bf16[128,3,128]{2,0,1:T(8,128)(2,1)S(1)}, u32[]{:S(2)}, u32[]{:S(2)}) %collective-permute-start.16) | collective-permute-done | bytes 98336 | tf_op jit(solution)/shard_map/ppermute | solution.py:15
  191.3 3.4 collective-permute-start.17
  194.7 8.4 %collective-permute-done.17 = bf16[128,3,128]{2,0,1:T(8,128)(2,1)S(1)} collective-permute-done((bf16[128,3,128]{2,0,1:T(8,128)(2,1)S(1)}, bf16[128,3,128]{2,0,1:T(8,128)(2,1)S(1)}, u32[]{:S(2)}, u32[]{:S(2)}) %collective-permute-start.17) | collective-permute-done | bytes 98336 | tf_op jit(solution)/shard_map/ppermute | solution.py:15
  205.0 13.9 %collective-permute-done.18 = bf16[128,3,128]{2,0,1:T(8,128)(2,1)S(1)} collective-permute-done((bf16[128,3,128]{2,0,1:T(8,128)(2,1)S(1)}, bf16[128,3,128]{2,0,1:T(8,128)(2,1)S(1)}, u32[]{:S(2)}, u32[]{:S(2)}) %collective-permute-start.18) | collective-permute-done | bytes 98336 | tf_op jit(solution)/shard_map/ppermute | solution.py:15
  218.9 8.7 %collective-permute-start.23 = (bf16[128,3,128]{2,0,1:T(8,128)(2,1)S(1)}, bf16[128,3,128]{2,0,1:T(8,128)(2,1)S(1)}, u32[]{:S(2)}, u32[]{:S(2)}) collective-permute-start(bf16[128,3,128]{2,0,1:T(8,128)(2,1)S(1)} %copy-done.10), channel_id=1, source_target_pairs={{256,0},{264,8},{272,16},{280,24},{288,32},{296,40},{304,48},{312,... | collective-permute-start | bytes 294920 | tf_op jit(solution)/shard_map/ppermute | solution.py:15
  238.9 5.8 %collective-permute-start.34 = (f32[128,3,128]{0,2,1:T(8,128)S(1)}, f32[128,3,128]{0,2,1:T(8,128)S(1)}, u32[]{:S(2)}, u32[]{:S(2)}) collective-permute-start(f32[128,3,128]{0,2,1:T(8,128)S(1)} %get-tuple-element.43), channel_id=1, source_target_pairs={{256,0},{264,8},{272,16},{280,24},{288,32},{296,40},{304,48},{312,... | collective-permute-start | bytes 589832 | tf_op jit(solution)/shard_map/ppermute | solution.py:15
  246.0 4.0 collective-permute-start.32
  252.5 2.7 collective-permute-start.31
  255.2 12.4 %collective-permute-start.30 = (f32[128,3,128]{0,2,1:T(8,128)S(1)}, f32[128,3,128]{0,2,1:T(8,128)S(1)}, u32[]{:S(2)}, u32[]{:S(2)}) collective-permute-start(f32[128,3,128]{0,2,1:T(8,128)S(1)} %get-tuple-element.47), channel_id=1, source_target_pairs={{64,0},{72,8},{80,16},{88,24},{96,32},{104,40},{112,48},{120,56},{... | collective-permute-start | bytes 589832 | tf_op jit(solution)/shard_map/ppermute | solution.py:15
  268.1 4.6 %collective-permute-start.29 = (f32[128,3,128]{0,2,1:T(8,128)}, f32[128,3,128]{0,2,1:T(8,128)}, u32[]{:S(2)}, u32[]{:S(2)}) collective-permute-start(f32[128,3,128]{0,2,1:T(8,128)} %get-tuple-element.48), channel_id=1, source_target_pairs={{0,32},{8,40},{16,48},{24,56},{32,64},{40,72},{48,80},{56,88},{64,... | collective-permute-start | bytes 589832 | tf_op jit(solution)/shard_map/ppermute | solution.py:15
  272.8 5.5 %collective-permute-start.28 = (f32[128,3,128]{0,2,1:T(8,128)}, f32[128,3,128]{0,2,1:T(8,128)}, u32[]{:S(2)}, u32[]{:S(2)}) collective-permute-start(f32[128,3,128]{0,2,1:T(8,128)} %get-tuple-element.49), channel_id=1, source_target_pairs={{32,0},{40,8},{48,16},{56,24},{64,32},{72,40},{80,48},{88,56},{96,... | collective-permute-start | bytes 589832 | tf_op jit(solution)/shard_map/ppermute | solution.py:15
  280.2 6.4 %collective-permute-start.26 = (f32[128,3,128]{0,2,1:T(8,128)}, f32[128,3,128]{0,2,1:T(8,128)}, u32[]{:S(2)}, u32[]{:S(2)}) collective-permute-start(f32[128,3,128]{0,2,1:T(8,128)} %get-tuple-element.51), channel_id=1, source_target_pairs={{16,0},{24,8},{32,16},{40,24},{48,32},{56,40},{64,48},{72,56},{80,... | collective-permute-start | bytes 589832 | tf_op jit(solution)/shard_map/ppermute | solution.py:15
  286.6 3.2 collective-permute-start.25
  291.3 4.2 collective-permute-start.36
  296.8 4.0 collective-permute-done.27
  300.9 2.8 collective-permute-start.46
  305.5 14.6 %collective-permute-done.25 = f32[128,3,128]{0,2,1:T(8,128)} collective-permute-done((f32[128,3,128]{0,2,1:T(8,128)}, f32[128,3,128]{0,2,1:T(8,128)}, u32[]{:S(2)}, u32[]{:S(2)}) %collective-permute-start.25) | collective-permute-done | bytes 196640 | tf_op jit(solution)/shard_map/ppermute | solution.py:15
  322.0 2.4 fusion.39
  324.4 37.9 %all-reduce = (f32[128]{0:T(128)}, f32[128]{0:T(128)}) all-reduce(f32[128]{0:T(128)} %fusion.33, f32[128]{0:T(128)} %get-tuple-element.25), channel_id=1, replica_groups=mesh['seq'=64,'head'=8] {'head'}, use_global_device_ids=true, to_apply=%region_27.28 | all-reduce | flops 256 | bytes 2048 | tf_op jit(solution)/shard_map/psum | solution.py:123
  363.0 8.5 %collective-permute-start.43 = (f32[128,3,128]{2,0,1:T(8,128)}, f32[128,3,128]{2,0,1:T(8,128)}, u32[]{:S(2)}, u32[]{:S(2)}) collective-permute-start(f32[128,3,128]{2,0,1:T(8,128)} %get-tuple-element.34), channel_id=1, source_target_pairs={{0,64},{8,72},{16,80},{24,88},{32,96},{40,104},{48,112},{56,120},{... | collective-permute-start | bytes 589832 | tf_op jit(solution)/shard_map/ppermute | solution.py:15
  371.5 6.4 %collective-permute-start.42 = (f32[128,3,128]{2,0,1:T(8,128)}, f32[128,3,128]{2,0,1:T(8,128)}, u32[]{:S(2)}, u32[]{:S(2)}) collective-permute-start(f32[128,3,128]{2,0,1:T(8,128)} %get-tuple-element.35), channel_id=1, source_target_pairs={{64,0},{72,8},{80,16},{88,24},{96,32},{104,40},{112,48},{120,56},{... | collective-permute-start | bytes 589832 | tf_op jit(solution)/shard_map/ppermute | solution.py:15
  378.8 6.0 %collective-permute-start.41 = (f32[128,3,128]{2,0,1:T(8,128)}, f32[128,3,128]{2,0,1:T(8,128)S(1)}, u32[]{:S(2)}, u32[]{:S(2)}) collective-permute-start(f32[128,3,128]{2,0,1:T(8,128)} %get-tuple-element.36), channel_id=1, source_target_pairs={{0,32},{8,40},{16,48},{24,56},{32,64},{40,72},{48,80},{56,88},{64,... | collective-permute-start | bytes 589832 | tf_op jit(solution)/shard_map/ppermute | solution.py:15
  384.8 4.0 collective-permute-start.40
  388.9 3.9 collective-permute-start.39
  392.8 9.9 %collective-permute-done.43 = f32[128,3,128]{2,0,1:T(8,128)} collective-permute-done((f32[128,3,128]{2,0,1:T(8,128)}, f32[128,3,128]{2,0,1:T(8,128)}, u32[]{:S(2)}, u32[]{:S(2)}) %collective-permute-start.43) | collective-permute-done | bytes 196640 | tf_op jit(solution)/shard_map/ppermute | solution.py:15
  404.7 15.0 %collective-permute-start.37 = (f32[128,3,128]{2,0,1:T(8,128)S(1)}, f32[128,3,128]{2,0,1:T(8,128)}, u32[]{:S(2)}, u32[]{:S(2)}) collective-permute-start(f32[128,3,128]{2,0,1:T(8,128)S(1)} %get-tuple-element.40), channel_id=1, source_target_pairs={{0,8},{8,16},{16,24},{24,32},{32,40},{40,48},{48,56},{56,64},{64,7... | collective-permute-start | bytes 589832 | tf_op jit(solution)/shard_map/ppermute | solution.py:15
  422.6 2.2 collective-permute-done.38
  424.8 12.7 %collective-permute-done.37 = f32[128,3,128]{2,0,1:T(8,128)} collective-permute-done((f32[128,3,128]{2,0,1:T(8,128)S(1)}, f32[128,3,128]{2,0,1:T(8,128)}, u32[]{:S(2)}, u32[]{:S(2)}) %collective-permute-start.37) | collective-permute-done | bytes 196640 | tf_op jit(solution)/shard_map/ppermute | solution.py:15
  437.5 2.3 fusion.65
  (157 shorter events, 72.2 us)
Async XLA Ops:
  0.7 227.1 %collective-permute-start.22 = (bf16[128,3,128]{2,0,1:T(8,128)(2,1)}, bf16[128,3,128]{2,0,1:T(8,128)(2,1)S(1)}, u32[]{:S(2)}, u32[]{:S(2)}) collective-permute-start(bf16[128,3,128]{2,0,1:T(8,128)(2,1)} %param.9), channel_id=1, source_target_pairs={{0,256},{8,264},{16,272},{24,280},{32,288},{40,296},{48,304},{56,3... | collective-permute-start | bytes 294920 | tf_op jit(solution)/shard_map/ppermute | solution.py:15
  2.1 225.7 %collective-permute-start.21 = (bf16[128,3,128]{2,0,1:T(8,128)(2,1)}, bf16[128,3,128]{2,0,1:T(8,128)(2,1)S(1)}, u32[]{:S(2)}, u32[]{:S(2)}) collective-permute-start(bf16[128,3,128]{2,0,1:T(8,128)(2,1)} %param.9), channel_id=1, source_target_pairs={{128,0},{136,8},{144,16},{152,24},{160,32},{168,40},{176,48},{184,... | collective-permute-start | bytes 294920 | tf_op jit(solution)/shard_map/ppermute | solution.py:15
  4.5 223.2 %collective-permute-start.20 = (bf16[128,3,128]{2,0,1:T(8,128)(2,1)}, bf16[128,3,128]{2,0,1:T(8,128)(2,1)S(1)}, u32[]{:S(2)}, u32[]{:S(2)}) collective-permute-start(bf16[128,3,128]{2,0,1:T(8,128)(2,1)} %param.9), channel_id=1, source_target_pairs={{0,128},{8,136},{16,144},{24,152},{32,160},{40,168},{48,176},{56,1... | collective-permute-start | bytes 294920 | tf_op jit(solution)/shard_map/ppermute | solution.py:15
  5.8 221.8 %collective-permute-start.19 = (bf16[128,3,128]{2,0,1:T(8,128)(2,1)}, bf16[128,3,128]{2,0,1:T(8,128)(2,1)S(1)}, u32[]{:S(2)}, u32[]{:S(2)}) collective-permute-start(bf16[128,3,128]{2,0,1:T(8,128)(2,1)} %param.9), channel_id=1, source_target_pairs={{64,0},{72,8},{80,16},{88,24},{96,32},{104,40},{112,48},{120,56},{... | collective-permute-start | bytes 294920 | tf_op jit(solution)/shard_map/ppermute | solution.py:15
  40.8 14.2 %collective-permute-start = (bf16[128,3,128]{0,2,1:T(8,128)(2,1)S(1)}, bf16[128,3,128]{0,2,1:T(8,128)(2,1)S(1)}, u32[]{:S(2)}, u32[]{:S(2)}) collective-permute-start(bf16[128,3,128]{0,2,1:T(8,128)(2,1)S(1)} %get-tuple-element.28), channel_id=1, source_target_pairs={{0,8},{8,16},{16,24},{24,32},{32,40},{40,48},{48,56},{56,64},{64,7... | collective-permute-start | bytes 294920 | tf_op jit(solution)/shard_map/ppermute | solution.py:15
  55.0 6.4 %collective-permute-start.1 = (bf16[128,3,128]{0,2,1:T(8,128)(2,1)S(1)}, bf16[128,3,128]{0,2,1:T(8,128)(2,1)S(1)}, u32[]{:S(2)}, u32[]{:S(2)}) collective-permute-start(bf16[128,3,128]{0,2,1:T(8,128)(2,1)S(1)} %get-tuple-element.28), channel_id=1, source_target_pairs={{8,0},{16,8},{24,16},{32,24},{40,32},{48,40},{56,48},{64,56},{72,6... | collective-permute-start | bytes 294920 | tf_op jit(solution)/shard_map/ppermute | solution.py:15
  61.4 8.5 %collective-permute-start.2 = (bf16[128,3,128]{0,2,1:T(8,128)(2,1)S(1)}, bf16[128,3,128]{0,2,1:T(8,128)(2,1)S(1)}, u32[]{:S(2)}, u32[]{:S(2)}) collective-permute-start(bf16[128,3,128]{0,2,1:T(8,128)(2,1)S(1)} %get-tuple-element.28), channel_id=1, source_target_pairs={{0,16},{8,24},{16,32},{24,40},{32,48},{40,56},{48,64},{56,72},{64,... | collective-permute-start | bytes 294920 | tf_op jit(solution)/shard_map/ppermute | solution.py:15
  69.8 6.3 %collective-permute-start.3 = (bf16[128,3,128]{0,2,1:T(8,128)(2,1)S(1)}, bf16[128,3,128]{0,2,1:T(8,128)(2,1)S(1)}, u32[]{:S(2)}, u32[]{:S(2)}) collective-permute-start(bf16[128,3,128]{0,2,1:T(8,128)(2,1)S(1)} %get-tuple-element.28), channel_id=1, source_target_pairs={{16,0},{24,8},{32,16},{40,24},{48,32},{56,40},{64,48},{72,56},{80,... | collective-permute-start | bytes 294920 | tf_op jit(solution)/shard_map/ppermute | solution.py:15
  76.1 13.4 %collective-permute-start.4 = (bf16[128,3,128]{0,2,1:T(8,128)(2,1)S(1)}, bf16[128,3,128]{0,2,1:T(8,128)(2,1)S(1)}, u32[]{:S(2)}, u32[]{:S(2)}) collective-permute-start(bf16[128,3,128]{0,2,1:T(8,128)(2,1)S(1)} %get-tuple-element.28), channel_id=1, source_target_pairs={{0,32},{8,40},{16,48},{24,56},{32,64},{40,72},{48,80},{56,88},{64,... | collective-permute-start | bytes 294920 | tf_op jit(solution)/shard_map/ppermute | solution.py:15
  89.6 10.7 %collective-permute-start.5 = (bf16[128,3,128]{0,2,1:T(8,128)(2,1)S(1)}, bf16[128,3,128]{0,2,1:T(8,128)(2,1)S(1)}, u32[]{:S(2)}, u32[]{:S(2)}) collective-permute-start(bf16[128,3,128]{0,2,1:T(8,128)(2,1)S(1)} %get-tuple-element.28), channel_id=1, source_target_pairs={{32,0},{40,8},{48,16},{56,24},{64,32},{72,40},{80,48},{88,56},{96,... | collective-permute-start | bytes 294920 | tf_op jit(solution)/shard_map/ppermute | solution.py:15
  100.2 15.0 %collective-permute-start.6 = (bf16[128,3,128]{0,2,1:T(8,128)(2,1)S(1)}, bf16[128,3,128]{0,2,1:T(8,128)(2,1)S(1)}, u32[]{:S(2)}, u32[]{:S(2)}) collective-permute-start(bf16[128,3,128]{0,2,1:T(8,128)(2,1)S(1)} %get-tuple-element.28), channel_id=1, source_target_pairs={{0,64},{8,72},{16,80},{24,88},{32,96},{40,104},{48,112},{56,120},{... | collective-permute-start | bytes 294920 | tf_op jit(solution)/shard_map/ppermute | solution.py:15
  115.2 14.1 %collective-permute-start.7 = (bf16[128,3,128]{0,2,1:T(8,128)(2,1)S(1)}, bf16[128,3,128]{0,2,1:T(8,128)(2,1)S(1)}, u32[]{:S(2)}, u32[]{:S(2)}) collective-permute-start(bf16[128,3,128]{0,2,1:T(8,128)(2,1)S(1)} %get-tuple-element.28), channel_id=1, source_target_pairs={{64,0},{72,8},{80,16},{88,24},{96,32},{104,40},{112,48},{120,56},{... | collective-permute-start | bytes 294920 | tf_op jit(solution)/shard_map/ppermute | solution.py:15
  129.2 5.4 %collective-permute-start.8 = (bf16[128,3,128]{0,2,1:T(8,128)(2,1)S(1)}, bf16[128,3,128]{0,2,1:T(8,128)(2,1)S(1)}, u32[]{:S(2)}, u32[]{:S(2)}) collective-permute-start(bf16[128,3,128]{0,2,1:T(8,128)(2,1)S(1)} %get-tuple-element.28), channel_id=1, source_target_pairs={{0,128},{8,136},{16,144},{24,152},{32,160},{40,168},{48,176},{56,1... | collective-permute-start | bytes 294920 | tf_op jit(solution)/shard_map/ppermute | solution.py:15
  134.6 5.0 %collective-permute-start.9 = (bf16[128,3,128]{0,2,1:T(8,128)(2,1)S(1)}, bf16[128,3,128]{0,2,1:T(8,128)(2,1)S(1)}, u32[]{:S(2)}, u32[]{:S(2)}) collective-permute-start(bf16[128,3,128]{0,2,1:T(8,128)(2,1)S(1)} %get-tuple-element.28), channel_id=1, source_target_pairs={{128,0},{136,8},{144,16},{152,24},{160,32},{168,40},{176,48},{184,... | collective-permute-start | bytes 294920 | tf_op jit(solution)/shard_map/ppermute | solution.py:15
  139.6 6.9 %collective-permute-start.10 = (bf16[128,3,128]{0,2,1:T(8,128)(2,1)S(1)}, bf16[128,3,128]{0,2,1:T(8,128)(2,1)S(1)}, u32[]{:S(2)}, u32[]{:S(2)}) collective-permute-start(bf16[128,3,128]{0,2,1:T(8,128)(2,1)S(1)} %get-tuple-element.28), channel_id=1, source_target_pairs={{0,256},{8,264},{16,272},{24,280},{32,288},{40,296},{48,304},{56,3... | collective-permute-start | bytes 294920 | tf_op jit(solution)/shard_map/ppermute | solution.py:15
  146.5 3.2 collective-permute-start.11
  149.6 8.8 %collective-permute-start.12 = (bf16[128,3,128]{2,0,1:T(8,128)(2,1)S(1)}, bf16[128,3,128]{2,0,1:T(8,128)(2,1)S(1)}, u32[]{:S(2)}, u32[]{:S(2)}) collective-permute-start(bf16[128,3,128]{2,0,1:T(8,128)(2,1)S(1)} %copy-done.10), channel_id=1, source_target_pairs={{0,8},{8,16},{16,24},{24,32},{32,40},{40,48},{48,56},{56,64},{64,7... | collective-permute-start | bytes 294920 | tf_op jit(solution)/shard_map/ppermute | solution.py:15
  158.5 5.3 %collective-permute-start.13 = (bf16[128,3,128]{2,0,1:T(8,128)(2,1)S(1)}, bf16[128,3,128]{2,0,1:T(8,128)(2,1)S(1)}, u32[]{:S(2)}, u32[]{:S(2)}) collective-permute-start(bf16[128,3,128]{2,0,1:T(8,128)(2,1)S(1)} %copy-done.10), channel_id=1, source_target_pairs={{8,0},{16,8},{24,16},{32,24},{40,32},{48,40},{56,48},{64,56},{72,6... | collective-permute-start | bytes 294920 | tf_op jit(solution)/shard_map/ppermute | solution.py:15
  163.8 8.5 %collective-permute-start.14 = (bf16[128,3,128]{2,0,1:T(8,128)(2,1)S(1)}, bf16[128,3,128]{2,0,1:T(8,128)(2,1)S(1)}, u32[]{:S(2)}, u32[]{:S(2)}) collective-permute-start(bf16[128,3,128]{2,0,1:T(8,128)(2,1)S(1)} %copy-done.10), channel_id=1, source_target_pairs={{0,16},{8,24},{16,32},{24,40},{32,48},{40,56},{48,64},{56,72},{64,... | collective-permute-start | bytes 294920 | tf_op jit(solution)/shard_map/ppermute | solution.py:15
  172.3 6.3 %collective-permute-start.15 = (bf16[128,3,128]{2,0,1:T(8,128)(2,1)S(1)}, bf16[128,3,128]{2,0,1:T(8,128)(2,1)S(1)}, u32[]{:S(2)}, u32[]{:S(2)}) collective-permute-start(bf16[128,3,128]{2,0,1:T(8,128)(2,1)S(1)} %copy-done.10), channel_id=1, source_target_pairs={{16,0},{24,8},{32,16},{40,24},{48,32},{56,40},{64,48},{72,56},{80,... | collective-permute-start | bytes 294920 | tf_op jit(solution)/shard_map/ppermute | solution.py:15
  178.6 12.7 %collective-permute-start.16 = (bf16[128,3,128]{2,0,1:T(8,128)(2,1)S(1)}, bf16[128,3,128]{2,0,1:T(8,128)(2,1)S(1)}, u32[]{:S(2)}, u32[]{:S(2)}) collective-permute-start(bf16[128,3,128]{2,0,1:T(8,128)(2,1)S(1)} %copy-done.10), channel_id=1, source_target_pairs={{0,32},{8,40},{16,48},{24,56},{32,64},{40,72},{48,80},{56,88},{64,... | collective-permute-start | bytes 294920 | tf_op jit(solution)/shard_map/ppermute | solution.py:15
  191.3 11.8 %collective-permute-start.17 = (bf16[128,3,128]{2,0,1:T(8,128)(2,1)S(1)}, bf16[128,3,128]{2,0,1:T(8,128)(2,1)S(1)}, u32[]{:S(2)}, u32[]{:S(2)}) collective-permute-start(bf16[128,3,128]{2,0,1:T(8,128)(2,1)S(1)} %copy-done.10), channel_id=1, source_target_pairs={{32,0},{40,8},{48,16},{56,24},{64,32},{72,40},{80,48},{88,56},{96,... | collective-permute-start | bytes 294920 | tf_op jit(solution)/shard_map/ppermute | solution.py:15
  203.1 15.9 %collective-permute-start.18 = (bf16[128,3,128]{2,0,1:T(8,128)(2,1)S(1)}, bf16[128,3,128]{2,0,1:T(8,128)(2,1)S(1)}, u32[]{:S(2)}, u32[]{:S(2)}) collective-permute-start(bf16[128,3,128]{2,0,1:T(8,128)(2,1)S(1)} %copy-done.10), channel_id=1, source_target_pairs={{0,64},{8,72},{16,80},{24,88},{32,96},{40,104},{48,112},{56,120},{... | collective-permute-start | bytes 294920 | tf_op jit(solution)/shard_map/ppermute | solution.py:15
  218.9 10.3 %collective-permute-start.23 = (bf16[128,3,128]{2,0,1:T(8,128)(2,1)S(1)}, bf16[128,3,128]{2,0,1:T(8,128)(2,1)S(1)}, u32[]{:S(2)}, u32[]{:S(2)}) collective-permute-start(bf16[128,3,128]{2,0,1:T(8,128)(2,1)S(1)} %copy-done.10), channel_id=1, source_target_pairs={{256,0},{264,8},{272,16},{280,24},{288,32},{296,40},{304,48},{312,... | collective-permute-start | bytes 294920 | tf_op jit(solution)/shard_map/ppermute | solution.py:15
  235.7 16.8 %collective-permute-start.24 = (f32[128,3,128]{0,2,1:T(8,128)S(1)}, f32[128,3,128]{0,2,1:T(8,128)S(1)}, u32[]{:S(2)}, u32[]{:S(2)}) collective-permute-start(f32[128,3,128]{0,2,1:T(8,128)S(1)} %get-tuple-element.41), channel_id=1, source_target_pairs={{8,0},{16,8},{24,16},{32,24},{40,32},{48,40},{56,48},{64,56},{72,6... | collective-permute-start | bytes 589832 | tf_op jit(solution)/shard_map/ppermute | solution.py:15
  237.6 17.6 %collective-permute-start.35 = (f32[128,3,128]{0,2,1:T(8,128)S(1)}, f32[128,3,128]{0,2,1:T(8,128)S(1)}, u32[]{:S(2)}, u32[]{:S(2)}) collective-permute-start(f32[128,3,128]{0,2,1:T(8,128)S(1)} %get-tuple-element.42), channel_id=1, source_target_pairs={{0,256},{8,264},{16,272},{24,280},{32,288},{40,296},{48,304},{56,3... | collective-permute-start | bytes 589832 | tf_op jit(solution)/shard_map/ppermute | solution.py:15
  238.9 29.2 %collective-permute-start.34 = (f32[128,3,128]{0,2,1:T(8,128)S(1)}, f32[128,3,128]{0,2,1:T(8,128)S(1)}, u32[]{:S(2)}, u32[]{:S(2)}) collective-permute-start(f32[128,3,128]{0,2,1:T(8,128)S(1)} %get-tuple-element.43), channel_id=1, source_target_pairs={{256,0},{264,8},{272,16},{280,24},{288,32},{296,40},{304,48},{312,... | collective-permute-start | bytes 589832 | tf_op jit(solution)/shard_map/ppermute | solution.py:15
  244.7 28.1 %collective-permute-start.33 = (f32[128,3,128]{0,2,1:T(8,128)S(1)}, f32[128,3,128]{0,2,1:T(8,128)S(1)}, u32[]{:S(2)}, u32[]{:S(2)}) collective-permute-start(f32[128,3,128]{0,2,1:T(8,128)S(1)} %get-tuple-element.44), channel_id=1, source_target_pairs={{0,128},{8,136},{16,144},{24,152},{32,160},{40,168},{48,176},{56,1... | collective-permute-start | bytes 589832 | tf_op jit(solution)/shard_map/ppermute | solution.py:15
  246.0 32.3 %collective-permute-start.32 = (f32[128,3,128]{0,2,1:T(8,128)S(1)}, f32[128,3,128]{0,2,1:T(8,128)S(1)}, u32[]{:S(2)}, u32[]{:S(2)}) collective-permute-start(f32[128,3,128]{0,2,1:T(8,128)S(1)} %get-tuple-element.45), channel_id=1, source_target_pairs={{128,0},{136,8},{144,16},{152,24},{160,32},{168,40},{176,48},{184,... | collective-permute-start | bytes 589832 | tf_op jit(solution)/shard_map/ppermute | solution.py:15
  252.5 27.8 %collective-permute-start.31 = (f32[128,3,128]{0,2,1:T(8,128)S(1)}, f32[128,3,128]{0,2,1:T(8,128)S(1)}, u32[]{:S(2)}, u32[]{:S(2)}) collective-permute-start(f32[128,3,128]{0,2,1:T(8,128)S(1)} %get-tuple-element.46), channel_id=1, source_target_pairs={{0,64},{8,72},{16,80},{24,88},{32,96},{40,104},{48,112},{56,120},{... | collective-permute-start | bytes 589832 | tf_op jit(solution)/shard_map/ppermute | solution.py:15
  255.2 31.4 %collective-permute-start.30 = (f32[128,3,128]{0,2,1:T(8,128)S(1)}, f32[128,3,128]{0,2,1:T(8,128)S(1)}, u32[]{:S(2)}, u32[]{:S(2)}) collective-permute-start(f32[128,3,128]{0,2,1:T(8,128)S(1)} %get-tuple-element.47), channel_id=1, source_target_pairs={{64,0},{72,8},{80,16},{88,24},{96,32},{104,40},{112,48},{120,56},{... | collective-permute-start | bytes 589832 | tf_op jit(solution)/shard_map/ppermute | solution.py:15
  268.1 23.2 %collective-permute-start.29 = (f32[128,3,128]{0,2,1:T(8,128)}, f32[128,3,128]{0,2,1:T(8,128)}, u32[]{:S(2)}, u32[]{:S(2)}) collective-permute-start(f32[128,3,128]{0,2,1:T(8,128)} %get-tuple-element.48), channel_id=1, source_target_pairs={{0,32},{8,40},{16,48},{24,56},{32,64},{40,72},{48,80},{56,88},{64,... | collective-permute-start | bytes 589832 | tf_op jit(solution)/shard_map/ppermute | solution.py:15
  272.8 22.8 %collective-permute-start.28 = (f32[128,3,128]{0,2,1:T(8,128)}, f32[128,3,128]{0,2,1:T(8,128)}, u32[]{:S(2)}, u32[]{:S(2)}) collective-permute-start(f32[128,3,128]{0,2,1:T(8,128)} %get-tuple-element.49), channel_id=1, source_target_pairs={{32,0},{40,8},{48,16},{56,24},{64,32},{72,40},{80,48},{88,56},{96,... | collective-permute-start | bytes 589832 | tf_op jit(solution)/shard_map/ppermute | solution.py:15
  278.3 22.6 %collective-permute-start.27 = (f32[128,3,128]{0,2,1:T(8,128)}, f32[128,3,128]{0,2,1:T(8,128)}, u32[]{:S(2)}, u32[]{:S(2)}) collective-permute-start(f32[128,3,128]{0,2,1:T(8,128)} %get-tuple-element.50), channel_id=1, source_target_pairs={{0,16},{8,24},{16,32},{24,40},{32,48},{40,56},{48,64},{56,72},{64,... | collective-permute-start | bytes 589832 | tf_op jit(solution)/shard_map/ppermute | solution.py:15
  280.2 23.9 %collective-permute-start.26 = (f32[128,3,128]{0,2,1:T(8,128)}, f32[128,3,128]{0,2,1:T(8,128)}, u32[]{:S(2)}, u32[]{:S(2)}) collective-permute-start(f32[128,3,128]{0,2,1:T(8,128)} %get-tuple-element.51), channel_id=1, source_target_pairs={{16,0},{24,8},{32,16},{40,24},{48,32},{56,40},{64,48},{72,56},{80,... | collective-permute-start | bytes 589832 | tf_op jit(solution)/shard_map/ppermute | solution.py:15
  286.6 33.4 %collective-permute-start.25 = (f32[128,3,128]{0,2,1:T(8,128)}, f32[128,3,128]{0,2,1:T(8,128)}, u32[]{:S(2)}, u32[]{:S(2)}) collective-permute-start(f32[128,3,128]{0,2,1:T(8,128)} %get-tuple-element.52), channel_id=1, source_target_pairs={{0,8},{8,16},{16,24},{24,32},{32,40},{40,48},{48,56},{56,64},{64,7... | collective-permute-start | bytes 589832 | tf_op jit(solution)/shard_map/ppermute | solution.py:15
  291.3 71.7 %collective-permute-start.36 = (f32[128,3,128]{2,0,1:T(8,128)}, f32[128,3,128]{2,0,1:T(8,128)}, u32[]{:S(2)}, u32[]{:S(2)}) collective-permute-start(f32[128,3,128]{2,0,1:T(8,128)} %get-tuple-element.29), channel_id=1, source_target_pairs={{8,0},{16,8},{24,16},{32,24},{40,32},{48,40},{56,48},{64,56},{72,6... | collective-permute-start | bytes 589832 | tf_op jit(solution)/shard_map/ppermute | solution.py:15
  295.5 76.0 %collective-permute-start.47 = (f32[128,3,128]{2,0,1:T(8,128)S(1)}, f32[128,3,128]{2,0,1:T(8,128)}, u32[]{:S(2)}, u32[]{:S(2)}) collective-permute-start(f32[128,3,128]{2,0,1:T(8,128)S(1)} %get-tuple-element.30), channel_id=1, source_target_pairs={{0,256},{8,264},{16,272},{24,280},{32,288},{40,296},{48,304},{56,3... | collective-permute-start | bytes 589832 | tf_op jit(solution)/shard_map/ppermute | solution.py:15
  300.9 77.9 %collective-permute-start.46 = (f32[128,3,128]{2,0,1:T(8,128)}, f32[128,3,128]{2,0,1:T(8,128)}, u32[]{:S(2)}, u32[]{:S(2)}) collective-permute-start(f32[128,3,128]{2,0,1:T(8,128)} %get-tuple-element.31), channel_id=1, source_target_pairs={{256,0},{264,8},{272,16},{280,24},{288,32},{296,40},{304,48},{312,... | collective-permute-start | bytes 589832 | tf_op jit(solution)/shard_map/ppermute | solution.py:15
  304.2 80.6 %collective-permute-start.45 = (f32[128,3,128]{2,0,1:T(8,128)}, f32[128,3,128]{2,0,1:T(8,128)}, u32[]{:S(2)}, u32[]{:S(2)}) collective-permute-start(f32[128,3,128]{2,0,1:T(8,128)} %get-tuple-element.32), channel_id=1, source_target_pairs={{0,128},{8,136},{16,144},{24,152},{32,160},{40,168},{48,176},{56,1... | collective-permute-start | bytes 589832 | tf_op jit(solution)/shard_map/ppermute | solution.py:15
  320.0 68.8 %collective-permute-start.44 = (f32[128,3,128]{2,0,1:T(8,128)}, f32[128,3,128]{2,0,1:T(8,128)}, u32[]{:S(2)}, u32[]{:S(2)}) collective-permute-start(f32[128,3,128]{2,0,1:T(8,128)} %get-tuple-element.33), channel_id=1, source_target_pairs={{128,0},{136,8},{144,16},{152,24},{160,32},{168,40},{176,48},{184,... | collective-permute-start | bytes 589832 | tf_op jit(solution)/shard_map/ppermute | solution.py:15
  363.0 39.7 %collective-permute-start.43 = (f32[128,3,128]{2,0,1:T(8,128)}, f32[128,3,128]{2,0,1:T(8,128)}, u32[]{:S(2)}, u32[]{:S(2)}) collective-permute-start(f32[128,3,128]{2,0,1:T(8,128)} %get-tuple-element.34), channel_id=1, source_target_pairs={{0,64},{8,72},{16,80},{24,88},{32,96},{40,104},{48,112},{56,120},{... | collective-permute-start | bytes 589832 | tf_op jit(solution)/shard_map/ppermute | solution.py:15
  371.5 33.2 %collective-permute-start.42 = (f32[128,3,128]{2,0,1:T(8,128)}, f32[128,3,128]{2,0,1:T(8,128)}, u32[]{:S(2)}, u32[]{:S(2)}) collective-permute-start(f32[128,3,128]{2,0,1:T(8,128)} %get-tuple-element.35), channel_id=1, source_target_pairs={{64,0},{72,8},{80,16},{88,24},{96,32},{104,40},{112,48},{120,56},{... | collective-permute-start | bytes 589832 | tf_op jit(solution)/shard_map/ppermute | solution.py:15
  378.8 41.8 %collective-permute-start.41 = (f32[128,3,128]{2,0,1:T(8,128)}, f32[128,3,128]{2,0,1:T(8,128)S(1)}, u32[]{:S(2)}, u32[]{:S(2)}) collective-permute-start(f32[128,3,128]{2,0,1:T(8,128)} %get-tuple-element.36), channel_id=1, source_target_pairs={{0,32},{8,40},{16,48},{24,56},{32,64},{40,72},{48,80},{56,88},{64,... | collective-permute-start | bytes 589832 | tf_op jit(solution)/shard_map/ppermute | solution.py:15
  384.8 35.7 %collective-permute-start.40 = (f32[128,3,128]{2,0,1:T(8,128)}, f32[128,3,128]{2,0,1:T(8,128)S(1)}, u32[]{:S(2)}, u32[]{:S(2)}) collective-permute-start(f32[128,3,128]{2,0,1:T(8,128)} %get-tuple-element.37), channel_id=1, source_target_pairs={{32,0},{40,8},{48,16},{56,24},{64,32},{72,40},{80,48},{88,56},{96,... | collective-permute-start | bytes 589832 | tf_op jit(solution)/shard_map/ppermute | solution.py:15
  388.9 33.7 %collective-permute-start.39 = (f32[128,3,128]{2,0,1:T(8,128)}, f32[128,3,128]{2,0,1:T(8,128)}, u32[]{:S(2)}, u32[]{:S(2)}) collective-permute-start(f32[128,3,128]{2,0,1:T(8,128)} %get-tuple-element.38), channel_id=1, source_target_pairs={{0,16},{8,24},{16,32},{24,40},{32,48},{40,56},{48,64},{56,72},{64,... | collective-permute-start | bytes 589832 | tf_op jit(solution)/shard_map/ppermute | solution.py:15
  402.8 22.0 %collective-permute-start.38 = (f32[128,3,128]{2,0,1:T(8,128)}, f32[128,3,128]{2,0,1:T(8,128)}, u32[]{:S(2)}, u32[]{:S(2)}) collective-permute-start(f32[128,3,128]{2,0,1:T(8,128)} %get-tuple-element.39), channel_id=1, source_target_pairs={{16,0},{24,8},{32,16},{40,24},{48,32},{56,40},{64,48},{72,56},{80,... | collective-permute-start | bytes 589832 | tf_op jit(solution)/shard_map/ppermute | solution.py:15
  404.7 32.8 %collective-permute-start.37 = (f32[128,3,128]{2,0,1:T(8,128)S(1)}, f32[128,3,128]{2,0,1:T(8,128)}, u32[]{:S(2)}, u32[]{:S(2)}) collective-permute-start(f32[128,3,128]{2,0,1:T(8,128)S(1)} %get-tuple-element.40), channel_id=1, source_target_pairs={{0,8},{8,16},{16,24},{24,32},{32,40},{40,48},{48,56},{56,64},{64,7... | collective-permute-start | bytes 589832 | tf_op jit(solution)/shard_map/ppermute | solution.py:15
  (16 other events, 343.5 us)
where the time goes:
time: 442 us; the launch traced here: 440 us
  starting transfers between devices  188 us (43%)
  waiting for transfers between devices  164 us (37%)
  blocking collectives  51.3 us (12%)
  local copies, waits for them, and re-layouts  10.5 us (2%)
  other arithmetic  10.2 us (2%)
  between operations  10 us (2%)
  matrix products  6.25 us (1%)
    ppermute x48, starting transfers between devices, passed_along(): lax.ppermute(value, axis, [(source, source + steps) for source in range(l...  188 us
    ppermute x48, waiting for transfers between devices, passed_along(): lax.ppermute(value, axis, [(source, source + steps) for source in range(l...  164 us
    psum x1, blocking collectives, per_device(): lax.psum((jnp.sum(query_floats * query_scaled, axis=(1, 2)), jnp.sum(key_...  37.9 us
    psum x1, blocking collectives, per_device(): lax.psum((jnp.sum(query_floats * query_floats, axis=(1, 2)), jnp.sum(key_...  13.5 us
  transfers between devices with their start and end apart: 48, of which 26 were waited for; matrix products, arithmetic and copies ran while one was open for 4% of the time, Pallas kernels for 0%

commit v1 on v0

v1 whole, which is shorter than its diff:
```python
import functools

import jax
import jax.numpy as jnp
from jax import lax
from jax.experimental import pallas as pl
from jax.experimental.pallas import tpu as pltpu
from jax.sharding import Mesh, PartitionSpec as P

TILE = 128
EPS = 1e-06
OFFSETS = (0, -1, 1, -2, 2, -4, 4, -8, 8, -16, 16, -32, 32)
NT = (((1,), (1,)), ((), ()))
NN = (((1,), (0,)), ((), ()))
F32 = jnp.float32
BF16 = jnp.bfloat16
VMEM_LIMIT = 48 * 1024 * 1024


def dot(left, right, dims):
    return lax.dot_general(left, right, dims, preferred_element_type=F32)


def row_sums(square):
    ones = jnp.ones((8, TILE), BF16)
    high = square.astype(BF16)
    low = (square - high.astype(F32)).astype(BF16)
    return dot(ones, high, NT) + dot(ones, low, NT)


def columns(rows):
    fill = jnp.zeros((TILE - rows.shape[0], TILE), F32)
    return jnp.transpose(jnp.concatenate([rows, fill], axis=0))


def squares_kernel(heads, q_ref, *refs):
    tiles, out_ref = refs[:-1], refs[-1]
    for place, ref in enumerate(tiles + (q_ref,)):
        total = jnp.zeros((TILE, TILE), F32)
        for head in range(heads):
            floats = ref[head].astype(F32)
            total = total + floats * floats
        out_ref[place : place + 1, :] = row_sums(total)[0:1]
    out_ref[len(tiles) + 1 :, :] = jnp.zeros((16 - len(tiles) - 1, TILE), F32)


def forward_kernel(
    heads, channels, listed_ref, sums_ref, q_ref, do_ref, qg_ref, kg_ref, *refs
):
    count = len(OFFSETS)
    tiles = refs[:count]
    out_ref, dq_ref, kn_ref, stat_refs = refs[count], refs[count + 1], refs[count + 2], refs[count + 3 : -3]
    norm_ref, work_ref, part_ref = refs[-3:]
    scale = TILE ** (-0.5)
    inverse = lax.rsqrt(sums_ref[...] / channels + EPS)
    turned = columns(inverse)
    usable = [listed_ref[0, t] >= 0 for t in range(count)]
    lane = lax.broadcasted_iota(jnp.int32, (TILE, TILE), 1)
    stats = jnp.zeros((TILE, TILE), F32)
    query_terms = jnp.zeros((TILE, TILE), F32)
    for head in range(heads):
        query = (
            q_ref[head].astype(F32) * turned[:, count : count + 1] * qg_ref[head : head + 1]
        ).astype(BF16)
        upstream = do_ref[head]
        top = jnp.full((TILE, TILE), -1e30, F32)
        for t in range(count):
            key = (
                tiles[t][head].astype(F32) * turned[:, t : t + 1] * kg_ref[head : head + 1]
            ).astype(BF16)
            norm_ref[t] = key
            if t == 0:
                kn_ref[head] = key
            score = dot(query, key, NT) * scale
            score = jnp.where(usable[t], score, -1e30)
            work_ref[t] = score
            top = jnp.maximum(top, score)
        top = jnp.max(top, axis=1, keepdims=True)
        total = jnp.zeros((TILE, TILE), F32)
        for t in range(count):
            total = total + jnp.exp(work_ref[t] - top)
        total = jnp.sum(total, axis=1, keepdims=True)
        level = top + jnp.log(total)
        share = 1.0 / total
        out = jnp.zeros((TILE, TILE), F32)
        for t in range(count):
            prob = jnp.exp(work_ref[t] - top) * share
            out = out + dot(prob.astype(BF16), tiles[t][heads + head], NN)
        out = out.astype(BF16)
        out_ref[head] = out
        delta = jnp.sum(
            upstream.astype(F32) * out.astype(F32), axis=1, keepdims=True
        )
        query_grad = jnp.zeros((TILE, TILE), F32)
        for t in range(count):
            score = work_ref[t]
            prob = jnp.exp(score - top) * share
            dscore = (prob * (dot(upstream, tiles[t][heads + head], NT) - delta)).astype(BF16)
            query_grad = query_grad + dot(dscore, norm_ref[t], NN)
            term = dscore.astype(F32) * score
            query_terms = query_terms + term
            term = jnp.sum(term, axis=0, keepdims=True)
            if head:
                term = term + part_ref[t : t + 1, :]
            part_ref[t : t + 1, :] = term
        dq_ref[head] = query_grad * scale
        stats = jnp.where(lane == head, level, stats)
        stats = jnp.where(lane == heads + head, delta, stats)
    query_total = jnp.sum(query_terms, axis=1, keepdims=True)
    stats = jnp.where(lane == 2 * heads + 1, query_total, stats)
    rows = jnp.transpose(stats)[0:8]
    place = lax.broadcasted_iota(jnp.int32, (8, TILE), 0)
    rows = jnp.where(place == 2 * heads, inverse[count : count + 1], rows)
    stat_refs[0][...] = rows
    for t in range(1, count):
        stat_refs[t][...] = jnp.where(place == 2 * heads + 1, part_ref[t : t + 1, :], rows)
    stat_refs[count][...] = jnp.where(
        place == 0, rows[2 * heads + 1 : 2 * heads + 2], jnp.where(place == 1, part_ref[0:1, :], 0.0)
    )


def backward_kernel(heads, listed_ref, kn_ref, v_ref, qg_ref, *refs):
    count = len(OFFSETS)
    tiles, stat_refs = refs[:count], refs[count : 2 * count]
    dk_ref, dv_ref = refs[-2:]
    scale = TILE ** (-0.5)
    turned = columns(
        jnp.concatenate([ref[2 * heads : 2 * heads + 1] for ref in stat_refs], axis=0)
    )
    usable = [listed_ref[0, t] >= 0 for t in range(count)]
    for head in range(heads):
        key, value = kn_ref[head], v_ref[head]
        key_grad = jnp.zeros((TILE, TILE), F32)
        value_grad = jnp.zeros((TILE, TILE), F32)
        for t in range(count):
            query = (
                tiles[t][head].astype(F32) * turned[:, t : t + 1] * qg_ref[head : head + 1]
            ).astype(BF16)
            upstream = tiles[t][heads + head]
            score = dot(key, query, NT) * scale - stat_refs[t][head : head + 1]
            prob = jnp.exp(jnp.where(usable[t], score, -1e30))
            value_grad = value_grad + dot(prob.astype(BF16), upstream, NN)
            dprob = dot(value, upstream, NT)
            dscore = prob * (dprob - stat_refs[t][heads + head : heads + head + 1])
            key_grad = key_grad + dot(dscore.astype(BF16), query, NN)
        dk_ref[head] = key_grad * scale
        dv_ref[head] = value_grad.astype(BF16)


def final_kernel(
    heads, channels, sums_ref, terms_ref, q_ref, k_ref, dq_ref, dk_ref, qg_ref, kg_ref, gq_ref, gk_ref
):
    count = len(OFFSETS)
    inverse = lax.rsqrt(sums_ref[...] / channels + EPS)
    squared = inverse * inverse / channels
    turned = columns(
        jnp.concatenate(
            [
                inverse[count : count + 1],
                inverse[0:1],
                squared[count : count + 1] * terms_ref[0:1],
                squared[0:1] * terms_ref[1:2],
            ],
            axis=0,
        )
    )
    for head in range(heads):
        gq_ref[head] = (
            turned[:, 0:1] * (qg_ref[head : head + 1] * dq_ref[head])
            - q_ref[head].astype(F32) * turned[:, 2:3]
        ).astype(BF16)
        gk_ref[head] = (
            turned[:, 1:2] * (kg_ref[head : head + 1] * dk_ref[head])
            - k_ref[head].astype(F32) * turned[:, 3:4]
        ).astype(BF16)


def passed(value, steps, count):
    pairs = [(i, i + steps) for i in range(count) if 0 <= i + steps < count]
    return lax.ppermute(value, "seq", pairs)


def spread(value, count):
    got = {0: value}
    for facing in (-1, 1):
        got[16 * facing] = passed(value, -16 * facing, count)
        got[32 * facing] = passed(value, -32 * facing, count)
    for distance in (1, 2, 4, 8):
        for facing in (-1, 1):
            near = distance // 2
            source = got[facing * near] if near else value
            got[facing * distance] = passed(source, -facing * (distance - near), count)
    return [got[offset] for offset in OFFSETS]


def per_device(seq_count, total_heads, q_raw, k_raw, values, grad_out, q_gain, k_gain, key_tiles):
    place = lax.axis_index("seq")
    heads = q_raw.shape[1]
    channels = float(total_heads * q_raw.shape[2])
    q_raw, k_raw, values, grad_out = [
        jnp.transpose(array, (1, 0, 2)) for array in (q_raw, k_raw, values, grad_out)
    ]
    listed = lax.dynamic_slice_in_dim(key_tiles, place, 1, 0)
    first = jnp.concatenate([k_raw, values], axis=0)
    second = jnp.concatenate([q_raw, grad_out], axis=0)
    first_all = spread(first, seq_count)
    second_all = spread(second, seq_count)

    count = len(OFFSETS)
    vmem = pl.BlockSpec(memory_space=pltpu.VMEM)
    smem = pl.BlockSpec(memory_space=pltpu.SMEM)
    params = pltpu.CompilerParams(vmem_limit_bytes=VMEM_LIMIT)
    whole = (heads, TILE, TILE)
    sums = pl.pallas_call(
        functools.partial(squares_kernel, heads),
        out_shape=jax.ShapeDtypeStruct((16, TILE), F32),
        in_specs=[vmem] * (count + 1),
        out_specs=vmem,
        compiler_params=params,
        name="squares",
    )(q_raw, *first_all)
    sums = lax.psum(lax.psum(sums, "c"), "y")
    results = pl.pallas_call(
        functools.partial(forward_kernel, heads, channels),
        out_shape=[
            jax.ShapeDtypeStruct(whole, BF16),
            jax.ShapeDtypeStruct(whole, F32),
            jax.ShapeDtypeStruct(whole, BF16),
        ]
        + [jax.ShapeDtypeStruct((8, TILE), F32)] * (count + 1),
        in_specs=[smem] + [vmem] * (5 + count),
        out_specs=[vmem] * (count + 4),
        scratch_shapes=[
            pltpu.VMEM((count, TILE, TILE), BF16),
            pltpu.VMEM((count, TILE, TILE), F32),
            pltpu.VMEM((16, TILE), F32),
        ],
        compiler_params=params,
        name="forward",
    )(listed, sums, q_raw, grad_out, q_gain, k_gain, *first_all)
    attended, dq, k_norm = results[:3]
    stats = results[3:-1]
    got_stats = [stats[0]] + [
        passed(stat, OFFSETS[t], seq_count) for t, stat in enumerate(stats) if t
    ]
    order = [OFFSETS.index(-offset) for offset in OFFSETS]
    got_stats = [got_stats[at] for at in order]
    own_terms = results[-1]
    key_total = sum(stat[2 * heads + 1] for stat in got_stats[1:]) + own_terms[1]
    terms = jnp.stack([own_terms[0], key_total])
    terms = lax.psum(lax.psum(terms, "c"), "y")
    dk, grad_v = pl.pallas_call(
        functools.partial(backward_kernel, heads),
        out_shape=[jax.ShapeDtypeStruct(whole, F32), jax.ShapeDtypeStruct(whole, BF16)],
        in_specs=[smem] + [vmem] * (3 + 2 * count),
        out_specs=[vmem] * 2,
        compiler_params=params,
        name="backward",
    )(listed, k_norm, values, q_gain, *second_all, *got_stats)
    grad_q, grad_k = pl.pallas_call(
        functools.partial(final_kernel, heads, channels),
        out_shape=[jax.ShapeDtypeStruct(whole, BF16)] * 2,
        in_specs=[vmem] * 8,
        out_specs=[vmem] * 2,
        compiler_params=params,
        name="final",
    )(sums, terms, q_raw, k_raw, dq, dk, q_gain, k_gain)
    return tuple(
        jnp.transpose(array, (1, 0, 2)) for array in (attended, grad_q, grad_k, grad_v)
    )


def solution(mesh):
    shape = dict(mesh.shape)
    cores = 2 if shape["head"] % 2 == 0 else 1
    split = Mesh(
        mesh.devices.reshape(shape["seq"], shape["head"] // cores, cores), ("seq", "y", "c")
    )
    heads = ("y", "c")

    def whole(q_raw, k_raw, values, grad_out, q_gain, k_gain, key_tiles):
        tokens = P("seq", heads, None)
        return jax.shard_map(
            functools.partial(per_device, shape["seq"], q_raw.shape[1]),
            mesh=split,
            in_specs=(tokens,) * 4 + (P(heads, None), P(heads, None), P()),
            out_specs=(tokens,) * 4,
            check_vma=False,
        )(q_raw, k_raw, values, grad_out, q_gain, k_gain, key_tiles)

    return whole
```

time: 442 us -> 204 us (0.46)
  waiting for transfers between devices: 164 us -> 6.21 us
  starting transfers between devices: 188 us -> 144 us
  blocking collectives: 51.3 us -> 28.1 us
  Pallas kernels: 0 us -> 15 us
  other arithmetic: 10.2 us -> 1.05 us
  between operations: 10 us -> 1.34 us
  matrix products: 6.25 us -> 0 us
  local copies, waits for them, and re-layouts: 10.5 us -> 4.96 us
    ppermute x48 -> x36, waiting for transfers between devices: 164 us -> 6.21 us  [passed(): return lax.ppermute(value, 'seq', pairs)]
    ppermute x48 -> x36, starting transfers between devices: 188 us -> 144 us  [passed(): return lax.ppermute(value, 'seq', pairs)]
    psum x2 -> x4, blocking collectives: 51.3 us -> 28.1 us  [the longest x2 15.5 us: per_device(): terms = lax.psum(lax.psum(terms, 'c'), 'y')]
    pallas_call x0 -> x4, Pallas kernels: none -> 15 us  [the longest x1 6.76 us: per_device(): pl.pallas_call(functools.partial(forward_kernel, heads, channels), out_sh...]
    dot_general x18 -> x0, matrix products: 6.25 us -> none  [contract(): lax.dot_general(left, right, (((left_dim,), (right_dim,)), ((), ())), pre...]
  transfers between devices with their start and end apart: 48 -> 36, of which waited for: 26 -> 2; matrix products, arithmetic and copies ran while one was open for 4% -> 0% of each run, Pallas kernels for 0% -> 4%
where the time goes in v1:
time: 204 us; the launch traced here: 200 us
  starting transfers between devices  144 us (71%)
  blocking collectives  28.1 us (14%)
  Pallas kernels  15 us (7%)
  waiting for transfers between devices  6.21 us (3%)
  local copies, waits for them, and re-layouts  4.96 us (2%)
    ppermute x36, starting transfers between devices, passed(): return lax.ppermute(value, 'seq', pairs)  144 us
    psum x2, blocking collectives, per_device(): terms = lax.psum(lax.psum(terms, 'c'), 'y')  15.5 us
    psum x2, blocking collectives, per_device(): sums = lax.psum(lax.psum(sums, 'c'), 'y')  12.6 us
    pallas_call x1, Pallas kernels, per_device(): pl.pallas_call(functools.partial(forward_kernel, heads, channels), out_sh...  6.76 us
    pallas_call x1, Pallas kernels, per_device(): pl.pallas_call(functools.partial(backward_kernel, heads), out_shape=[jax....  6.72 us
    ppermute x36, waiting for transfers between devices, passed(): return lax.ppermute(value, 'seq', pairs)  6.21 us
    unnamed x31, local copies, waits for them, and re-layouts  4.89 us
  transfers between devices with their start and end apart: 36, of which 2 were waited for; matrix products, arithmetic and copies ran while one was open for 0% of the time, Pallas kernels for 4%

profile of v1, /device:TPU:7, one launch (start us, length us, event | category | flops | bytes accessed | tf_op | source)
XLA Modules:
  0.0 200.4 jit_solution(16492834135857761349)
XLA Ops:
  0.7 1.0 pad_maximum_fusion.refs_0_
  1.7 3.5 %collective-permute-start = (bf16[6,128,128]{2,1,0:T(8,128)(2,1)S(1)}, bf16[6,128,128]{2,1,0:T(8,128)(2,1)S(1)}, u32[]{:S(2)}, u32[]{:S(2)}) collective-permute-start(bf16[6,128,128]{2,1,0:T(8,128)(2,1)S(1)} %pad_maximum_fusion.refs_0_), channel_id=1, source_target_pairs={{0,8},{8,16},{16,24},{24,32},{32,40},{40,48},{48,56},{56,64},{64,7... | collective-permute-start | bytes 589832 | tf_op jit(solution)/shard_map/ppermute | solution.py:180
  5.2 9.8 %collective-permute-start.1 = (bf16[6,128,128]{2,1,0:T(8,128)(2,1)S(1)}, bf16[6,128,128]{2,1,0:T(8,128)(2,1)S(1)}, u32[]{:S(2)}, u32[]{:S(2)}) collective-permute-start(bf16[6,128,128]{2,1,0:T(8,128)(2,1)S(1)} %pad_maximum_fusion.refs_0_), channel_id=1, source_target_pairs={{8,0},{16,8},{24,16},{32,24},{40,32},{48,40},{56,48},{64,56},{72,6... | collective-permute-start | bytes 589832 | tf_op jit(solution)/shard_map/ppermute | solution.py:180
  15.0 1.3 collective-permute-start.8
  16.3 4.0 %collective-permute-start.9 = (bf16[6,128,128]{2,1,0:T(8,128)(2,1)S(1)}, bf16[6,128,128]{2,1,0:T(8,128)(2,1)S(1)}, u32[]{:S(2)}, u32[]{:S(2)}) collective-permute-start(bf16[6,128,128]{2,1,0:T(8,128)(2,1)S(1)} %pad_maximum_fusion.refs_0_), channel_id=1, source_target_pairs={{128,0},{136,8},{144,16},{152,24},{160,32},{168,40},{176,48},{184,... | collective-permute-start | bytes 589832 | tf_op jit(solution)/shard_map/ppermute | solution.py:180
  20.3 1.3 collective-permute-start.10
  21.6 1.9 collective-permute-start.2
  23.5 5.5 %collective-permute-start.3 = (bf16[6,128,128]{2,1,0:T(8,128)(2,1)S(1)}, bf16[6,128,128]{2,1,0:T(8,128)(2,1)S(1)}, u32[]{:S(2)}, u32[]{:S(2)}) collective-permute-start(bf16[6,128,128]{2,1,0:T(8,128)(2,1)S(1)} %collective-permute-done.1.refs_2_), channel_id=1, source_target_pairs={{8,0},{16,8},{24,16},{32,24},{40,32},{48,40},{56,48},{64,56},{72,6... | collective-permute-start | bytes 589832 | tf_op jit(solution)/shard_map/ppermute | solution.py:180
  29.1 1.9 collective-permute-start.24
  31.0 5.5 %collective-permute-start.25 = (bf16[6,128,128]{2,1,0:T(8,128)(2,1)S(1)}, bf16[6,128,128]{2,1,0:T(8,128)(2,1)S(1)}, u32[]{:S(2)}, u32[]{:S(2)}) collective-permute-start(bf16[6,128,128]{2,1,0:T(8,128)(2,1)S(1)} %pad_maximum_fusion.1.refs_0_), channel_id=1, source_target_pairs={{8,0},{16,8},{24,16},{32,24},{40,32},{48,40},{56,48},{64,56},{72,6... | collective-permute-start | bytes 589832 | tf_op jit(solution)/shard_map/ppermute | solution.py:180
  36.5 1.9 collective-permute-start.4
  38.5 6.4 %collective-permute-start.5 = (bf16[6,128,128]{2,1,0:T(8,128)(2,1)S(1)}, bf16[6,128,128]{2,1,0:T(8,128)(2,1)S(1)}, u32[]{:S(2)}, u32[]{:S(2)}) collective-permute-start(bf16[6,128,128]{2,1,0:T(8,128)(2,1)S(1)} %collective-permute-done.3.refs_4_), channel_id=1, source_target_pairs={{16,0},{24,8},{32,16},{40,24},{48,32},{56,40},{64,48},{72,56},{80,... | collective-permute-start | bytes 589832 | tf_op jit(solution)/shard_map/ppermute | solution.py:180
  44.8 5.5 %collective-permute-start.11 = (bf16[6,128,128]{2,1,0:T(8,128)(2,1)S(1)}, bf16[6,128,128]{2,1,0:T(8,128)(2,1)S(1)}, u32[]{:S(2)}, u32[]{:S(2)}) collective-permute-start(bf16[6,128,128]{2,1,0:T(8,128)(2,1)S(1)} %pad_maximum_fusion.refs_0_), channel_id=1, source_target_pairs={{256,0},{264,8},{272,16},{280,24},{288,32},{296,40},{304,48},{312,... | collective-permute-start | bytes 589832 | tf_op jit(solution)/shard_map/ppermute | solution.py:180
  50.4 1.9 collective-permute-start.26
  52.3 5.5 %collective-permute-start.27 = (bf16[6,128,128]{2,1,0:T(8,128)(2,1)S(1)}, bf16[6,128,128]{2,1,0:T(8,128)(2,1)}, u32[]{:S(2)}, u32[]{:S(2)}) collective-permute-start(bf16[6,128,128]{2,1,0:T(8,128)(2,1)S(1)} %collective-permute-done.25.refs_2_), channel_id=1, source_target_pairs={{8,0},{16,8},{24,16},{32,24},{40,32},{48,40},{56,48},{64,56},{72,6... | collective-permute-start | bytes 589832 | tf_op jit(solution)/shard_map/ppermute | solution.py:180
  57.8 1.9 collective-permute-start.6
  59.8 8.2 %collective-permute-start.7 = (bf16[6,128,128]{2,1,0:T(8,128)(2,1)S(1)}, bf16[6,128,128]{2,1,0:T(8,128)(2,1)S(1)}, u32[]{:S(2)}, u32[]{:S(2)}) collective-permute-start(bf16[6,128,128]{2,1,0:T(8,128)(2,1)S(1)} %collective-permute-done.5.refs_6_), channel_id=1, source_target_pairs={{32,0},{40,8},{48,16},{56,24},{64,32},{72,40},{80,48},{88,56},{96,... | collective-permute-start | bytes 589832 | tf_op jit(solution)/shard_map/ppermute | solution.py:180
  67.9 1.3 collective-permute-start.32
  69.2 1.9 collective-permute-start.28
  71.2 6.4 %collective-permute-start.29 = (bf16[6,128,128]{2,1,0:T(8,128)(2,1)}, bf16[6,128,128]{2,1,0:T(8,128)(2,1)}, u32[]{:S(2)}, u32[]{:S(2)}) collective-permute-start(bf16[6,128,128]{2,1,0:T(8,128)(2,1)} %collective-permute-done.27.refs_4_), channel_id=1, source_target_pairs={{16,0},{24,8},{32,16},{40,24},{48,32},{56,40},{64,48},{72,56},{80,... | collective-permute-start | bytes 589832 | tf_op jit(solution)/shard_map/ppermute | solution.py:180
  78.3 1.3 collective-permute-done.6.refs_7_
  79.6 4.8 %collective-permute-done.7.refs_8_ = bf16[6,128,128]{2,1,0:T(8,128)(2,1)S(1)} collective-permute-done((bf16[6,128,128]{2,1,0:T(8,128)(2,1)S(1)}, bf16[6,128,128]{2,1,0:T(8,128)(2,1)S(1)}, u32[]{:S(2)}, u32[]{:S(2)}) %collective-permute-start.7) | collective-permute-done | bytes 196640 | tf_op jit(solution)/shard_map/ppermute | solution.py:180
  85.0 3.8 %psum.28 = f32[16,128]{1,0:T(8,128)S(1)} all-reduce(f32[16,128]{1,0:T(8,128)S(1)} %squares.1), channel_id=1, replica_groups=mesh['seq'=64,'y'=4,'c'=2] {'c'}, use_global_device_ids=true, to_apply=%region_0.0 | all-reduce | flops 2048 | bytes 16384 | tf_op jit(solution)/shard_map/psum | solution.py:222
  88.8 8.8 %psum.29.sums_ref = f32[16,128]{1,0:T(8,128)S(1)} all-reduce(f32[16,128]{1,0:T(8,128)S(1)} %psum.28), channel_id=1, replica_groups=mesh['seq'=64,'y'=4,'c'=2] {'y'}, use_global_device_ids=true, to_apply=%region_1.0 | all-reduce | flops 2048 | bytes 16384 | tf_op jit(solution)/shard_map/psum | solution.py:222
  98.3 0.7 copy-done.9
  99.6 6.8 %forward.1 = (bf16[3,128,128]{2,1,0:T(8,128)(2,1)}, f32[3,128,128]{2,1,0:T(8,128)S(1)}, bf16[3,128,128]{2,1,0:T(8,128)(2,1)S(1)}, f32[8,128]{1,0:T(8,128)S(1)}, ...) custom-call(s32[1,13]{1,0:T(1,128)S(1)} %copy-done.11, ...), custom_call_target="tpu_custom_call" | custom-call | tf_op jit(solution)/shard_map/forward/pallas_call | solution.py:223
  106.4 1.7 collective-permute-start.23
  108.1 1.3 collective-permute-start.22
  109.4 3.0 %collective-permute-start.21 = (f32[8,128]{1,0:T(8,128)S(1)}, f32[8,128]{1,0:T(8,128)S(1)}, u32[]{:S(2)}, u32[]{:S(2)}) collective-permute-start(f32[8,128]{1,0:T(8,128)S(1)} %get-tuple-element.36), channel_id=1, source_target_pairs={{128,0},{136,8},{144,16},{152,24},{160,32},{168,40},{176,48},{184,... | collective-permute-start | bytes 12296 | tf_op jit(solution)/shard_map/ppermute | solution.py:180
  112.4 1.3 collective-permute-start.20
  113.7 10.4 %collective-permute-start.19 = (f32[8,128]{1,0:T(8,128)S(1)}, f32[8,128]{1,0:T(8,128)S(1)}, u32[]{:S(2)}, u32[]{:S(2)}) collective-permute-start(f32[8,128]{1,0:T(8,128)S(1)} %get-tuple-element.34), channel_id=1, source_target_pairs={{64,0},{72,8},{80,16},{88,24},{96,32},{104,40},{112,48},{120,56},{... | collective-permute-start | bytes 12296 | tf_op jit(solution)/shard_map/ppermute | solution.py:180
  124.2 3.5 %collective-permute-start.18 = (f32[8,128]{1,0:T(8,128)S(1)}, f32[8,128]{1,0:T(8,128)S(1)}, u32[]{:S(2)}, u32[]{:S(2)}) collective-permute-start(f32[8,128]{1,0:T(8,128)S(1)} %get-tuple-element.33), channel_id=1, source_target_pairs={{0,64},{8,72},{16,80},{24,88},{32,96},{40,104},{48,112},{56,120},{... | collective-permute-start | bytes 12296 | tf_op jit(solution)/shard_map/ppermute | solution.py:180
  127.7 8.5 %collective-permute-start.17 = (f32[8,128]{1,0:T(8,128)S(1)}, f32[8,128]{1,0:T(8,128)S(1)}, u32[]{:S(2)}, u32[]{:S(2)}) collective-permute-start(f32[8,128]{1,0:T(8,128)S(1)} %get-tuple-element.32), channel_id=1, source_target_pairs={{32,0},{40,8},{48,16},{56,24},{64,32},{72,40},{80,48},{88,56},{96,... | collective-permute-start | bytes 12296 | tf_op jit(solution)/shard_map/ppermute | solution.py:180
  136.3 1.9 collective-permute-start.16
  138.2 7.3 %collective-permute-start.15 = (f32[8,128]{1,0:T(8,128)S(1)}, f32[8,128]{1,0:T(8,128)S(1)}, u32[]{:S(2)}, u32[]{:S(2)}) collective-permute-start(f32[8,128]{1,0:T(8,128)S(1)} %get-tuple-element.30), channel_id=1, source_target_pairs={{16,0},{24,8},{32,16},{40,24},{48,32},{56,40},{64,48},{72,56},{80,... | collective-permute-start | bytes 12296 | tf_op jit(solution)/shard_map/ppermute | solution.py:180
  145.6 1.9 collective-permute-start.14
  147.5 5.1 %collective-permute-start.13 = (f32[8,128]{1,0:T(8,128)S(1)}, f32[8,128]{1,0:T(8,128)S(1)}, u32[]{:S(2)}, u32[]{:S(2)}) collective-permute-start(f32[8,128]{1,0:T(8,128)S(1)} %get-tuple-element.28), channel_id=1, source_target_pairs={{8,0},{16,8},{24,16},{32,24},{40,32},{48,40},{56,48},{64,56},{72,6... | collective-permute-start | bytes 12296 | tf_op jit(solution)/shard_map/ppermute | solution.py:180
  152.6 1.9 collective-permute-start.12
  154.5 3.4 %collective-permute-start.33 = (bf16[6,128,128]{2,1,0:T(8,128)(2,1)S(1)}, bf16[6,128,128]{2,1,0:T(8,128)(2,1)S(1)}, u32[]{:S(2)}, u32[]{:S(2)}) collective-permute-start(bf16[6,128,128]{2,1,0:T(8,128)(2,1)S(1)} %pad_maximum_fusion.1.refs_0_), channel_id=1, source_target_pairs={{128,0},{136,8},{144,16},{152,24},{160,32},{168,40},{176,48},{184,... | collective-permute-start | bytes 589832 | tf_op jit(solution)/shard_map/ppermute | solution.py:180
  157.9 1.3 collective-permute-start.34
  159.2 5.5 %collective-permute-start.35 = (bf16[6,128,128]{2,1,0:T(8,128)(2,1)S(1)}, bf16[6,128,128]{2,1,0:T(8,128)(2,1)S(1)}, u32[]{:S(2)}, u32[]{:S(2)}) collective-permute-start(bf16[6,128,128]{2,1,0:T(8,128)(2,1)S(1)} %pad_maximum_fusion.1.refs_0_), channel_id=1, source_target_pairs={{256,0},{264,8},{272,16},{280,24},{288,32},{296,40},{304,48},{312,... | collective-permute-start | bytes 589832 | tf_op jit(solution)/shard_map/ppermute | solution.py:180
  164.8 1.9 collective-permute-start.30
  166.7 8.2 %collective-permute-start.31 = (bf16[6,128,128]{2,1,0:T(8,128)(2,1)}, bf16[6,128,128]{2,1,0:T(8,128)(2,1)S(1)}, u32[]{:S(2)}, u32[]{:S(2)}) collective-permute-start(bf16[6,128,128]{2,1,0:T(8,128)(2,1)} %collective-permute-done.29.refs_6_), channel_id=1, source_target_pairs={{32,0},{40,8},{48,16},{56,24},{64,32},{72,40},{80,48},{88,56},{96,... | collective-permute-start | bytes 589832 | tf_op jit(solution)/shard_map/ppermute | solution.py:180
  174.9 9.0 %psum.30 = f32[2,128]{1,0:T(2,128)S(1)} all-reduce(f32[2,128]{1,0:T(2,128)S(1)} %pad_maximum_fusion.2), channel_id=1, replica_groups=mesh['seq'=64,'y'=4,'c'=2] {'c'}, use_global_device_ids=true, to_apply=%region_2.0 | all-reduce | flops 256 | bytes 2048 | tf_op jit(solution)/shard_map/psum | solution.py:251
  183.9 6.6 %psum.31.terms_ref = f32[2,128]{1,0:T(2,128)S(1)} all-reduce(f32[2,128]{1,0:T(2,128)S(1)} %psum.30), channel_id=1, replica_groups=mesh['seq'=64,'y'=4,'c'=2] {'y'}, use_global_device_ids=true, to_apply=%region_3.0 | all-reduce | flops 256 | bytes 2048 | tf_op jit(solution)/shard_map/psum | solution.py:251
  191.2 0.9 copy-done.6
  192.1 6.7 %backward.1 = (f32[3,128,128]{2,1,0:T(8,128)S(1)}, bf16[3,128,128]{2,1,0:T(8,128)(2,1)}) custom-call(s32[1,13]{1,0:T(1,128)S(1)} %copy-done.12, bf16[3,128,128]{2,1,0:T(8,128)(2,1)S(1)} %get-tuple-element.40.kn_ref, bf16[3,128,128]{2,1,0:T(8,128)(2,1)S(1)} %bitcast.17, f32[3,128]{1,0:T(4,128)S(1)} %copy-done.8, ...), custom_call_target="tpu_custom_call" | custom-call | tf_op jit(solution)/shard_map/backward/pallas_call | solution.py:252
  199.5 0.9 final.1
  (68 shorter events, 4.1 us)
Async XLA Ops:
  0.6 76.9 %copy-start = (s32[64,13]{0,1:T(8,128)S(1)}, s32[64,13]{0,1:T(8,128)}, u32[]{:S(2)}) copy-start(s32[64,13]{0,1:T(8,128)} %param.13) | copy-start | bytes 9988
  0.6 28.4 %copy-start.1 = (bf16[128,3,128]{2,0,1:T(8,128)(2,1)S(1)}, bf16[128,3,128]{2,0,1:T(8,128)(2,1)}, u32[]{:S(2)}) copy-start(bf16[128,3,128]{2,0,1:T(8,128)(2,1)} %param.7) | copy-start | bytes 294916
  0.7 28.4 %copy-start.2 = (bf16[128,3,128]{2,0,1:T(8,128)(2,1)S(1)}, bf16[128,3,128]{2,0,1:T(8,128)(2,1)}, u32[]{:S(2)}) copy-start(bf16[128,3,128]{2,0,1:T(8,128)(2,1)} %param.10) | copy-start | bytes 294916
  1.7 19.9 %collective-permute-start = (bf16[6,128,128]{2,1,0:T(8,128)(2,1)S(1)}, bf16[6,128,128]{2,1,0:T(8,128)(2,1)S(1)}, u32[]{:S(2)}, u32[]{:S(2)}) collective-permute-start(bf16[6,128,128]{2,1,0:T(8,128)(2,1)S(1)} %pad_maximum_fusion.refs_0_), channel_id=1, source_target_pairs={{0,8},{8,16},{16,24},{24,32},{32,40},{40,48},{48,56},{56,64},{64,7... | collective-permute-start | bytes 589832 | tf_op jit(solution)/shard_map/ppermute | solution.py:180
  5.2 18.3 %collective-permute-start.1 = (bf16[6,128,128]{2,1,0:T(8,128)(2,1)S(1)}, bf16[6,128,128]{2,1,0:T(8,128)(2,1)S(1)}, u32[]{:S(2)}, u32[]{:S(2)}) collective-permute-start(bf16[6,128,128]{2,1,0:T(8,128)(2,1)S(1)} %pad_maximum_fusion.refs_0_), channel_id=1, source_target_pairs={{8,0},{16,8},{24,16},{32,24},{40,32},{48,40},{56,48},{64,56},{72,6... | collective-permute-start | bytes 589832 | tf_op jit(solution)/shard_map/ppermute | solution.py:180
  15.0 14.1 %collective-permute-start.8 = (bf16[6,128,128]{2,1,0:T(8,128)(2,1)S(1)}, bf16[6,128,128]{2,1,0:T(8,128)(2,1)S(1)}, u32[]{:S(2)}, u32[]{:S(2)}) collective-permute-start(bf16[6,128,128]{2,1,0:T(8,128)(2,1)S(1)} %pad_maximum_fusion.refs_0_), channel_id=1, source_target_pairs={{0,128},{8,136},{16,144},{24,152},{32,160},{40,168},{48,176},{56,1... | collective-permute-start | bytes 589832 | tf_op jit(solution)/shard_map/ppermute | solution.py:180
  16.3 14.7 %collective-permute-start.9 = (bf16[6,128,128]{2,1,0:T(8,128)(2,1)S(1)}, bf16[6,128,128]{2,1,0:T(8,128)(2,1)S(1)}, u32[]{:S(2)}, u32[]{:S(2)}) collective-permute-start(bf16[6,128,128]{2,1,0:T(8,128)(2,1)S(1)} %pad_maximum_fusion.refs_0_), channel_id=1, source_target_pairs={{128,0},{136,8},{144,16},{152,24},{160,32},{168,40},{176,48},{184,... | collective-permute-start | bytes 589832 | tf_op jit(solution)/shard_map/ppermute | solution.py:180
  20.3 24.5 %collective-permute-start.10 = (bf16[6,128,128]{2,1,0:T(8,128)(2,1)S(1)}, bf16[6,128,128]{2,1,0:T(8,128)(2,1)S(1)}, u32[]{:S(2)}, u32[]{:S(2)}) collective-permute-start(bf16[6,128,128]{2,1,0:T(8,128)(2,1)S(1)} %pad_maximum_fusion.refs_0_), channel_id=1, source_target_pairs={{0,256},{8,264},{16,272},{24,280},{32,288},{40,296},{48,304},{56,3... | collective-permute-start | bytes 589832 | tf_op jit(solution)/shard_map/ppermute | solution.py:180
  21.6 14.9 %collective-permute-start.2 = (bf16[6,128,128]{2,1,0:T(8,128)(2,1)S(1)}, bf16[6,128,128]{2,1,0:T(8,128)(2,1)S(1)}, u32[]{:S(2)}, u32[]{:S(2)}) collective-permute-start(bf16[6,128,128]{2,1,0:T(8,128)(2,1)S(1)} %collective-permute-done.refs_1_), channel_id=1, source_target_pairs={{0,8},{8,16},{16,24},{24,32},{32,40},{40,48},{48,56},{56,64},{64,7... | collective-permute-start | bytes 589832 | tf_op jit(solution)/shard_map/ppermute | solution.py:180
  23.5 14.9 %collective-permute-start.3 = (bf16[6,128,128]{2,1,0:T(8,128)(2,1)S(1)}, bf16[6,128,128]{2,1,0:T(8,128)(2,1)S(1)}, u32[]{:S(2)}, u32[]{:S(2)}) collective-permute-start(bf16[6,128,128]{2,1,0:T(8,128)(2,1)S(1)} %collective-permute-done.1.refs_2_), channel_id=1, source_target_pairs={{8,0},{16,8},{24,16},{32,24},{40,32},{48,40},{56,48},{64,56},{72,6... | collective-permute-start | bytes 589832 | tf_op jit(solution)/shard_map/ppermute | solution.py:180
  29.1 21.3 %collective-permute-start.24 = (bf16[6,128,128]{2,1,0:T(8,128)(2,1)S(1)}, bf16[6,128,128]{2,1,0:T(8,128)(2,1)S(1)}, u32[]{:S(2)}, u32[]{:S(2)}) collective-permute-start(bf16[6,128,128]{2,1,0:T(8,128)(2,1)S(1)} %pad_maximum_fusion.1.refs_0_), channel_id=1, source_target_pairs={{0,8},{8,16},{16,24},{24,32},{32,40},{40,48},{48,56},{56,64},{64,7... | collective-permute-start | bytes 589832 | tf_op jit(solution)/shard_map/ppermute | solution.py:180
  31.0 21.3 %collective-permute-start.25 = (bf16[6,128,128]{2,1,0:T(8,128)(2,1)S(1)}, bf16[6,128,128]{2,1,0:T(8,128)(2,1)S(1)}, u32[]{:S(2)}, u32[]{:S(2)}) collective-permute-start(bf16[6,128,128]{2,1,0:T(8,128)(2,1)S(1)} %pad_maximum_fusion.1.refs_0_), channel_id=1, source_target_pairs={{8,0},{16,8},{24,16},{32,24},{40,32},{48,40},{56,48},{64,56},{72,6... | collective-permute-start | bytes 589832 | tf_op jit(solution)/shard_map/ppermute | solution.py:180
  36.5 21.3 %collective-permute-start.4 = (bf16[6,128,128]{2,1,0:T(8,128)(2,1)S(1)}, bf16[6,128,128]{2,1,0:T(8,128)(2,1)S(1)}, u32[]{:S(2)}, u32[]{:S(2)}) collective-permute-start(bf16[6,128,128]{2,1,0:T(8,128)(2,1)S(1)} %collective-permute-done.2.refs_3_), channel_id=1, source_target_pairs={{0,16},{8,24},{16,32},{24,40},{32,48},{40,56},{48,64},{56,72},{64,... | collective-permute-start | bytes 589832 | tf_op jit(solution)/shard_map/ppermute | solution.py:180
  38.5 21.3 %collective-permute-start.5 = (bf16[6,128,128]{2,1,0:T(8,128)(2,1)S(1)}, bf16[6,128,128]{2,1,0:T(8,128)(2,1)S(1)}, u32[]{:S(2)}, u32[]{:S(2)}) collective-permute-start(bf16[6,128,128]{2,1,0:T(8,128)(2,1)S(1)} %collective-permute-done.3.refs_4_), channel_id=1, source_target_pairs={{16,0},{24,8},{32,16},{40,24},{48,32},{56,40},{64,48},{72,56},{80,... | collective-permute-start | bytes 589832 | tf_op jit(solution)/shard_map/ppermute | solution.py:180
  44.8 23.1 %collective-permute-start.11 = (bf16[6,128,128]{2,1,0:T(8,128)(2,1)S(1)}, bf16[6,128,128]{2,1,0:T(8,128)(2,1)S(1)}, u32[]{:S(2)}, u32[]{:S(2)}) collective-permute-start(bf16[6,128,128]{2,1,0:T(8,128)(2,1)S(1)} %pad_maximum_fusion.refs_0_), channel_id=1, source_target_pairs={{256,0},{264,8},{272,16},{280,24},{288,32},{296,40},{304,48},{312,... | collective-permute-start | bytes 589832 | tf_op jit(solution)/shard_map/ppermute | solution.py:180
  50.4 18.9 %collective-permute-start.26 = (bf16[6,128,128]{2,1,0:T(8,128)(2,1)S(1)}, bf16[6,128,128]{2,1,0:T(8,128)(2,1)}, u32[]{:S(2)}, u32[]{:S(2)}) collective-permute-start(bf16[6,128,128]{2,1,0:T(8,128)(2,1)S(1)} %collective-permute-done.24.refs_1_), channel_id=1, source_target_pairs={{0,8},{8,16},{16,24},{24,32},{32,40},{40,48},{48,56},{56,64},{64,7... | collective-permute-start | bytes 589832 | tf_op jit(solution)/shard_map/ppermute | solution.py:180
  52.3 32.7 %copy-start.5 = (bf16[6,128,128]{2,1,0:T(8,128)(2,1)}, bf16[6,128,128]{2,1,0:T(8,128)(2,1)S(1)}, u32[]{:S(2)}) copy-start(bf16[6,128,128]{2,1,0:T(8,128)(2,1)S(1)} %collective-permute-done.25.refs_2_) | copy-start | bytes 589828
  52.3 18.9 %collective-permute-start.27 = (bf16[6,128,128]{2,1,0:T(8,128)(2,1)S(1)}, bf16[6,128,128]{2,1,0:T(8,128)(2,1)}, u32[]{:S(2)}, u32[]{:S(2)}) collective-permute-start(bf16[6,128,128]{2,1,0:T(8,128)(2,1)S(1)} %collective-permute-done.25.refs_2_), channel_id=1, source_target_pairs={{8,0},{16,8},{24,16},{32,24},{40,32},{48,40},{56,48},{64,56},{72,6... | collective-permute-start | bytes 589832 | tf_op jit(solution)/shard_map/ppermute | solution.py:180
  57.8 21.8 %collective-permute-start.6 = (bf16[6,128,128]{2,1,0:T(8,128)(2,1)S(1)}, bf16[6,128,128]{2,1,0:T(8,128)(2,1)S(1)}, u32[]{:S(2)}, u32[]{:S(2)}) collective-permute-start(bf16[6,128,128]{2,1,0:T(8,128)(2,1)S(1)} %collective-permute-done.4.refs_5_), channel_id=1, source_target_pairs={{0,32},{8,40},{16,48},{24,56},{32,64},{40,72},{48,80},{56,88},{64,... | collective-permute-start | bytes 589832 | tf_op jit(solution)/shard_map/ppermute | solution.py:180
  59.8 24.6 %collective-permute-start.7 = (bf16[6,128,128]{2,1,0:T(8,128)(2,1)S(1)}, bf16[6,128,128]{2,1,0:T(8,128)(2,1)S(1)}, u32[]{:S(2)}, u32[]{:S(2)}) collective-permute-start(bf16[6,128,128]{2,1,0:T(8,128)(2,1)S(1)} %collective-permute-done.5.refs_6_), channel_id=1, source_target_pairs={{32,0},{40,8},{48,16},{56,24},{64,32},{72,40},{80,48},{88,56},{96,... | collective-permute-start | bytes 589832 | tf_op jit(solution)/shard_map/ppermute | solution.py:180
  67.9 41.5 %collective-permute-start.32 = (bf16[6,128,128]{2,1,0:T(8,128)(2,1)S(1)}, bf16[6,128,128]{2,1,0:T(8,128)(2,1)}, u32[]{:S(2)}, u32[]{:S(2)}) collective-permute-start(bf16[6,128,128]{2,1,0:T(8,128)(2,1)S(1)} %pad_maximum_fusion.1.refs_0_), channel_id=1, source_target_pairs={{0,128},{8,136},{16,144},{24,152},{32,160},{40,168},{48,176},{56,1... | collective-permute-start | bytes 589832 | tf_op jit(solution)/shard_map/ppermute | solution.py:180
  69.2 43.1 %collective-permute-start.28 = (bf16[6,128,128]{2,1,0:T(8,128)(2,1)}, bf16[6,128,128]{2,1,0:T(8,128)(2,1)}, u32[]{:S(2)}, u32[]{:S(2)}) collective-permute-start(bf16[6,128,128]{2,1,0:T(8,128)(2,1)} %collective-permute-done.26.refs_3_), channel_id=1, source_target_pairs={{0,16},{8,24},{16,32},{24,40},{32,48},{40,56},{48,64},{56,72},{64,... | collective-permute-start | bytes 589832 | tf_op jit(solution)/shard_map/ppermute | solution.py:180
  71.2 42.5 %collective-permute-start.29 = (bf16[6,128,128]{2,1,0:T(8,128)(2,1)}, bf16[6,128,128]{2,1,0:T(8,128)(2,1)}, u32[]{:S(2)}, u32[]{:S(2)}) collective-permute-start(bf16[6,128,128]{2,1,0:T(8,128)(2,1)} %collective-permute-done.27.refs_4_), channel_id=1, source_target_pairs={{16,0},{24,8},{32,16},{40,24},{48,32},{56,40},{64,48},{72,56},{80,... | collective-permute-start | bytes 589832 | tf_op jit(solution)/shard_map/ppermute | solution.py:180
  97.6 0.7 copy-start.7
  98.3 0.7 copy-start.9
  99.6 90.9 %copy-start.4 = (bf16[128,3,128]{2,0,1:T(8,128)(2,1)S(1)}, bf16[128,3,128]{2,0,1:T(8,128)(2,1)}, u32[]{:S(2)}) copy-start(bf16[128,3,128]{2,0,1:T(8,128)(2,1)} %param.9) | copy-start | bytes 294916
  106.4 7.3 %copy-start.13 = (f32[8,128]{1,0:T(8,128)}, f32[8,128]{1,0:T(8,128)S(1)}, u32[]{:S(2)}) copy-start(f32[8,128]{1,0:T(8,128)S(1)} %get-tuple-element.41.refs_13_) | copy-start | bytes 12292
  106.4 17.8 %collective-permute-start.23 = (f32[8,128]{1,0:T(8,128)S(1)}, f32[8,128]{1,0:T(8,128)S(1)}, u32[]{:S(2)}, u32[]{:S(2)}) collective-permute-start(f32[8,128]{1,0:T(8,128)S(1)} %get-tuple-element.38), channel_id=1, source_target_pairs={{256,0},{264,8},{272,16},{280,24},{288,32},{296,40},{304,48},{312,... | collective-permute-start | bytes 12296 | tf_op jit(solution)/shard_map/ppermute | solution.py:180
  108.1 19.6 %collective-permute-start.22 = (f32[8,128]{1,0:T(8,128)S(1)}, f32[8,128]{1,0:T(8,128)S(1)}, u32[]{:S(2)}, u32[]{:S(2)}) collective-permute-start(f32[8,128]{1,0:T(8,128)S(1)} %get-tuple-element.37), channel_id=1, source_target_pairs={{0,256},{8,264},{16,272},{24,280},{32,288},{40,296},{48,304},{56,3... | collective-permute-start | bytes 12296 | tf_op jit(solution)/shard_map/ppermute | solution.py:180
  109.4 26.9 %collective-permute-start.21 = (f32[8,128]{1,0:T(8,128)S(1)}, f32[8,128]{1,0:T(8,128)S(1)}, u32[]{:S(2)}, u32[]{:S(2)}) collective-permute-start(f32[8,128]{1,0:T(8,128)S(1)} %get-tuple-element.36), channel_id=1, source_target_pairs={{128,0},{136,8},{144,16},{152,24},{160,32},{168,40},{176,48},{184,... | collective-permute-start | bytes 12296 | tf_op jit(solution)/shard_map/ppermute | solution.py:180
  112.4 25.8 %collective-permute-start.20 = (f32[8,128]{1,0:T(8,128)S(1)}, f32[8,128]{1,0:T(8,128)S(1)}, u32[]{:S(2)}, u32[]{:S(2)}) collective-permute-start(f32[8,128]{1,0:T(8,128)S(1)} %get-tuple-element.35), channel_id=1, source_target_pairs={{0,128},{8,136},{16,144},{24,152},{32,160},{40,168},{48,176},{56,1... | collective-permute-start | bytes 12296 | tf_op jit(solution)/shard_map/ppermute | solution.py:180
  113.7 31.8 %collective-permute-start.19 = (f32[8,128]{1,0:T(8,128)S(1)}, f32[8,128]{1,0:T(8,128)S(1)}, u32[]{:S(2)}, u32[]{:S(2)}) collective-permute-start(f32[8,128]{1,0:T(8,128)S(1)} %get-tuple-element.34), channel_id=1, source_target_pairs={{64,0},{72,8},{80,16},{88,24},{96,32},{104,40},{112,48},{120,56},{... | collective-permute-start | bytes 12296 | tf_op jit(solution)/shard_map/ppermute | solution.py:180
  124.2 23.3 %collective-permute-start.18 = (f32[8,128]{1,0:T(8,128)S(1)}, f32[8,128]{1,0:T(8,128)S(1)}, u32[]{:S(2)}, u32[]{:S(2)}) collective-permute-start(f32[8,128]{1,0:T(8,128)S(1)} %get-tuple-element.33), channel_id=1, source_target_pairs={{0,64},{8,72},{16,80},{24,88},{32,96},{40,104},{48,112},{56,120},{... | collective-permute-start | bytes 12296 | tf_op jit(solution)/shard_map/ppermute | solution.py:180
  127.7 24.8 %collective-permute-start.17 = (f32[8,128]{1,0:T(8,128)S(1)}, f32[8,128]{1,0:T(8,128)S(1)}, u32[]{:S(2)}, u32[]{:S(2)}) collective-permute-start(f32[8,128]{1,0:T(8,128)S(1)} %get-tuple-element.32), channel_id=1, source_target_pairs={{32,0},{40,8},{48,16},{56,24},{64,32},{72,40},{80,48},{88,56},{96,... | collective-permute-start | bytes 12296 | tf_op jit(solution)/shard_map/ppermute | solution.py:180
  136.3 18.2 %collective-permute-start.16 = (f32[8,128]{1,0:T(8,128)S(1)}, f32[8,128]{1,0:T(8,128)S(1)}, u32[]{:S(2)}, u32[]{:S(2)}) collective-permute-start(f32[8,128]{1,0:T(8,128)S(1)} %get-tuple-element.31), channel_id=1, source_target_pairs={{0,32},{8,40},{16,48},{24,56},{32,64},{40,72},{48,80},{56,88},{64,... | collective-permute-start | bytes 12296 | tf_op jit(solution)/shard_map/ppermute | solution.py:180
  138.2 19.7 %collective-permute-start.15 = (f32[8,128]{1,0:T(8,128)S(1)}, f32[8,128]{1,0:T(8,128)S(1)}, u32[]{:S(2)}, u32[]{:S(2)}) collective-permute-start(f32[8,128]{1,0:T(8,128)S(1)} %get-tuple-element.30), channel_id=1, source_target_pairs={{16,0},{24,8},{32,16},{40,24},{48,32},{56,40},{64,48},{72,56},{80,... | collective-permute-start | bytes 12296 | tf_op jit(solution)/shard_map/ppermute | solution.py:180
  145.6 13.7 %collective-permute-start.14 = (f32[8,128]{1,0:T(8,128)S(1)}, f32[8,128]{1,0:T(8,128)S(1)}, u32[]{:S(2)}, u32[]{:S(2)}) collective-permute-start(f32[8,128]{1,0:T(8,128)S(1)} %get-tuple-element.29), channel_id=1, source_target_pairs={{0,16},{8,24},{16,32},{24,40},{32,48},{40,56},{48,64},{56,72},{64,... | collective-permute-start | bytes 12296 | tf_op jit(solution)/shard_map/ppermute | solution.py:180
  147.5 17.2 %collective-permute-start.13 = (f32[8,128]{1,0:T(8,128)S(1)}, f32[8,128]{1,0:T(8,128)S(1)}, u32[]{:S(2)}, u32[]{:S(2)}) collective-permute-start(f32[8,128]{1,0:T(8,128)S(1)} %get-tuple-element.28), channel_id=1, source_target_pairs={{8,0},{16,8},{24,16},{32,24},{40,32},{48,40},{56,48},{64,56},{72,6... | collective-permute-start | bytes 12296 | tf_op jit(solution)/shard_map/ppermute | solution.py:180
  152.6 14.1 %collective-permute-start.12 = (f32[8,128]{1,0:T(8,128)S(1)}, f32[8,128]{1,0:T(8,128)S(1)}, u32[]{:S(2)}, u32[]{:S(2)}) collective-permute-start(f32[8,128]{1,0:T(8,128)S(1)} %get-tuple-element.27), channel_id=1, source_target_pairs={{0,8},{8,16},{16,24},{24,32},{32,40},{40,48},{48,56},{56,64},{64,7... | collective-permute-start | bytes 12296 | tf_op jit(solution)/shard_map/ppermute | solution.py:180
  154.5 35.9 %collective-permute-start.33 = (bf16[6,128,128]{2,1,0:T(8,128)(2,1)S(1)}, bf16[6,128,128]{2,1,0:T(8,128)(2,1)S(1)}, u32[]{:S(2)}, u32[]{:S(2)}) collective-permute-start(bf16[6,128,128]{2,1,0:T(8,128)(2,1)S(1)} %pad_maximum_fusion.1.refs_0_), channel_id=1, source_target_pairs={{128,0},{136,8},{144,16},{152,24},{160,32},{168,40},{176,48},{184,... | collective-permute-start | bytes 589832 | tf_op jit(solution)/shard_map/ppermute | solution.py:180
  157.9 32.5 %collective-permute-start.34 = (bf16[6,128,128]{2,1,0:T(8,128)(2,1)S(1)}, bf16[6,128,128]{2,1,0:T(8,128)(2,1)S(1)}, u32[]{:S(2)}, u32[]{:S(2)}) collective-permute-start(bf16[6,128,128]{2,1,0:T(8,128)(2,1)S(1)} %pad_maximum_fusion.1.refs_0_), channel_id=1, source_target_pairs={{0,256},{8,264},{16,272},{24,280},{32,288},{40,296},{48,304},{56,3... | collective-permute-start | bytes 589832 | tf_op jit(solution)/shard_map/ppermute | solution.py:180
  159.2 31.2 %collective-permute-start.35 = (bf16[6,128,128]{2,1,0:T(8,128)(2,1)S(1)}, bf16[6,128,128]{2,1,0:T(8,128)(2,1)S(1)}, u32[]{:S(2)}, u32[]{:S(2)}) collective-permute-start(bf16[6,128,128]{2,1,0:T(8,128)(2,1)S(1)} %pad_maximum_fusion.1.refs_0_), channel_id=1, source_target_pairs={{256,0},{264,8},{272,16},{280,24},{288,32},{296,40},{304,48},{312,... | collective-permute-start | bytes 589832 | tf_op jit(solution)/shard_map/ppermute | solution.py:180
  164.8 25.7 %collective-permute-start.30 = (bf16[6,128,128]{2,1,0:T(8,128)(2,1)}, bf16[6,128,128]{2,1,0:T(8,128)(2,1)S(1)}, u32[]{:S(2)}, u32[]{:S(2)}) collective-permute-start(bf16[6,128,128]{2,1,0:T(8,128)(2,1)} %collective-permute-done.28.refs_5_), channel_id=1, source_target_pairs={{0,32},{8,40},{16,48},{24,56},{32,64},{40,72},{48,80},{56,88},{64,... | collective-permute-start | bytes 589832 | tf_op jit(solution)/shard_map/ppermute | solution.py:180
  166.7 23.8 %collective-permute-start.31 = (bf16[6,128,128]{2,1,0:T(8,128)(2,1)}, bf16[6,128,128]{2,1,0:T(8,128)(2,1)S(1)}, u32[]{:S(2)}, u32[]{:S(2)}) collective-permute-start(bf16[6,128,128]{2,1,0:T(8,128)(2,1)} %collective-permute-done.29.refs_6_), channel_id=1, source_target_pairs={{32,0},{40,8},{48,16},{56,24},{64,32},{72,40},{80,48},{88,56},{96,... | collective-permute-start | bytes 589832 | tf_op jit(solution)/shard_map/ppermute | solution.py:180
  174.9 15.6 %copy-start.14 = (f32[8,128]{1,0:T(8,128)S(1)}, f32[8,128]{1,0:T(8,128)}, u32[]{:S(2)}) copy-start(f32[8,128]{1,0:T(8,128)} %copy-done.13) | copy-start | bytes 12292
  190.4 0.7 copy-start.8
  191.1 0.9 copy-start.6
  192.1 6.7 %copy-start.3 = (bf16[128,3,128]{2,0,1:T(8,128)(2,1)S(1)}, bf16[128,3,128]{2,0,1:T(8,128)(2,1)}, u32[]{:S(2)}) copy-start(bf16[128,3,128]{2,0,1:T(8,128)(2,1)} %param.8) | copy-start | bytes 294916
  (3 other events, 2.0 us)

commit v2 on v1

v2 whole, which is shorter than its diff:
```python
import functools

import jax
import jax.numpy as jnp
from jax import lax
from jax.experimental import pallas as pl
from jax.experimental.pallas import tpu as pltpu
from jax.sharding import Mesh, PartitionSpec as P

TILE = 128
EPS = 1e-06
OFFSETS = (0, -1, 1, -2, 2, -4, 4, -8, 8, -16, 16, -32, 32)
NT = (((1,), (1,)), ((), ()))
NN = (((1,), (0,)), ((), ()))
F32 = jnp.float32
BF16 = jnp.bfloat16
VMEM_LIMIT = 48 * 1024 * 1024


def dot(left, right, dims):
    return lax.dot_general(left, right, dims, preferred_element_type=F32)


def row_sums(square):
    ones = jnp.ones((8, TILE), BF16)
    high = square.astype(BF16)
    low = (square - high.astype(F32)).astype(BF16)
    return dot(ones, high, NT) + dot(ones, low, NT)


def columns(rows):
    fill = jnp.zeros((TILE - rows.shape[0], TILE), F32)
    return jnp.transpose(jnp.concatenate([rows, fill], axis=0))


def tile_of(tiles, gathered_ref, frame, near, line, place, skip=0):
    if place < near:
        return lambda i: tiles[place][i]
    at = frame // line + OFFSETS[place] // line
    at = jnp.minimum(jnp.maximum(at, 0), gathered_ref.shape[0] - 1)
    return lambda i: gathered_ref[at, skip + i]


def squares_kernel(heads, near, line, listed_ref, q_ref, gathered_ref, *refs):
    tiles, out_ref = refs[:-1], refs[-1]
    count = len(OFFSETS)
    reads = [tile_of(tiles, gathered_ref, listed_ref[0, 0], near, line, t) for t in range(count)]
    reads.append(lambda i: q_ref[i])
    for place, read in enumerate(reads):
        total = jnp.zeros((TILE, TILE), F32)
        for head in range(heads):
            floats = read(head).astype(F32)
            total = total + floats * floats
        out_ref[place : place + 1, :] = row_sums(total)[0:1]
    out_ref[count + 1 :, :] = jnp.zeros((16 - count - 1, TILE), F32)


def forward_kernel(
    heads, near, line, channels, listed_ref, sums_ref, q_ref, do_ref, qg_ref, kg_ref, gathered_ref, *refs
):
    count = len(OFFSETS)
    tiles = refs[:near]
    out_ref, dq_ref, kn_ref, stat_ref, norm_ref, work_ref = refs[near:]
    scale = TILE ** (-0.5)
    inverse = lax.rsqrt(sums_ref[...] / channels + EPS)
    turned = columns(inverse)
    usable = [listed_ref[0, t] >= 0 for t in range(count)]
    reads = [tile_of(tiles, gathered_ref, listed_ref[0, 0], near, line, t) for t in range(count)]
    lane = lax.broadcasted_iota(jnp.int32, (TILE, TILE), 1)
    stats = jnp.zeros((TILE, TILE), F32)
    query_terms = jnp.zeros((TILE, TILE), F32)
    for head in range(heads):
        query = (
            q_ref[head].astype(F32) * turned[:, count : count + 1] * qg_ref[head : head + 1]
        ).astype(BF16)
        upstream = do_ref[head]
        top = jnp.full((TILE, TILE), -1e30, F32)
        for t in range(count):
            key = (
                reads[t](head).astype(F32) * turned[:, t : t + 1] * kg_ref[head : head + 1]
            ).astype(BF16)
            norm_ref[t] = key
            if t == 0:
                kn_ref[head] = key
            score = dot(query, key, NT) * scale
            score = jnp.where(usable[t], score, -1e30)
            work_ref[t] = score
            top = jnp.maximum(top, score)
        top = jnp.max(top, axis=1, keepdims=True)
        total = jnp.zeros((TILE, TILE), F32)
        for t in range(count):
            total = total + jnp.exp(work_ref[t] - top)
        total = jnp.sum(total, axis=1, keepdims=True)
        level = top + jnp.log(total)
        share = 1.0 / total
        out = jnp.zeros((TILE, TILE), F32)
        for t in range(count):
            prob = jnp.exp(work_ref[t] - top) * share
            out = out + dot(prob.astype(BF16), reads[t](heads + head), NN)
        out = out.astype(BF16)
        out_ref[head] = out
        delta = jnp.sum(
            upstream.astype(F32) * out.astype(F32), axis=1, keepdims=True
        )
        query_grad = jnp.zeros((TILE, TILE), F32)
        for t in range(count):
            score = work_ref[t]
            prob = jnp.exp(score - top) * share
            dscore = (prob * (dot(upstream, reads[t](heads + head), NT) - delta)).astype(BF16)
            query_grad = query_grad + dot(dscore, norm_ref[t], NN)
            term = dscore.astype(F32) * score
            query_terms = query_terms + term
            term = jnp.sum(term, axis=0, keepdims=True)
            if head:
                term = term + stat_ref[8 + t : 9 + t, :]
            stat_ref[8 + t : 9 + t, :] = term
        dq_ref[head] = query_grad * scale
        stats = jnp.where(lane == head, level, stats)
        stats = jnp.where(lane == heads + head, delta, stats)
    query_total = jnp.sum(query_terms, axis=1, keepdims=True)
    stats = jnp.where(lane == 2 * heads + 1, query_total, stats)
    rows = jnp.transpose(stats)[0:8]
    place = lax.broadcasted_iota(jnp.int32, (8, TILE), 0)
    stat_ref[0:8, :] = jnp.where(place == 2 * heads, inverse[count : count + 1], rows)
    stat_ref[8 + count : 9 + count, :] = rows[2 * heads + 1 : 2 * heads + 2]
    stat_ref[9 + count :, :] = jnp.zeros((24 - 9 - count, TILE), F32)


def lanes_kernel(heads, near, place_ref, stats_ref, near_ref, far_ref, terms_ref, total_ref):
    count = len(OFFSETS)
    lane, frame, half = place_ref[0], place_ref[1], place_ref[2]
    groups = stats_ref.shape[0]
    total = stats_ref[0]
    for group in range(1, groups):
        total = total + stats_ref[group]
    total_ref[...] = total
    last = 2 * heads + 1
    far = jnp.where(lane < 2, near + lane, jnp.where(frame < half, near + 3, near + 2))
    for ref, slot in ((near_ref, 1 + lane), (far_ref, far)):
        term = total_ref[pl.ds(8 + slot, 1), :]
        for group in range(groups):
            ref[group] = stats_ref[group, 0:8]
            ref[group, last : last + 1, :] = term
    terms_ref[0:1, :] = total[8 + count : 9 + count]
    terms_ref[1:2, :] = total[8:9]
    terms_ref[2:, :] = jnp.zeros((6, TILE), F32)


def backward_kernel(
    heads, near, line, channels, listed_ref, sums_ref, terms_ref, own_ref, got_ref,
    q_ref, k_ref, kn_ref, v_ref, dq_ref, qg_ref, kg_ref, gathered_ref, *refs
):
    count = len(OFFSETS)
    tiles = refs[:near]
    gq_ref, gk_ref, dv_ref = refs[near:]
    scale = TILE ** (-0.5)
    inverse_at, term_at = 2 * heads, 2 * heads + 1

    def stat(t, row):
        if t == 0:
            return own_ref[row : row + 1]
        if t < near:
            return got_ref[(t - 1) ^ 1, row : row + 1]
        lane = {0: 1, 1: 0, 2: 2, 3: 2}[t - near]
        return got_ref[lane, 8 + row : 9 + row]

    inverse = lax.rsqrt(sums_ref[...] / channels + EPS)
    squared = inverse * inverse / channels
    key_term = terms_ref[1:2]
    for t in range(1, count):
        if t != count - 1:
            key_term = key_term + stat(t, term_at)
    turned = columns(
        jnp.concatenate(
            [stat(t, inverse_at) for t in range(count)]
            + [
                inverse[0:1],
                squared[count : count + 1] * terms_ref[0:1],
                squared[0:1] * key_term,
            ],
            axis=0,
        )
    )
    usable = [listed_ref[0, t] >= 0 for t in range(count)]
    reads = [
        tile_of(tiles, gathered_ref, listed_ref[0, 0], near, line, t, 2 * heads) for t in range(count)
    ]
    for head in range(heads):
        key, value = kn_ref[head], v_ref[head]
        key_grad = jnp.zeros((TILE, TILE), F32)
        value_grad = jnp.zeros((TILE, TILE), F32)
        for t in range(count):
            query = (
                reads[t](head).astype(F32) * turned[:, t : t + 1] * qg_ref[head : head + 1]
            ).astype(BF16)
            upstream = reads[t](heads + head)
            score = dot(key, query, NT) * scale - stat(t, head)
            prob = jnp.exp(jnp.where(usable[t], score, -1e30))
            value_grad = value_grad + dot(prob.astype(BF16), upstream, NN)
            dprob = dot(value, upstream, NT)
            dscore = prob * (dprob - stat(t, heads + head))
            key_grad = key_grad + dot(dscore.astype(BF16), query, NN)
        dv_ref[head] = value_grad.astype(BF16)
        gk_ref[head] = (
            turned[:, count : count + 1] * (kg_ref[head : head + 1] * (key_grad * scale))
            - k_ref[head].astype(F32) * turned[:, count + 2 : count + 3]
        ).astype(BF16)
        gq_ref[head] = (
            turned[:, 0:1] * (qg_ref[head : head + 1] * dq_ref[head])
            - q_ref[head].astype(F32) * turned[:, count + 1 : count + 2]
        ).astype(BF16)


SEQ, HEAD = ("x", "z"), ("y", "c")


def passed(value, steps, count):
    pairs = [(i, i + steps) for i in range(count) if 0 <= i + steps < count]
    return lax.ppermute(value, SEQ, pairs)


def spread(value, count, line):
    got = {0: value}
    distance = 1
    while distance < line:
        for facing in (-1, 1):
            near = distance // 2
            source = got[facing * near]
            got[facing * distance] = passed(source, -facing * (distance - near), count)
        distance *= 2
    return [got[offset] for offset in OFFSETS if offset in got]


def per_device(total_heads, q_raw, k_raw, values, grad_out, q_gain, k_gain, key_tiles):
    lines, line = lax.axis_size("x"), lax.axis_size("z")
    seq_count = lines * line
    groups = lax.axis_size("y") * lax.axis_size("c")
    place = lax.axis_index(SEQ)
    lane = lax.axis_index(HEAD)
    heads = q_raw.shape[1]
    channels = float(total_heads * q_raw.shape[2])
    q_raw, k_raw, values, grad_out = [
        jnp.transpose(array, (1, 0, 2)) for array in (q_raw, k_raw, values, grad_out)
    ]
    listed = lax.dynamic_slice_in_dim(key_tiles, place, 1, 0)
    first = jnp.concatenate([k_raw, values], axis=0)
    second = jnp.concatenate([q_raw, grad_out], axis=0)
    column = lax.all_gather(
        jnp.concatenate([k_raw, values, q_raw, grad_out], axis=0), "x"
    )
    first_all = spread(first, seq_count, line)
    second_all = spread(second, seq_count, line)
    near = len(first_all)

    vmem = pl.BlockSpec(memory_space=pltpu.VMEM)
    smem = pl.BlockSpec(memory_space=pltpu.SMEM)
    params = pltpu.CompilerParams(vmem_limit_bytes=VMEM_LIMIT)
    whole = (heads, TILE, TILE)
    count = len(OFFSETS)
    sums = pl.pallas_call(
        functools.partial(squares_kernel, heads, near, line),
        out_shape=jax.ShapeDtypeStruct((16, TILE), F32),
        in_specs=[smem] + [vmem] * (near + 2),
        out_specs=vmem,
        compiler_params=params,
        name="squares",
    )(listed, q_raw, column, *first_all)
    sums = lax.psum(lax.psum(sums, "c"), "y")
    attended, dq, k_norm, stats = pl.pallas_call(
        functools.partial(forward_kernel, heads, near, line, channels),
        out_shape=[
            jax.ShapeDtypeStruct(whole, BF16),
            jax.ShapeDtypeStruct(whole, F32),
            jax.ShapeDtypeStruct(whole, BF16),
            jax.ShapeDtypeStruct((24, TILE), F32),
        ],
        in_specs=[smem] + [vmem] * (6 + near),
        out_specs=[vmem] * 4,
        scratch_shapes=[
            pltpu.VMEM((count, TILE, TILE), BF16),
            pltpu.VMEM((count, TILE, TILE), F32),
        ],
        compiler_params=params,
        name="forward",
    )(listed, sums, q_raw, grad_out, q_gain, k_gain, column, *first_all)

    stats, *second_all = lax.optimization_barrier((stats, *second_all))
    gathered = lax.all_gather(stats, HEAD)
    spot = jnp.stack([lane, place, jnp.int32(seq_count // 2)]).astype(jnp.int32)
    row = jax.ShapeDtypeStruct((groups, 8, TILE), F32)
    near_out, far_out, terms = pl.pallas_call(
        functools.partial(lanes_kernel, heads, near),
        out_shape=[row, row, jax.ShapeDtypeStruct((8, TILE), F32)],
        in_specs=[smem, vmem],
        out_specs=[vmem] * 3,
        scratch_shapes=[pltpu.VMEM((24, TILE), F32)],
        compiler_params=params,
        name="lanes",
    )(spot, gathered)
    near_pairs = [
        (frame * groups + at, (frame + OFFSETS[1 + at]) * groups + at)
        for frame in range(seq_count)
        for at in range(near - 1)
        if 0 <= frame + OFFSETS[1 + at] < seq_count
    ]
    far_pairs = [
        (frame * groups + at, (frame + shift) % seq_count * groups + at)
        for frame in range(seq_count)
        for at, shift in enumerate((-line, line, seq_count // 2))
        if at == 2 or 0 <= frame + shift < seq_count
    ]
    near_in = lax.ppermute(near_out, SEQ + HEAD, near_pairs)
    far_in = lax.ppermute(far_out, SEQ + HEAD, far_pairs)
    got = lax.all_to_all(
        jnp.concatenate([near_in, far_in], axis=1), HEAD, 0, 0, tiled=True
    )
    grad_q, grad_k, grad_v = pl.pallas_call(
        functools.partial(backward_kernel, heads, near, line, channels),
        out_shape=[jax.ShapeDtypeStruct(whole, BF16)] * 3,
        in_specs=[smem] + [vmem] * (12 + near),
        out_specs=[vmem] * 3,
        compiler_params=params,
        name="backward",
    )(
        listed, sums, terms, stats, got, q_raw, k_raw, k_norm, values, dq, q_gain, k_gain,
        column, *second_all,
    )
    return tuple(
        jnp.transpose(array, (1, 0, 2)) for array in (attended, grad_q, grad_k, grad_v)
    )


def solution(mesh):
    split = Mesh(mesh.devices.reshape(4, -1, mesh.shape["head"] // 2, 2), SEQ + HEAD)

    def whole(q_raw, k_raw, values, grad_out, q_gain, k_gain, key_tiles):
        tokens = P(SEQ, HEAD, None)
        return jax.shard_map(
            functools.partial(per_device, q_raw.shape[1]),
            mesh=split,
            in_specs=(tokens,) * 4 + (P(HEAD, None), P(HEAD, None), P()),
            out_specs=(tokens,) * 4,
            check_vma=False,
        )(q_raw, k_raw, values, grad_out, q_gain, k_gain, key_tiles)

    return whole
```

time: 204 us -> 183 us (0.90)
  the two profiles are of different devices: /device:TPU:7 before, /device:TPU:70 now
where the time goes in v2:
time: 183 us; the launch traced here: 182 us
  starting transfers between devices  94.1 us (51%)
  blocking collectives  40.9 us (22%)
  Pallas kernels  15.3 us (8%)
  between operations  14.5 us (8%)
  local copies, waits for them, and re-layouts  9.97 us (5%)
  waiting for transfers between devices  3.93 us (2%)
  other arithmetic  3.51 us (2%)
    ppermute x16, starting transfers between devices, passed(): return lax.ppermute(value, SEQ, pairs)  90.1 us
    all_to_all x1, blocking collectives, per_device(): lax.all_to_all(jnp.concatenate([near_in, far_in], axis=1), HEAD, 0, 0, ti...  14.1 us
    psum x2, blocking collectives, per_device(): sums = lax.psum(lax.psum(sums, 'c'), 'y')  14 us
    all_gather x1, blocking collectives, per_device(): gathered = lax.all_gather(stats, HEAD)  12.7 us
    unnamed x47, local copies, waits for them, and re-layouts  9.9 us
    pallas_call x1, Pallas kernels, per_device(): pl.pallas_call(functools.partial(backward_kernel, heads, near, line, chan...  6.85 us
    pallas_call x1, Pallas kernels, per_device(): pl.pallas_call(functools.partial(forward_kernel, heads, near, line, chann...  6.77 us
    ppermute x1, waiting for transfers between devices, per_device(): near_in = lax.ppermute(near_out, SEQ + HEAD, near_pairs)  3.87 us
  transfers between devices with their start and end apart: 19, of which 1 were waited for; matrix products, arithmetic and copies ran while one was open for 1% of the time, Pallas kernels for 4%

profile of v2, /device:TPU:70, one launch (start us, length us, event | category | flops | bytes accessed | tf_op | source)
XLA Modules:
  0.0 182.1 jit_solution(15318529869833059874)
XLA Ops:
  7.2 0.0 copy-start
  7.2 0.0 all-gather.4.cloned.1.call-start
  7.2 1.9 %pad_maximum_fusion = bf16[12,128,128]{2,1,0:T(8,128)(2,1)} fusion(bf16[3,128,128]{2,1,0:T(8,128)(2,1)} %bitcast.20, bf16[3,128,128]{2,1,0:T(8,128)(2,1)} %bitcast.15, bf16[3,128,128]{2,1,0:T(8,128)(2,1)} %bitcast.23, bf16[3,128,128]{2,1,0:T(8,128)(2,1)} %bitcast.26), kind=kLoop, calls=%fused_computation | loop fusion | flops 589824 | bytes 786432 | tf_op jit(solution)/shard_map/concatenate | solution.py:249
  9.1 0.0 all-gather.4.cloned.1.call-update
  9.1 1.0 pad_maximum_fusion.1.refs_0_
  10.1 3.8 %collective-permute-start = (bf16[6,128,128]{2,1,0:T(8,128)(2,1)S(1)}, bf16[6,128,128]{2,1,0:T(8,128)(2,1)S(1)}, u32[]{:S(2)}, u32[]{:S(2)}) collective-permute-start(bf16[6,128,128]{2,1,0:T(8,128)(2,1)S(1)} %pad_maximum_fusion.1.refs_0_), channel_id=1, source_target_pairs={{0,8},{8,16},{16,24},{24,32},{32,40},{40,48},{48,56},{56,64},{64,7... | collective-permute-start | bytes 589832 | tf_op jit(solution)/shard_map/ppermute | solution.py:219
  13.9 2.0 %collective-permute-start.1 = (bf16[6,128,128]{2,1,0:T(8,128)(2,1)S(1)}, bf16[6,128,128]{2,1,0:T(8,128)(2,1)S(1)}, u32[]{:S(2)}, u32[]{:S(2)}) collective-permute-start(bf16[6,128,128]{2,1,0:T(8,128)(2,1)S(1)} %pad_maximum_fusion.1.refs_0_), channel_id=1, source_target_pairs={{8,0},{16,8},{24,16},{32,24},{40,32},{48,40},{56,48},{64,56},{72,6... | collective-permute-start | bytes 589832 | tf_op jit(solution)/shard_map/ppermute | solution.py:219
  16.0 4.9 %collective-permute-start.8 = (bf16[6,128,128]{2,1,0:T(8,128)(2,1)S(1)}, bf16[6,128,128]{2,1,0:T(8,128)(2,1)S(1)}, u32[]{:S(2)}, u32[]{:S(2)}) collective-permute-start(bf16[6,128,128]{2,1,0:T(8,128)(2,1)S(1)} %pad_maximum_fusion.2.refs_0_), channel_id=1, source_target_pairs={{0,8},{8,16},{16,24},{24,32},{32,40},{40,48},{48,56},{56,64},{64,7... | collective-permute-start | bytes 589832 | tf_op jit(solution)/shard_map/ppermute | solution.py:219
  21.0 1.9 %collective-permute-start.9 = (bf16[6,128,128]{2,1,0:T(8,128)(2,1)S(1)}, bf16[6,128,128]{2,1,0:T(8,128)(2,1)S(1)}, u32[]{:S(2)}, u32[]{:S(2)}) collective-permute-start(bf16[6,128,128]{2,1,0:T(8,128)(2,1)S(1)} %pad_maximum_fusion.2.refs_0_), channel_id=1, source_target_pairs={{8,0},{16,8},{24,16},{32,24},{40,32},{48,40},{56,48},{64,56},{72,6... | collective-permute-start | bytes 589832 | tf_op jit(solution)/shard_map/ppermute | solution.py:219
  22.9 0.0 collective-permute-done.refs_1_
  22.9 5.1 %collective-permute-start.2 = (bf16[6,128,128]{2,1,0:T(8,128)(2,1)S(1)}, bf16[6,128,128]{2,1,0:T(8,128)(2,1)S(1)}, u32[]{:S(2)}, u32[]{:S(2)}) collective-permute-start(bf16[6,128,128]{2,1,0:T(8,128)(2,1)S(1)} %collective-permute-done.refs_1_), channel_id=1, source_target_pairs={{0,8},{8,16},{16,24},{24,32},{32,40},{40,48},{48,56},{56,64},{64,7... | collective-permute-start | bytes 589832 | tf_op jit(solution)/shard_map/ppermute | solution.py:219
  28.0 3.6 %collective-permute-start.3 = (bf16[6,128,128]{2,1,0:T(8,128)(2,1)S(1)}, bf16[6,128,128]{2,1,0:T(8,128)(2,1)S(1)}, u32[]{:S(2)}, u32[]{:S(2)}) collective-permute-start(bf16[6,128,128]{2,1,0:T(8,128)(2,1)S(1)} %collective-permute-done.1.refs_2_), channel_id=1, source_target_pairs={{8,0},{16,8},{24,16},{32,24},{40,32},{48,40},{56,48},{64,56},{72,6... | collective-permute-start | bytes 589832 | tf_op jit(solution)/shard_map/ppermute | solution.py:219
  31.7 3.4 %collective-permute-start.10 = (bf16[6,128,128]{2,1,0:T(8,128)(2,1)S(1)}, bf16[6,128,128]{2,1,0:T(8,128)(2,1)S(1)}, u32[]{:S(2)}, u32[]{:S(2)}) collective-permute-start(bf16[6,128,128]{2,1,0:T(8,128)(2,1)S(1)} %collective-permute-done.8.refs_1_), channel_id=1, source_target_pairs={{0,8},{8,16},{16,24},{24,32},{32,40},{40,48},{48,56},{56,64},{64,7... | collective-permute-start | bytes 589832 | tf_op jit(solution)/shard_map/ppermute | solution.py:219
  35.1 0.7 copy-done.10
  35.8 4.5 %collective-permute-start.11 = (bf16[6,128,128]{2,1,0:T(8,128)(2,1)S(1)}, bf16[6,128,128]{2,1,0:T(8,128)(2,1)S(1)}, u32[]{:S(2)}, u32[]{:S(2)}) collective-permute-start(bf16[6,128,128]{2,1,0:T(8,128)(2,1)S(1)} %collective-permute-done.9.refs_2_), channel_id=1, source_target_pairs={{8,0},{16,8},{24,16},{32,24},{40,32},{48,40},{56,48},{64,56},{72,6... | collective-permute-start | bytes 589832 | tf_op jit(solution)/shard_map/ppermute | solution.py:219
  40.3 0.7 copy-done.12
  41.0 5.2 %collective-permute-start.4 = (bf16[6,128,128]{2,1,0:T(8,128)(2,1)S(1)}, bf16[6,128,128]{2,1,0:T(8,128)(2,1)S(1)}, u32[]{:S(2)}, u32[]{:S(2)}) collective-permute-start(bf16[6,128,128]{2,1,0:T(8,128)(2,1)S(1)} %collective-permute-done.2.refs_3_), channel_id=1, source_target_pairs={{0,16},{8,24},{16,32},{24,40},{32,48},{40,56},{48,64},{56,72},{64,... | collective-permute-start | bytes 589832 | tf_op jit(solution)/shard_map/ppermute | solution.py:219
  46.2 6.3 %collective-permute-start.5 = (bf16[6,128,128]{2,1,0:T(8,128)(2,1)S(1)}, bf16[6,128,128]{2,1,0:T(8,128)(2,1)S(1)}, u32[]{:S(2)}, u32[]{:S(2)}) collective-permute-start(bf16[6,128,128]{2,1,0:T(8,128)(2,1)S(1)} %collective-permute-done.3.refs_4_), channel_id=1, source_target_pairs={{16,0},{24,8},{32,16},{40,24},{48,32},{56,40},{64,48},{72,56},{80,... | collective-permute-start | bytes 589832 | tf_op jit(solution)/shard_map/ppermute | solution.py:219
  52.6 1.9 %collective-permute-start.12 = (bf16[6,128,128]{2,1,0:T(8,128)(2,1)S(1)}, bf16[6,128,128]{2,1,0:T(8,128)(2,1)}, u32[]{:S(2)}, u32[]{:S(2)}) collective-permute-start(bf16[6,128,128]{2,1,0:T(8,128)(2,1)S(1)} %collective-permute-done.10.refs_3_), channel_id=1, source_target_pairs={{0,16},{8,24},{16,32},{24,40},{32,48},{40,56},{48,64},{56,72},{64,... | collective-permute-start | bytes 589832 | tf_op jit(solution)/shard_map/ppermute | solution.py:219
  54.5 0.7 copy-done.14
  55.1 6.9 %collective-permute-start.13 = (bf16[6,128,128]{2,1,0:T(8,128)(2,1)S(1)}, bf16[6,128,128]{2,1,0:T(8,128)(2,1)}, u32[]{:S(2)}, u32[]{:S(2)}) collective-permute-start(bf16[6,128,128]{2,1,0:T(8,128)(2,1)S(1)} %collective-permute-done.11.refs_4_), channel_id=1, source_target_pairs={{16,0},{24,8},{32,16},{40,24},{48,32},{56,40},{64,48},{72,56},{80,... | collective-permute-start | bytes 589832 | tf_op jit(solution)/shard_map/ppermute | solution.py:219
  62.1 0.7 copy-done.16
  62.8 3.8 %collective-permute-start.6 = (bf16[6,128,128]{2,1,0:T(8,128)(2,1)S(1)}, bf16[6,128,128]{2,1,0:T(8,128)(2,1)S(1)}, u32[]{:S(2)}, u32[]{:S(2)}) collective-permute-start(bf16[6,128,128]{2,1,0:T(8,128)(2,1)S(1)} %collective-permute-done.4.refs_5_), channel_id=1, source_target_pairs={{0,32},{8,40},{16,48},{24,56},{32,64},{40,72},{48,80},{56,88},{64,... | collective-permute-start | bytes 589832 | tf_op jit(solution)/shard_map/ppermute | solution.py:219
  66.6 6.9 %collective-permute-start.7 = (bf16[6,128,128]{2,1,0:T(8,128)(2,1)S(1)}, bf16[6,128,128]{2,1,0:T(8,128)(2,1)S(1)}, u32[]{:S(2)}, u32[]{:S(2)}) collective-permute-start(bf16[6,128,128]{2,1,0:T(8,128)(2,1)S(1)} %collective-permute-done.5.refs_6_), channel_id=1, source_target_pairs={{32,0},{40,8},{48,16},{56,24},{64,32},{72,40},{80,48},{88,56},{96,... | collective-permute-start | bytes 589832 | tf_op jit(solution)/shard_map/ppermute | solution.py:219
  73.4 7.0 %collective-permute-start.14 = (bf16[6,128,128]{2,1,0:T(8,128)(2,1)}, bf16[6,128,128]{2,1,0:T(8,128)(2,1)}, u32[]{:S(2)}, u32[]{:S(2)}) collective-permute-start(bf16[6,128,128]{2,1,0:T(8,128)(2,1)} %collective-permute-done.12.refs_5_), channel_id=1, source_target_pairs={{0,32},{8,40},{16,48},{24,56},{32,64},{40,72},{48,80},{56,88},{64,... | collective-permute-start | bytes 589832 | tf_op jit(solution)/shard_map/ppermute | solution.py:219
  80.5 22.7 %collective-permute-start.15 = (bf16[6,128,128]{2,1,0:T(8,128)(2,1)}, bf16[6,128,128]{2,1,0:T(8,128)(2,1)}, u32[]{:S(2)}, u32[]{:S(2)}) collective-permute-start(bf16[6,128,128]{2,1,0:T(8,128)(2,1)} %collective-permute-done.13.refs_6_), channel_id=1, source_target_pairs={{32,0},{40,8},{48,16},{56,24},{64,32},{72,40},{80,48},{88,56},{96,... | collective-permute-start | bytes 589832 | tf_op jit(solution)/shard_map/ppermute | solution.py:219
  103.2 0.1 constant_dynamic-slice_fusion
  103.3 0.6 copy.13.listed_ref
  103.9 0.7 pad_add_fusion.place_ref
  104.5 0.7 copy-done.7
  105.2 1.4 copy-done.1
  106.6 0.9 copy-done.8
  107.5 0.7 copy-done.20
  108.2 1.1 squares.1
  109.3 3.1 %psum.14 = f32[16,128]{1,0:T(8,128)} all-reduce(f32[16,128]{1,0:T(8,128)S(1)} %squares.1), channel_id=1, replica_groups=mesh['x'=4,'z'=16,'y'=4,'c'=2] {'c'}, use_global_device_ids=true, to_apply=%region_0.0 | all-reduce | flops 2048 | bytes 16384 | tf_op jit(solution)/shard_map/psum | solution.py:268
  112.4 11.0 %psum.15.sums_ref = f32[16,128]{1,0:T(8,128)S(1)} all-reduce(f32[16,128]{1,0:T(8,128)} %psum.14), channel_id=1, replica_groups=mesh['x'=4,'z'=16,'y'=4,'c'=2] {'y'}, use_global_device_ids=true, to_apply=%region_1.0 | all-reduce | flops 2048 | bytes 16384 | tf_op jit(solution)/shard_map/psum | solution.py:268
  123.4 0.9 copy-done.9
  124.3 0.7 copy-done.18
  125.0 0.7 copy-done.19
  125.7 0.7 copy-done.21
  126.4 6.8 %forward.1 = (bf16[3,128,128]{2,1,0:T(8,128)(2,1)}, f32[3,128,128]{2,1,0:T(8,128)S(1)}, bf16[3,128,128]{2,1,0:T(8,128)(2,1)S(1)}, f32[24,128]{1,0:T(8,128)S(1)}) custom-call(s32[1,13]{1,0:T(1,128)S(1)} %copy-done.21, f32[16,128]{1,0:T(8,128)S(1)} %psum.15.sums_ref, bf16[3,128,128]{2,1,0:T(8,128)(2,1)S(1)} %bitcast.18, bf16[3,128,128]{2,1,0:T(8,128)(2,1)S(1)} %bitcast.22, ...), custom_call_target="tpu_custom_call" | custom-call | tf_op jit(solution)/shard_map/forward/pallas_call | solution.py:269
  133.2 12.7 %all-gather.1 = f32[192,128]{1,0:T(8,128)S(1)} all-gather(f32[24,128]{1,0:T(8,128)S(1)} %get-tuple-element.26.own_ref), channel_id=3, replica_groups=mesh['x'=4,'z'=16,'y'=4,'c'=2] {'y','c'}, dimensions={0}, use_global_device_ids=true | all-gather | bytes 110592 | tf_op jit(solution)/shard_map/all_gather | solution.py:288
  145.9 0.6 lanes.1
  146.5 2.0 %collective-permute-start.17 = (f32[8,8,128]{2,1,0:T(8,128)S(1)}, f32[8,8,128]{2,1,0:T(8,128)S(1)}, u32[]{:S(2)}, u32[]{:S(2)}) collective-permute-start(f32[8,8,128]{2,1,0:T(8,128)S(1)} %get-tuple-element.29), channel_id=1, source_target_pairs={{1,129},{2,258},{9,137},{10,266},{17,145},{18,274},{25,153},{26,28... | collective-permute-start | bytes 98312 | tf_op jit(solution)/shard_map/ppermute | solution.py:313
  148.5 1.9 %collective-permute-start.16 = (f32[8,8,128]{2,1,0:T(8,128)S(1)}, f32[8,8,128]{2,1,0:T(8,128)S(1)}, u32[]{:S(2)}, u32[]{:S(2)}) collective-permute-start(f32[8,8,128]{2,1,0:T(8,128)S(1)} %get-tuple-element.28), channel_id=1, source_target_pairs={{1,9},{3,19},{5,37},{7,71},{8,0},{9,17},{11,27},{13,45},{15,79},{1... | collective-permute-start | bytes 98312 | tf_op jit(solution)/shard_map/ppermute | solution.py:312
  150.4 3.9 %collective-permute-done.16 = f32[8,8,128]{2,1,0:T(8,128)S(1)} collective-permute-done((f32[8,8,128]{2,1,0:T(8,128)S(1)}, f32[8,8,128]{2,1,0:T(8,128)S(1)}, u32[]{:S(2)}, u32[]{:S(2)}) %collective-permute-start.16) | collective-permute-done | bytes 32800 | tf_op jit(solution)/shard_map/ppermute | solution.py:312
  154.3 14.1 %all_to_all.5.got_ref = f32[8,16,128]{2,1,0:T(8,128)S(1)} all-to-all(f32[8,16,128]{2,1,0:T(8,128)S(1)} %pad_maximum_fusion.3), channel_id=1, replica_groups=mesh['x'=4,'z'=16,'y'=4,'c'=2] {'y','c'}, dimensions={0} | all-to-all | bytes 131072 | tf_op jit(solution)/shard_map/all_to_all | solution.py:314
  168.4 6.9 %backward.1 = (bf16[3,128,128]{2,1,0:T(8,128)(2,1)}, bf16[3,128,128]{2,1,0:T(8,128)(2,1)}, bf16[3,128,128]{2,1,0:T(8,128)(2,1)}) custom-call(s32[1,13]{1,0:T(1,128)S(1)} %copy-done.21, f32[16,128]{1,0:T(8,128)S(1)} %psum.15.sums_ref, f32[8,128]{1,0:T(8,128)S(1)} %get-tuple-element.27.terms_ref, f32[24,128]{1,0:T(8,128)S(1)} %get-tuple-element.26.own_ref, ...), custom_call_target="tpu_custom_call" | custom-call | tf_op jit(solution)/shard_map/backward/pallas_call | solution.py:317
  (52 shorter events, 0.1 us)
Async XLA Ops:
  7.2 96.0 %copy-start = (s32[64,13]{0,1:T(8,128)S(1)}, s32[64,13]{0,1:T(8,128)}, u32[]{:S(2)}) copy-start(s32[64,13]{0,1:T(8,128)} %param.13) | copy-start | bytes 9988
  7.2 8.8 %copy-start.3 = (bf16[128,3,128]{2,0,1:T(8,128)(2,1)S(1)}, bf16[128,3,128]{2,0,1:T(8,128)(2,1)}, u32[]{:S(2)}) copy-start(bf16[128,3,128]{2,0,1:T(8,128)(2,1)} %param.7) | copy-start | bytes 294916
  7.2 8.8 %copy-start.4 = (bf16[128,3,128]{2,0,1:T(8,128)(2,1)S(1)}, bf16[128,3,128]{2,0,1:T(8,128)(2,1)}, u32[]{:S(2)}) copy-start(bf16[128,3,128]{2,0,1:T(8,128)(2,1)} %param.10) | copy-start | bytes 294916
  7.2 98.0 %all-gather.4.cloned.1.call-start = ((), (), s32[]{:S(2)}) async-start(), calls=%async_computation.1 | async-start | bytes 1966080 | tf_op jit(solution)/shard_map/all_gather | solution.py:248
  10.1 12.8 %collective-permute-start = (bf16[6,128,128]{2,1,0:T(8,128)(2,1)S(1)}, bf16[6,128,128]{2,1,0:T(8,128)(2,1)S(1)}, u32[]{:S(2)}, u32[]{:S(2)}) collective-permute-start(bf16[6,128,128]{2,1,0:T(8,128)(2,1)S(1)} %pad_maximum_fusion.1.refs_0_), channel_id=1, source_target_pairs={{0,8},{8,16},{16,24},{24,32},{32,40},{40,48},{48,56},{56,64},{64,7... | collective-permute-start | bytes 589832 | tf_op jit(solution)/shard_map/ppermute | solution.py:219
  13.9 14.1 %collective-permute-start.1 = (bf16[6,128,128]{2,1,0:T(8,128)(2,1)S(1)}, bf16[6,128,128]{2,1,0:T(8,128)(2,1)S(1)}, u32[]{:S(2)}, u32[]{:S(2)}) collective-permute-start(bf16[6,128,128]{2,1,0:T(8,128)(2,1)S(1)} %pad_maximum_fusion.1.refs_0_), channel_id=1, source_target_pairs={{8,0},{16,8},{24,16},{32,24},{40,32},{48,40},{56,48},{64,56},{72,6... | collective-permute-start | bytes 589832 | tf_op jit(solution)/shard_map/ppermute | solution.py:219
  16.0 15.7 %collective-permute-start.8 = (bf16[6,128,128]{2,1,0:T(8,128)(2,1)S(1)}, bf16[6,128,128]{2,1,0:T(8,128)(2,1)S(1)}, u32[]{:S(2)}, u32[]{:S(2)}) collective-permute-start(bf16[6,128,128]{2,1,0:T(8,128)(2,1)S(1)} %pad_maximum_fusion.2.refs_0_), channel_id=1, source_target_pairs={{0,8},{8,16},{16,24},{24,32},{32,40},{40,48},{48,56},{56,64},{64,7... | collective-permute-start | bytes 589832 | tf_op jit(solution)/shard_map/ppermute | solution.py:219
  21.0 14.9 %collective-permute-start.9 = (bf16[6,128,128]{2,1,0:T(8,128)(2,1)S(1)}, bf16[6,128,128]{2,1,0:T(8,128)(2,1)S(1)}, u32[]{:S(2)}, u32[]{:S(2)}) collective-permute-start(bf16[6,128,128]{2,1,0:T(8,128)(2,1)S(1)} %pad_maximum_fusion.2.refs_0_), channel_id=1, source_target_pairs={{8,0},{16,8},{24,16},{32,24},{40,32},{48,40},{56,48},{64,56},{72,6... | collective-permute-start | bytes 589832 | tf_op jit(solution)/shard_map/ppermute | solution.py:219
  22.9 18.1 %collective-permute-start.2 = (bf16[6,128,128]{2,1,0:T(8,128)(2,1)S(1)}, bf16[6,128,128]{2,1,0:T(8,128)(2,1)S(1)}, u32[]{:S(2)}, u32[]{:S(2)}) collective-permute-start(bf16[6,128,128]{2,1,0:T(8,128)(2,1)S(1)} %collective-permute-done.refs_1_), channel_id=1, source_target_pairs={{0,8},{8,16},{16,24},{24,32},{32,40},{40,48},{48,56},{56,64},{64,7... | collective-permute-start | bytes 589832 | tf_op jit(solution)/shard_map/ppermute | solution.py:219
  28.0 18.2 %collective-permute-start.3 = (bf16[6,128,128]{2,1,0:T(8,128)(2,1)S(1)}, bf16[6,128,128]{2,1,0:T(8,128)(2,1)S(1)}, u32[]{:S(2)}, u32[]{:S(2)}) collective-permute-start(bf16[6,128,128]{2,1,0:T(8,128)(2,1)S(1)} %collective-permute-done.1.refs_2_), channel_id=1, source_target_pairs={{8,0},{16,8},{24,16},{32,24},{40,32},{48,40},{56,48},{64,56},{72,6... | collective-permute-start | bytes 589832 | tf_op jit(solution)/shard_map/ppermute | solution.py:219
  31.7 20.8 %collective-permute-start.10 = (bf16[6,128,128]{2,1,0:T(8,128)(2,1)S(1)}, bf16[6,128,128]{2,1,0:T(8,128)(2,1)S(1)}, u32[]{:S(2)}, u32[]{:S(2)}) collective-permute-start(bf16[6,128,128]{2,1,0:T(8,128)(2,1)S(1)} %collective-permute-done.8.refs_1_), channel_id=1, source_target_pairs={{0,8},{8,16},{16,24},{24,32},{32,40},{40,48},{48,56},{56,64},{64,7... | collective-permute-start | bytes 589832 | tf_op jit(solution)/shard_map/ppermute | solution.py:219
  35.1 0.7 copy-start.10
  35.8 19.3 %collective-permute-start.11 = (bf16[6,128,128]{2,1,0:T(8,128)(2,1)S(1)}, bf16[6,128,128]{2,1,0:T(8,128)(2,1)S(1)}, u32[]{:S(2)}, u32[]{:S(2)}) collective-permute-start(bf16[6,128,128]{2,1,0:T(8,128)(2,1)S(1)} %collective-permute-done.9.refs_2_), channel_id=1, source_target_pairs={{8,0},{16,8},{24,16},{32,24},{40,32},{48,40},{56,48},{64,56},{72,6... | collective-permute-start | bytes 589832 | tf_op jit(solution)/shard_map/ppermute | solution.py:219
  40.3 0.7 copy-start.12
  41.0 21.7 %collective-permute-start.4 = (bf16[6,128,128]{2,1,0:T(8,128)(2,1)S(1)}, bf16[6,128,128]{2,1,0:T(8,128)(2,1)S(1)}, u32[]{:S(2)}, u32[]{:S(2)}) collective-permute-start(bf16[6,128,128]{2,1,0:T(8,128)(2,1)S(1)} %collective-permute-done.2.refs_3_), channel_id=1, source_target_pairs={{0,16},{8,24},{16,32},{24,40},{32,48},{40,56},{48,64},{56,72},{64,... | collective-permute-start | bytes 589832 | tf_op jit(solution)/shard_map/ppermute | solution.py:219
  46.2 20.3 %collective-permute-start.5 = (bf16[6,128,128]{2,1,0:T(8,128)(2,1)S(1)}, bf16[6,128,128]{2,1,0:T(8,128)(2,1)S(1)}, u32[]{:S(2)}, u32[]{:S(2)}) collective-permute-start(bf16[6,128,128]{2,1,0:T(8,128)(2,1)S(1)} %collective-permute-done.3.refs_4_), channel_id=1, source_target_pairs={{16,0},{24,8},{32,16},{40,24},{48,32},{56,40},{64,48},{72,56},{80,... | collective-permute-start | bytes 589832 | tf_op jit(solution)/shard_map/ppermute | solution.py:219
  52.6 20.9 %collective-permute-start.12 = (bf16[6,128,128]{2,1,0:T(8,128)(2,1)S(1)}, bf16[6,128,128]{2,1,0:T(8,128)(2,1)}, u32[]{:S(2)}, u32[]{:S(2)}) collective-permute-start(bf16[6,128,128]{2,1,0:T(8,128)(2,1)S(1)} %collective-permute-done.10.refs_3_), channel_id=1, source_target_pairs={{0,16},{8,24},{16,32},{24,40},{32,48},{40,56},{48,64},{56,72},{64,... | collective-permute-start | bytes 589832 | tf_op jit(solution)/shard_map/ppermute | solution.py:219
  54.5 0.7 copy-start.14
  55.1 25.3 %collective-permute-start.13 = (bf16[6,128,128]{2,1,0:T(8,128)(2,1)S(1)}, bf16[6,128,128]{2,1,0:T(8,128)(2,1)}, u32[]{:S(2)}, u32[]{:S(2)}) collective-permute-start(bf16[6,128,128]{2,1,0:T(8,128)(2,1)S(1)} %collective-permute-done.11.refs_4_), channel_id=1, source_target_pairs={{16,0},{24,8},{32,16},{40,24},{48,32},{56,40},{64,48},{72,56},{80,... | collective-permute-start | bytes 589832 | tf_op jit(solution)/shard_map/ppermute | solution.py:219
  62.1 0.7 copy-start.16
  62.8 41.8 %collective-permute-start.6 = (bf16[6,128,128]{2,1,0:T(8,128)(2,1)S(1)}, bf16[6,128,128]{2,1,0:T(8,128)(2,1)S(1)}, u32[]{:S(2)}, u32[]{:S(2)}) collective-permute-start(bf16[6,128,128]{2,1,0:T(8,128)(2,1)S(1)} %collective-permute-done.4.refs_5_), channel_id=1, source_target_pairs={{0,32},{8,40},{16,48},{24,56},{32,64},{40,72},{48,80},{56,88},{64,... | collective-permute-start | bytes 589832 | tf_op jit(solution)/shard_map/ppermute | solution.py:219
  66.6 38.0 %collective-permute-start.7 = (bf16[6,128,128]{2,1,0:T(8,128)(2,1)S(1)}, bf16[6,128,128]{2,1,0:T(8,128)(2,1)S(1)}, u32[]{:S(2)}, u32[]{:S(2)}) collective-permute-start(bf16[6,128,128]{2,1,0:T(8,128)(2,1)S(1)} %collective-permute-done.5.refs_6_), channel_id=1, source_target_pairs={{32,0},{40,8},{48,16},{56,24},{64,32},{72,40},{80,48},{88,56},{96,... | collective-permute-start | bytes 589832 | tf_op jit(solution)/shard_map/ppermute | solution.py:219
  73.4 59.7 %collective-permute-start.14 = (bf16[6,128,128]{2,1,0:T(8,128)(2,1)}, bf16[6,128,128]{2,1,0:T(8,128)(2,1)}, u32[]{:S(2)}, u32[]{:S(2)}) collective-permute-start(bf16[6,128,128]{2,1,0:T(8,128)(2,1)} %collective-permute-done.12.refs_5_), channel_id=1, source_target_pairs={{0,32},{8,40},{16,48},{24,56},{32,64},{40,72},{48,80},{56,88},{64,... | collective-permute-start | bytes 589832 | tf_op jit(solution)/shard_map/ppermute | solution.py:219
  80.5 52.7 %collective-permute-start.15 = (bf16[6,128,128]{2,1,0:T(8,128)(2,1)}, bf16[6,128,128]{2,1,0:T(8,128)(2,1)}, u32[]{:S(2)}, u32[]{:S(2)}) collective-permute-start(bf16[6,128,128]{2,1,0:T(8,128)(2,1)} %collective-permute-done.13.refs_6_), channel_id=1, source_target_pairs={{32,0},{40,8},{48,16},{56,24},{64,32},{72,40},{80,48},{88,56},{96,... | collective-permute-start | bytes 589832 | tf_op jit(solution)/shard_map/ppermute | solution.py:219
  104.5 0.7 copy-start.7
  105.2 1.4 copy-start.1
  106.6 0.9 copy-start.8
  107.5 0.7 copy-start.20
  108.2 15.2 %copy-start.2 = (bf16[48,128,128]{2,1,0:T(8,128)(2,1)S(1)}, bf16[48,128,128]{2,1,0:T(8,128)(2,1)}, u32[]{:S(2)}) copy-start(bf16[48,128,128]{2,1,0:T(8,128)(2,1)} %all-gather.4.cloned.1.call-done) | copy-start | bytes 4718596
  123.4 0.9 copy-start.9
  124.3 0.7 copy-start.18
  125.0 0.7 copy-start.19
  125.7 0.7 copy-start.21
  126.3 19.6 %copy-start.22 = (s32[3]{0:T(128)S(1)}, s32[3]{0:T(128)}, u32[]{:S(2)}) copy-start(s32[3]{0:T(128)} %pad_add_fusion.place_ref) | copy-start | bytes 40
  126.3 42.1 %copy-start.5 = (bf16[128,3,128]{2,0,1:T(8,128)(2,1)S(1)}, bf16[128,3,128]{2,0,1:T(8,128)(2,1)}, u32[]{:S(2)}) copy-start(bf16[128,3,128]{2,0,1:T(8,128)(2,1)} %param.9) | copy-start | bytes 294916
  126.3 42.1 %copy-start.6 = (bf16[128,3,128]{2,0,1:T(8,128)(2,1)S(1)}, bf16[128,3,128]{2,0,1:T(8,128)(2,1)}, u32[]{:S(2)}) copy-start(bf16[128,3,128]{2,0,1:T(8,128)(2,1)} %param.8) | copy-start | bytes 294916
  126.3 42.1 %copy-start.11 = (bf16[6,128,128]{2,1,0:T(8,128)(2,1)S(1)}, bf16[6,128,128]{2,1,0:T(8,128)(2,1)}, u32[]{:S(2)}) copy-start(bf16[6,128,128]{2,1,0:T(8,128)(2,1)} %copy-done.10) | copy-start | bytes 589828
  126.3 42.1 %copy-start.13 = (bf16[6,128,128]{2,1,0:T(8,128)(2,1)S(1)}, bf16[6,128,128]{2,1,0:T(8,128)(2,1)}, u32[]{:S(2)}) copy-start(bf16[6,128,128]{2,1,0:T(8,128)(2,1)} %copy-done.12) | copy-start | bytes 589828
  126.3 42.1 %copy-start.15 = (bf16[6,128,128]{2,1,0:T(8,128)(2,1)S(1)}, bf16[6,128,128]{2,1,0:T(8,128)(2,1)}, u32[]{:S(2)}) copy-start(bf16[6,128,128]{2,1,0:T(8,128)(2,1)} %copy-done.14) | copy-start | bytes 589828
  126.3 42.1 %copy-start.17 = (bf16[6,128,128]{2,1,0:T(8,128)(2,1)S(1)}, bf16[6,128,128]{2,1,0:T(8,128)(2,1)}, u32[]{:S(2)}) copy-start(bf16[6,128,128]{2,1,0:T(8,128)(2,1)} %copy-done.16) | copy-start | bytes 589828
  146.5 3.9 %collective-permute-start.17 = (f32[8,8,128]{2,1,0:T(8,128)S(1)}, f32[8,8,128]{2,1,0:T(8,128)S(1)}, u32[]{:S(2)}, u32[]{:S(2)}) collective-permute-start(f32[8,8,128]{2,1,0:T(8,128)S(1)} %get-tuple-element.29), channel_id=1, source_target_pairs={{1,129},{2,258},{9,137},{10,266},{17,145},{18,274},{25,153},{26,28... | collective-permute-start | bytes 98312 | tf_op jit(solution)/shard_map/ppermute | solution.py:313
  148.5 5.8 %collective-permute-start.16 = (f32[8,8,128]{2,1,0:T(8,128)S(1)}, f32[8,8,128]{2,1,0:T(8,128)S(1)}, u32[]{:S(2)}, u32[]{:S(2)}) collective-permute-start(f32[8,8,128]{2,1,0:T(8,128)S(1)} %get-tuple-element.28), channel_id=1, source_target_pairs={{1,9},{3,19},{5,37},{7,71},{8,0},{9,17},{11,27},{13,45},{15,79},{1... | collective-permute-start | bytes 98312 | tf_op jit(solution)/shard_map/ppermute | solution.py:312
Sparse Core Ops, SparseCore 0:
  10.1 36.7 all-gather.3

commit v3 on v2

--- a/solution.py
+++ b/solution.py
@@ -33,6 +33,15 @@
     return jnp.transpose(jnp.concatenate([rows, fill], axis=0))
 
 
+def own_frame():
+    return lax.axis_index("x") * lax.axis_size("z") + lax.axis_index("z")
+
+
+def inside(frame, line, place):
+    at = frame + OFFSETS[place]
+    return (at >= 0) & (at < line * lax.axis_size("x"))
+
+
 def tile_of(tiles, gathered_ref, frame, near, line, place, skip=0):
     if place < near:
         return lambda i: tiles[place][i]
@@ -41,10 +50,11 @@
     return lambda i: gathered_ref[at, skip + i]
 
 
-def squares_kernel(heads, near, line, listed_ref, q_ref, gathered_ref, *refs):
+def squares_kernel(heads, near, line, q_ref, gathered_ref, *refs):
     tiles, out_ref = refs[:-1], refs[-1]
     count = len(OFFSETS)
-    reads = [tile_of(tiles, gathered_ref, listed_ref[0, 0], near, line, t) for t in range(count)]
+    frame = own_frame()
+    reads = [tile_of(tiles, gathered_ref, frame, near, line, t) for t in range(count)]
     reads.append(lambda i: q_ref[i])
     for place, read in enumerate(reads):
         total = jnp.zeros((TILE, TILE), F32)
@@ -56,7 +66,7 @@
 
 
 def forward_kernel(
-    heads, near, line, channels, listed_ref, sums_ref, q_ref, do_ref, qg_ref, kg_ref, gathered_ref, *refs
+    heads, near, line, channels, sums_ref, q_ref, do_ref, gain_ref, gathered_ref, *refs
 ):
     count = len(OFFSETS)
     tiles = refs[:near]
@@ -64,20 +74,21 @@
     scale = TILE ** (-0.5)
     inverse = lax.rsqrt(sums_ref[...] / channels + EPS)
     turned = columns(inverse)
-    usable = [listed_ref[0, t] >= 0 for t in range(count)]
-    reads = [tile_of(tiles, gathered_ref, listed_ref[0, 0], near, line, t) for t in range(count)]
+    frame = own_frame()
+    usable = [inside(frame, line, t) for t in range(count)]
+    reads = [tile_of(tiles, gathered_ref, frame, near, line, t) for t in range(count)]
     lane = lax.broadcasted_iota(jnp.int32, (TILE, TILE), 1)
     stats = jnp.zeros((TILE, TILE), F32)
     query_terms = jnp.zeros((TILE, TILE), F32)
     for head in range(heads):
         query = (
-            q_ref[head].astype(F32) * turned[:, count : count + 1] * qg_ref[head : head + 1]
+            q_ref[head].astype(F32) * turned[:, count : count + 1] * gain_ref[head : head + 1]
         ).astype(BF16)
         upstream = do_ref[head]
         top = jnp.full((TILE, TILE), -1e30, F32)
         for t in range(count):
             key = (
-                reads[t](head).astype(F32) * turned[:, t : t + 1] * kg_ref[head : head + 1]
+                reads[t](head).astype(F32) * turned[:, t : t + 1] * gain_ref[heads + head : heads + head + 1]
             ).astype(BF16)
             norm_ref[t] = key
             if t == 0:
@@ -126,9 +137,11 @@
     stat_ref[9 + count :, :] = jnp.zeros((24 - 9 - count, TILE), F32)
 
 
-def lanes_kernel(heads, near, place_ref, stats_ref, near_ref, far_ref, terms_ref, total_ref):
-    count = len(OFFSETS)
-    lane, frame, half = place_ref[0], place_ref[1], place_ref[2]
+def lanes_kernel(heads, near, line, stats_ref, near_ref, far_ref, terms_ref, total_ref):
+    count = len(OFFSETS)
+    lane = lax.axis_index("y") * lax.axis_size("c") + lax.axis_index("c")
+    frame = own_frame()
+    half = line * lax.axis_size("x") // 2
     groups = stats_ref.shape[0]
     total = stats_ref[0]
     for group in range(1, groups):
@@ -147,8 +160,8 @@
 
 
 def backward_kernel(
-    heads, near, line, channels, listed_ref, sums_ref, terms_ref, own_ref, got_ref,
-    q_ref, k_ref, kn_ref, v_ref, dq_ref, qg_ref, kg_ref, gathered_ref, *refs
+    heads, near, line, channels, sums_ref, terms_ref, own_ref, got_ref,
+    q_ref, k_ref, kn_ref, v_ref, dq_ref, gain_ref, gathered_ref, *refs
 ):
     count = len(OFFSETS)
     tiles = refs[:near]
@@ -181,9 +194,10 @@
             axis=0,
         )
     )
-    usable = [listed_ref[0, t] >= 0 for t in range(count)]
+    frame = own_frame()
+    usable = [inside(frame, line, t) for t in range(count)]
     reads = [
-        tile_of(tiles, gathered_ref, listed_ref[0, 0], near, line, t, 2 * heads) for t in range(count)
+        tile_of(tiles, gathered_ref, frame, near, line, t, 2 * heads) for t in range(count)
     ]
     for head in range(heads):
         key, value = kn_ref[head], v_ref[head]
@@ -191,7 +205,7 @@
         value_grad = jnp.zeros((TILE, TILE), F32)
         for t in range(count):
             query = (
-                reads[t](head).astype(F32) * turned[:, t : t + 1] * qg_ref[head : head + 1]
+                reads[t](head).astype(F32) * turned[:, t : t + 1] * gain_ref[head : head + 1]
             ).astype(BF16)
             upstream = reads[t](heads + head)
             score = dot(key, query, NT) * scale - stat(t, head)
@@ -202,11 +216,11 @@
             key_grad = key_grad + dot(dscore.astype(BF16), query, NN)
         dv_ref[head] = value_grad.astype(BF16)
         gk_ref[head] = (
-            turned[:, count : count + 1] * (kg_ref[head : head + 1] * (key_grad * scale))
+            turned[:, count : count + 1] * (gain_ref[heads + head : heads + head + 1] * (key_grad * scale))
             - k_ref[head].astype(F32) * turned[:, count + 2 : count + 3]
         ).astype(BF16)
         gq_ref[head] = (
-            turned[:, 0:1] * (qg_ref[head : head + 1] * dq_ref[head])
+            turned[:, 0:1] * (gain_ref[head : head + 1] * dq_ref[head])
             - q_ref[head].astype(F32) * turned[:, count + 1 : count + 2]
         ).astype(BF16)
 
@@ -219,13 +233,15 @@
     return lax.ppermute(value, SEQ, pairs)
 
 
-def spread(value, count, line):
+def spread(value, count, line, after=None):
     got = {0: value}
     distance = 1
     while distance < line:
-        for facing in (-1, 1):
-            near = distance // 2
-            source = got[facing * near]
+        near = distance // 2
+        sources = [got[-near], got[near]]
+        if after and distance in after:
+            sources = lax.optimization_barrier((*sources, *after[distance]))[:2]
+        for facing, source in zip((-1, 1), sources):
             got[facing * distance] = passed(source, -facing * (distance - near), count)
         distance *= 2
     return [got[offset] for offset in OFFSETS if offset in got]
@@ -235,37 +251,36 @@
     lines, line = lax.axis_size("x"), lax.axis_size("z")
     seq_count = lines * line
     groups = lax.axis_size("y") * lax.axis_size("c")
-    place = lax.axis_index(SEQ)
-    lane = lax.axis_index(HEAD)
     heads = q_raw.shape[1]
     channels = float(total_heads * q_raw.shape[2])
     q_raw, k_raw, values, grad_out = [
         jnp.transpose(array, (1, 0, 2)) for array in (q_raw, k_raw, values, grad_out)
     ]
-    listed = lax.dynamic_slice_in_dim(key_tiles, place, 1, 0)
+    gains = jnp.concatenate([q_gain, k_gain], axis=0)
     first = jnp.concatenate([k_raw, values], axis=0)
-    second = jnp.concatenate([q_raw, grad_out], axis=0)
     column = lax.all_gather(
         jnp.concatenate([k_raw, values, q_raw, grad_out], axis=0), "x"
     )
     first_all = spread(first, seq_count, line)
-    second_all = spread(second, seq_count, line)
     near = len(first_all)
 
     vmem = pl.BlockSpec(memory_space=pltpu.VMEM)
-    smem = pl.BlockSpec(memory_space=pltpu.SMEM)
     params = pltpu.CompilerParams(vmem_limit_bytes=VMEM_LIMIT)
     whole = (heads, TILE, TILE)
     count = len(OFFSETS)
     sums = pl.pallas_call(
         functools.partial(squares_kernel, heads, near, line),
         out_shape=jax.ShapeDtypeStruct((16, TILE), F32),
-        in_specs=[smem] + [vmem] * (near + 2),
+        in_specs=[vmem] * (near + 2),
         out_specs=vmem,
         compiler_params=params,
         name="squares",
-    )(listed, q_raw, column, *first_all)
+    )(q_raw, column, *first_all)
     sums = lax.psum(lax.psum(sums, "c"), "y")
+    q_late, do_late, *_ = lax.optimization_barrier((q_raw, grad_out, first_all[5], first_all[6]))
+    second_all = spread(
+        jnp.concatenate([q_late, do_late], axis=0), seq_count, line, {4: (sums,)}
+    )
     attended, dq, k_norm, stats = pl.pallas_call(
         functools.partial(forward_kernel, heads, near, line, channels),
         out_shape=[
@@ -274,7 +289,7 @@
             jax.ShapeDtypeStruct(whole, BF16),
             jax.ShapeDtypeStruct((24, TILE), F32),
         ],
-        in_specs=[smem] + [vmem] * (6 + near),
+        in_specs=[vmem] * (5 + near),
         out_specs=[vmem] * 4,
         scratch_shapes=[
             pltpu.VMEM((count, TILE, TILE), BF16),
@@ -282,21 +297,20 @@
         ],
         compiler_params=params,
         name="forward",
-    )(listed, sums, q_raw, grad_out, q_gain, k_gain, column, *first_all)
-
-    stats, *second_all = lax.optimization_barrier((stats, *second_all))
-    gathered = lax.all_gather(stats, HEAD)
-    spot = jnp.stack([lane, place, jnp.int32(seq_count // 2)]).astype(jnp.int32)
+    )(sums, q_raw, grad_out, gains, column, *first_all)
+
+    stats, *second_all[5:7] = lax.optimization_barrier((stats, *second_all[5:7]))
+    gathered = lax.all_gather(lax.all_gather(stats, "c"), "y").reshape(groups, 24, TILE)
     row = jax.ShapeDtypeStruct((groups, 8, TILE), F32)
     near_out, far_out, terms = pl.pallas_call(
-        functools.partial(lanes_kernel, heads, near),
+        functools.partial(lanes_kernel, heads, near, line),
         out_shape=[row, row, jax.ShapeDtypeStruct((8, TILE), F32)],
-        in_specs=[smem, vmem],
+        in_specs=[vmem],
         out_specs=[vmem] * 3,
         scratch_shapes=[pltpu.VMEM((24, TILE), F32)],
         compiler_params=params,
         name="lanes",
-    )(spot, gathered)
+    )(gathered)
     near_pairs = [
         (frame * groups + at, (frame + OFFSETS[1 + at]) * groups + at)
         for frame in range(seq_count)
@@ -317,13 +331,12 @@
     grad_q, grad_k, grad_v = pl.pallas_call(
         functools.partial(backward_kernel, heads, near, line, channels),
         out_shape=[jax.ShapeDtypeStruct(whole, BF16)] * 3,
-        in_specs=[smem] + [vmem] * (12 + near),
+        in_specs=[vmem] * (11 + near),
         out_specs=[vmem] * 3,
         compiler_params=params,
         name="backward",
     )(
-        listed, sums, terms, stats, got, q_raw, k_raw, k_norm, values, dq, q_gain, k_gain,
-        column, *second_all,
+        sums, terms, stats, got, q_raw, k_raw, k_norm, values, dq, gains, column, *second_all,
     )
     return tuple(
         jnp.transpose(array, (1, 0, 2)) for array in (attended, grad_q, grad_k, grad_v)

time: 183 us -> 180 us (0.984)
  the two profiles are of different devices: /device:TPU:70 before, /device:TPU:34 now
where the time goes in v3:
time: 180 us; the launch traced here: 179 us
  starting transfers between devices  80.9 us (45%)
  blocking collectives  35.3 us (20%)
  waiting for transfers between devices  29.3 us (16%)
  between operations  14.4 us (8%)
  Pallas kernels  13.6 us (8%)
  other arithmetic  3.57 us (2%)
  local copies, waits for them, and re-layouts  2.13 us (1%)
    ppermute x16, starting transfers between devices, passed(): return lax.ppermute(value, SEQ, pairs)  74.3 us
    ppermute x16, waiting for transfers between devices, passed(): return lax.ppermute(value, SEQ, pairs)  29.3 us
    psum x2, blocking collectives, per_device(): sums = lax.psum(lax.psum(sums, 'c'), 'y')  13.3 us
    all_gather x1, blocking collectives, per_device(): lax.all_gather(lax.all_gather(stats, 'c'), 'y').reshape(groups, 24, TILE)  11.9 us
    all_to_all x1, blocking collectives, per_device(): lax.all_to_all(jnp.concatenate([near_in, far_in], axis=1), HEAD, 0, 0, ti...  8.21 us
    pallas_call x1, Pallas kernels, per_device(): pl.pallas_call(functools.partial(backward_kernel, heads, near, line, chan...  6.83 us
    pallas_call x1, Pallas kernels, per_device(): pl.pallas_call(functools.partial(forward_kernel, heads, near, line, chann...  6.16 us
    ppermute x1, starting transfers between devices, per_device(): far_in = lax.ppermute(far_out, SEQ + HEAD, far_pairs)  4.58 us
  transfers between devices with their start and end apart: 19, of which 5 were waited for; matrix products, arithmetic and copies ran while one was open for 1% of the time, Pallas kernels for 4%

profile of v3, /device:TPU:34, one launch (start us, length us, event | category | flops | bytes accessed | tf_op | source)
XLA Modules:
  0.0 179.1 jit_solution(18143595672533696337)
XLA Ops:
  7.2 0.0 all-gather.5.cloned.1.call-start
  7.2 1.9 %pad_maximum_fusion = bf16[12,128,128]{2,1,0:T(8,128)(2,1)} fusion(bf16[3,128,128]{2,1,0:T(8,128)(2,1)} %bitcast.18, bf16[3,128,128]{2,1,0:T(8,128)(2,1)} %bitcast.13, bf16[3,128,128]{2,1,0:T(8,128)(2,1)} %bitcast.21, bf16[3,128,128]{2,1,0:T(8,128)(2,1)} %bitcast.24), kind=kLoop, calls=%fused_computation | loop fusion | flops 589824 | bytes 786432 | tf_op jit(solution)/shard_map/concatenate | solution.py:262
  9.1 0.0 all-gather.5.cloned.1.call-update
  9.1 1.0 pad_maximum_fusion.1.refs_0_
  10.1 3.8 %collective-permute-start = (bf16[6,128,128]{2,1,0:T(8,128)(2,1)S(1)}, bf16[6,128,128]{2,1,0:T(8,128)(2,1)S(1)}, u32[]{:S(2)}, u32[]{:S(2)}) collective-permute-start(bf16[6,128,128]{2,1,0:T(8,128)(2,1)S(1)} %pad_maximum_fusion.1.refs_0_), channel_id=1, source_target_pairs={{0,8},{8,16},{16,24},{24,32},{32,40},{40,48},{48,56},{56,64},{64,7... | collective-permute-start | bytes 589832 | tf_op jit(solution)/shard_map/ppermute | solution.py:233
  13.9 2.0 %collective-permute-start.1 = (bf16[6,128,128]{2,1,0:T(8,128)(2,1)S(1)}, bf16[6,128,128]{2,1,0:T(8,128)(2,1)S(1)}, u32[]{:S(2)}, u32[]{:S(2)}) collective-permute-start(bf16[6,128,128]{2,1,0:T(8,128)(2,1)S(1)} %pad_maximum_fusion.1.refs_0_), channel_id=1, source_target_pairs={{8,0},{16,8},{24,16},{32,24},{40,32},{48,40},{56,48},{64,56},{72,6... | collective-permute-start | bytes 589832 | tf_op jit(solution)/shard_map/ppermute | solution.py:233
  16.0 2.7 %collective-permute-done.refs_1_ = bf16[6,128,128]{2,1,0:T(8,128)(2,1)S(1)} collective-permute-done((bf16[6,128,128]{2,1,0:T(8,128)(2,1)S(1)}, bf16[6,128,128]{2,1,0:T(8,128)(2,1)S(1)}, u32[]{:S(2)}, u32[]{:S(2)}) %collective-permute-start) | collective-permute-done | bytes 196640 | tf_op jit(solution)/shard_map/ppermute | solution.py:233
  18.6 3.8 %collective-permute-start.2 = (bf16[6,128,128]{2,1,0:T(8,128)(2,1)S(1)}, bf16[6,128,128]{2,1,0:T(8,128)(2,1)S(1)}, u32[]{:S(2)}, u32[]{:S(2)}) collective-permute-start(bf16[6,128,128]{2,1,0:T(8,128)(2,1)S(1)} %collective-permute-done.refs_1_), channel_id=1, source_target_pairs={{0,8},{8,16},{16,24},{24,32},{32,40},{40,48},{48,56},{56,64},{64,7... | collective-permute-start | bytes 589832 | tf_op jit(solution)/shard_map/ppermute | solution.py:233
  22.5 0.0 collective-permute-done.1.refs_2_
  22.5 7.8 %collective-permute-start.3 = (bf16[6,128,128]{2,1,0:T(8,128)(2,1)S(1)}, bf16[6,128,128]{2,1,0:T(8,128)(2,1)S(1)}, u32[]{:S(2)}, u32[]{:S(2)}) collective-permute-start(bf16[6,128,128]{2,1,0:T(8,128)(2,1)S(1)} %collective-permute-done.1.refs_2_), channel_id=1, source_target_pairs={{8,0},{16,8},{24,16},{32,24},{40,32},{48,40},{56,48},{64,56},{72,6... | collective-permute-start | bytes 589832 | tf_op jit(solution)/shard_map/ppermute | solution.py:233
  30.3 2.4 %collective-permute-done.2.refs_3_ = bf16[6,128,128]{2,1,0:T(8,128)(2,1)S(1)} collective-permute-done((bf16[6,128,128]{2,1,0:T(8,128)(2,1)S(1)}, bf16[6,128,128]{2,1,0:T(8,128)(2,1)S(1)}, u32[]{:S(2)}, u32[]{:S(2)}) %collective-permute-start.2) | collective-permute-done | bytes 196640 | tf_op jit(solution)/shard_map/ppermute | solution.py:233
  32.7 1.9 %collective-permute-start.4 = (bf16[6,128,128]{2,1,0:T(8,128)(2,1)S(1)}, bf16[6,128,128]{2,1,0:T(8,128)(2,1)S(1)}, u32[]{:S(2)}, u32[]{:S(2)}) collective-permute-start(bf16[6,128,128]{2,1,0:T(8,128)(2,1)S(1)} %collective-permute-done.2.refs_3_), channel_id=1, source_target_pairs={{0,16},{8,24},{16,32},{24,40},{32,48},{40,56},{48,64},{56,72},{64,... | collective-permute-start | bytes 589832 | tf_op jit(solution)/shard_map/ppermute | solution.py:233
  34.6 0.0 collective-permute-done.3.refs_4_
  34.7 9.1 %collective-permute-start.5 = (bf16[6,128,128]{2,1,0:T(8,128)(2,1)S(1)}, bf16[6,128,128]{2,1,0:T(8,128)(2,1)S(1)}, u32[]{:S(2)}, u32[]{:S(2)}) collective-permute-start(bf16[6,128,128]{2,1,0:T(8,128)(2,1)S(1)} %collective-permute-done.3.refs_4_), channel_id=1, source_target_pairs={{16,0},{24,8},{32,16},{40,24},{48,32},{56,40},{64,48},{72,56},{80,... | collective-permute-start | bytes 589832 | tf_op jit(solution)/shard_map/ppermute | solution.py:233
  43.8 0.0 collective-permute-done.4.refs_5_
  43.8 6.2 %collective-permute-done.5.refs_6_ = bf16[6,128,128]{2,1,0:T(8,128)(2,1)S(1)} collective-permute-done((bf16[6,128,128]{2,1,0:T(8,128)(2,1)S(1)}, bf16[6,128,128]{2,1,0:T(8,128)(2,1)S(1)}, u32[]{:S(2)}, u32[]{:S(2)}) %collective-permute-start.5) | collective-permute-done | bytes 196640 | tf_op jit(solution)/shard_map/ppermute | solution.py:233
  50.1 1.9 %collective-permute-start.8 = (bf16[6,128,128]{2,1,0:T(8,128)(2,1)S(1)}, bf16[6,128,128]{2,1,0:T(8,128)(2,1)}, u32[]{:S(2)}, u32[]{:S(2)}) collective-permute-start(bf16[6,128,128]{2,1,0:T(8,128)(2,1)S(1)} %constant_dynamic-update-slice_fusion.refs_0_), channel_id=1, source_target_pairs={{0,8},{8,16},{16,24},{24,32},{32,40},{40,48},{48,56},{56,64},{64,7... | collective-permute-start | bytes 589832 | tf_op jit(solution)/shard_map/ppermute | solution.py:233
  52.0 4.4 %collective-permute-start.10 = (bf16[6,128,128]{2,1,0:T(8,128)(2,1)S(1)}, bf16[6,128,128]{2,1,0:T(8,128)(2,1)}, u32[]{:S(2)}, u32[]{:S(2)}) collective-permute-start(bf16[6,128,128]{2,1,0:T(8,128)(2,1)S(1)} %constant_dynamic-update-slice_fusion.refs_0_), channel_id=1, source_target_pairs={{8,0},{16,8},{24,16},{32,24},{40,32},{48,40},{56,48},{64,56},{72,6... | collective-permute-start | bytes 589832 | tf_op jit(solution)/shard_map/ppermute | solution.py:233
  56.4 0.7 copy-done.6
  57.1 4.5 %collective-permute-start.6 = (bf16[6,128,128]{2,1,0:T(8,128)(2,1)S(1)}, bf16[6,128,128]{2,1,0:T(8,128)(2,1)S(1)}, u32[]{:S(2)}, u32[]{:S(2)}) collective-permute-start(bf16[6,128,128]{2,1,0:T(8,128)(2,1)S(1)} %collective-permute-done.4.refs_5_), channel_id=1, source_target_pairs={{0,32},{8,40},{16,48},{24,56},{32,64},{40,72},{48,80},{56,88},{64,... | collective-permute-start | bytes 589832 | tf_op jit(solution)/shard_map/ppermute | solution.py:233
  61.6 6.1 %collective-permute-start.7 = (bf16[6,128,128]{2,1,0:T(8,128)(2,1)S(1)}, bf16[6,128,128]{2,1,0:T(8,128)(2,1)S(1)}, u32[]{:S(2)}, u32[]{:S(2)}) collective-permute-start(bf16[6,128,128]{2,1,0:T(8,128)(2,1)S(1)} %collective-permute-done.5.refs_6_), channel_id=1, source_target_pairs={{32,0},{40,8},{48,16},{56,24},{64,32},{72,40},{80,48},{88,56},{96,... | collective-permute-start | bytes 589832 | tf_op jit(solution)/shard_map/ppermute | solution.py:233
  67.7 0.0 collective-permute-done.8.refs_1_
  67.7 3.5 %collective-permute-start.9 = (bf16[6,128,128]{2,1,0:T(8,128)(2,1)}, bf16[6,128,128]{2,1,0:T(8,128)(2,1)}, u32[]{:S(2)}, u32[]{:S(2)}) collective-permute-start(bf16[6,128,128]{2,1,0:T(8,128)(2,1)} %collective-permute-done.8.refs_1_), channel_id=1, source_target_pairs={{0,8},{8,16},{16,24},{24,32},{32,40},{40,48},{48,56},{56,64},{64,7... | collective-permute-start | bytes 589832 | tf_op jit(solution)/shard_map/ppermute | solution.py:233
  71.2 0.0 collective-permute-done.10.refs_2_
  71.2 4.5 %collective-permute-start.11 = (bf16[6,128,128]{2,1,0:T(8,128)(2,1)}, bf16[6,128,128]{2,1,0:T(8,128)(2,1)}, u32[]{:S(2)}, u32[]{:S(2)}) collective-permute-start(bf16[6,128,128]{2,1,0:T(8,128)(2,1)} %collective-permute-done.10.refs_2_), channel_id=1, source_target_pairs={{8,0},{16,8},{24,16},{32,24},{40,32},{48,40},{56,48},{64,56},{72,6... | collective-permute-start | bytes 589832 | tf_op jit(solution)/shard_map/ppermute | solution.py:233
  75.7 8.0 %collective-permute-done.7.refs_8_ = bf16[6,128,128]{2,1,0:T(8,128)(2,1)S(1)} collective-permute-done((bf16[6,128,128]{2,1,0:T(8,128)(2,1)S(1)}, bf16[6,128,128]{2,1,0:T(8,128)(2,1)S(1)}, u32[]{:S(2)}, u32[]{:S(2)}) %collective-permute-start.7) | collective-permute-done | bytes 196640 | tf_op jit(solution)/shard_map/ppermute | solution.py:233
  83.7 1.4 copy-done
  85.2 0.6 squares.1
  85.7 2.5 %psum.14 = f32[16,128]{1,0:T(8,128)S(1)} all-reduce(f32[16,128]{1,0:T(8,128)S(1)} %squares.1), channel_id=1, replica_groups=mesh['x'=4,'z'=16,'y'=4,'c'=2] {'c'}, use_global_device_ids=true, to_apply=%region_0.0 | all-reduce | flops 2048 | bytes 16384 | tf_op jit(solution)/shard_map/psum | solution.py:279
  88.2 10.8 %psum.15.sums_ref = f32[16,128]{1,0:T(8,128)S(1)} all-reduce(f32[16,128]{1,0:T(8,128)S(1)} %psum.14), channel_id=1, replica_groups=mesh['x'=4,'z'=16,'y'=4,'c'=2] {'y'}, use_global_device_ids=true, to_apply=%region_1.0 | all-reduce | flops 2048 | bytes 16384 | tf_op jit(solution)/shard_map/psum | solution.py:279
  99.1 5.4 %collective-permute-start.12 = (bf16[6,128,128]{2,1,0:T(8,128)(2,1)}, bf16[6,128,128]{2,1,0:T(8,128)(2,1)S(1)}, u32[]{:S(2)}, u32[]{:S(2)}) collective-permute-start(bf16[6,128,128]{2,1,0:T(8,128)(2,1)} %collective-permute-done.9.refs_3_), channel_id=1, source_target_pairs={{0,16},{8,24},{16,32},{24,40},{32,48},{40,56},{48,64},{56,72},{64,... | collective-permute-start | bytes 589832 | tf_op jit(solution)/shard_map/ppermute | solution.py:233
  104.5 4.8 %collective-permute-start.13 = (bf16[6,128,128]{2,1,0:T(8,128)(2,1)}, bf16[6,128,128]{2,1,0:T(8,128)(2,1)S(1)}, u32[]{:S(2)}, u32[]{:S(2)}) collective-permute-start(bf16[6,128,128]{2,1,0:T(8,128)(2,1)} %collective-permute-done.11.refs_4_), channel_id=1, source_target_pairs={{16,0},{24,8},{32,16},{40,24},{48,32},{56,40},{64,48},{72,56},{80,... | collective-permute-start | bytes 589832 | tf_op jit(solution)/shard_map/ppermute | solution.py:233
  109.4 0.7 pad_maximum_fusion.3.gain_ref
  110.1 0.0 copy-start.4
  110.1 0.0 copy-start.5
  110.1 6.2 %forward.1 = (bf16[3,128,128]{2,1,0:T(8,128)(2,1)}, f32[3,128,128]{2,1,0:T(8,128)S(1)}, bf16[3,128,128]{2,1,0:T(8,128)(2,1)S(1)}, f32[24,128]{1,0:T(8,128)S(1)}) custom-call(f32[16,128]{1,0:T(8,128)S(1)} %psum.15.sums_ref, bf16[3,128,128]{2,1,0:T(8,128)(2,1)S(1)} %bitcast.16, bf16[3,128,128]{2,1,0:T(8,128)(2,1)S(1)} %bitcast.20, ...), custom_call_target="tpu_custom_call" | custom-call | tf_op jit(solution)/shard_map/forward/pallas_call | solution.py:284
  116.3 0.0 collective-permute-done.12.refs_5_
  116.3 1.8 %all-gather.1 = f32[48,128]{1,0:T(8,128)S(1)} all-gather(f32[24,128]{1,0:T(8,128)S(1)} %get-tuple-element.27.own_ref), channel_id=3, replica_groups=mesh['x'=4,'z'=16,'y'=4,'c'=2] {'c'}, dimensions={0}, use_global_device_ids=true | all-gather | bytes 36864 | tf_op jit(solution)/shard_map/all_gather | solution.py:303
  118.1 11.9 %all-gather.2.stats_ref = f32[8,24,128]{2,1,0:T(8,128)S(1)} all-gather(f32[2,24,128]{2,1,0:T(8,128)S(1)} %bitcast.27), channel_id=4, replica_groups=mesh['x'=4,'z'=16,'y'=4,'c'=2] {'y'}, dimensions={0}, use_global_device_ids=true | all-gather | bytes 122880 | tf_op jit(solution)/shard_map/all_gather | solution.py:303
  130.1 4.6 %collective-permute-start.15 = (f32[8,8,128]{2,1,0:T(8,128)S(1)}, f32[8,8,128]{2,1,0:T(8,128)S(1)}, u32[]{:S(2)}, u32[]{:S(2)}) collective-permute-start(f32[8,8,128]{2,1,0:T(8,128)S(1)} %get-tuple-element.30), channel_id=1, source_target_pairs={{1,129},{2,258},{9,137},{10,266},{17,145},{18,274},{25,153},{26,28... | collective-permute-start | bytes 98312 | tf_op jit(solution)/shard_map/ppermute | solution.py:327
  134.6 1.9 %collective-permute-start.14 = (f32[8,8,128]{2,1,0:T(8,128)S(1)}, f32[8,8,128]{2,1,0:T(8,128)S(1)}, u32[]{:S(2)}, u32[]{:S(2)}) collective-permute-start(f32[8,8,128]{2,1,0:T(8,128)S(1)} %get-tuple-element.29), channel_id=1, source_target_pairs={{1,9},{3,19},{5,37},{7,71},{8,0},{9,17},{11,27},{13,45},{15,79},{1... | collective-permute-start | bytes 98312 | tf_op jit(solution)/shard_map/ppermute | solution.py:326
  136.6 4.7 %collective-permute-start.16 = (bf16[6,128,128]{2,1,0:T(8,128)(2,1)S(1)}, bf16[6,128,128]{2,1,0:T(8,128)(2,1)S(1)}, u32[]{:S(2)}, u32[]{:S(2)}) collective-permute-start(bf16[6,128,128]{2,1,0:T(8,128)(2,1)S(1)} %collective-permute-done.12.refs_5_), channel_id=1, source_target_pairs={{0,32},{8,40},{16,48},{24,56},{32,64},{40,72},{48,80},{56,88},{64,... | collective-permute-start | bytes 589832 | tf_op jit(solution)/shard_map/ppermute | solution.py:233
  141.3 6.0 %collective-permute-start.17 = (bf16[6,128,128]{2,1,0:T(8,128)(2,1)S(1)}, bf16[6,128,128]{2,1,0:T(8,128)(2,1)S(1)}, u32[]{:S(2)}, u32[]{:S(2)}) collective-permute-start(bf16[6,128,128]{2,1,0:T(8,128)(2,1)S(1)} %collective-permute-done.13.refs_6_), channel_id=1, source_target_pairs={{32,0},{40,8},{48,16},{56,24},{64,32},{72,40},{80,48},{88,56},{96,... | collective-permute-start | bytes 589832 | tf_op jit(solution)/shard_map/ppermute | solution.py:233
  147.2 0.0 collective-permute-done.15
  147.2 0.0 collective-permute-done.14
  147.3 8.2 %all_to_all.5.got_ref = f32[8,16,128]{2,1,0:T(8,128)S(1)} all-to-all(f32[8,16,128]{2,1,0:T(8,128)S(1)} %pad_maximum_fusion.2), channel_id=1, replica_groups=mesh['x'=4,'z'=16,'y'=4,'c'=2] {'y','c'}, dimensions={0} | all-to-all | bytes 131072 | tf_op jit(solution)/shard_map/all_to_all | solution.py:328
  155.5 10.0 %collective-permute-done.17.refs_8_ = bf16[6,128,128]{2,1,0:T(8,128)(2,1)S(1)} collective-permute-done((bf16[6,128,128]{2,1,0:T(8,128)(2,1)S(1)}, bf16[6,128,128]{2,1,0:T(8,128)(2,1)S(1)}, u32[]{:S(2)}, u32[]{:S(2)}) %collective-permute-start.17) | collective-permute-done | bytes 196640 | tf_op jit(solution)/shard_map/ppermute | solution.py:233
  165.5 6.8 %backward.1 = (bf16[3,128,128]{2,1,0:T(8,128)(2,1)}, bf16[3,128,128]{2,1,0:T(8,128)(2,1)}, bf16[3,128,128]{2,1,0:T(8,128)(2,1)}) custom-call(f32[16,128]{1,0:T(8,128)S(1)} %psum.15.sums_ref, f32[8,128]{1,0:T(8,128)S(1)} %get-tuple-element.28.terms_ref, f32[24,128]{1,0:T(8,128)S(1)} %get-tuple-element.27.own_ref, f32[8,16,128]{2,1,0:T(8,128)S(1)} %all_to_all.5.got_ref, ...), custom_call_target="tpu_custom_call" | custom-call | tf_op jit(solution)/shard_map/backward/pallas_call | solution.py:331
  (22 shorter events, 0.1 us)
Async XLA Ops:
  7.2 42.9 %copy-start.2 = (bf16[128,3,128]{2,0,1:T(8,128)(2,1)S(1)}, bf16[128,3,128]{2,0,1:T(8,128)(2,1)}, u32[]{:S(2)}) copy-start(bf16[128,3,128]{2,0,1:T(8,128)(2,1)} %param.7) | copy-start | bytes 294916
  7.2 42.9 %copy-start.3 = (bf16[128,3,128]{2,0,1:T(8,128)(2,1)S(1)}, bf16[128,3,128]{2,0,1:T(8,128)(2,1)}, u32[]{:S(2)}) copy-start(bf16[128,3,128]{2,0,1:T(8,128)(2,1)} %param.10) | copy-start | bytes 294916
  7.2 76.6 %all-gather.5.cloned.1.call-start = ((), (), s32[]{:S(2)}) async-start(), calls=%async_computation.1 | async-start | bytes 1966080 | tf_op jit(solution)/shard_map/all_gather | solution.py:261
  10.1 8.5 %collective-permute-start = (bf16[6,128,128]{2,1,0:T(8,128)(2,1)S(1)}, bf16[6,128,128]{2,1,0:T(8,128)(2,1)S(1)}, u32[]{:S(2)}, u32[]{:S(2)}) collective-permute-start(bf16[6,128,128]{2,1,0:T(8,128)(2,1)S(1)} %pad_maximum_fusion.1.refs_0_), channel_id=1, source_target_pairs={{0,8},{8,16},{16,24},{24,32},{32,40},{40,48},{48,56},{56,64},{64,7... | collective-permute-start | bytes 589832 | tf_op jit(solution)/shard_map/ppermute | solution.py:233
  13.9 8.5 %collective-permute-start.1 = (bf16[6,128,128]{2,1,0:T(8,128)(2,1)S(1)}, bf16[6,128,128]{2,1,0:T(8,128)(2,1)S(1)}, u32[]{:S(2)}, u32[]{:S(2)}) collective-permute-start(bf16[6,128,128]{2,1,0:T(8,128)(2,1)S(1)} %pad_maximum_fusion.1.refs_0_), channel_id=1, source_target_pairs={{8,0},{16,8},{24,16},{32,24},{40,32},{48,40},{56,48},{64,56},{72,6... | collective-permute-start | bytes 589832 | tf_op jit(solution)/shard_map/ppermute | solution.py:233
  18.6 14.1 %collective-permute-start.2 = (bf16[6,128,128]{2,1,0:T(8,128)(2,1)S(1)}, bf16[6,128,128]{2,1,0:T(8,128)(2,1)S(1)}, u32[]{:S(2)}, u32[]{:S(2)}) collective-permute-start(bf16[6,128,128]{2,1,0:T(8,128)(2,1)S(1)} %collective-permute-done.refs_1_), channel_id=1, source_target_pairs={{0,8},{8,16},{16,24},{24,32},{32,40},{40,48},{48,56},{56,64},{64,7... | collective-permute-start | bytes 589832 | tf_op jit(solution)/shard_map/ppermute | solution.py:233
  22.5 12.2 %collective-permute-start.3 = (bf16[6,128,128]{2,1,0:T(8,128)(2,1)S(1)}, bf16[6,128,128]{2,1,0:T(8,128)(2,1)S(1)}, u32[]{:S(2)}, u32[]{:S(2)}) collective-permute-start(bf16[6,128,128]{2,1,0:T(8,128)(2,1)S(1)} %collective-permute-done.1.refs_2_), channel_id=1, source_target_pairs={{8,0},{16,8},{24,16},{32,24},{40,32},{48,40},{56,48},{64,56},{72,6... | collective-permute-start | bytes 589832 | tf_op jit(solution)/shard_map/ppermute | solution.py:233
  32.7 11.1 %collective-permute-start.4 = (bf16[6,128,128]{2,1,0:T(8,128)(2,1)S(1)}, bf16[6,128,128]{2,1,0:T(8,128)(2,1)S(1)}, u32[]{:S(2)}, u32[]{:S(2)}) collective-permute-start(bf16[6,128,128]{2,1,0:T(8,128)(2,1)S(1)} %collective-permute-done.2.refs_3_), channel_id=1, source_target_pairs={{0,16},{8,24},{16,32},{24,40},{32,48},{40,56},{48,64},{56,72},{64,... | collective-permute-start | bytes 589832 | tf_op jit(solution)/shard_map/ppermute | solution.py:233
  34.7 15.4 %collective-permute-start.5 = (bf16[6,128,128]{2,1,0:T(8,128)(2,1)S(1)}, bf16[6,128,128]{2,1,0:T(8,128)(2,1)S(1)}, u32[]{:S(2)}, u32[]{:S(2)}) collective-permute-start(bf16[6,128,128]{2,1,0:T(8,128)(2,1)S(1)} %collective-permute-done.3.refs_4_), channel_id=1, source_target_pairs={{16,0},{24,8},{32,16},{40,24},{48,32},{56,40},{64,48},{72,56},{80,... | collective-permute-start | bytes 589832 | tf_op jit(solution)/shard_map/ppermute | solution.py:233
  50.1 17.7 %collective-permute-start.8 = (bf16[6,128,128]{2,1,0:T(8,128)(2,1)S(1)}, bf16[6,128,128]{2,1,0:T(8,128)(2,1)}, u32[]{:S(2)}, u32[]{:S(2)}) collective-permute-start(bf16[6,128,128]{2,1,0:T(8,128)(2,1)S(1)} %constant_dynamic-update-slice_fusion.refs_0_), channel_id=1, source_target_pairs={{0,8},{8,16},{16,24},{24,32},{32,40},{40,48},{48,56},{56,64},{64,7... | collective-permute-start | bytes 589832 | tf_op jit(solution)/shard_map/ppermute | solution.py:233
  52.0 19.2 %collective-permute-start.10 = (bf16[6,128,128]{2,1,0:T(8,128)(2,1)S(1)}, bf16[6,128,128]{2,1,0:T(8,128)(2,1)}, u32[]{:S(2)}, u32[]{:S(2)}) collective-permute-start(bf16[6,128,128]{2,1,0:T(8,128)(2,1)S(1)} %constant_dynamic-update-slice_fusion.refs_0_), channel_id=1, source_target_pairs={{8,0},{16,8},{24,16},{32,24},{40,32},{48,40},{56,48},{64,56},{72,6... | collective-permute-start | bytes 589832 | tf_op jit(solution)/shard_map/ppermute | solution.py:233
  56.4 0.7 copy-start.6
  57.1 18.6 %collective-permute-start.6 = (bf16[6,128,128]{2,1,0:T(8,128)(2,1)S(1)}, bf16[6,128,128]{2,1,0:T(8,128)(2,1)S(1)}, u32[]{:S(2)}, u32[]{:S(2)}) collective-permute-start(bf16[6,128,128]{2,1,0:T(8,128)(2,1)S(1)} %collective-permute-done.4.refs_5_), channel_id=1, source_target_pairs={{0,32},{8,40},{16,48},{24,56},{32,64},{40,72},{48,80},{56,88},{64,... | collective-permute-start | bytes 589832 | tf_op jit(solution)/shard_map/ppermute | solution.py:233
  61.6 22.1 %collective-permute-start.7 = (bf16[6,128,128]{2,1,0:T(8,128)(2,1)S(1)}, bf16[6,128,128]{2,1,0:T(8,128)(2,1)S(1)}, u32[]{:S(2)}, u32[]{:S(2)}) collective-permute-start(bf16[6,128,128]{2,1,0:T(8,128)(2,1)S(1)} %collective-permute-done.5.refs_6_), channel_id=1, source_target_pairs={{32,0},{40,8},{48,16},{56,24},{64,32},{72,40},{80,48},{88,56},{96,... | collective-permute-start | bytes 589832 | tf_op jit(solution)/shard_map/ppermute | solution.py:233
  67.7 31.3 %collective-permute-start.9 = (bf16[6,128,128]{2,1,0:T(8,128)(2,1)}, bf16[6,128,128]{2,1,0:T(8,128)(2,1)}, u32[]{:S(2)}, u32[]{:S(2)}) collective-permute-start(bf16[6,128,128]{2,1,0:T(8,128)(2,1)} %collective-permute-done.8.refs_1_), channel_id=1, source_target_pairs={{0,8},{8,16},{16,24},{24,32},{32,40},{40,48},{48,56},{56,64},{64,7... | collective-permute-start | bytes 589832 | tf_op jit(solution)/shard_map/ppermute | solution.py:233
  71.2 27.9 %collective-permute-start.11 = (bf16[6,128,128]{2,1,0:T(8,128)(2,1)}, bf16[6,128,128]{2,1,0:T(8,128)(2,1)}, u32[]{:S(2)}, u32[]{:S(2)}) collective-permute-start(bf16[6,128,128]{2,1,0:T(8,128)(2,1)} %collective-permute-done.10.refs_2_), channel_id=1, source_target_pairs={{8,0},{16,8},{24,16},{32,24},{40,32},{48,40},{56,48},{64,56},{72,6... | collective-permute-start | bytes 589832 | tf_op jit(solution)/shard_map/ppermute | solution.py:233
  83.7 1.4 copy-start
  85.2 24.9 %copy-start.1 = (bf16[48,128,128]{2,1,0:T(8,128)(2,1)S(1)}, bf16[48,128,128]{2,1,0:T(8,128)(2,1)}, u32[]{:S(2)}) copy-start(bf16[48,128,128]{2,1,0:T(8,128)(2,1)} %all-gather.5.cloned.1.call-done) | copy-start | bytes 4718596
  99.1 17.2 %collective-permute-start.12 = (bf16[6,128,128]{2,1,0:T(8,128)(2,1)}, bf16[6,128,128]{2,1,0:T(8,128)(2,1)S(1)}, u32[]{:S(2)}, u32[]{:S(2)}) collective-permute-start(bf16[6,128,128]{2,1,0:T(8,128)(2,1)} %collective-permute-done.9.refs_3_), channel_id=1, source_target_pairs={{0,16},{8,24},{16,32},{24,40},{32,48},{40,56},{48,64},{56,72},{64,... | collective-permute-start | bytes 589832 | tf_op jit(solution)/shard_map/ppermute | solution.py:233
  104.5 11.8 %collective-permute-start.13 = (bf16[6,128,128]{2,1,0:T(8,128)(2,1)}, bf16[6,128,128]{2,1,0:T(8,128)(2,1)S(1)}, u32[]{:S(2)}, u32[]{:S(2)}) collective-permute-start(bf16[6,128,128]{2,1,0:T(8,128)(2,1)} %collective-permute-done.11.refs_4_), channel_id=1, source_target_pairs={{16,0},{24,8},{32,16},{40,24},{48,32},{56,40},{64,48},{72,56},{80,... | collective-permute-start | bytes 589832 | tf_op jit(solution)/shard_map/ppermute | solution.py:233
  110.1 55.4 %copy-start.4 = (bf16[128,3,128]{2,0,1:T(8,128)(2,1)S(1)}, bf16[128,3,128]{2,0,1:T(8,128)(2,1)}, u32[]{:S(2)}) copy-start(bf16[128,3,128]{2,0,1:T(8,128)(2,1)} %param.9) | copy-start | bytes 294916
  110.1 55.4 %copy-start.5 = (bf16[128,3,128]{2,0,1:T(8,128)(2,1)S(1)}, bf16[128,3,128]{2,0,1:T(8,128)(2,1)}, u32[]{:S(2)}) copy-start(bf16[128,3,128]{2,0,1:T(8,128)(2,1)} %param.8) | copy-start | bytes 294916
  110.1 55.4 %copy-start.7 = (bf16[6,128,128]{2,1,0:T(8,128)(2,1)S(1)}, bf16[6,128,128]{2,1,0:T(8,128)(2,1)}, u32[]{:S(2)}) copy-start(bf16[6,128,128]{2,1,0:T(8,128)(2,1)} %copy-done.6) | copy-start | bytes 589828
  130.1 17.2 %collective-permute-start.15 = (f32[8,8,128]{2,1,0:T(8,128)S(1)}, f32[8,8,128]{2,1,0:T(8,128)S(1)}, u32[]{:S(2)}, u32[]{:S(2)}) collective-permute-start(f32[8,8,128]{2,1,0:T(8,128)S(1)} %get-tuple-element.30), channel_id=1, source_target_pairs={{1,129},{2,258},{9,137},{10,266},{17,145},{18,274},{25,153},{26,28... | collective-permute-start | bytes 98312 | tf_op jit(solution)/shard_map/ppermute | solution.py:327
  134.6 12.6 %collective-permute-start.14 = (f32[8,8,128]{2,1,0:T(8,128)S(1)}, f32[8,8,128]{2,1,0:T(8,128)S(1)}, u32[]{:S(2)}, u32[]{:S(2)}) collective-permute-start(f32[8,8,128]{2,1,0:T(8,128)S(1)} %get-tuple-element.29), channel_id=1, source_target_pairs={{1,9},{3,19},{5,37},{7,71},{8,0},{9,17},{11,27},{13,45},{15,79},{1... | collective-permute-start | bytes 98312 | tf_op jit(solution)/shard_map/ppermute | solution.py:326
  136.6 18.9 %collective-permute-start.16 = (bf16[6,128,128]{2,1,0:T(8,128)(2,1)S(1)}, bf16[6,128,128]{2,1,0:T(8,128)(2,1)S(1)}, u32[]{:S(2)}, u32[]{:S(2)}) collective-permute-start(bf16[6,128,128]{2,1,0:T(8,128)(2,1)S(1)} %collective-permute-done.12.refs_5_), channel_id=1, source_target_pairs={{0,32},{8,40},{16,48},{24,56},{32,64},{40,72},{48,80},{56,88},{64,... | collective-permute-start | bytes 589832 | tf_op jit(solution)/shard_map/ppermute | solution.py:233
  141.3 24.2 %collective-permute-start.17 = (bf16[6,128,128]{2,1,0:T(8,128)(2,1)S(1)}, bf16[6,128,128]{2,1,0:T(8,128)(2,1)S(1)}, u32[]{:S(2)}, u32[]{:S(2)}) collective-permute-start(bf16[6,128,128]{2,1,0:T(8,128)(2,1)S(1)} %collective-permute-done.13.refs_6_), channel_id=1, source_target_pairs={{32,0},{40,8},{48,16},{56,24},{64,32},{72,40},{80,48},{88,56},{96,... | collective-permute-start | bytes 589832 | tf_op jit(solution)/shard_map/ppermute | solution.py:233
Sparse Core Ops, SparseCore 0:
  10.1 41.2 all-gather.4

commit v4 on v3

--- a/solution.py
+++ b/solution.py
@@ -37,15 +37,23 @@
     return lax.axis_index("x") * lax.axis_size("z") + lax.axis_index("z")
 
 
+def mirrored(value):
+    return value * (1 - 2 * lax.axis_index("c"))
+
+
+def shared_place(place):
+    return 1 + ((place - 1) ^ lax.axis_index("c")) if place else 0
+
+
 def inside(frame, line, place):
-    at = frame + OFFSETS[place]
+    at = frame + mirrored(OFFSETS[place])
     return (at >= 0) & (at < line * lax.axis_size("x"))
 
 
 def tile_of(tiles, gathered_ref, frame, near, line, place, skip=0):
     if place < near:
         return lambda i: tiles[place][i]
-    at = frame // line + OFFSETS[place] // line
+    at = frame // line + mirrored(OFFSETS[place] // line)
     at = jnp.minimum(jnp.maximum(at, 0), gathered_ref.shape[0] - 1)
     return lambda i: gathered_ref[at, skip + i]
 
@@ -61,7 +69,8 @@
         for head in range(heads):
             floats = read(head).astype(F32)
             total = total + floats * floats
-        out_ref[place : place + 1, :] = row_sums(total)[0:1]
+        row = shared_place(place) if place < count else place
+        out_ref[pl.ds(row, 1), :] = row_sums(total)[0:1]
     out_ref[count + 1 :, :] = jnp.zeros((16 - count - 1, TILE), F32)
 
 
@@ -72,7 +81,9 @@
     tiles = refs[:near]
     out_ref, dq_ref, kn_ref, stat_ref, norm_ref, work_ref = refs[near:]
     scale = TILE ** (-0.5)
-    inverse = lax.rsqrt(sums_ref[...] / channels + EPS)
+    places = [shared_place(t) for t in range(count)] + [count]
+    sums = jnp.concatenate([sums_ref[pl.ds(place, 1), :] for place in places], axis=0)
+    inverse = lax.rsqrt(sums / channels + EPS)
     turned = columns(inverse)
     frame = own_frame()
     usable = [inside(frame, line, t) for t in range(count)]
@@ -122,9 +133,10 @@
             term = dscore.astype(F32) * score
             query_terms = query_terms + term
             term = jnp.sum(term, axis=0, keepdims=True)
+            row = pl.ds(8 + places[t], 1)
             if head:
-                term = term + stat_ref[8 + t : 9 + t, :]
-            stat_ref[8 + t : 9 + t, :] = term
+                term = term + stat_ref[row, :]
+            stat_ref[row, :] = term
         dq_ref[head] = query_grad * scale
         stats = jnp.where(lane == head, level, stats)
         stats = jnp.where(lane == heads + head, delta, stats)
@@ -168,13 +180,14 @@
     gq_ref, gk_ref, dv_ref = refs[near:]
     scale = TILE ** (-0.5)
     inverse_at, term_at = 2 * heads, 2 * heads + 1
+    core = lax.axis_index("c")
 
     def stat(t, row):
         if t == 0:
             return own_ref[row : row + 1]
         if t < near:
-            return got_ref[(t - 1) ^ 1, row : row + 1]
-        lane = {0: 1, 1: 0, 2: 2, 3: 2}[t - near]
+            return got_ref[(t - 1) ^ 1 ^ core, row : row + 1]
+        lane = (t - near) ^ 1 ^ core if t - near < 2 else 2
         return got_ref[lane, 8 + row : 9 + row]
 
     inverse = lax.rsqrt(sums_ref[...] / channels + EPS)
@@ -229,8 +242,13 @@
 
 
 def passed(value, steps, count):
-    pairs = [(i, i + steps) for i in range(count) if 0 <= i + steps < count]
-    return lax.ppermute(value, SEQ, pairs)
+    pairs = [
+        (2 * i + core, 2 * (i + way * steps) + core)
+        for i in range(count)
+        for core, way in enumerate((1, -1))
+        if 0 <= i + way * steps < count
+    ]
+    return lax.ppermute(value, SEQ + ("c",), pairs)
 
 
 def spread(value, count, line, after=None):
@@ -277,10 +295,6 @@
         name="squares",
     )(q_raw, column, *first_all)
     sums = lax.psum(lax.psum(sums, "c"), "y")
-    q_late, do_late, *_ = lax.optimization_barrier((q_raw, grad_out, first_all[5], first_all[6]))
-    second_all = spread(
-        jnp.concatenate([q_late, do_late], axis=0), seq_count, line, {4: (sums,)}
-    )
     attended, dq, k_norm, stats = pl.pallas_call(
         functools.partial(forward_kernel, heads, near, line, channels),
         out_shape=[
@@ -299,7 +313,11 @@
         name="forward",
     )(sums, q_raw, grad_out, gains, column, *first_all)
 
-    stats, *second_all[5:7] = lax.optimization_barrier((stats, *second_all[5:7]))
+    q_late, do_late, *_ = lax.optimization_barrier((q_raw, grad_out, *first_all[-4:-2]))
+    second_all = spread(
+        jnp.concatenate([q_late, do_late], axis=0), seq_count, line, {2: (sums,), 4: (attended,)}
+    )
+    stats, *second_all[-4:-2] = lax.optimization_barrier((stats, *second_all[-4:-2]))
     gathered = lax.all_gather(lax.all_gather(stats, "c"), "y").reshape(groups, 24, TILE)
     row = jax.ShapeDtypeStruct((groups, 8, TILE), F32)
     near_out, far_out, terms = pl.pallas_call(

time: 180 us -> 184 us (1.022)
  the two profiles are of different devices: /device:TPU:34 before, /device:TPU:4 now
where the time goes in v4:
time: 184 us; the launch traced here: 183 us
  starting transfers between devices  82.5 us (45%)
  blocking collectives  41.3 us (22%)
  waiting for transfers between devices  25.5 us (14%)
  between operations  14.3 us (8%)
  Pallas kernels  13.6 us (7%)
  other arithmetic  3.58 us (2%)
  local copies, waits for them, and re-layouts  2.73 us (1%)
    ppermute x16, starting transfers between devices, passed(): return lax.ppermute(value, SEQ + ('c',), pairs)  76.1 us
    ppermute x16, waiting for transfers between devices, passed(): return lax.ppermute(value, SEQ + ('c',), pairs)  25.4 us
    psum x2, blocking collectives, per_device(): sums = lax.psum(lax.psum(sums, 'c'), 'y')  19.1 us
    all_gather x1, blocking collectives, per_device(): lax.all_gather(lax.all_gather(stats, 'c'), 'y').reshape(groups, 24, TILE)  11.9 us
    all_to_all x1, blocking collectives, per_device(): lax.all_to_all(jnp.concatenate([near_in, far_in], axis=1), HEAD, 0, 0, ti...  8.41 us
    pallas_call x1, Pallas kernels, per_device(): pl.pallas_call(functools.partial(backward_kernel, heads, near, line, chan...  6.74 us
    pallas_call x1, Pallas kernels, per_device(): pl.pallas_call(functools.partial(forward_kernel, heads, near, line, chann...  6.2 us
  transfers between devices with their start and end apart: 19, of which 6 were waited for; matrix products, arithmetic and copies ran while one was open for 2% of the time, Pallas kernels for 4%

profile of v4, /device:TPU:4, one launch (start us, length us, event | category | flops | bytes accessed | tf_op | source)
XLA Modules:
  0.0 183.4 jit_solution(10290609433362154367)
XLA Ops:
  7.2 0.0 all-gather.5.cloned.1.call-start
  7.2 1.9 %pad_maximum_fusion = bf16[12,128,128]{2,1,0:T(8,128)(2,1)} fusion(bf16[3,128,128]{2,1,0:T(8,128)(2,1)} %bitcast.18, bf16[3,128,128]{2,1,0:T(8,128)(2,1)} %bitcast.13, bf16[3,128,128]{2,1,0:T(8,128)(2,1)} %bitcast.21, bf16[3,128,128]{2,1,0:T(8,128)(2,1)} %bitcast.24), kind=kLoop, calls=%fused_computation | loop fusion | flops 589824 | bytes 786432 | tf_op jit(solution)/shard_map/concatenate | solution.py:280
  9.1 0.0 all-gather.5.cloned.1.call-update
  9.2 1.0 pad_maximum_fusion.1.refs_0_
  10.1 3.8 %collective-permute-start = (bf16[6,128,128]{2,1,0:T(8,128)(2,1)S(1)}, bf16[6,128,128]{2,1,0:T(8,128)(2,1)S(1)}, u32[]{:S(2)}, u32[]{:S(2)}) collective-permute-start(bf16[6,128,128]{2,1,0:T(8,128)(2,1)S(1)} %pad_maximum_fusion.1.refs_0_), channel_id=1, source_target_pairs={{0,8},{8,16},{9,1},{16,24},{17,9},{24,32},{25,17},{32,40},{33,25},... | collective-permute-start | bytes 589832 | tf_op jit(solution)/shard_map/ppermute | solution.py:251
  14.0 9.5 %collective-permute-start.1 = (bf16[6,128,128]{2,1,0:T(8,128)(2,1)S(1)}, bf16[6,128,128]{2,1,0:T(8,128)(2,1)S(1)}, u32[]{:S(2)}, u32[]{:S(2)}) collective-permute-start(bf16[6,128,128]{2,1,0:T(8,128)(2,1)S(1)} %pad_maximum_fusion.1.refs_0_), channel_id=1, source_target_pairs={{1,9},{8,0},{9,17},{16,8},{17,25},{24,16},{25,33},{32,24},{33,41},... | collective-permute-start | bytes 589832 | tf_op jit(solution)/shard_map/ppermute | solution.py:251
  23.4 1.7 collective-permute-done.refs_1_
  25.1 1.9 %collective-permute-start.2 = (bf16[6,128,128]{2,1,0:T(8,128)(2,1)S(1)}, bf16[6,128,128]{2,1,0:T(8,128)(2,1)S(1)}, u32[]{:S(2)}, u32[]{:S(2)}) collective-permute-start(bf16[6,128,128]{2,1,0:T(8,128)(2,1)S(1)} %collective-permute-done.refs_1_), channel_id=1, source_target_pairs={{0,8},{8,16},{9,1},{16,24},{17,9},{24,32},{25,17},{32,40},{33,25},... | collective-permute-start | bytes 589832 | tf_op jit(solution)/shard_map/ppermute | solution.py:251
  27.1 0.0 collective-permute-done.1.refs_2_
  27.1 6.0 %collective-permute-start.3 = (bf16[6,128,128]{2,1,0:T(8,128)(2,1)S(1)}, bf16[6,128,128]{2,1,0:T(8,128)(2,1)S(1)}, u32[]{:S(2)}, u32[]{:S(2)}) collective-permute-start(bf16[6,128,128]{2,1,0:T(8,128)(2,1)S(1)} %collective-permute-done.1.refs_2_), channel_id=1, source_target_pairs={{1,9},{8,0},{9,17},{16,8},{17,25},{24,16},{25,33},{32,24},{33,41},... | collective-permute-start | bytes 589832 | tf_op jit(solution)/shard_map/ppermute | solution.py:251
  33.1 1.8 collective-permute-done.2.refs_3_
  34.9 1.9 %collective-permute-start.4 = (bf16[6,128,128]{2,1,0:T(8,128)(2,1)S(1)}, bf16[6,128,128]{2,1,0:T(8,128)(2,1)S(1)}, u32[]{:S(2)}, u32[]{:S(2)}) collective-permute-start(bf16[6,128,128]{2,1,0:T(8,128)(2,1)S(1)} %collective-permute-done.2.refs_3_), channel_id=1, source_target_pairs={{0,16},{8,24},{16,32},{17,1},{24,40},{25,9},{32,48},{33,17},{40,56... | collective-permute-start | bytes 589832 | tf_op jit(solution)/shard_map/ppermute | solution.py:251
  36.8 6.9 %collective-permute-start.5 = (bf16[6,128,128]{2,1,0:T(8,128)(2,1)S(1)}, bf16[6,128,128]{2,1,0:T(8,128)(2,1)S(1)}, u32[]{:S(2)}, u32[]{:S(2)}) collective-permute-start(bf16[6,128,128]{2,1,0:T(8,128)(2,1)S(1)} %collective-permute-done.3.refs_4_), channel_id=1, source_target_pairs={{1,17},{9,25},{16,0},{17,33},{24,8},{25,41},{32,16},{33,49},{40,24... | collective-permute-start | bytes 589832 | tf_op jit(solution)/shard_map/ppermute | solution.py:251
  43.8 6.5 %collective-permute-done.4.refs_5_ = bf16[6,128,128]{2,1,0:T(8,128)(2,1)S(1)} collective-permute-done((bf16[6,128,128]{2,1,0:T(8,128)(2,1)S(1)}, bf16[6,128,128]{2,1,0:T(8,128)(2,1)S(1)}, u32[]{:S(2)}, u32[]{:S(2)}) %collective-permute-start.4) | collective-permute-done | bytes 196640 | tf_op jit(solution)/shard_map/ppermute | solution.py:251
  50.3 0.0 collective-permute-done.5.refs_6_
  50.3 6.9 %collective-permute-start.6 = (bf16[6,128,128]{2,1,0:T(8,128)(2,1)S(1)}, bf16[6,128,128]{2,1,0:T(8,128)(2,1)S(1)}, u32[]{:S(2)}, u32[]{:S(2)}) collective-permute-start(bf16[6,128,128]{2,1,0:T(8,128)(2,1)S(1)} %collective-permute-done.4.refs_5_), channel_id=1, source_target_pairs={{0,32},{8,40},{16,48},{24,56},{32,64},{33,1},{40,72},{41,9},{48,80... | collective-permute-start | bytes 589832 | tf_op jit(solution)/shard_map/ppermute | solution.py:251
  57.1 3.8 %collective-permute-start.7 = (bf16[6,128,128]{2,1,0:T(8,128)(2,1)S(1)}, bf16[6,128,128]{2,1,0:T(8,128)(2,1)S(1)}, u32[]{:S(2)}, u32[]{:S(2)}) collective-permute-start(bf16[6,128,128]{2,1,0:T(8,128)(2,1)S(1)} %collective-permute-done.5.refs_6_), channel_id=1, source_target_pairs={{1,33},{9,41},{17,49},{25,57},{32,0},{33,65},{40,8},{41,73},{48,16... | collective-permute-start | bytes 589832 | tf_op jit(solution)/shard_map/ppermute | solution.py:251
  60.9 0.7 constant_dynamic-update-slice_fusion.1
  61.6 0.6 constant_dynamic-update-slice_fusion.refs_0_
  62.2 1.9 %collective-permute-start.8 = (bf16[6,128,128]{2,1,0:T(8,128)(2,1)}, bf16[6,128,128]{2,1,0:T(8,128)(2,1)}, u32[]{:S(2)}, u32[]{:S(2)}) collective-permute-start(bf16[6,128,128]{2,1,0:T(8,128)(2,1)} %constant_dynamic-update-slice_fusion.refs_0_), channel_id=1, source_target_pairs={{0,8},{8,16},{9,1},{16,24},{17,9},{24,32},{25,17},{32,40},{33,25},... | collective-permute-start | bytes 589832 | tf_op jit(solution)/shard_map/ppermute | solution.py:251
  64.2 6.0 %collective-permute-start.9 = (bf16[6,128,128]{2,1,0:T(8,128)(2,1)}, bf16[6,128,128]{2,1,0:T(8,128)(2,1)}, u32[]{:S(2)}, u32[]{:S(2)}) collective-permute-start(bf16[6,128,128]{2,1,0:T(8,128)(2,1)} %constant_dynamic-update-slice_fusion.refs_0_), channel_id=1, source_target_pairs={{1,9},{8,0},{9,17},{16,8},{17,25},{24,16},{25,33},{32,24},{33,41},... | collective-permute-start | bytes 589832 | tf_op jit(solution)/shard_map/ppermute | solution.py:251
  70.2 2.9 %collective-permute-done.6.refs_7_ = bf16[6,128,128]{2,1,0:T(8,128)(2,1)S(1)} collective-permute-done((bf16[6,128,128]{2,1,0:T(8,128)(2,1)S(1)}, bf16[6,128,128]{2,1,0:T(8,128)(2,1)S(1)}, u32[]{:S(2)}, u32[]{:S(2)}) %collective-permute-start.6) | collective-permute-done | bytes 196640 | tf_op jit(solution)/shard_map/ppermute | solution.py:251
  73.1 0.0 collective-permute-done.7.refs_8_
  73.1 1.4 copy-done
  74.5 0.6 squares.1
  75.1 8.3 %psum.14 = f32[16,128]{1,0:T(8,128)S(1)} all-reduce(f32[16,128]{1,0:T(8,128)S(1)} %squares.1), channel_id=1, replica_groups=mesh['x'=4,'z'=16,'y'=4,'c'=2] {'c'}, use_global_device_ids=true, to_apply=%region_0.0 | all-reduce | flops 2048 | bytes 16384 | tf_op jit(solution)/shard_map/psum | solution.py:297
  83.4 10.8 %psum.15.sums_ref = f32[16,128]{1,0:T(8,128)S(1)} all-reduce(f32[16,128]{1,0:T(8,128)S(1)} %psum.14), channel_id=1, replica_groups=mesh['x'=4,'z'=16,'y'=4,'c'=2] {'y'}, use_global_device_ids=true, to_apply=%region_1.0 | all-reduce | flops 2048 | bytes 16384 | tf_op jit(solution)/shard_map/psum | solution.py:297
  94.2 0.0 collective-permute-done.8.refs_1_
  94.2 0.0 collective-permute-done.9.refs_2_
  94.2 1.9 %collective-permute-start.10 = (bf16[6,128,128]{2,1,0:T(8,128)(2,1)}, bf16[6,128,128]{2,1,0:T(8,128)(2,1)S(1)}, u32[]{:S(2)}, u32[]{:S(2)}) collective-permute-start(bf16[6,128,128]{2,1,0:T(8,128)(2,1)} %collective-permute-done.8.refs_1_), channel_id=1, source_target_pairs={{0,8},{8,16},{9,1},{16,24},{17,9},{24,32},{25,17},{32,40},{33,25},... | collective-permute-start | bytes 589832 | tf_op jit(solution)/shard_map/ppermute | solution.py:251
  96.2 6.0 %collective-permute-start.11 = (bf16[6,128,128]{2,1,0:T(8,128)(2,1)}, bf16[6,128,128]{2,1,0:T(8,128)(2,1)S(1)}, u32[]{:S(2)}, u32[]{:S(2)}) collective-permute-start(bf16[6,128,128]{2,1,0:T(8,128)(2,1)} %collective-permute-done.9.refs_2_), channel_id=1, source_target_pairs={{1,9},{8,0},{9,17},{16,8},{17,25},{24,16},{25,33},{32,24},{33,41},... | collective-permute-start | bytes 589832 | tf_op jit(solution)/shard_map/ppermute | solution.py:251
  102.2 0.7 pad_maximum_fusion.3.gain_ref
  102.9 0.0 copy-start.4
  102.9 0.0 copy-start.5
  102.9 6.2 %forward.1 = (bf16[3,128,128]{2,1,0:T(8,128)(2,1)}, f32[3,128,128]{2,1,0:T(8,128)S(1)}, bf16[3,128,128]{2,1,0:T(8,128)(2,1)S(1)}, f32[24,128]{1,0:T(8,128)S(1)}) custom-call(f32[16,128]{1,0:T(8,128)S(1)} %psum.15.sums_ref, bf16[3,128,128]{2,1,0:T(8,128)(2,1)S(1)} %bitcast.16, bf16[3,128,128]{2,1,0:T(8,128)(2,1)S(1)} %bitcast.20, ...), custom_call_target="tpu_custom_call" | custom-call | tf_op jit(solution)/shard_map/forward/pallas_call | solution.py:298
  109.2 1.9 %collective-permute-start.12 = (bf16[6,128,128]{2,1,0:T(8,128)(2,1)S(1)}, bf16[6,128,128]{2,1,0:T(8,128)(2,1)S(1)}, u32[]{:S(2)}, u32[]{:S(2)}) collective-permute-start(bf16[6,128,128]{2,1,0:T(8,128)(2,1)S(1)} %collective-permute-done.10.refs_3_), channel_id=1, source_target_pairs={{0,16},{8,24},{16,32},{17,1},{24,40},{25,9},{32,48},{33,17},{40,56... | collective-permute-start | bytes 589832 | tf_op jit(solution)/shard_map/ppermute | solution.py:251
  111.1 6.9 %collective-permute-start.13 = (bf16[6,128,128]{2,1,0:T(8,128)(2,1)S(1)}, bf16[6,128,128]{2,1,0:T(8,128)(2,1)S(1)}, u32[]{:S(2)}, u32[]{:S(2)}) collective-permute-start(bf16[6,128,128]{2,1,0:T(8,128)(2,1)S(1)} %collective-permute-done.11.refs_4_), channel_id=1, source_target_pairs={{1,17},{9,25},{16,0},{17,33},{24,8},{25,41},{32,16},{33,49},{40,24... | collective-permute-start | bytes 589832 | tf_op jit(solution)/shard_map/ppermute | solution.py:251
  118.0 4.8 %collective-permute-done.12.refs_5_ = bf16[6,128,128]{2,1,0:T(8,128)(2,1)S(1)} collective-permute-done((bf16[6,128,128]{2,1,0:T(8,128)(2,1)S(1)}, bf16[6,128,128]{2,1,0:T(8,128)(2,1)S(1)}, u32[]{:S(2)}, u32[]{:S(2)}) %collective-permute-start.12) | collective-permute-done | bytes 196640 | tf_op jit(solution)/shard_map/ppermute | solution.py:251
  122.9 0.0 collective-permute-done.13.refs_6_
  122.9 1.8 all-gather.1
  124.7 11.9 %all-gather.2.stats_ref = f32[8,24,128]{2,1,0:T(8,128)S(1)} all-gather(f32[2,24,128]{2,1,0:T(8,128)S(1)} %bitcast.27), channel_id=4, replica_groups=mesh['x'=4,'z'=16,'y'=4,'c'=2] {'y'}, dimensions={0}, use_global_device_ids=true | all-gather | bytes 122880 | tf_op jit(solution)/shard_map/all_gather | solution.py:321
  136.6 3.0 %collective-permute-start.15 = (f32[8,8,128]{2,1,0:T(8,128)S(1)}, f32[8,8,128]{2,1,0:T(8,128)S(1)}, u32[]{:S(2)}, u32[]{:S(2)}) collective-permute-start(f32[8,8,128]{2,1,0:T(8,128)S(1)} %get-tuple-element.34), channel_id=1, source_target_pairs={{1,129},{2,258},{9,137},{10,266},{17,145},{18,274},{25,153},{26,28... | collective-permute-start | bytes 98312 | tf_op jit(solution)/shard_map/ppermute | solution.py:345
  139.7 3.3 %collective-permute-start.14 = (f32[8,8,128]{2,1,0:T(8,128)S(1)}, f32[8,8,128]{2,1,0:T(8,128)S(1)}, u32[]{:S(2)}, u32[]{:S(2)}) collective-permute-start(f32[8,8,128]{2,1,0:T(8,128)S(1)} %get-tuple-element.33), channel_id=1, source_target_pairs={{1,9},{3,19},{5,37},{7,71},{8,0},{9,17},{11,27},{13,45},{15,79},{1... | collective-permute-start | bytes 98312 | tf_op jit(solution)/shard_map/ppermute | solution.py:344
  142.9 1.9 %collective-permute-start.16 = (bf16[6,128,128]{2,1,0:T(8,128)(2,1)S(1)}, bf16[6,128,128]{2,1,0:T(8,128)(2,1)S(1)}, u32[]{:S(2)}, u32[]{:S(2)}) collective-permute-start(bf16[6,128,128]{2,1,0:T(8,128)(2,1)S(1)} %collective-permute-done.12.refs_5_), channel_id=1, source_target_pairs={{0,32},{8,40},{16,48},{24,56},{32,64},{33,1},{40,72},{41,9},{48,80... | collective-permute-start | bytes 589832 | tf_op jit(solution)/shard_map/ppermute | solution.py:251
  144.9 8.7 %collective-permute-start.17 = (bf16[6,128,128]{2,1,0:T(8,128)(2,1)S(1)}, bf16[6,128,128]{2,1,0:T(8,128)(2,1)S(1)}, u32[]{:S(2)}, u32[]{:S(2)}) collective-permute-start(bf16[6,128,128]{2,1,0:T(8,128)(2,1)S(1)} %collective-permute-done.13.refs_6_), channel_id=1, source_target_pairs={{1,33},{9,41},{17,49},{25,57},{32,0},{33,65},{40,8},{41,73},{48,16... | collective-permute-start | bytes 589832 | tf_op jit(solution)/shard_map/ppermute | solution.py:251
  153.6 8.4 %all_to_all.5.got_ref = f32[8,16,128]{2,1,0:T(8,128)S(1)} all-to-all(f32[8,16,128]{2,1,0:T(8,128)S(1)} %pad_maximum_fusion.2), channel_id=1, replica_groups=mesh['x'=4,'z'=16,'y'=4,'c'=2] {'y','c'}, dimensions={0} | all-to-all | bytes 131072 | tf_op jit(solution)/shard_map/all_to_all | solution.py:346
  162.1 7.7 %collective-permute-done.16.refs_7_ = bf16[6,128,128]{2,1,0:T(8,128)(2,1)S(1)} collective-permute-done((bf16[6,128,128]{2,1,0:T(8,128)(2,1)S(1)}, bf16[6,128,128]{2,1,0:T(8,128)(2,1)S(1)}, u32[]{:S(2)}, u32[]{:S(2)}) %collective-permute-start.16) | collective-permute-done | bytes 196640 | tf_op jit(solution)/shard_map/ppermute | solution.py:251
  169.8 6.7 %backward.1 = (bf16[3,128,128]{2,1,0:T(8,128)(2,1)}, bf16[3,128,128]{2,1,0:T(8,128)(2,1)}, bf16[3,128,128]{2,1,0:T(8,128)(2,1)}) custom-call(f32[16,128]{1,0:T(8,128)S(1)} %psum.15.sums_ref, f32[8,128]{1,0:T(8,128)S(1)} %get-tuple-element.32.terms_ref, f32[24,128]{1,0:T(8,128)S(1)} %get-tuple-element.31.own_ref, f32[8,16,128]{2,1,0:T(8,128)S(1)} %all_to_all.5.got_ref, ...), custom_call_target="tpu_custom_call" | custom-call | tf_op jit(solution)/shard_map/backward/pallas_call | solution.py:349
  (18 shorter events, 0.1 us)
Async XLA Ops:
  7.2 53.8 %copy-start.2 = (bf16[128,3,128]{2,0,1:T(8,128)(2,1)S(1)}, bf16[128,3,128]{2,0,1:T(8,128)(2,1)}, u32[]{:S(2)}) copy-start(bf16[128,3,128]{2,0,1:T(8,128)(2,1)} %param.7) | copy-start | bytes 294916
  7.2 54.4 %copy-start.3 = (bf16[128,3,128]{2,0,1:T(8,128)(2,1)S(1)}, bf16[128,3,128]{2,0,1:T(8,128)(2,1)}, u32[]{:S(2)}) copy-start(bf16[128,3,128]{2,0,1:T(8,128)(2,1)} %param.10) | copy-start | bytes 294916
  7.2 65.9 %all-gather.5.cloned.1.call-start = ((), (), s32[]{:S(2)}) async-start(), calls=%async_computation.1 | async-start | bytes 1966080 | tf_op jit(solution)/shard_map/all_gather | solution.py:279
  10.1 15.0 %collective-permute-start = (bf16[6,128,128]{2,1,0:T(8,128)(2,1)S(1)}, bf16[6,128,128]{2,1,0:T(8,128)(2,1)S(1)}, u32[]{:S(2)}, u32[]{:S(2)}) collective-permute-start(bf16[6,128,128]{2,1,0:T(8,128)(2,1)S(1)} %pad_maximum_fusion.1.refs_0_), channel_id=1, source_target_pairs={{0,8},{8,16},{9,1},{16,24},{17,9},{24,32},{25,17},{32,40},{33,25},... | collective-permute-start | bytes 589832 | tf_op jit(solution)/shard_map/ppermute | solution.py:251
  14.0 13.1 %collective-permute-start.1 = (bf16[6,128,128]{2,1,0:T(8,128)(2,1)S(1)}, bf16[6,128,128]{2,1,0:T(8,128)(2,1)S(1)}, u32[]{:S(2)}, u32[]{:S(2)}) collective-permute-start(bf16[6,128,128]{2,1,0:T(8,128)(2,1)S(1)} %pad_maximum_fusion.1.refs_0_), channel_id=1, source_target_pairs={{1,9},{8,0},{9,17},{16,8},{17,25},{24,16},{25,33},{32,24},{33,41},... | collective-permute-start | bytes 589832 | tf_op jit(solution)/shard_map/ppermute | solution.py:251
  25.1 9.8 %collective-permute-start.2 = (bf16[6,128,128]{2,1,0:T(8,128)(2,1)S(1)}, bf16[6,128,128]{2,1,0:T(8,128)(2,1)S(1)}, u32[]{:S(2)}, u32[]{:S(2)}) collective-permute-start(bf16[6,128,128]{2,1,0:T(8,128)(2,1)S(1)} %collective-permute-done.refs_1_), channel_id=1, source_target_pairs={{0,8},{8,16},{9,1},{16,24},{17,9},{24,32},{25,17},{32,40},{33,25},... | collective-permute-start | bytes 589832 | tf_op jit(solution)/shard_map/ppermute | solution.py:251
  27.1 9.8 %collective-permute-start.3 = (bf16[6,128,128]{2,1,0:T(8,128)(2,1)S(1)}, bf16[6,128,128]{2,1,0:T(8,128)(2,1)S(1)}, u32[]{:S(2)}, u32[]{:S(2)}) collective-permute-start(bf16[6,128,128]{2,1,0:T(8,128)(2,1)S(1)} %collective-permute-done.1.refs_2_), channel_id=1, source_target_pairs={{1,9},{8,0},{9,17},{16,8},{17,25},{24,16},{25,33},{32,24},{33,41},... | collective-permute-start | bytes 589832 | tf_op jit(solution)/shard_map/ppermute | solution.py:251
  34.9 15.4 %collective-permute-start.4 = (bf16[6,128,128]{2,1,0:T(8,128)(2,1)S(1)}, bf16[6,128,128]{2,1,0:T(8,128)(2,1)S(1)}, u32[]{:S(2)}, u32[]{:S(2)}) collective-permute-start(bf16[6,128,128]{2,1,0:T(8,128)(2,1)S(1)} %collective-permute-done.2.refs_3_), channel_id=1, source_target_pairs={{0,16},{8,24},{16,32},{17,1},{24,40},{25,9},{32,48},{33,17},{40,56... | collective-permute-start | bytes 589832 | tf_op jit(solution)/shard_map/ppermute | solution.py:251
  36.8 13.4 %collective-permute-start.5 = (bf16[6,128,128]{2,1,0:T(8,128)(2,1)S(1)}, bf16[6,128,128]{2,1,0:T(8,128)(2,1)S(1)}, u32[]{:S(2)}, u32[]{:S(2)}) collective-permute-start(bf16[6,128,128]{2,1,0:T(8,128)(2,1)S(1)} %collective-permute-done.3.refs_4_), channel_id=1, source_target_pairs={{1,17},{9,25},{16,0},{17,33},{24,8},{25,41},{32,16},{33,49},{40,24... | collective-permute-start | bytes 589832 | tf_op jit(solution)/shard_map/ppermute | solution.py:251
  50.3 22.8 %collective-permute-start.6 = (bf16[6,128,128]{2,1,0:T(8,128)(2,1)S(1)}, bf16[6,128,128]{2,1,0:T(8,128)(2,1)S(1)}, u32[]{:S(2)}, u32[]{:S(2)}) collective-permute-start(bf16[6,128,128]{2,1,0:T(8,128)(2,1)S(1)} %collective-permute-done.4.refs_5_), channel_id=1, source_target_pairs={{0,32},{8,40},{16,48},{24,56},{32,64},{33,1},{40,72},{41,9},{48,80... | collective-permute-start | bytes 589832 | tf_op jit(solution)/shard_map/ppermute | solution.py:251
  57.1 15.9 %collective-permute-start.7 = (bf16[6,128,128]{2,1,0:T(8,128)(2,1)S(1)}, bf16[6,128,128]{2,1,0:T(8,128)(2,1)S(1)}, u32[]{:S(2)}, u32[]{:S(2)}) collective-permute-start(bf16[6,128,128]{2,1,0:T(8,128)(2,1)S(1)} %collective-permute-done.5.refs_6_), channel_id=1, source_target_pairs={{1,33},{9,41},{17,49},{25,57},{32,0},{33,65},{40,8},{41,73},{48,16... | collective-permute-start | bytes 589832 | tf_op jit(solution)/shard_map/ppermute | solution.py:251
  62.2 32.0 %collective-permute-start.8 = (bf16[6,128,128]{2,1,0:T(8,128)(2,1)}, bf16[6,128,128]{2,1,0:T(8,128)(2,1)}, u32[]{:S(2)}, u32[]{:S(2)}) collective-permute-start(bf16[6,128,128]{2,1,0:T(8,128)(2,1)} %constant_dynamic-update-slice_fusion.refs_0_), channel_id=1, source_target_pairs={{0,8},{8,16},{9,1},{16,24},{17,9},{24,32},{25,17},{32,40},{33,25},... | collective-permute-start | bytes 589832 | tf_op jit(solution)/shard_map/ppermute | solution.py:251
  64.2 30.1 %collective-permute-start.9 = (bf16[6,128,128]{2,1,0:T(8,128)(2,1)}, bf16[6,128,128]{2,1,0:T(8,128)(2,1)}, u32[]{:S(2)}, u32[]{:S(2)}) collective-permute-start(bf16[6,128,128]{2,1,0:T(8,128)(2,1)} %constant_dynamic-update-slice_fusion.refs_0_), channel_id=1, source_target_pairs={{1,9},{8,0},{9,17},{16,8},{17,25},{24,16},{25,33},{32,24},{33,41},... | collective-permute-start | bytes 589832 | tf_op jit(solution)/shard_map/ppermute | solution.py:251
  73.1 1.4 copy-start
  74.5 28.4 %copy-start.1 = (bf16[48,128,128]{2,1,0:T(8,128)(2,1)S(1)}, bf16[48,128,128]{2,1,0:T(8,128)(2,1)}, u32[]{:S(2)}) copy-start(bf16[48,128,128]{2,1,0:T(8,128)(2,1)} %all-gather.5.cloned.1.call-done) | copy-start | bytes 4718596
  94.2 14.9 %collective-permute-start.10 = (bf16[6,128,128]{2,1,0:T(8,128)(2,1)}, bf16[6,128,128]{2,1,0:T(8,128)(2,1)S(1)}, u32[]{:S(2)}, u32[]{:S(2)}) collective-permute-start(bf16[6,128,128]{2,1,0:T(8,128)(2,1)} %collective-permute-done.8.refs_1_), channel_id=1, source_target_pairs={{0,8},{8,16},{9,1},{16,24},{17,9},{24,32},{25,17},{32,40},{33,25},... | collective-permute-start | bytes 589832 | tf_op jit(solution)/shard_map/ppermute | solution.py:251
  96.2 13.0 %collective-permute-start.11 = (bf16[6,128,128]{2,1,0:T(8,128)(2,1)}, bf16[6,128,128]{2,1,0:T(8,128)(2,1)S(1)}, u32[]{:S(2)}, u32[]{:S(2)}) collective-permute-start(bf16[6,128,128]{2,1,0:T(8,128)(2,1)} %collective-permute-done.9.refs_2_), channel_id=1, source_target_pairs={{1,9},{8,0},{9,17},{16,8},{17,25},{24,16},{25,33},{32,24},{33,41},... | collective-permute-start | bytes 589832 | tf_op jit(solution)/shard_map/ppermute | solution.py:251
  102.9 66.9 %copy-start.4 = (bf16[128,3,128]{2,0,1:T(8,128)(2,1)S(1)}, bf16[128,3,128]{2,0,1:T(8,128)(2,1)}, u32[]{:S(2)}) copy-start(bf16[128,3,128]{2,0,1:T(8,128)(2,1)} %param.9) | copy-start | bytes 294916
  102.9 66.9 %copy-start.5 = (bf16[128,3,128]{2,0,1:T(8,128)(2,1)S(1)}, bf16[128,3,128]{2,0,1:T(8,128)(2,1)}, u32[]{:S(2)}) copy-start(bf16[128,3,128]{2,0,1:T(8,128)(2,1)} %param.8) | copy-start | bytes 294916
  109.2 13.7 %collective-permute-start.12 = (bf16[6,128,128]{2,1,0:T(8,128)(2,1)S(1)}, bf16[6,128,128]{2,1,0:T(8,128)(2,1)S(1)}, u32[]{:S(2)}, u32[]{:S(2)}) collective-permute-start(bf16[6,128,128]{2,1,0:T(8,128)(2,1)S(1)} %collective-permute-done.10.refs_3_), channel_id=1, source_target_pairs={{0,16},{8,24},{16,32},{17,1},{24,40},{25,9},{32,48},{33,17},{40,56... | collective-permute-start | bytes 589832 | tf_op jit(solution)/shard_map/ppermute | solution.py:251
  111.1 11.7 %collective-permute-start.13 = (bf16[6,128,128]{2,1,0:T(8,128)(2,1)S(1)}, bf16[6,128,128]{2,1,0:T(8,128)(2,1)S(1)}, u32[]{:S(2)}, u32[]{:S(2)}) collective-permute-start(bf16[6,128,128]{2,1,0:T(8,128)(2,1)S(1)} %collective-permute-done.11.refs_4_), channel_id=1, source_target_pairs={{1,17},{9,25},{16,0},{17,33},{24,8},{25,41},{32,16},{33,49},{40,24... | collective-permute-start | bytes 589832 | tf_op jit(solution)/shard_map/ppermute | solution.py:251
  136.6 17.0 %collective-permute-start.15 = (f32[8,8,128]{2,1,0:T(8,128)S(1)}, f32[8,8,128]{2,1,0:T(8,128)S(1)}, u32[]{:S(2)}, u32[]{:S(2)}) collective-permute-start(f32[8,8,128]{2,1,0:T(8,128)S(1)} %get-tuple-element.34), channel_id=1, source_target_pairs={{1,129},{2,258},{9,137},{10,266},{17,145},{18,274},{25,153},{26,28... | collective-permute-start | bytes 98312 | tf_op jit(solution)/shard_map/ppermute | solution.py:345
  139.7 14.0 %collective-permute-start.14 = (f32[8,8,128]{2,1,0:T(8,128)S(1)}, f32[8,8,128]{2,1,0:T(8,128)S(1)}, u32[]{:S(2)}, u32[]{:S(2)}) collective-permute-start(f32[8,8,128]{2,1,0:T(8,128)S(1)} %get-tuple-element.33), channel_id=1, source_target_pairs={{1,9},{3,19},{5,37},{7,71},{8,0},{9,17},{11,27},{13,45},{15,79},{1... | collective-permute-start | bytes 98312 | tf_op jit(solution)/shard_map/ppermute | solution.py:344
  142.9 26.8 %collective-permute-start.16 = (bf16[6,128,128]{2,1,0:T(8,128)(2,1)S(1)}, bf16[6,128,128]{2,1,0:T(8,128)(2,1)S(1)}, u32[]{:S(2)}, u32[]{:S(2)}) collective-permute-start(bf16[6,128,128]{2,1,0:T(8,128)(2,1)S(1)} %collective-permute-done.12.refs_5_), channel_id=1, source_target_pairs={{0,32},{8,40},{16,48},{24,56},{32,64},{33,1},{40,72},{41,9},{48,80... | collective-permute-start | bytes 589832 | tf_op jit(solution)/shard_map/ppermute | solution.py:251
  144.9 24.9 %collective-permute-start.17 = (bf16[6,128,128]{2,1,0:T(8,128)(2,1)S(1)}, bf16[6,128,128]{2,1,0:T(8,128)(2,1)S(1)}, u32[]{:S(2)}, u32[]{:S(2)}) collective-permute-start(bf16[6,128,128]{2,1,0:T(8,128)(2,1)S(1)} %collective-permute-done.13.refs_6_), channel_id=1, source_target_pairs={{1,33},{9,41},{17,49},{25,57},{32,0},{33,65},{40,8},{41,73},{48,16... | collective-permute-start | bytes 589832 | tf_op jit(solution)/shard_map/ppermute | solution.py:251
Sparse Core Ops, SparseCore 0:
  10.1 43.9 all-gather.4

commit v5 on v1

v5 whole, which is shorter than its diff:
```python
import functools

import jax
import jax.numpy as jnp
from jax import lax
from jax.experimental import pallas as pl
from jax.experimental.pallas import tpu as pltpu
from jax.sharding import Mesh, PartitionSpec as P

TILE = 128
EPS = 1e-06
NEAR = (0, -1, 1, -2, 2, -4, 4, -8, 8)
FAR = 3
NT = (((1,), (1,)), ((), ()))
NN = (((1,), (0,)), ((), ()))
TN = (((0,), (0,)), ((), ()))
F32 = jnp.float32
BF16 = jnp.bfloat16
VMEM_LIMIT = 48 * 1024 * 1024


def dot(left, right, dims):
    return lax.dot_general(left, right, dims, preferred_element_type=F32)


def row_sums(square):
    ones = jnp.ones((8, TILE), BF16)
    high = square.astype(BF16)
    low = (square - high.astype(F32)).astype(BF16)
    return dot(ones, high, NT) + dot(ones, low, NT)


def columns(rows):
    fill = jnp.zeros((TILE - rows.shape[0], TILE), F32)
    return jnp.transpose(jnp.concatenate([rows, fill], axis=0))


def own_frame():
    return lax.axis_index("x") * lax.axis_size("z") + lax.axis_index("z")


def mirrored(value):
    return value * (1 - 2 * lax.axis_index("c"))


def shared_place(place):
    if place == 0 or place == len(NEAR) + FAR - 1:
        return place
    return 1 + ((place - 1) ^ lax.axis_index("c"))


def inside(place):
    line, lines = lax.axis_size("z"), lax.axis_size("x")
    near = len(NEAR)
    if place == 0 or place == near + FAR - 1:
        return None
    offset = NEAR[place] if place < near else (-line, line)[place - near]
    at = own_frame() + mirrored(offset)
    return (at >= 0) & (at < line * lines)


def reader(tiles, gathered_ref, place):
    if place < len(NEAR):
        return lambda i: tiles[place][i]
    lines = lax.axis_size("x")
    step = (mirrored(-1), mirrored(1), lines // 2)[place - len(NEAR)]
    at = lax.rem(lax.axis_index("x") + step + lines, lines)
    return lambda i: gathered_ref[at, i]


def squares_kernel(heads, q_ref, gathered_ref, *refs):
    tiles, out_ref = refs[:-1], refs[-1]
    count = len(NEAR) + FAR
    out_ref[...] = jnp.zeros(out_ref.shape, F32)
    for place in range(count + 1):
        if len(tiles) <= place < len(NEAR):
            continue
        read = reader(tiles, gathered_ref, place) if place < count else lambda i: q_ref[i]
        total = jnp.zeros((TILE, TILE), F32)
        for head in range(heads):
            floats = read(head).astype(F32)
            total = total + floats * floats
        row = shared_place(place) if place < count else place
        out_ref[pl.ds(row, 1), :] = row_sums(total)[0:1]


def attention_kernel(
    heads, channels, sums_ref, before_ref, after_ref, q_ref, do_ref, gain_ref, gathered_ref, *refs
):
    near = len(NEAR)
    count = near + FAR
    tiles = refs[:near]
    out_ref, dq_ref = refs[near : near + 2]
    part_refs = refs[near + 2 : -2]
    norm_ref, work_ref = refs[-2:]
    scale = TILE ** (-0.5)
    rows = []
    for place in range(count):
        if near - 2 <= place < near:
            ref = (before_ref, after_ref)[place - near + 2]
            rows.append(ref[pl.ds(shared_place(place - 2), 1), :])
        else:
            rows.append(sums_ref[pl.ds(shared_place(place), 1), :])
    rows.append(sums_ref[count : count + 1, :])
    turned = columns(lax.rsqrt(jnp.concatenate(rows, axis=0) / channels + EPS))
    usable = [inside(t) for t in range(count)]
    reads = [reader(tiles, gathered_ref, t) for t in range(count)]
    for head in range(heads):
        query = (
            q_ref[head].astype(F32) * turned[:, count : count + 1] * gain_ref[head : head + 1]
        ).astype(BF16)
        upstream = do_ref[head]
        top = jnp.full((TILE, TILE), -1e30, F32)
        for t in range(count):
            key = (
                reads[t](head).astype(F32)
                * turned[:, t : t + 1]
                * gain_ref[heads + head : heads + head + 1]
            ).astype(BF16)
            norm_ref[t] = key
            score = dot(query, key, NT) * scale
            if usable[t] is not None:
                score = jnp.where(usable[t], score, -1e30)
            work_ref[t] = score
            top = jnp.maximum(top, score)
        top = jnp.max(top, axis=1, keepdims=True)
        total = jnp.zeros((TILE, TILE), F32)
        for t in range(count):
            weight = jnp.exp(work_ref[t] - top)
            work_ref[t] = weight
            total = total + weight
        share = 1.0 / jnp.sum(total, axis=1, keepdims=True)
        out = jnp.zeros((TILE, TILE), F32)
        for t in range(count):
            prob = (work_ref[t] * share).astype(BF16)
            out = out + dot(prob, reads[t](heads + head), NN)
            part = part_refs[t]
            part[heads + head] = dot(prob, upstream, TN).astype(part.dtype)
        out = out.astype(BF16)
        out_ref[head] = out
        delta = jnp.sum(upstream.astype(F32) * out.astype(F32), axis=1, keepdims=True)
        query_grad = jnp.zeros((TILE, TILE), F32)
        for t in range(count):
            prob = work_ref[t] * share
            dscore = (prob * (dot(upstream, reads[t](heads + head), NT) - delta)).astype(BF16)
            query_grad = query_grad + dot(dscore, norm_ref[t], NN)
            part = part_refs[t]
            part[head] = (dot(dscore, query, TN) * scale).astype(part.dtype)
        dq_ref[head] = query_grad * scale


def terms_kernel(heads, q_ref, k_ref, dq_ref, gain_ref, *refs):
    parts, (dk_ref, dv_ref, terms_ref) = refs[:-3], refs[-3:]
    query_total = jnp.zeros((TILE, TILE), F32)
    key_total = jnp.zeros((TILE, TILE), F32)
    for head in range(heads):
        key_grad, value_grad = parts[0][head], parts[0][heads + head]
        for part in parts[1:]:
            key_grad = key_grad + part[head].astype(F32)
            value_grad = value_grad + part[heads + head].astype(F32)
        dk_ref[head] = key_grad
        dv_ref[head] = value_grad.astype(BF16)
        query_total = query_total + q_ref[head].astype(F32) * (
            dq_ref[head] * gain_ref[head : head + 1]
        )
        key_total = key_total + k_ref[head].astype(F32) * (
            key_grad * gain_ref[heads + head : heads + head + 1]
        )
    terms_ref[...] = jnp.zeros(terms_ref.shape, F32)
    terms_ref[0:1, :] = row_sums(query_total)[0:1]
    terms_ref[1:2, :] = row_sums(key_total)[0:1]


def final_kernel(
    heads, channels, sums_ref, terms_ref, q_ref, k_ref, dq_ref, dk_ref, gain_ref, gq_ref, gk_ref
):
    count = len(NEAR) + FAR
    inverse = lax.rsqrt(
        jnp.concatenate([sums_ref[count : count + 1], sums_ref[0:1]], axis=0) / channels + EPS
    )
    cubes = inverse * inverse * inverse * terms_ref[0:2] / channels
    turned = columns(jnp.concatenate([inverse, cubes], axis=0))
    for head in range(heads):
        gq_ref[head] = (
            turned[:, 0:1] * (gain_ref[head : head + 1] * dq_ref[head])
            - q_ref[head].astype(F32) * turned[:, 2:3]
        ).astype(BF16)
        gk_ref[head] = (
            turned[:, 1:2] * (gain_ref[heads + head : heads + head + 1] * dk_ref[head])
            - k_ref[head].astype(F32) * turned[:, 3:4]
        ).astype(BF16)


SEQ, HEAD = ("x", "z"), ("y", "c")


def passed(value, steps):
    count = lax.axis_size("x") * lax.axis_size("z")
    pairs = [
        (2 * i + core, 2 * (i + way * steps) + core)
        for i in range(count)
        for core, way in enumerate((1, -1))
        if 0 <= i + way * steps < count
    ]
    return lax.ppermute(value, SEQ + ("c",), pairs)


def spread(value):
    got = {0: value}
    for offset in NEAR[1:]:
        half = abs(offset) // 2 * (1 if offset > 0 else -1)
        got[offset] = passed(got[half], half - offset)
    return [got[offset] for offset in NEAR]


def collect(parts):
    arrived = []
    for side in (1, 2):
        carried = parts[len(NEAR) - 3 + side]
        for place in range(len(NEAR) - 3 + side, 0, -2):
            offset = NEAR[place]
            half = abs(offset) // 2 * (1 if offset > 0 else -1)
            carried = passed(carried, offset - half)
            if half:
                carried = (carried.astype(F32) + parts[place - 2]).astype(BF16)
        arrived.append(carried)
    return arrived


def per_device(total_heads, q_raw, k_raw, values, grad_out, q_gain, k_gain, key_tiles):
    lines, line = lax.axis_size("x"), lax.axis_size("z")
    seq_count = lines * line
    near = len(NEAR)
    count = near + FAR
    heads = q_raw.shape[1]
    channels = float(total_heads * q_raw.shape[2])
    q_raw, k_raw, values, grad_out = [
        jnp.transpose(array, (1, 0, 2)) for array in (q_raw, k_raw, values, grad_out)
    ]
    gains = jnp.concatenate([q_gain, k_gain], axis=0)
    first = jnp.concatenate([k_raw, values], axis=0)
    column = lax.all_gather(jnp.concatenate([first, jnp.zeros_like(k_raw[:2])], axis=0), "x")
    tiles = spread(first)

    vmem = pl.BlockSpec(memory_space=pltpu.VMEM)
    params = pltpu.CompilerParams(vmem_limit_bytes=VMEM_LIMIT)
    whole, pair = (heads, TILE, TILE), (2 * heads, TILE, TILE)
    sums = pl.pallas_call(
        functools.partial(squares_kernel, heads),
        out_shape=jax.ShapeDtypeStruct((16, TILE), F32),
        in_specs=[vmem] * near,
        out_specs=vmem,
        compiler_params=params,
        name="squares",
    )(q_raw, column, *tiles[: near - 2])
    sums = lax.psum(lax.psum(sums, "c"), "y")
    reach = NEAR[near - 3]
    before, after = passed(sums, reach), passed(sums, -reach)
    attended, dq, *parts = pl.pallas_call(
        functools.partial(attention_kernel, heads, channels),
        out_shape=[jax.ShapeDtypeStruct(whole, BF16), jax.ShapeDtypeStruct(whole, F32)]
        + [jax.ShapeDtypeStruct(pair, F32 if t < near - 2 else BF16) for t in range(count)],
        in_specs=[vmem] * (7 + near),
        out_specs=[vmem] * (2 + count),
        scratch_shapes=[
            pltpu.VMEM((count, TILE, TILE), BF16),
            pltpu.VMEM((count, TILE, TILE), F32),
        ],
        compiler_params=params,
        name="attention",
    )(sums, before, after, q_raw, grad_out, gains, column, *tiles)
    arrived = collect(parts) + [passed(parts[near], -line), passed(parts[near + 1], line)]
    arrived.append(
        lax.ppermute(
            parts[near + 2], SEQ, [(i, (i + seq_count // 2) % seq_count) for i in range(seq_count)]
        )
    )
    dk, grad_v, terms = pl.pallas_call(
        functools.partial(terms_kernel, heads),
        out_shape=[
            jax.ShapeDtypeStruct(whole, F32),
            jax.ShapeDtypeStruct(whole, BF16),
            jax.ShapeDtypeStruct((8, TILE), F32),
        ],
        in_specs=[vmem] * (5 + len(arrived)),
        out_specs=[vmem] * 3,
        compiler_params=params,
        name="terms",
    )(q_raw, k_raw, dq, gains, parts[0], *arrived)
    terms = lax.psum(lax.psum(terms, "c"), "y")
    grad_q, grad_k = pl.pallas_call(
        functools.partial(final_kernel, heads, channels),
        out_shape=[jax.ShapeDtypeStruct(whole, BF16)] * 2,
        in_specs=[vmem] * 7,
        out_specs=[vmem] * 2,
        compiler_params=params,
        name="final",
    )(sums, terms, q_raw, k_raw, dq, dk, gains)
    return tuple(
        jnp.transpose(array, (1, 0, 2)) for array in (attended, grad_q, grad_k, grad_v)
    )


def solution(mesh):
    split = Mesh(mesh.devices.reshape(4, -1, mesh.shape["head"] // 2, 2), SEQ + HEAD)

    def whole(q_raw, k_raw, values, grad_out, q_gain, k_gain, key_tiles):
        tokens = P(SEQ, HEAD, None)
        return jax.shard_map(
            functools.partial(per_device, q_raw.shape[1]),
            mesh=split,
            in_specs=(tokens,) * 4 + (P(HEAD, None), P(HEAD, None), P()),
            out_specs=(tokens,) * 4,
            check_vma=False,
        )(q_raw, k_raw, values, grad_out, q_gain, k_gain, key_tiles)

    return whole
```

time: 204 us -> 190 us (0.931)
  the two profiles are of different devices: /device:TPU:7 before, /device:TPU:12 now
where the time goes in v5:
time: 190 us; the launch traced here: 189 us
  starting transfers between devices  84.3 us (44%)
  waiting for transfers between devices  49.1 us (26%)
  blocking collectives  23.8 us (13%)
  between operations  14.4 us (8%)
  Pallas kernels  13.4 us (7%)
  local copies, waits for them, and re-layouts  2.23 us (1%)
  other arithmetic  2.08 us (1%)
    ppermute x20, starting transfers between devices, passed(): return lax.ppermute(value, SEQ + ('c',), pairs)  82.4 us
    ppermute x20, waiting for transfers between devices, passed(): return lax.ppermute(value, SEQ + ('c',), pairs)  49 us
    psum x2, blocking collectives, per_device(): terms = lax.psum(lax.psum(terms, 'c'), 'y')  12.5 us
    psum x2, blocking collectives, per_device(): sums = lax.psum(lax.psum(sums, 'c'), 'y')  11.3 us
    pallas_call x1, Pallas kernels, per_device(): pl.pallas_call(functools.partial(attention_kernel, heads, channels), out_...  11.1 us
  transfers between devices with their start and end apart: 22, of which 11 were waited for; matrix products, arithmetic and copies ran while one was open for 0% of the time, Pallas kernels for 0%

profile of v5, /device:TPU:12, one launch (start us, length us, event | category | flops | bytes accessed | tf_op | source)
XLA Modules:
  0.0 189.3 jit_solution(4991176508915545248)
XLA Ops:
  7.2 0.1 pad.6.clone
  7.3 1.7 maximum_maximum_fusion
  9.1 0.9 copy-done.2
  10.0 11.5 %collective-permute-start.1 = (bf16[6,128,128]{2,1,0:T(8,128)(2,1)S(1)}, bf16[6,128,128]{2,1,0:T(8,128)(2,1)S(1)}, u32[]{:S(2)}, u32[]{:S(2)}) collective-permute-start(bf16[6,128,128]{2,1,0:T(8,128)(2,1)S(1)} %pad_maximum_fusion.refs_0_), channel_id=1, source_target_pairs={{1,9},{8,0},{9,17},{16,8},{17,25},{24,16},{25,33},{32,24},{33,41},... | collective-permute-start | bytes 589832 | tf_op jit(solution)/shard_map/ppermute | solution.py:205
  21.5 1.9 %collective-permute-start = (bf16[6,128,128]{2,1,0:T(8,128)(2,1)S(1)}, bf16[6,128,128]{2,1,0:T(8,128)(2,1)S(1)}, u32[]{:S(2)}, u32[]{:S(2)}) collective-permute-start(bf16[6,128,128]{2,1,0:T(8,128)(2,1)S(1)} %pad_maximum_fusion.refs_0_), channel_id=1, source_target_pairs={{0,8},{8,16},{9,1},{16,24},{17,9},{24,32},{25,17},{32,40},{33,25},... | collective-permute-start | bytes 589832 | tf_op jit(solution)/shard_map/ppermute | solution.py:205
  23.4 2.6 %collective-permute-done.1.refs_2_ = bf16[6,128,128]{2,1,0:T(8,128)(2,1)S(1)} collective-permute-done((bf16[6,128,128]{2,1,0:T(8,128)(2,1)S(1)}, bf16[6,128,128]{2,1,0:T(8,128)(2,1)S(1)}, u32[]{:S(2)}, u32[]{:S(2)}) %collective-permute-start.1) | collective-permute-done | bytes 196640 | tf_op jit(solution)/shard_map/ppermute | solution.py:205
  26.0 6.5 %collective-permute-start.3 = (bf16[6,128,128]{2,1,0:T(8,128)(2,1)S(1)}, bf16[6,128,128]{2,1,0:T(8,128)(2,1)S(1)}, u32[]{:S(2)}, u32[]{:S(2)}) collective-permute-start(bf16[6,128,128]{2,1,0:T(8,128)(2,1)S(1)} %collective-permute-done.1.refs_2_), channel_id=1, source_target_pairs={{1,9},{8,0},{9,17},{16,8},{17,25},{24,16},{25,33},{32,24},{33,41},... | collective-permute-start | bytes 589832 | tf_op jit(solution)/shard_map/ppermute | solution.py:205
  32.5 1.9 %collective-permute-start.2 = (bf16[6,128,128]{2,1,0:T(8,128)(2,1)S(1)}, bf16[6,128,128]{2,1,0:T(8,128)(2,1)S(1)}, u32[]{:S(2)}, u32[]{:S(2)}) collective-permute-start(bf16[6,128,128]{2,1,0:T(8,128)(2,1)S(1)} %collective-permute-done.refs_1_), channel_id=1, source_target_pairs={{0,8},{8,16},{9,1},{16,24},{17,9},{24,32},{25,17},{32,40},{33,25},... | collective-permute-start | bytes 589832 | tf_op jit(solution)/shard_map/ppermute | solution.py:205
  34.4 3.0 %collective-permute-done.3.refs_4_ = bf16[6,128,128]{2,1,0:T(8,128)(2,1)S(1)} collective-permute-done((bf16[6,128,128]{2,1,0:T(8,128)(2,1)S(1)}, bf16[6,128,128]{2,1,0:T(8,128)(2,1)S(1)}, u32[]{:S(2)}, u32[]{:S(2)}) %collective-permute-start.3) | collective-permute-done | bytes 196640 | tf_op jit(solution)/shard_map/ppermute | solution.py:205
  37.4 4.1 %collective-permute-start.5 = (bf16[6,128,128]{2,1,0:T(8,128)(2,1)S(1)}, bf16[6,128,128]{2,1,0:T(8,128)(2,1)S(1)}, u32[]{:S(2)}, u32[]{:S(2)}) collective-permute-start(bf16[6,128,128]{2,1,0:T(8,128)(2,1)S(1)} %collective-permute-done.3.refs_4_), channel_id=1, source_target_pairs={{1,17},{9,25},{16,0},{17,33},{24,8},{25,41},{32,16},{33,49},{40,24... | collective-permute-start | bytes 589832 | tf_op jit(solution)/shard_map/ppermute | solution.py:205
  41.5 2.9 %collective-permute-done.2.refs_3_ = bf16[6,128,128]{2,1,0:T(8,128)(2,1)S(1)} collective-permute-done((bf16[6,128,128]{2,1,0:T(8,128)(2,1)S(1)}, bf16[6,128,128]{2,1,0:T(8,128)(2,1)S(1)}, u32[]{:S(2)}, u32[]{:S(2)}) %collective-permute-start.2) | collective-permute-done | bytes 196640 | tf_op jit(solution)/shard_map/ppermute | solution.py:205
  44.4 1.9 %collective-permute-start.4 = (bf16[6,128,128]{2,1,0:T(8,128)(2,1)S(1)}, bf16[6,128,128]{2,1,0:T(8,128)(2,1)S(1)}, u32[]{:S(2)}, u32[]{:S(2)}) collective-permute-start(bf16[6,128,128]{2,1,0:T(8,128)(2,1)S(1)} %collective-permute-done.2.refs_3_), channel_id=1, source_target_pairs={{0,16},{8,24},{16,32},{17,1},{24,40},{25,9},{32,48},{33,17},{40,56... | collective-permute-start | bytes 589832 | tf_op jit(solution)/shard_map/ppermute | solution.py:205
  46.3 3.5 %collective-permute-done.5.refs_6_ = bf16[6,128,128]{2,1,0:T(8,128)(2,1)S(1)} collective-permute-done((bf16[6,128,128]{2,1,0:T(8,128)(2,1)S(1)}, bf16[6,128,128]{2,1,0:T(8,128)(2,1)S(1)}, u32[]{:S(2)}, u32[]{:S(2)}) %collective-permute-start.5) | collective-permute-done | bytes 196640 | tf_op jit(solution)/shard_map/ppermute | solution.py:205
  49.9 1.9 %collective-permute-start.9 = (bf16[6,128,128]{2,1,0:T(8,128)(2,1)S(1)}, bf16[6,128,128]{2,1,0:T(8,128)(2,1)S(1)}, u32[]{:S(2)}, u32[]{:S(2)}) collective-permute-start(bf16[6,128,128]{2,1,0:T(8,128)(2,1)S(1)} %collective-permute-done.5.refs_6_), channel_id=1, source_target_pairs={{1,33},{9,41},{17,49},{25,57},{32,0},{33,65},{40,8},{41,73},{48,16... | collective-permute-start | bytes 589832 | tf_op jit(solution)/shard_map/ppermute | solution.py:205
  51.8 12.4 %collective-permute-done.4.refs_5_ = bf16[6,128,128]{2,1,0:T(8,128)(2,1)S(1)} collective-permute-done((bf16[6,128,128]{2,1,0:T(8,128)(2,1)S(1)}, bf16[6,128,128]{2,1,0:T(8,128)(2,1)S(1)}, u32[]{:S(2)}, u32[]{:S(2)}) %collective-permute-start.4) | collective-permute-done | bytes 196640 | tf_op jit(solution)/shard_map/ppermute | solution.py:205
  64.1 1.9 %collective-permute-start.8 = (bf16[6,128,128]{2,1,0:T(8,128)(2,1)S(1)}, bf16[6,128,128]{2,1,0:T(8,128)(2,1)S(1)}, u32[]{:S(2)}, u32[]{:S(2)}) collective-permute-start(bf16[6,128,128]{2,1,0:T(8,128)(2,1)S(1)} %collective-permute-done.4.refs_5_), channel_id=1, source_target_pairs={{0,32},{8,40},{16,48},{24,56},{32,64},{33,1},{40,72},{41,9},{48,80... | collective-permute-start | bytes 589832 | tf_op jit(solution)/shard_map/ppermute | solution.py:205
  66.1 1.2 copy-done
  67.3 0.5 squares.1
  67.8 2.5 %psum.28 = f32[16,128]{1,0:T(8,128)S(1)} all-reduce(f32[16,128]{1,0:T(8,128)S(1)} %squares.1), channel_id=1, replica_groups=mesh['x'=4,'z'=16,'y'=4,'c'=2] {'c'}, use_global_device_ids=true, to_apply=%region_0.0 | all-reduce | flops 2048 | bytes 16384 | tf_op jit(solution)/shard_map/psum | solution.py:256
  70.3 8.8 %psum.29.sums_ref = f32[16,128]{1,0:T(8,128)S(1)} all-reduce(f32[16,128]{1,0:T(8,128)S(1)} %psum.28), channel_id=1, replica_groups=mesh['x'=4,'z'=16,'y'=4,'c'=2] {'y'}, use_global_device_ids=true, to_apply=%region_1.0 | all-reduce | flops 2048 | bytes 16384 | tf_op jit(solution)/shard_map/psum | solution.py:256
  79.1 8.7 %collective-permute-start.7 = (f32[16,128]{1,0:T(8,128)S(1)}, f32[16,128]{1,0:T(8,128)S(1)}, u32[]{:S(2)}, u32[]{:S(2)}) collective-permute-start(f32[16,128]{1,0:T(8,128)S(1)} %psum.29.sums_ref), channel_id=1, source_target_pairs={{1,33},{9,41},{17,49},{25,57},{32,0},{33,65},{40,8},{41,73},{48,16... | collective-permute-start | bytes 24584 | tf_op jit(solution)/shard_map/ppermute | solution.py:205
  87.9 1.9 %collective-permute-start.6 = (f32[16,128]{1,0:T(8,128)S(1)}, f32[16,128]{1,0:T(8,128)S(1)}, u32[]{:S(2)}, u32[]{:S(2)}) collective-permute-start(f32[16,128]{1,0:T(8,128)S(1)} %psum.29.sums_ref), channel_id=1, source_target_pairs={{0,32},{8,40},{16,48},{24,56},{32,64},{33,1},{40,72},{41,9},{48,80... | collective-permute-start | bytes 24584 | tf_op jit(solution)/shard_map/ppermute | solution.py:205
  89.9 8.4 %collective-permute-done.6.before_ref = f32[16,128]{1,0:T(8,128)S(1)} collective-permute-done((f32[16,128]{1,0:T(8,128)S(1)}, f32[16,128]{1,0:T(8,128)S(1)}, u32[]{:S(2)}, u32[]{:S(2)}) %collective-permute-start.6) | collective-permute-done | bytes 8224 | tf_op jit(solution)/shard_map/ppermute | solution.py:205
  98.2 11.1 %attention.1 = (bf16[3,128,128]{2,1,0:T(8,128)(2,1)}, f32[3,128,128]{2,1,0:T(8,128)S(1)}, f32[6,128,128]{2,1,0:T(8,128)S(1)}, f32[6,128,128]{2,1,0:T(8,128)S(1)}...) custom-call(f32[16,128]{1,0:T(8,128)S(1)} %psum.29.sums_ref, ...), custom_call_target="tpu_custom_call" | custom-call | tf_op jit(solution)/shard_map/attention/pallas_call | solution.py:259
  109.3 1.9 %collective-permute-start.10 = (bf16[6,128,128]{2,1,0:T(8,128)(2,1)S(1)}, bf16[6,128,128]{2,1,0:T(8,128)(2,1)S(1)}, u32[]{:S(2)}, u32[]{:S(2)}) collective-permute-start(bf16[6,128,128]{2,1,0:T(8,128)(2,1)S(1)} %get-tuple-element.26), channel_id=1, source_target_pairs={{1,33},{9,41},{17,49},{25,57},{32,0},{33,65},{40,8},{41,73},{48,16... | collective-permute-start | bytes 589832 | tf_op jit(solution)/shard_map/ppermute | solution.py:205
  111.2 7.8 %collective-permute-start.14 = (bf16[6,128,128]{2,1,0:T(8,128)(2,1)S(1)}, bf16[6,128,128]{2,1,0:T(8,128)(2,1)S(1)}, u32[]{:S(2)}, u32[]{:S(2)}) collective-permute-start(bf16[6,128,128]{2,1,0:T(8,128)(2,1)S(1)} %get-tuple-element.30), channel_id=1, source_target_pairs={{0,32},{8,40},{16,48},{24,56},{32,64},{33,1},{40,72},{41,9},{48,80... | collective-permute-start | bytes 589832 | tf_op jit(solution)/shard_map/ppermute | solution.py:205
  119.1 2.4 %collective-permute-start.18 = (bf16[6,128,128]{2,1,0:T(8,128)(2,1)S(1)}, bf16[6,128,128]{2,1,0:T(8,128)(2,1)S(1)}, u32[]{:S(2)}, u32[]{:S(2)}) collective-permute-start(bf16[6,128,128]{2,1,0:T(8,128)(2,1)S(1)} %get-tuple-element.34), channel_id=1, source_target_pairs={{1,129},{9,137},{17,145},{25,153},{33,161},{41,169},{49,177},{57,1... | collective-permute-start | bytes 589832 | tf_op jit(solution)/shard_map/ppermute | solution.py:205
  121.5 3.4 %collective-permute-start.19 = (bf16[6,128,128]{2,1,0:T(8,128)(2,1)S(1)}, bf16[6,128,128]{2,1,0:T(8,128)(2,1)S(1)}, u32[]{:S(2)}, u32[]{:S(2)}) collective-permute-start(bf16[6,128,128]{2,1,0:T(8,128)(2,1)S(1)} %get-tuple-element.35), channel_id=1, source_target_pairs={{0,128},{8,136},{16,144},{24,152},{32,160},{40,168},{48,176},{56,1... | collective-permute-start | bytes 589832 | tf_op jit(solution)/shard_map/ppermute | solution.py:205
  124.9 1.9 %collective-permute-start.20 = (bf16[6,128,128]{2,1,0:T(8,128)(2,1)S(1)}, bf16[6,128,128]{2,1,0:T(8,128)(2,1)S(1)}, u32[]{:S(2)}, u32[]{:S(2)}) collective-permute-start(bf16[6,128,128]{2,1,0:T(8,128)(2,1)S(1)} %get-tuple-element.36), channel_id=1, source_target_pairs={{0,256},{8,264},{16,272},{24,280},{32,288},{40,296},{48,304},{56,3... | collective-permute-start | bytes 589832 | tf_op jit(solution)/shard_map/ppermute | solution.py:274
  126.9 2.3 %collective-permute-done.10 = bf16[6,128,128]{2,1,0:T(8,128)(2,1)S(1)} collective-permute-done((bf16[6,128,128]{2,1,0:T(8,128)(2,1)S(1)}, bf16[6,128,128]{2,1,0:T(8,128)(2,1)S(1)}, u32[]{:S(2)}, u32[]{:S(2)}) %collective-permute-start.10) | collective-permute-done | bytes 196640 | tf_op jit(solution)/shard_map/ppermute | solution.py:205
  129.2 0.1 add_convert_fusion.5
  129.3 1.9 %collective-permute-start.11 = (bf16[6,128,128]{2,1,0:T(8,128)(2,1)S(1)}, bf16[6,128,128]{2,1,0:T(8,128)(2,1)S(1)}, u32[]{:S(2)}, u32[]{:S(2)}) collective-permute-start(bf16[6,128,128]{2,1,0:T(8,128)(2,1)S(1)} %add_convert_fusion.5), channel_id=1, source_target_pairs={{1,17},{9,25},{16,0},{17,33},{24,8},{25,41},{32,16},{33,49},{40,24... | collective-permute-start | bytes 589832 | tf_op jit(solution)/shard_map/ppermute | solution.py:205
  131.2 0.1 add_convert_fusion.2
  131.3 4.8 %collective-permute-start.15 = (bf16[6,128,128]{2,1,0:T(8,128)(2,1)S(1)}, bf16[6,128,128]{2,1,0:T(8,128)(2,1)S(1)}, u32[]{:S(2)}, u32[]{:S(2)}) collective-permute-start(bf16[6,128,128]{2,1,0:T(8,128)(2,1)S(1)} %add_convert_fusion.2), channel_id=1, source_target_pairs={{0,16},{8,24},{16,32},{17,1},{24,40},{25,9},{32,48},{33,17},{40,56... | collective-permute-start | bytes 589832 | tf_op jit(solution)/shard_map/ppermute | solution.py:205
  136.1 4.2 %collective-permute-done.11 = bf16[6,128,128]{2,1,0:T(8,128)(2,1)S(1)} collective-permute-done((bf16[6,128,128]{2,1,0:T(8,128)(2,1)S(1)}, bf16[6,128,128]{2,1,0:T(8,128)(2,1)S(1)}, u32[]{:S(2)}, u32[]{:S(2)}) %collective-permute-start.11) | collective-permute-done | bytes 196640 | tf_op jit(solution)/shard_map/ppermute | solution.py:205
  140.3 7.4 %collective-permute-start.12 = (bf16[6,128,128]{2,1,0:T(8,128)(2,1)S(1)}, bf16[6,128,128]{2,1,0:T(8,128)(2,1)S(1)}, u32[]{:S(2)}, u32[]{:S(2)}) collective-permute-start(bf16[6,128,128]{2,1,0:T(8,128)(2,1)S(1)} %add_convert_fusion.4), channel_id=1, source_target_pairs={{1,9},{8,0},{9,17},{16,8},{17,25},{24,16},{25,33},{32,24},{33,41},... | collective-permute-start | bytes 589832 | tf_op jit(solution)/shard_map/ppermute | solution.py:205
  147.8 0.1 add_convert_fusion.1
  147.8 1.9 %collective-permute-start.16 = (bf16[6,128,128]{2,1,0:T(8,128)(2,1)S(1)}, bf16[6,128,128]{2,1,0:T(8,128)(2,1)S(1)}, u32[]{:S(2)}, u32[]{:S(2)}) collective-permute-start(bf16[6,128,128]{2,1,0:T(8,128)(2,1)S(1)} %add_convert_fusion.1), channel_id=1, source_target_pairs={{0,8},{8,16},{9,1},{16,24},{17,9},{24,32},{25,17},{32,40},{33,25},... | collective-permute-start | bytes 589832 | tf_op jit(solution)/shard_map/ppermute | solution.py:205
  149.7 2.0 %collective-permute-done.12 = bf16[6,128,128]{2,1,0:T(8,128)(2,1)S(1)} collective-permute-done((bf16[6,128,128]{2,1,0:T(8,128)(2,1)S(1)}, bf16[6,128,128]{2,1,0:T(8,128)(2,1)S(1)}, u32[]{:S(2)}, u32[]{:S(2)}) %collective-permute-start.12) | collective-permute-done | bytes 196640 | tf_op jit(solution)/shard_map/ppermute | solution.py:205
  151.8 6.5 %collective-permute-start.13 = (bf16[6,128,128]{2,1,0:T(8,128)(2,1)S(1)}, bf16[6,128,128]{2,1,0:T(8,128)(2,1)S(1)}, u32[]{:S(2)}, u32[]{:S(2)}) collective-permute-start(bf16[6,128,128]{2,1,0:T(8,128)(2,1)S(1)} %add_convert_fusion.3), channel_id=1, source_target_pairs={{1,9},{8,0},{9,17},{16,8},{17,25},{24,16},{25,33},{32,24},{33,41},... | collective-permute-start | bytes 589832 | tf_op jit(solution)/shard_map/ppermute | solution.py:205
  158.3 0.1 add_convert_fusion
  158.4 1.9 %collective-permute-start.17 = (bf16[6,128,128]{2,1,0:T(8,128)(2,1)S(1)}, bf16[6,128,128]{2,1,0:T(8,128)(2,1)S(1)}, u32[]{:S(2)}, u32[]{:S(2)}) collective-permute-start(bf16[6,128,128]{2,1,0:T(8,128)(2,1)S(1)} %add_convert_fusion), channel_id=1, source_target_pairs={{0,8},{8,16},{9,1},{16,24},{17,9},{24,32},{25,17},{32,40},{33,25},... | collective-permute-start | bytes 589832 | tf_op jit(solution)/shard_map/ppermute | solution.py:205
  160.4 1.1 collective-permute-done.13.refs_1_
  161.5 6.6 %collective-permute-done.17.refs_2_ = bf16[6,128,128]{2,1,0:T(8,128)(2,1)S(1)} collective-permute-done((bf16[6,128,128]{2,1,0:T(8,128)(2,1)S(1)}, bf16[6,128,128]{2,1,0:T(8,128)(2,1)S(1)}, u32[]{:S(2)}, u32[]{:S(2)}) %collective-permute-start.17) | collective-permute-done | bytes 196640 | tf_op jit(solution)/shard_map/ppermute | solution.py:205
  168.1 0.9 terms.1
  169.0 2.4 %psum.30 = f32[8,128]{1,0:T(8,128)S(1)} all-reduce(f32[8,128]{1,0:T(8,128)S(1)} %get-tuple-element.37), channel_id=1, replica_groups=mesh['x'=4,'z'=16,'y'=4,'c'=2] {'c'}, use_global_device_ids=true, to_apply=%region_2.0 | all-reduce | flops 1024 | bytes 8192 | tf_op jit(solution)/shard_map/psum | solution.py:290
  171.4 10.1 %psum.31.terms_ref = f32[8,128]{1,0:T(8,128)S(1)} all-reduce(f32[8,128]{1,0:T(8,128)S(1)} %psum.30), channel_id=1, replica_groups=mesh['x'=4,'z'=16,'y'=4,'c'=2] {'y'}, use_global_device_ids=true, to_apply=%region_3.0 | all-reduce | flops 1024 | bytes 8192 | tf_op jit(solution)/shard_map/psum | solution.py:290
  181.5 0.9 final.1
  (30 shorter events, 0.3 us)
Async XLA Ops:
  7.2 58.9 %all-gather.3.cloned.1.call-start = ((), (), s32[]{:S(2)}) async-start(), calls=%async_computation | async-start | bytes 1310720 | tf_op jit(solution)/shard_map/all_gather | solution.py:242
  9.0 0.9 copy-start.2
  9.0 0.9 copy-start.4
  10.0 56.1 %copy-start.1 = (bf16[128,3,128]{2,0,1:T(8,128)(2,1)S(1)}, bf16[128,3,128]{2,0,1:T(8,128)(2,1)}, u32[]{:S(2)}) copy-start(bf16[128,3,128]{2,0,1:T(8,128)(2,1)} %param.7) | copy-start | bytes 294916
  10.0 16.0 %collective-permute-start.1 = (bf16[6,128,128]{2,1,0:T(8,128)(2,1)S(1)}, bf16[6,128,128]{2,1,0:T(8,128)(2,1)S(1)}, u32[]{:S(2)}, u32[]{:S(2)}) collective-permute-start(bf16[6,128,128]{2,1,0:T(8,128)(2,1)S(1)} %pad_maximum_fusion.refs_0_), channel_id=1, source_target_pairs={{1,9},{8,0},{9,17},{16,8},{17,25},{24,16},{25,33},{32,24},{33,41},... | collective-permute-start | bytes 589832 | tf_op jit(solution)/shard_map/ppermute | solution.py:205
  21.5 11.0 %collective-permute-start = (bf16[6,128,128]{2,1,0:T(8,128)(2,1)S(1)}, bf16[6,128,128]{2,1,0:T(8,128)(2,1)S(1)}, u32[]{:S(2)}, u32[]{:S(2)}) collective-permute-start(bf16[6,128,128]{2,1,0:T(8,128)(2,1)S(1)} %pad_maximum_fusion.refs_0_), channel_id=1, source_target_pairs={{0,8},{8,16},{9,1},{16,24},{17,9},{24,32},{25,17},{32,40},{33,25},... | collective-permute-start | bytes 589832 | tf_op jit(solution)/shard_map/ppermute | solution.py:205
  26.0 11.4 %collective-permute-start.3 = (bf16[6,128,128]{2,1,0:T(8,128)(2,1)S(1)}, bf16[6,128,128]{2,1,0:T(8,128)(2,1)S(1)}, u32[]{:S(2)}, u32[]{:S(2)}) collective-permute-start(bf16[6,128,128]{2,1,0:T(8,128)(2,1)S(1)} %collective-permute-done.1.refs_2_), channel_id=1, source_target_pairs={{1,9},{8,0},{9,17},{16,8},{17,25},{24,16},{25,33},{32,24},{33,41},... | collective-permute-start | bytes 589832 | tf_op jit(solution)/shard_map/ppermute | solution.py:205
  32.5 11.9 %collective-permute-start.2 = (bf16[6,128,128]{2,1,0:T(8,128)(2,1)S(1)}, bf16[6,128,128]{2,1,0:T(8,128)(2,1)S(1)}, u32[]{:S(2)}, u32[]{:S(2)}) collective-permute-start(bf16[6,128,128]{2,1,0:T(8,128)(2,1)S(1)} %collective-permute-done.refs_1_), channel_id=1, source_target_pairs={{0,8},{8,16},{9,1},{16,24},{17,9},{24,32},{25,17},{32,40},{33,25},... | collective-permute-start | bytes 589832 | tf_op jit(solution)/shard_map/ppermute | solution.py:205
  37.4 12.4 %collective-permute-start.5 = (bf16[6,128,128]{2,1,0:T(8,128)(2,1)S(1)}, bf16[6,128,128]{2,1,0:T(8,128)(2,1)S(1)}, u32[]{:S(2)}, u32[]{:S(2)}) collective-permute-start(bf16[6,128,128]{2,1,0:T(8,128)(2,1)S(1)} %collective-permute-done.3.refs_4_), channel_id=1, source_target_pairs={{1,17},{9,25},{16,0},{17,33},{24,8},{25,41},{32,16},{33,49},{40,24... | collective-permute-start | bytes 589832 | tf_op jit(solution)/shard_map/ppermute | solution.py:205
  44.4 19.7 %collective-permute-start.4 = (bf16[6,128,128]{2,1,0:T(8,128)(2,1)S(1)}, bf16[6,128,128]{2,1,0:T(8,128)(2,1)S(1)}, u32[]{:S(2)}, u32[]{:S(2)}) collective-permute-start(bf16[6,128,128]{2,1,0:T(8,128)(2,1)S(1)} %collective-permute-done.2.refs_3_), channel_id=1, source_target_pairs={{0,16},{8,24},{16,32},{17,1},{24,40},{25,9},{32,48},{33,17},{40,56... | collective-permute-start | bytes 589832 | tf_op jit(solution)/shard_map/ppermute | solution.py:205
  49.9 40.0 %collective-permute-start.9 = (bf16[6,128,128]{2,1,0:T(8,128)(2,1)S(1)}, bf16[6,128,128]{2,1,0:T(8,128)(2,1)S(1)}, u32[]{:S(2)}, u32[]{:S(2)}) collective-permute-start(bf16[6,128,128]{2,1,0:T(8,128)(2,1)S(1)} %collective-permute-done.5.refs_6_), channel_id=1, source_target_pairs={{1,33},{9,41},{17,49},{25,57},{32,0},{33,65},{40,8},{41,73},{48,16... | collective-permute-start | bytes 589832 | tf_op jit(solution)/shard_map/ppermute | solution.py:205
  64.1 25.7 %collective-permute-start.8 = (bf16[6,128,128]{2,1,0:T(8,128)(2,1)S(1)}, bf16[6,128,128]{2,1,0:T(8,128)(2,1)S(1)}, u32[]{:S(2)}, u32[]{:S(2)}) collective-permute-start(bf16[6,128,128]{2,1,0:T(8,128)(2,1)S(1)} %collective-permute-done.4.refs_5_), channel_id=1, source_target_pairs={{0,32},{8,40},{16,48},{24,56},{32,64},{33,1},{40,72},{41,9},{48,80... | collective-permute-start | bytes 589832 | tf_op jit(solution)/shard_map/ppermute | solution.py:205
  66.1 1.2 copy-start
  67.3 30.9 %copy-start.3 = (bf16[128,3,128]{2,0,1:T(8,128)(2,1)S(1)}, bf16[128,3,128]{2,0,1:T(8,128)(2,1)}, u32[]{:S(2)}) copy-start(bf16[128,3,128]{2,0,1:T(8,128)(2,1)} %param.10) | copy-start | bytes 294916
  70.3 19.5 %copy-start.5 = (f32[3,128]{1,0:T(4,128)S(1)}, f32[3,128]{1,0:T(4,128)}, u32[]{:S(2)}) copy-start(f32[3,128]{1,0:T(4,128)} %param.12) | copy-start | bytes 4612
  70.3 19.5 %copy-start.6 = (f32[3,128]{1,0:T(4,128)S(1)}, f32[3,128]{1,0:T(4,128)}, u32[]{:S(2)}) copy-start(f32[3,128]{1,0:T(4,128)} %param.11) | copy-start | bytes 4612
  79.1 10.7 %collective-permute-start.7 = (f32[16,128]{1,0:T(8,128)S(1)}, f32[16,128]{1,0:T(8,128)S(1)}, u32[]{:S(2)}, u32[]{:S(2)}) collective-permute-start(f32[16,128]{1,0:T(8,128)S(1)} %psum.29.sums_ref), channel_id=1, source_target_pairs={{1,33},{9,41},{17,49},{25,57},{32,0},{33,65},{40,8},{41,73},{48,16... | collective-permute-start | bytes 24584 | tf_op jit(solution)/shard_map/ppermute | solution.py:205
  87.9 10.4 %collective-permute-start.6 = (f32[16,128]{1,0:T(8,128)S(1)}, f32[16,128]{1,0:T(8,128)S(1)}, u32[]{:S(2)}, u32[]{:S(2)}) collective-permute-start(f32[16,128]{1,0:T(8,128)S(1)} %psum.29.sums_ref), channel_id=1, source_target_pairs={{0,32},{8,40},{16,48},{24,56},{32,64},{33,1},{40,72},{41,9},{48,80... | collective-permute-start | bytes 24584 | tf_op jit(solution)/shard_map/ppermute | solution.py:205
  109.3 19.9 %collective-permute-start.10 = (bf16[6,128,128]{2,1,0:T(8,128)(2,1)S(1)}, bf16[6,128,128]{2,1,0:T(8,128)(2,1)S(1)}, u32[]{:S(2)}, u32[]{:S(2)}) collective-permute-start(bf16[6,128,128]{2,1,0:T(8,128)(2,1)S(1)} %get-tuple-element.26), channel_id=1, source_target_pairs={{1,33},{9,41},{17,49},{25,57},{32,0},{33,65},{40,8},{41,73},{48,16... | collective-permute-start | bytes 589832 | tf_op jit(solution)/shard_map/ppermute | solution.py:205
  111.2 20.0 %collective-permute-start.14 = (bf16[6,128,128]{2,1,0:T(8,128)(2,1)S(1)}, bf16[6,128,128]{2,1,0:T(8,128)(2,1)S(1)}, u32[]{:S(2)}, u32[]{:S(2)}) collective-permute-start(bf16[6,128,128]{2,1,0:T(8,128)(2,1)S(1)} %get-tuple-element.30), channel_id=1, source_target_pairs={{0,32},{8,40},{16,48},{24,56},{32,64},{33,1},{40,72},{41,9},{48,80... | collective-permute-start | bytes 589832 | tf_op jit(solution)/shard_map/ppermute | solution.py:205
  119.1 41.3 %collective-permute-start.18 = (bf16[6,128,128]{2,1,0:T(8,128)(2,1)S(1)}, bf16[6,128,128]{2,1,0:T(8,128)(2,1)S(1)}, u32[]{:S(2)}, u32[]{:S(2)}) collective-permute-start(bf16[6,128,128]{2,1,0:T(8,128)(2,1)S(1)} %get-tuple-element.34), channel_id=1, source_target_pairs={{1,129},{9,137},{17,145},{25,153},{33,161},{41,169},{49,177},{57,1... | collective-permute-start | bytes 589832 | tf_op jit(solution)/shard_map/ppermute | solution.py:205
  121.5 38.8 %collective-permute-start.19 = (bf16[6,128,128]{2,1,0:T(8,128)(2,1)S(1)}, bf16[6,128,128]{2,1,0:T(8,128)(2,1)S(1)}, u32[]{:S(2)}, u32[]{:S(2)}) collective-permute-start(bf16[6,128,128]{2,1,0:T(8,128)(2,1)S(1)} %get-tuple-element.35), channel_id=1, source_target_pairs={{0,128},{8,136},{16,144},{24,152},{32,160},{40,168},{48,176},{56,1... | collective-permute-start | bytes 589832 | tf_op jit(solution)/shard_map/ppermute | solution.py:205
  124.9 35.4 %collective-permute-start.20 = (bf16[6,128,128]{2,1,0:T(8,128)(2,1)S(1)}, bf16[6,128,128]{2,1,0:T(8,128)(2,1)S(1)}, u32[]{:S(2)}, u32[]{:S(2)}) collective-permute-start(bf16[6,128,128]{2,1,0:T(8,128)(2,1)S(1)} %get-tuple-element.36), channel_id=1, source_target_pairs={{0,256},{8,264},{16,272},{24,280},{32,288},{40,296},{48,304},{56,3... | collective-permute-start | bytes 589832 | tf_op jit(solution)/shard_map/ppermute | solution.py:274
  129.3 11.0 %collective-permute-start.11 = (bf16[6,128,128]{2,1,0:T(8,128)(2,1)S(1)}, bf16[6,128,128]{2,1,0:T(8,128)(2,1)S(1)}, u32[]{:S(2)}, u32[]{:S(2)}) collective-permute-start(bf16[6,128,128]{2,1,0:T(8,128)(2,1)S(1)} %add_convert_fusion.5), channel_id=1, source_target_pairs={{1,17},{9,25},{16,0},{17,33},{24,8},{25,41},{32,16},{33,49},{40,24... | collective-permute-start | bytes 589832 | tf_op jit(solution)/shard_map/ppermute | solution.py:205
  131.3 16.5 %collective-permute-start.15 = (bf16[6,128,128]{2,1,0:T(8,128)(2,1)S(1)}, bf16[6,128,128]{2,1,0:T(8,128)(2,1)S(1)}, u32[]{:S(2)}, u32[]{:S(2)}) collective-permute-start(bf16[6,128,128]{2,1,0:T(8,128)(2,1)S(1)} %add_convert_fusion.2), channel_id=1, source_target_pairs={{0,16},{8,24},{16,32},{17,1},{24,40},{25,9},{32,48},{33,17},{40,56... | collective-permute-start | bytes 589832 | tf_op jit(solution)/shard_map/ppermute | solution.py:205
  140.3 11.4 %collective-permute-start.12 = (bf16[6,128,128]{2,1,0:T(8,128)(2,1)S(1)}, bf16[6,128,128]{2,1,0:T(8,128)(2,1)S(1)}, u32[]{:S(2)}, u32[]{:S(2)}) collective-permute-start(bf16[6,128,128]{2,1,0:T(8,128)(2,1)S(1)} %add_convert_fusion.4), channel_id=1, source_target_pairs={{1,9},{8,0},{9,17},{16,8},{17,25},{24,16},{25,33},{32,24},{33,41},... | collective-permute-start | bytes 589832 | tf_op jit(solution)/shard_map/ppermute | solution.py:205
  147.8 10.5 %collective-permute-start.16 = (bf16[6,128,128]{2,1,0:T(8,128)(2,1)S(1)}, bf16[6,128,128]{2,1,0:T(8,128)(2,1)S(1)}, u32[]{:S(2)}, u32[]{:S(2)}) collective-permute-start(bf16[6,128,128]{2,1,0:T(8,128)(2,1)S(1)} %add_convert_fusion.1), channel_id=1, source_target_pairs={{0,8},{8,16},{9,1},{16,24},{17,9},{24,32},{25,17},{32,40},{33,25},... | collective-permute-start | bytes 589832 | tf_op jit(solution)/shard_map/ppermute | solution.py:205
  151.8 9.7 %collective-permute-start.13 = (bf16[6,128,128]{2,1,0:T(8,128)(2,1)S(1)}, bf16[6,128,128]{2,1,0:T(8,128)(2,1)S(1)}, u32[]{:S(2)}, u32[]{:S(2)}) collective-permute-start(bf16[6,128,128]{2,1,0:T(8,128)(2,1)S(1)} %add_convert_fusion.3), channel_id=1, source_target_pairs={{1,9},{8,0},{9,17},{16,8},{17,25},{24,16},{25,33},{32,24},{33,41},... | collective-permute-start | bytes 589832 | tf_op jit(solution)/shard_map/ppermute | solution.py:205
  158.4 9.7 %collective-permute-start.17 = (bf16[6,128,128]{2,1,0:T(8,128)(2,1)S(1)}, bf16[6,128,128]{2,1,0:T(8,128)(2,1)S(1)}, u32[]{:S(2)}, u32[]{:S(2)}) collective-permute-start(bf16[6,128,128]{2,1,0:T(8,128)(2,1)S(1)} %add_convert_fusion), channel_id=1, source_target_pairs={{0,8},{8,16},{9,1},{16,24},{17,9},{24,32},{25,17},{32,40},{33,25},... | collective-permute-start | bytes 589832 | tf_op jit(solution)/shard_map/ppermute | solution.py:205
Sparse Core Ops, SparseCore 0:
  10.1 38.6 all-gather.2

commit v6 on v5

v6 whole, which is shorter than its diff:
```python
import functools

import jax
import jax.numpy as jnp
from jax import lax
from jax.experimental import pallas as pl
from jax.experimental.pallas import tpu as pltpu
from jax.sharding import Mesh, PartitionSpec as P

TILE = 128
EPS = 1e-06
NEAR = (0, -1, 1, -2, 2, -4, 4, -8, 8)
FAR = 3
NT = (((1,), (1,)), ((), ()))
NN = (((1,), (0,)), ((), ()))
TN = (((0,), (0,)), ((), ()))
F32 = jnp.float32
BF16 = jnp.bfloat16
VMEM_LIMIT = 48 * 1024 * 1024


def dot(left, right, dims):
    return lax.dot_general(left, right, dims, preferred_element_type=F32)


def row_sums(square):
    ones = jnp.ones((8, TILE), BF16)
    high = square.astype(BF16)
    low = (square - high.astype(F32)).astype(BF16)
    return dot(ones, high, NT) + dot(ones, low, NT)


def columns(rows):
    fill = jnp.zeros((TILE - rows.shape[0], TILE), F32)
    return jnp.transpose(jnp.concatenate([rows, fill], axis=0))


def own_frame():
    return lax.axis_index("x") * lax.axis_size("z") + lax.axis_index("z")


def mirrored(value):
    return value * (1 - 2 * lax.axis_index("c"))


def inside(place):
    line, lines = lax.axis_size("z"), lax.axis_size("x")
    near = len(NEAR)
    if place == 0 or place == near + FAR - 1:
        return None
    offset = NEAR[place] if place < near else (-line, line)[place - near]
    at = own_frame() + mirrored(offset)
    return (at >= 0) & (at < line * lines)


def squares_kernel(heads, q_ref, k_ref, out_ref):
    out_ref[...] = jnp.zeros(out_ref.shape, F32)
    for row, ref in enumerate((q_ref, k_ref)):
        total = jnp.zeros((TILE, TILE), F32)
        for head in range(heads):
            floats = ref[head].astype(F32)
            total = total + floats * floats
        total = row_sums(total)[0:1]
        for group in range(out_ref.shape[0]):
            out_ref[group, row : row + 1, :] = total


def group_sum(ref):
    total = ref[0]
    for group in range(1, ref.shape[0]):
        total = total + ref[group]
    return total


def norm_kernel(heads, channels, sums_ref, q_ref, k_ref, v_ref, gain_ref, qn_ref, kv_ref, inverse_ref):
    inverse = lax.rsqrt(group_sum(sums_ref) / channels + EPS)
    inverse_ref[...] = inverse
    turned = columns(inverse)
    for head in range(heads):
        qn_ref[head] = (
            q_ref[head].astype(F32) * turned[:, 0:1] * gain_ref[head : head + 1]
        ).astype(BF16)
        kv_ref[head] = (
            k_ref[head].astype(F32) * turned[:, 1:2] * gain_ref[heads + head : heads + head + 1]
        ).astype(BF16)
        kv_ref[heads + head] = v_ref[head]


def attention_kernel(heads, q_ref, do_ref, *refs):
    count = len(NEAR) + FAR
    tiles = refs[:count]
    out_ref, dq_ref = refs[count : count + 2]
    part_refs = refs[count + 2 : -1]
    work_ref = refs[-1]
    scale = TILE ** (-0.5)
    usable = [inside(t) for t in range(count)]
    tops, shares, deltas = [], [], []
    for head in range(heads):
        top = jnp.full((TILE, TILE), -1e30, F32)
        for t in range(count):
            score = dot(q_ref[head], tiles[t][head], NT) * scale
            if usable[t] is not None:
                score = jnp.where(usable[t], score, -1e30)
            work_ref[head, t] = score
            top = jnp.maximum(top, score)
        tops.append(jnp.max(top, axis=1, keepdims=True))
    for head in range(heads):
        total = jnp.zeros((TILE, TILE), F32)
        for t in range(count):
            weight = jnp.exp(work_ref[head, t] - tops[head])
            work_ref[head, t] = weight
            total = total + weight
        shares.append(1.0 / jnp.sum(total, axis=1, keepdims=True))
    for head in range(heads):
        upstream = do_ref[head]
        out = jnp.zeros((TILE, TILE), F32)
        for t in range(count):
            prob = work_ref[head, t] * shares[head]
            work_ref[head, t] = prob
            prob = prob.astype(BF16)
            out = out + dot(prob, tiles[t][heads + head], NN)
            part = part_refs[t]
            part[heads + head] = dot(prob, upstream, TN).astype(part.dtype)
        out = out.astype(BF16)
        out_ref[head] = out
        deltas.append(jnp.sum(upstream.astype(F32) * out.astype(F32), axis=1, keepdims=True))
    for head in range(heads):
        query, upstream = q_ref[head], do_ref[head]
        query_grad = jnp.zeros((TILE, TILE), F32)
        for t in range(count):
            dprob = dot(upstream, tiles[t][heads + head], NT)
            dscore = (work_ref[head, t] * (dprob - deltas[head])).astype(BF16)
            query_grad = query_grad + dot(dscore, tiles[t][head], NN)
            part = part_refs[t]
            part[head] = (dot(dscore, query, TN) * scale).astype(part.dtype)
        dq_ref[head] = query_grad * scale


def terms_kernel(heads, q_ref, k_ref, dq_ref, gain_ref, *refs):
    parts, (dk_ref, dv_ref, terms_ref) = refs[:-3], refs[-3:]
    query_total = jnp.zeros((TILE, TILE), F32)
    key_total = jnp.zeros((TILE, TILE), F32)
    for head in range(heads):
        key_grad, value_grad = parts[0][head], parts[0][heads + head]
        for part in parts[1:]:
            key_grad = key_grad + part[head].astype(F32)
            value_grad = value_grad + part[heads + head].astype(F32)
        dk_ref[head] = key_grad
        dv_ref[head] = value_grad.astype(BF16)
        query_total = query_total + q_ref[head].astype(F32) * (
            dq_ref[head] * gain_ref[head : head + 1]
        )
        key_total = key_total + k_ref[head].astype(F32) * (
            key_grad * gain_ref[heads + head : heads + head + 1]
        )
    terms_ref[...] = jnp.zeros(terms_ref.shape, F32)
    for row, total in enumerate((query_total, key_total)):
        total = row_sums(total)[0:1]
        for group in range(terms_ref.shape[0]):
            terms_ref[group, row : row + 1, :] = total


def final_kernel(
    heads, channels, inverse_ref, terms_ref, q_ref, k_ref, dq_ref, dk_ref, gain_ref, gq_ref, gk_ref
):
    inverse = inverse_ref[0:2]
    cubes = inverse * inverse * inverse * group_sum(terms_ref)[0:2] / channels
    turned = columns(jnp.concatenate([inverse, cubes], axis=0))
    for head in range(heads):
        gq_ref[head] = (
            turned[:, 0:1] * (gain_ref[head : head + 1] * dq_ref[head])
            - q_ref[head].astype(F32) * turned[:, 2:3]
        ).astype(BF16)
        gk_ref[head] = (
            turned[:, 1:2] * (gain_ref[heads + head : heads + head + 1] * dk_ref[head])
            - k_ref[head].astype(F32) * turned[:, 3:4]
        ).astype(BF16)


SEQ, HEAD = ("x", "z"), ("y", "c")


def passed(value, steps):
    count = lax.axis_size("x") * lax.axis_size("z")
    pairs = [
        (2 * i + core, 2 * (i + way * steps) + core)
        for i in range(count)
        for core, way in enumerate((1, -1))
        if 0 <= i + way * steps < count
    ]
    return lax.ppermute(value, SEQ + ("c",), pairs)


def half_round(value):
    count = lax.axis_size("x") * lax.axis_size("z")
    return lax.ppermute(value, SEQ, [(i, (i + count // 2) % count) for i in range(count)])


def relay(offset):
    return int(offset / 2) if abs(offset) > 2 else 0


def spread(value):
    got = {0: value}
    for offset in NEAR[1:]:
        got[offset] = passed(got[relay(offset)], relay(offset) - offset)
    return [got[offset] for offset in NEAR]


def collect(parts):
    arrived = [passed(parts[place], NEAR[place]) for place in (1, 2)]
    for place in (len(NEAR) - 2, len(NEAR) - 1):
        carried = parts[place]
        while place > 2:
            offset = NEAR[place]
            carried = passed(carried, offset - relay(offset))
            place = place - 2
            if relay(offset):
                carried = (carried.astype(F32) + parts[place]).astype(BF16)
            else:
                break
        arrived.append(carried)
    return arrived


def per_device(total_heads, q_raw, k_raw, values, grad_out, q_gain, k_gain, key_tiles):
    line = lax.axis_size("z")
    groups = lax.axis_size("y") * lax.axis_size("c")
    near = len(NEAR)
    count = near + FAR
    heads = q_raw.shape[1]
    channels = float(total_heads * q_raw.shape[2])
    q_raw, k_raw, values, grad_out = [
        jnp.transpose(array, (1, 0, 2)) for array in (q_raw, k_raw, values, grad_out)
    ]
    gains = jnp.concatenate([q_gain, k_gain], axis=0)
    vmem = pl.BlockSpec(memory_space=pltpu.VMEM)
    params = pltpu.CompilerParams(vmem_limit_bytes=VMEM_LIMIT)
    whole, pair = (heads, TILE, TILE), (2 * heads, TILE, TILE)

    def call(kernel, name, out_shape, *operands, scratch=()):
        return pl.pallas_call(
            kernel,
            out_shape=[jax.ShapeDtypeStruct(shape, dtype) for shape, dtype in out_shape],
            in_specs=[vmem] * len(operands),
            out_specs=[vmem] * len(out_shape),
            scratch_shapes=list(scratch),
            compiler_params=params,
            name=name,
        )(*operands)

    rows = ((groups, 8, TILE), F32)
    (squares,) = call(functools.partial(squares_kernel, heads), "squares", [rows], q_raw, k_raw)
    sums = lax.all_to_all(squares, HEAD, 0, 0, tiled=True)
    q_norm, pairs, inverse = call(
        functools.partial(norm_kernel, heads, channels),
        "norm",
        [(whole, BF16), (pair, BF16), ((8, TILE), F32)],
        sums, q_raw, k_raw, values, gains,
    )
    tiles = spread(pairs) + [passed(pairs, line), passed(pairs, -line), half_round(pairs)]
    attended, dq, *parts = call(
        functools.partial(attention_kernel, heads),
        "attention",
        [(whole, BF16), (whole, F32)] + [(pair, F32 if t == 0 or 2 < t < near - 2 else BF16) for t in range(count)],
        q_norm, grad_out, *tiles,
        scratch=[pltpu.VMEM((heads, count, TILE, TILE), F32)],
    )
    arrived = collect(parts) + [
        passed(parts[near], -line), passed(parts[near + 1], line), half_round(parts[near + 2])
    ]
    dk, grad_v, terms = call(
        functools.partial(terms_kernel, heads),
        "terms",
        [(whole, F32), (whole, BF16), rows],
        q_raw, k_raw, dq, gains, parts[0], *arrived,
    )
    terms = lax.all_to_all(terms, HEAD, 0, 0, tiled=True)
    grad_q, grad_k = call(
        functools.partial(final_kernel, heads, channels),
        "final",
        [(whole, BF16)] * 2,
        inverse, terms, q_raw, k_raw, dq, dk, gains,
    )
    return tuple(
        jnp.transpose(array, (1, 0, 2)) for array in (attended, grad_q, grad_k, grad_v)
    )


def solution(mesh):
    split = Mesh(mesh.devices.reshape(4, -1, mesh.shape["head"] // 2, 2), SEQ + HEAD)

    def whole(q_raw, k_raw, values, grad_out, q_gain, k_gain, key_tiles):
        tokens = P(SEQ, HEAD, None)
        return jax.shard_map(
            functools.partial(per_device, q_raw.shape[1]),
            mesh=split,
            in_specs=(tokens,) * 4 + (P(HEAD, None), P(HEAD, None), P()),
            out_specs=(tokens,) * 4,
            check_vma=False,
        )(q_raw, k_raw, values, grad_out, q_gain, k_gain, key_tiles)

    return whole
```

time: 190 us -> 166 us (0.87)
  the two profiles are of different devices: /device:TPU:12 before, /device:TPU:1 now
where the time goes in v6:
time: 166 us; the launch traced here: 165 us
  starting transfers between devices  80.1 us (48%)
  waiting for transfers between devices  56.6 us (34%)
  blocking collectives  12.6 us (8%)
  Pallas kernels  11.9 us (7%)
  local copies, waits for them, and re-layouts  1.81 us (1%)
    ppermute x20, waiting for transfers between devices, passed(): return lax.ppermute(value, SEQ + ('c',), pairs)  52.5 us
    ppermute x20, starting transfers between devices, passed(): return lax.ppermute(value, SEQ + ('c',), pairs)  50.3 us
    ppermute x2, starting transfers between devices, half_round(): lax.ppermute(value, SEQ, [(i, (i + count // 2) % count) for i in range(co...  19.6 us
    all_to_all x1, blocking collectives, per_device(): terms = lax.all_to_all(terms, HEAD, 0, 0, tiled=True)  12.6 us
    pallas_call x5, Pallas kernels, call(): pl.pallas_call(kernel, out_shape=[jax.ShapeDtypeStruct(shape, dtype) for...  11.9 us
    all_to_all x1, starting transfers between devices, per_device(): sums = lax.all_to_all(squares, HEAD, 0, 0, tiled=True)  10.1 us
    all_to_all x1, waiting for transfers between devices, per_device(): sums = lax.all_to_all(squares, HEAD, 0, 0, tiled=True)  4.05 us
  transfers between devices with their start and end apart: 23, of which 9 were waited for; matrix products, arithmetic and copies ran while one was open for 1% of the time, Pallas kernels for 0%

profile of v6, /device:TPU:1, one launch (start us, length us, event | category | flops | bytes accessed | tf_op | source)
XLA Modules:
  0.0 164.9 jit_solution(14576958363559872280)
XLA Ops:
  0.7 0.9 copy-done
  1.5 0.9 copy-done.2
  2.4 0.8 squares.1
  3.3 10.1 %all-to-all-start = ((f32[8,8,128]{2,1,0:T(8,128)}), f32[8,8,128]{2,1,0:T(8,128)S(1)}, u32[]{:S(2)}, u32[]{:S(2)}) async-start(f32[8,8,128]{2,1,0:T(8,128)} %squares.1), calls=%async_computation | async-start | bytes 65536 | tf_op jit(solution)/shard_map/all_to_all | solution.py:254
  13.4 0.7 pad_maximum_fusion.gain_ref
  14.1 4.0 %all-to-all-done.sums_ref = f32[8,8,128]{2,1,0:T(8,128)S(1)} async-done(((f32[8,8,128]{2,1,0:T(8,128)}), f32[8,8,128]{2,1,0:T(8,128)S(1)}, u32[]{:S(2)}, u32[]{:S(2)}) %all-to-all-start) | async-done | bytes 32800 | tf_op jit(solution)/shard_map/all_to_all | solution.py:254
  18.1 0.0 copy-start.4
  18.1 0.2 norm.1
  18.4 1.3 collective-permute-start.3
  19.7 1.3 collective-permute-start.2
  21.0 11.3 %collective-permute-start.10 = (bf16[6,128,128]{2,1,0:T(8,128)(2,1)S(1)}, bf16[6,128,128]{2,1,0:T(8,128)(2,1)S(1)}, u32[]{:S(2)}, u32[]{:S(2)}) collective-permute-start(bf16[6,128,128]{2,1,0:T(8,128)(2,1)S(1)} %get-tuple-element.27.refs_0_), channel_id=1, source_target_pairs={{0,256},{8,264},{16,272},{24,280},{32,288},{40,296},{48,304},{56,3... | collective-permute-start | bytes 589832 | tf_op jit(solution)/shard_map/ppermute | solution.py:196
  32.3 2.5 %collective-permute-start.9 = (bf16[6,128,128]{2,1,0:T(8,128)(2,1)S(1)}, bf16[6,128,128]{2,1,0:T(8,128)(2,1)S(1)}, u32[]{:S(2)}, u32[]{:S(2)}) collective-permute-start(bf16[6,128,128]{2,1,0:T(8,128)(2,1)S(1)} %get-tuple-element.27.refs_0_), channel_id=1, source_target_pairs={{1,129},{9,137},{17,145},{25,153},{33,161},{41,169},{49,177},{57,1... | collective-permute-start | bytes 589832 | tf_op jit(solution)/shard_map/ppermute | solution.py:191
  34.9 0.0 collective-permute-done.3.refs_4_
  34.9 1.3 collective-permute-start.5
  36.2 0.0 collective-permute-done.2.refs_3_
  36.2 1.3 collective-permute-start.4
  37.5 1.3 collective-permute-start.8
  38.8 0.0 collective-permute-done.10.refs_11_
  38.8 2.7 %collective-permute-start.1 = (bf16[6,128,128]{2,1,0:T(8,128)(2,1)S(1)}, bf16[6,128,128]{2,1,0:T(8,128)(2,1)S(1)}, u32[]{:S(2)}, u32[]{:S(2)}) collective-permute-start(bf16[6,128,128]{2,1,0:T(8,128)(2,1)S(1)} %get-tuple-element.27.refs_0_), channel_id=1, source_target_pairs={{1,9},{8,0},{9,17},{16,8},{17,25},{24,16},{25,33},{32,24},{33,41},... | collective-permute-start | bytes 589832 | tf_op jit(solution)/shard_map/ppermute | solution.py:191
  41.5 1.9 %collective-permute-done.9.refs_10_ = bf16[6,128,128]{2,1,0:T(8,128)(2,1)S(1)} collective-permute-done((bf16[6,128,128]{2,1,0:T(8,128)(2,1)S(1)}, bf16[6,128,128]{2,1,0:T(8,128)(2,1)S(1)}, u32[]{:S(2)}, u32[]{:S(2)}) %collective-permute-start.9) | collective-permute-done | bytes 196640 | tf_op jit(solution)/shard_map/ppermute | solution.py:191
  43.4 1.3 collective-permute-start
  44.7 0.0 collective-permute-done.5.refs_6_
  44.7 8.0 %collective-permute-start.7 = (bf16[6,128,128]{2,1,0:T(8,128)(2,1)S(1)}, bf16[6,128,128]{2,1,0:T(8,128)(2,1)S(1)}, u32[]{:S(2)}, u32[]{:S(2)}) collective-permute-start(bf16[6,128,128]{2,1,0:T(8,128)(2,1)S(1)} %collective-permute-done.5.refs_6_), channel_id=1, source_target_pairs={{1,33},{9,41},{17,49},{25,57},{32,0},{33,65},{40,8},{41,73},{48,16... | collective-permute-start | bytes 589832 | tf_op jit(solution)/shard_map/ppermute | solution.py:191
  52.7 1.3 collective-permute-start.6
  54.0 7.6 %collective-permute-done.7.refs_8_ = bf16[6,128,128]{2,1,0:T(8,128)(2,1)S(1)} collective-permute-done((bf16[6,128,128]{2,1,0:T(8,128)(2,1)S(1)}, bf16[6,128,128]{2,1,0:T(8,128)(2,1)S(1)}, u32[]{:S(2)}, u32[]{:S(2)}) %collective-permute-start.7) | collective-permute-done | bytes 196640 | tf_op jit(solution)/shard_map/ppermute | solution.py:191
  61.6 16.8 %collective-permute-done.6.refs_7_ = bf16[6,128,128]{2,1,0:T(8,128)(2,1)S(1)} collective-permute-done((bf16[6,128,128]{2,1,0:T(8,128)(2,1)S(1)}, bf16[6,128,128]{2,1,0:T(8,128)(2,1)S(1)}, u32[]{:S(2)}, u32[]{:S(2)}) %collective-permute-start.6) | collective-permute-done | bytes 196640 | tf_op jit(solution)/shard_map/ppermute | solution.py:191
  78.4 9.0 %attention.1 = (bf16[3,128,128]{2,1,0:T(8,128)(2,1)}, f32[3,128,128]{2,1,0:T(8,128)S(1)}, f32[6,128,128]{2,1,0:T(8,128)S(1)}, bf16[6,128,128]{2,1,0:T(8,128)(2,1...) custom-call(bf16[3,128,128]{2,1,0:T(8,128)(2,1)S(1)} %get-tuple-elem, ...), custom_call_target="tpu_custom_call" | custom-call | tf_op jit(solution)/shard_map/attention/pallas_call | solution.py:242
  87.4 3.2 %collective-permute-start.13 = (bf16[6,128,128]{2,1,0:T(8,128)(2,1)S(1)}, bf16[6,128,128]{2,1,0:T(8,128)(2,1)S(1)}, u32[]{:S(2)}, u32[]{:S(2)}) collective-permute-start(bf16[6,128,128]{2,1,0:T(8,128)(2,1)S(1)} %get-tuple-element.34), channel_id=1, source_target_pairs={{1,33},{9,41},{17,49},{25,57},{32,0},{33,65},{40,8},{41,73},{48,16... | collective-permute-start | bytes 589832 | tf_op jit(solution)/shard_map/ppermute | solution.py:191
  90.6 1.3 collective-permute-start.11
  91.9 1.3 collective-permute-start.12
  93.2 1.3 collective-permute-start.16
  94.5 13.7 %collective-permute-start.19 = (bf16[6,128,128]{2,1,0:T(8,128)(2,1)S(1)}, bf16[6,128,128]{2,1,0:T(8,128)(2,1)S(1)}, u32[]{:S(2)}, u32[]{:S(2)}) collective-permute-start(bf16[6,128,128]{2,1,0:T(8,128)(2,1)S(1)} %get-tuple-element.40), channel_id=1, source_target_pairs={{1,129},{9,137},{17,145},{25,153},{33,161},{41,169},{49,177},{57,1... | collective-permute-start | bytes 589832 | tf_op jit(solution)/shard_map/ppermute | solution.py:191
  108.3 1.3 collective-permute-start.20
  109.6 3.5 %collective-permute-done.16 = bf16[6,128,128]{2,1,0:T(8,128)(2,1)S(1)} collective-permute-done((bf16[6,128,128]{2,1,0:T(8,128)(2,1)S(1)}, bf16[6,128,128]{2,1,0:T(8,128)(2,1)S(1)}, u32[]{:S(2)}, u32[]{:S(2)}) %collective-permute-start.16) | collective-permute-done | bytes 196640 | tf_op jit(solution)/shard_map/ppermute | solution.py:191
  113.1 1.3 collective-permute-start.14
  114.4 0.1 add_convert_fusion.1
  114.5 2.6 %collective-permute-done.14 = bf16[6,128,128]{2,1,0:T(8,128)(2,1)S(1)} collective-permute-done((bf16[6,128,128]{2,1,0:T(8,128)(2,1)S(1)}, bf16[6,128,128]{2,1,0:T(8,128)(2,1)S(1)}, u32[]{:S(2)}, u32[]{:S(2)}) %collective-permute-start.14) | collective-permute-done | bytes 196640 | tf_op jit(solution)/shard_map/ppermute | solution.py:191
  117.1 1.3 collective-permute-start.17
  118.4 11.6 %collective-permute-done.17 = bf16[6,128,128]{2,1,0:T(8,128)(2,1)S(1)} collective-permute-done((bf16[6,128,128]{2,1,0:T(8,128)(2,1)S(1)}, bf16[6,128,128]{2,1,0:T(8,128)(2,1)S(1)}, u32[]{:S(2)}, u32[]{:S(2)}) %collective-permute-start.17) | collective-permute-done | bytes 196640 | tf_op jit(solution)/shard_map/ppermute | solution.py:191
  130.0 8.3 %collective-permute-start.21 = (bf16[6,128,128]{2,1,0:T(8,128)(2,1)S(1)}, bf16[6,128,128]{2,1,0:T(8,128)(2,1)S(1)}, u32[]{:S(2)}, u32[]{:S(2)}) collective-permute-start(bf16[6,128,128]{2,1,0:T(8,128)(2,1)S(1)} %get-tuple-element.42), channel_id=1, source_target_pairs={{0,256},{8,264},{16,272},{24,280},{32,288},{40,296},{48,304},{56,3... | collective-permute-start | bytes 589832 | tf_op jit(solution)/shard_map/ppermute | solution.py:196
  138.3 0.1 add_convert_fusion
  138.4 2.1 %collective-permute-start.15 = (bf16[6,128,128]{2,1,0:T(8,128)(2,1)S(1)}, bf16[6,128,128]{2,1,0:T(8,128)(2,1)S(1)}, u32[]{:S(2)}, u32[]{:S(2)}) collective-permute-start(bf16[6,128,128]{2,1,0:T(8,128)(2,1)S(1)} %add_convert_fusion.2), channel_id=1, source_target_pairs={{1,17},{9,25},{16,0},{17,33},{24,8},{25,41},{32,16},{33,49},{40,24... | collective-permute-start | bytes 589832 | tf_op jit(solution)/shard_map/ppermute | solution.py:191
  140.5 1.3 collective-permute-start.18
  141.8 1.3 collective-permute-done.15.refs_3_
  143.1 7.3 %collective-permute-done.18.refs_4_ = bf16[6,128,128]{2,1,0:T(8,128)(2,1)S(1)} collective-permute-done((bf16[6,128,128]{2,1,0:T(8,128)(2,1)S(1)}, bf16[6,128,128]{2,1,0:T(8,128)(2,1)S(1)}, u32[]{:S(2)}, u32[]{:S(2)}) %collective-permute-start.18) | collective-permute-done | bytes 196640 | tf_op jit(solution)/shard_map/ppermute | solution.py:191
  150.4 1.0 terms.1
  151.3 12.6 %all_to_all.10.terms_ref = f32[8,8,128]{2,1,0:T(8,128)S(1)} all-to-all(f32[8,8,128]{2,1,0:T(8,128)S(1)} %get-tuple-element.43), channel_id=1, replica_groups=mesh['x'=4,'z'=16,'y'=4,'c'=2] {'y','c'}, dimensions={0} | all-to-all | bytes 65536 | tf_op jit(solution)/shard_map/all_to_all | solution.py:278
  164.0 0.9 final.1
  (23 shorter events, 0.1 us)
Async XLA Ops:
  0.6 12.8 %copy-start.6 = (f32[3,128]{1,0:T(4,128)S(1)}, f32[3,128]{1,0:T(4,128)}, u32[]{:S(2)}) copy-start(f32[3,128]{1,0:T(4,128)} %param.12) | copy-start | bytes 4612
  0.6 0.9 copy-start
  1.5 0.9 copy-start.2
  2.4 15.7 %copy-start.1 = (bf16[128,3,128]{2,0,1:T(8,128)(2,1)S(1)}, bf16[128,3,128]{2,0,1:T(8,128)(2,1)}, u32[]{:S(2)}) copy-start(bf16[128,3,128]{2,0,1:T(8,128)(2,1)} %param.7) | copy-start | bytes 294916
  2.4 15.7 %copy-start.3 = (bf16[128,3,128]{2,0,1:T(8,128)(2,1)S(1)}, bf16[128,3,128]{2,0,1:T(8,128)(2,1)}, u32[]{:S(2)}) copy-start(bf16[128,3,128]{2,0,1:T(8,128)(2,1)} %param.8) | copy-start | bytes 294916
  2.4 15.7 %copy-start.5 = (bf16[128,3,128]{2,0,1:T(8,128)(2,1)S(1)}, bf16[128,3,128]{2,0,1:T(8,128)(2,1)}, u32[]{:S(2)}) copy-start(bf16[128,3,128]{2,0,1:T(8,128)(2,1)} %param.9) | copy-start | bytes 294916
  3.3 14.9 %all-to-all-start = ((f32[8,8,128]{2,1,0:T(8,128)}), f32[8,8,128]{2,1,0:T(8,128)S(1)}, u32[]{:S(2)}, u32[]{:S(2)}) async-start(f32[8,8,128]{2,1,0:T(8,128)} %squares.1), calls=%async_computation | async-start | bytes 65536 | tf_op jit(solution)/shard_map/all_to_all | solution.py:254
  18.1 60.3 %copy-start.4 = (bf16[128,3,128]{2,0,1:T(8,128)(2,1)S(1)}, bf16[128,3,128]{2,0,1:T(8,128)(2,1)}, u32[]{:S(2)}) copy-start(bf16[128,3,128]{2,0,1:T(8,128)(2,1)} %param.10) | copy-start | bytes 294916
  18.4 16.5 %collective-permute-start.3 = (bf16[6,128,128]{2,1,0:T(8,128)(2,1)S(1)}, bf16[6,128,128]{2,1,0:T(8,128)(2,1)S(1)}, u32[]{:S(2)}, u32[]{:S(2)}) collective-permute-start(bf16[6,128,128]{2,1,0:T(8,128)(2,1)S(1)} %get-tuple-element.27.refs_0_), channel_id=1, source_target_pairs={{1,17},{9,25},{16,0},{17,33},{24,8},{25,41},{32,16},{33,49},{40,24... | collective-permute-start | bytes 589832 | tf_op jit(solution)/shard_map/ppermute | solution.py:191
  19.7 16.5 %collective-permute-start.2 = (bf16[6,128,128]{2,1,0:T(8,128)(2,1)S(1)}, bf16[6,128,128]{2,1,0:T(8,128)(2,1)S(1)}, u32[]{:S(2)}, u32[]{:S(2)}) collective-permute-start(bf16[6,128,128]{2,1,0:T(8,128)(2,1)S(1)} %get-tuple-element.27.refs_0_), channel_id=1, source_target_pairs={{0,16},{8,24},{16,32},{17,1},{24,40},{25,9},{32,48},{33,17},{40,56... | collective-permute-start | bytes 589832 | tf_op jit(solution)/shard_map/ppermute | solution.py:191
  21.0 17.8 %collective-permute-start.10 = (bf16[6,128,128]{2,1,0:T(8,128)(2,1)S(1)}, bf16[6,128,128]{2,1,0:T(8,128)(2,1)S(1)}, u32[]{:S(2)}, u32[]{:S(2)}) collective-permute-start(bf16[6,128,128]{2,1,0:T(8,128)(2,1)S(1)} %get-tuple-element.27.refs_0_), channel_id=1, source_target_pairs={{0,256},{8,264},{16,272},{24,280},{32,288},{40,296},{48,304},{56,3... | collective-permute-start | bytes 589832 | tf_op jit(solution)/shard_map/ppermute | solution.py:196
  32.3 11.0 %collective-permute-start.9 = (bf16[6,128,128]{2,1,0:T(8,128)(2,1)S(1)}, bf16[6,128,128]{2,1,0:T(8,128)(2,1)S(1)}, u32[]{:S(2)}, u32[]{:S(2)}) collective-permute-start(bf16[6,128,128]{2,1,0:T(8,128)(2,1)S(1)} %get-tuple-element.27.refs_0_), channel_id=1, source_target_pairs={{1,129},{9,137},{17,145},{25,153},{33,161},{41,169},{49,177},{57,1... | collective-permute-start | bytes 589832 | tf_op jit(solution)/shard_map/ppermute | solution.py:191
  34.9 9.8 %collective-permute-start.5 = (bf16[6,128,128]{2,1,0:T(8,128)(2,1)S(1)}, bf16[6,128,128]{2,1,0:T(8,128)(2,1)S(1)}, u32[]{:S(2)}, u32[]{:S(2)}) collective-permute-start(bf16[6,128,128]{2,1,0:T(8,128)(2,1)S(1)} %collective-permute-done.3.refs_4_), channel_id=1, source_target_pairs={{1,17},{9,25},{16,0},{17,33},{24,8},{25,41},{32,16},{33,49},{40,24... | collective-permute-start | bytes 589832 | tf_op jit(solution)/shard_map/ppermute | solution.py:191
  36.2 16.5 %collective-permute-start.4 = (bf16[6,128,128]{2,1,0:T(8,128)(2,1)S(1)}, bf16[6,128,128]{2,1,0:T(8,128)(2,1)S(1)}, u32[]{:S(2)}, u32[]{:S(2)}) collective-permute-start(bf16[6,128,128]{2,1,0:T(8,128)(2,1)S(1)} %collective-permute-done.2.refs_3_), channel_id=1, source_target_pairs={{0,16},{8,24},{16,32},{17,1},{24,40},{25,9},{32,48},{33,17},{40,56... | collective-permute-start | bytes 589832 | tf_op jit(solution)/shard_map/ppermute | solution.py:191
  37.5 16.5 %collective-permute-start.8 = (bf16[6,128,128]{2,1,0:T(8,128)(2,1)S(1)}, bf16[6,128,128]{2,1,0:T(8,128)(2,1)S(1)}, u32[]{:S(2)}, u32[]{:S(2)}) collective-permute-start(bf16[6,128,128]{2,1,0:T(8,128)(2,1)S(1)} %get-tuple-element.27.refs_0_), channel_id=1, source_target_pairs={{0,128},{8,136},{16,144},{24,152},{32,160},{40,168},{48,176},{56,1... | collective-permute-start | bytes 589832 | tf_op jit(solution)/shard_map/ppermute | solution.py:191
  38.8 15.2 %collective-permute-start.1 = (bf16[6,128,128]{2,1,0:T(8,128)(2,1)S(1)}, bf16[6,128,128]{2,1,0:T(8,128)(2,1)S(1)}, u32[]{:S(2)}, u32[]{:S(2)}) collective-permute-start(bf16[6,128,128]{2,1,0:T(8,128)(2,1)S(1)} %get-tuple-element.27.refs_0_), channel_id=1, source_target_pairs={{1,9},{8,0},{9,17},{16,8},{17,25},{24,16},{25,33},{32,24},{33,41},... | collective-permute-start | bytes 589832 | tf_op jit(solution)/shard_map/ppermute | solution.py:191
  43.4 10.6 %collective-permute-start = (bf16[6,128,128]{2,1,0:T(8,128)(2,1)S(1)}, bf16[6,128,128]{2,1,0:T(8,128)(2,1)S(1)}, u32[]{:S(2)}, u32[]{:S(2)}) collective-permute-start(bf16[6,128,128]{2,1,0:T(8,128)(2,1)S(1)} %get-tuple-element.27.refs_0_), channel_id=1, source_target_pairs={{0,8},{8,16},{9,1},{16,24},{17,9},{24,32},{25,17},{32,40},{33,25},... | collective-permute-start | bytes 589832 | tf_op jit(solution)/shard_map/ppermute | solution.py:191
  44.7 17.0 %collective-permute-start.7 = (bf16[6,128,128]{2,1,0:T(8,128)(2,1)S(1)}, bf16[6,128,128]{2,1,0:T(8,128)(2,1)S(1)}, u32[]{:S(2)}, u32[]{:S(2)}) collective-permute-start(bf16[6,128,128]{2,1,0:T(8,128)(2,1)S(1)} %collective-permute-done.5.refs_6_), channel_id=1, source_target_pairs={{1,33},{9,41},{17,49},{25,57},{32,0},{33,65},{40,8},{41,73},{48,16... | collective-permute-start | bytes 589832 | tf_op jit(solution)/shard_map/ppermute | solution.py:191
  52.7 25.7 %collective-permute-start.6 = (bf16[6,128,128]{2,1,0:T(8,128)(2,1)S(1)}, bf16[6,128,128]{2,1,0:T(8,128)(2,1)S(1)}, u32[]{:S(2)}, u32[]{:S(2)}) collective-permute-start(bf16[6,128,128]{2,1,0:T(8,128)(2,1)S(1)} %collective-permute-done.4.refs_5_), channel_id=1, source_target_pairs={{0,32},{8,40},{16,48},{24,56},{32,64},{33,1},{40,72},{41,9},{48,80... | collective-permute-start | bytes 589832 | tf_op jit(solution)/shard_map/ppermute | solution.py:191
  87.4 20.9 %collective-permute-start.13 = (bf16[6,128,128]{2,1,0:T(8,128)(2,1)S(1)}, bf16[6,128,128]{2,1,0:T(8,128)(2,1)S(1)}, u32[]{:S(2)}, u32[]{:S(2)}) collective-permute-start(bf16[6,128,128]{2,1,0:T(8,128)(2,1)S(1)} %get-tuple-element.34), channel_id=1, source_target_pairs={{1,33},{9,41},{17,49},{25,57},{32,0},{33,65},{40,8},{41,73},{48,16... | collective-permute-start | bytes 589832 | tf_op jit(solution)/shard_map/ppermute | solution.py:191
  90.6 47.8 %collective-permute-start.11 = (bf16[6,128,128]{2,1,0:T(8,128)(2,1)S(1)}, bf16[6,128,128]{2,1,0:T(8,128)(2,1)S(1)}, u32[]{:S(2)}, u32[]{:S(2)}) collective-permute-start(bf16[6,128,128]{2,1,0:T(8,128)(2,1)S(1)} %get-tuple-element.32), channel_id=1, source_target_pairs={{1,9},{8,0},{9,17},{16,8},{17,25},{24,16},{25,33},{32,24},{33,41},... | collective-permute-start | bytes 589832 | tf_op jit(solution)/shard_map/ppermute | solution.py:191
  91.9 48.6 %collective-permute-start.12 = (bf16[6,128,128]{2,1,0:T(8,128)(2,1)S(1)}, bf16[6,128,128]{2,1,0:T(8,128)(2,1)S(1)}, u32[]{:S(2)}, u32[]{:S(2)}) collective-permute-start(bf16[6,128,128]{2,1,0:T(8,128)(2,1)S(1)} %get-tuple-element.33), channel_id=1, source_target_pairs={{0,8},{8,16},{9,1},{16,24},{17,9},{24,32},{25,17},{32,40},{33,25},... | collective-permute-start | bytes 589832 | tf_op jit(solution)/shard_map/ppermute | solution.py:191
  93.2 19.9 %collective-permute-start.16 = (bf16[6,128,128]{2,1,0:T(8,128)(2,1)S(1)}, bf16[6,128,128]{2,1,0:T(8,128)(2,1)S(1)}, u32[]{:S(2)}, u32[]{:S(2)}) collective-permute-start(bf16[6,128,128]{2,1,0:T(8,128)(2,1)S(1)} %get-tuple-element.37), channel_id=1, source_target_pairs={{0,32},{8,40},{16,48},{24,56},{32,64},{33,1},{40,72},{41,9},{48,80... | collective-permute-start | bytes 589832 | tf_op jit(solution)/shard_map/ppermute | solution.py:191
  94.5 47.3 %collective-permute-start.19 = (bf16[6,128,128]{2,1,0:T(8,128)(2,1)S(1)}, bf16[6,128,128]{2,1,0:T(8,128)(2,1)S(1)}, u32[]{:S(2)}, u32[]{:S(2)}) collective-permute-start(bf16[6,128,128]{2,1,0:T(8,128)(2,1)S(1)} %get-tuple-element.40), channel_id=1, source_target_pairs={{1,129},{9,137},{17,145},{25,153},{33,161},{41,169},{49,177},{57,1... | collective-permute-start | bytes 589832 | tf_op jit(solution)/shard_map/ppermute | solution.py:191
  108.3 33.6 %collective-permute-start.20 = (bf16[6,128,128]{2,1,0:T(8,128)(2,1)S(1)}, bf16[6,128,128]{2,1,0:T(8,128)(2,1)S(1)}, u32[]{:S(2)}, u32[]{:S(2)}) collective-permute-start(bf16[6,128,128]{2,1,0:T(8,128)(2,1)S(1)} %get-tuple-element.41), channel_id=1, source_target_pairs={{0,128},{8,136},{16,144},{24,152},{32,160},{40,168},{48,176},{56,1... | collective-permute-start | bytes 589832 | tf_op jit(solution)/shard_map/ppermute | solution.py:191
  113.1 3.9 %collective-permute-start.14 = (bf16[6,128,128]{2,1,0:T(8,128)(2,1)S(1)}, bf16[6,128,128]{2,1,0:T(8,128)(2,1)S(1)}, u32[]{:S(2)}, u32[]{:S(2)}) collective-permute-start(bf16[6,128,128]{2,1,0:T(8,128)(2,1)S(1)} %add_convert_fusion.3), channel_id=1, source_target_pairs={{1,17},{9,25},{16,0},{17,33},{24,8},{25,41},{32,16},{33,49},{40,24... | collective-permute-start | bytes 589832 | tf_op jit(solution)/shard_map/ppermute | solution.py:191
  117.1 12.9 %collective-permute-start.17 = (bf16[6,128,128]{2,1,0:T(8,128)(2,1)S(1)}, bf16[6,128,128]{2,1,0:T(8,128)(2,1)S(1)}, u32[]{:S(2)}, u32[]{:S(2)}) collective-permute-start(bf16[6,128,128]{2,1,0:T(8,128)(2,1)S(1)} %add_convert_fusion.1), channel_id=1, source_target_pairs={{0,16},{8,24},{16,32},{17,1},{24,40},{25,9},{32,48},{33,17},{40,56... | collective-permute-start | bytes 589832 | tf_op jit(solution)/shard_map/ppermute | solution.py:191
  130.0 11.8 %collective-permute-start.21 = (bf16[6,128,128]{2,1,0:T(8,128)(2,1)S(1)}, bf16[6,128,128]{2,1,0:T(8,128)(2,1)S(1)}, u32[]{:S(2)}, u32[]{:S(2)}) collective-permute-start(bf16[6,128,128]{2,1,0:T(8,128)(2,1)S(1)} %get-tuple-element.42), channel_id=1, source_target_pairs={{0,256},{8,264},{16,272},{24,280},{32,288},{40,296},{48,304},{56,3... | collective-permute-start | bytes 589832 | tf_op jit(solution)/shard_map/ppermute | solution.py:196
  138.4 4.8 %collective-permute-start.15 = (bf16[6,128,128]{2,1,0:T(8,128)(2,1)S(1)}, bf16[6,128,128]{2,1,0:T(8,128)(2,1)S(1)}, u32[]{:S(2)}, u32[]{:S(2)}) collective-permute-start(bf16[6,128,128]{2,1,0:T(8,128)(2,1)S(1)} %add_convert_fusion.2), channel_id=1, source_target_pairs={{1,17},{9,25},{16,0},{17,33},{24,8},{25,41},{32,16},{33,49},{40,24... | collective-permute-start | bytes 589832 | tf_op jit(solution)/shard_map/ppermute | solution.py:191
  140.5 9.9 %collective-permute-start.18 = (bf16[6,128,128]{2,1,0:T(8,128)(2,1)S(1)}, bf16[6,128,128]{2,1,0:T(8,128)(2,1)S(1)}, u32[]{:S(2)}, u32[]{:S(2)}) collective-permute-start(bf16[6,128,128]{2,1,0:T(8,128)(2,1)S(1)} %add_convert_fusion), channel_id=1, source_target_pairs={{0,16},{8,24},{16,32},{17,1},{24,40},{25,9},{32,48},{33,17},{40,56... | collective-permute-start | bytes 589832 | tf_op jit(solution)/shard_map/ppermute | solution.py:191

commit v7 on v6

--- a/solution.py
+++ b/solution.py
@@ -16,7 +16,7 @@
 TN = (((0,), (0,)), ((), ()))
 F32 = jnp.float32
 BF16 = jnp.bfloat16
-VMEM_LIMIT = 48 * 1024 * 1024
+VMEM_LIMIT = 24 * 1024 * 1024
 
 
 def dot(left, right, dims):
@@ -86,53 +86,99 @@
         kv_ref[heads + head] = v_ref[head]
 
 
-def attention_kernel(heads, q_ref, do_ref, *refs):
-    count = len(NEAR) + FAR
-    tiles = refs[:count]
-    out_ref, dq_ref = refs[count : count + 2]
-    part_refs = refs[count + 2 : -1]
-    work_ref = refs[-1]
+def early_kernel(heads, places, q_ref, *refs):
+    tiles, (weight_ref, out_ref, rows_ref) = refs[: len(places)], refs[len(places) :]
     scale = TILE ** (-0.5)
-    usable = [inside(t) for t in range(count)]
-    tops, shares, deltas = [], [], []
+    usable = [inside(place) for place in places]
+    lane = lax.broadcasted_iota(jnp.int32, (TILE, TILE), 1)
+    rows = jnp.zeros((TILE, TILE), F32)
+    tops = []
     for head in range(heads):
         top = jnp.full((TILE, TILE), -1e30, F32)
-        for t in range(count):
-            score = dot(q_ref[head], tiles[t][head], NT) * scale
+        for t, tile in enumerate(tiles):
+            score = dot(q_ref[head], tile[head], NT) * scale
             if usable[t] is not None:
                 score = jnp.where(usable[t], score, -1e30)
-            work_ref[head, t] = score
+            weight_ref[head, t] = score
             top = jnp.maximum(top, score)
         tops.append(jnp.max(top, axis=1, keepdims=True))
+        rows = jnp.where(lane == head, tops[head], rows)
     for head in range(heads):
         total = jnp.zeros((TILE, TILE), F32)
-        for t in range(count):
-            weight = jnp.exp(work_ref[head, t] - tops[head])
-            work_ref[head, t] = weight
+        out = jnp.zeros((TILE, TILE), F32)
+        for t, tile in enumerate(tiles):
+            weight = jnp.exp(weight_ref[head, t] - tops[head])
+            weight_ref[head, t] = weight
             total = total + weight
-        shares.append(1.0 / jnp.sum(total, axis=1, keepdims=True))
-    for head in range(heads):
-        upstream = do_ref[head]
-        out = jnp.zeros((TILE, TILE), F32)
-        for t in range(count):
-            prob = work_ref[head, t] * shares[head]
-            work_ref[head, t] = prob
-            prob = prob.astype(BF16)
-            out = out + dot(prob, tiles[t][heads + head], NN)
+            out = out + dot(weight.astype(BF16), tile[heads + head], NN)
+        out_ref[head] = out
+        rows = jnp.where(lane == heads + head, jnp.sum(total, axis=1, keepdims=True), rows)
+    rows_ref[...] = rows
+
+
+def late_kernel(heads, places, q_ref, do_ref, early_ref, rows_ref, *refs):
+    count = len(places)
+    tiles = refs[:count]
+    out_ref, dq_ref, late_rows_ref = refs[count : count + 3]
+    part_refs = refs[count + 3 :]
+    scale = TILE ** (-0.5)
+    usable = [inside(place) for place in places]
+    lane = lax.broadcasted_iota(jnp.int32, (TILE, TILE), 1)
+    rows = jnp.zeros((TILE, TILE), F32)
+    for head in range(heads):
+        query, upstream = q_ref[head], do_ref[head]
+        early_top = rows_ref[:, head : head + 1]
+        scores = []
+        top = jnp.full((TILE, TILE), -1e30, F32)
+        for t, tile in enumerate(tiles):
+            score = dot(query, tile[head], NT) * scale
+            score = jnp.where(usable[t], score, -1e30)
+            scores.append(score)
+            top = jnp.maximum(top, score)
+        top = jnp.maximum(early_top, jnp.max(top, axis=1, keepdims=True))
+        keep = jnp.exp(early_top - top)
+        out = early_ref[head] * keep
+        weights = [jnp.exp(score - top) for score in scores]
+        total = weights[0]
+        for weight in weights[1:]:
+            total = total + weight
+        total = jnp.sum(total, axis=1, keepdims=True)
+        for t, tile in enumerate(tiles):
+            out = out + dot(weights[t].astype(BF16), tile[heads + head], NN)
+        share = 1.0 / (total + rows_ref[:, heads + head : heads + head + 1] * keep)
+        out = (out * share).astype(BF16)
+        out_ref[head] = out
+        delta = jnp.sum(upstream.astype(F32) * out.astype(F32), axis=1, keepdims=True)
+        query_grad = jnp.zeros((TILE, TILE), F32)
+        for t, tile in enumerate(tiles):
+            prob = weights[t] * share
             part = part_refs[t]
-            part[heads + head] = dot(prob, upstream, TN).astype(part.dtype)
-        out = out.astype(BF16)
-        out_ref[head] = out
-        deltas.append(jnp.sum(upstream.astype(F32) * out.astype(F32), axis=1, keepdims=True))
+            part[heads + head] = dot(prob.astype(BF16), upstream, TN).astype(part.dtype)
+            dscore = (prob * (dot(upstream, tile[heads + head], NT) - delta)).astype(BF16)
+            part[head] = (dot(dscore, query, TN) * scale).astype(part.dtype)
+            query_grad = query_grad + dot(dscore, tile[head], NN)
+        dq_ref[head] = query_grad
+        rows = jnp.where(lane == head, keep * share, rows)
+        rows = jnp.where(lane == heads + head, delta, rows)
+    late_rows_ref[...] = rows
+
+
+def rest_kernel(heads, q_ref, do_ref, weight_ref, late_dq_ref, rows_ref, *refs):
+    count = (len(refs) - 1) // 2
+    tiles, dq_ref, part_refs = refs[:count], refs[count], refs[count + 1 :]
+    scale = TILE ** (-0.5)
     for head in range(heads):
         query, upstream = q_ref[head], do_ref[head]
-        query_grad = jnp.zeros((TILE, TILE), F32)
-        for t in range(count):
-            dprob = dot(upstream, tiles[t][heads + head], NT)
-            dscore = (work_ref[head, t] * (dprob - deltas[head])).astype(BF16)
-            query_grad = query_grad + dot(dscore, tiles[t][head], NN)
+        share = rows_ref[:, head : head + 1]
+        delta = rows_ref[:, heads + head : heads + head + 1]
+        query_grad = late_dq_ref[head]
+        for t, tile in enumerate(tiles):
+            prob = weight_ref[head, t] * share
             part = part_refs[t]
+            part[heads + head] = dot(prob.astype(BF16), upstream, TN).astype(part.dtype)
+            dscore = (prob * (dot(upstream, tile[heads + head], NT) - delta)).astype(BF16)
             part[head] = (dot(dscore, query, TN) * scale).astype(part.dtype)
+            query_grad = query_grad + dot(dscore, tile[head], NN)
         dq_ref[head] = query_grad * scale
 
 
@@ -208,19 +254,28 @@
 
 
 def collect(parts):
-    arrived = [passed(parts[place], NEAR[place]) for place in (1, 2)]
-    for place in (len(NEAR) - 2, len(NEAR) - 1):
-        carried = parts[place]
-        while place > 2:
-            offset = NEAR[place]
-            carried = passed(carried, offset - relay(offset))
-            place = place - 2
-            if relay(offset):
-                carried = (carried.astype(F32) + parts[place]).astype(BF16)
-            else:
-                break
-        arrived.append(carried)
-    return arrived
+    places = [len(NEAR) - 2, len(NEAR) - 1]
+    carried = [parts[place] for place in places]
+    far = [parts[len(NEAR) + place] for place in range(FAR)]
+    while True:
+        steps = [NEAR[place] - relay(NEAR[place]) for place in places]
+        through = relay(NEAR[places[0]])
+        carried = [passed(part, step) for part, step in zip(carried, steps)]
+        if not through:
+            break
+        places = [place - 2 for place in places]
+        carried, far = lax.optimization_barrier((carried, far))
+        carried = [
+            (part.astype(F32) + parts[place]).astype(BF16) for part, place in zip(carried, places)
+        ]
+    line = lax.axis_size("z")
+    return [
+        *carried,
+        *(passed(parts[place], NEAR[place]) for place in (1, 2)),
+        passed(far[0], -line),
+        passed(far[1], line),
+        half_round(far[2]),
+    ]
 
 
 def per_device(total_heads, q_raw, k_raw, values, grad_out, q_gain, k_gain, key_tiles):
@@ -259,16 +314,30 @@
         sums, q_raw, k_raw, values, gains,
     )
     tiles = spread(pairs) + [passed(pairs, line), passed(pairs, -line), half_round(pairs)]
-    attended, dq, *parts = call(
-        functools.partial(attention_kernel, heads),
-        "attention",
-        [(whole, BF16), (whole, F32)] + [(pair, F32 if t == 0 or 2 < t < near - 2 else BF16) for t in range(count)],
-        q_norm, grad_out, *tiles,
-        scratch=[pltpu.VMEM((heads, count, TILE, TILE), F32)],
-    )
-    arrived = collect(parts) + [
-        passed(parts[near], -line), passed(parts[near + 1], line), half_round(parts[near + 2])
-    ]
+    late = [near - 2, near - 1]
+    early = [t for t in range(count) if t not in late]
+    early_tiles, late_tiles = [tiles[t] for t in early], [tiles[t] for t in late]
+    square = ((TILE, TILE), F32)
+    weights, early_out, early_rows = call(
+        functools.partial(early_kernel, heads, early),
+        "early",
+        [((heads, len(early), TILE, TILE), F32), (whole, F32), square],
+        q_norm, *early_tiles,
+    )
+    attended, late_dq, late_rows, *late_parts = call(
+        functools.partial(late_kernel, heads, late),
+        "late",
+        [(whole, BF16), (whole, F32), square] + [(pair, BF16)] * len(late),
+        q_norm, grad_out, early_out, early_rows, *late_tiles,
+    )
+    dq, *early_parts = call(
+        functools.partial(rest_kernel, heads),
+        "rest",
+        [(whole, F32)] + [(pair, F32 if t == 0 or 2 < t < near else BF16) for t in early],
+        q_norm, grad_out, weights, late_dq, late_rows, *early_tiles,
+    )
+    parts = dict(zip(early + late, early_parts + late_parts))
+    arrived = collect(parts)
     dk, grad_v, terms = call(
         functools.partial(terms_kernel, heads),
         "terms",

time: 166 us -> 160 us (0.964)
  waiting for transfers between devices: 56.6 us -> 48.6 us
  blocking collectives: 12.6 us -> 8.36 us
  local copies, waits for them, and re-layouts: 1.81 us -> 4.47 us
  Pallas kernels: 11.9 us -> 14.2 us
    ppermute x20, waiting for transfers between devices: 52.5 us -> 39.1 us  [passed(): return lax.ppermute(value, SEQ + ('c',), pairs)]
    ppermute x2, waiting for transfers between devices: 0.01 us -> 5.47 us  [half_round(): lax.ppermute(value, SEQ, [(i, (i + count // 2) % count) for i in range(co...]
    all_to_all x1, blocking collectives: 12.6 us -> 8.36 us  [per_device(): terms = lax.all_to_all(terms, HEAD, 0, 0, tiled=True)]
    unnamed x14 -> x16, local copies, waits for them, and re-layouts: 1.81 us -> 4.47 us
    pallas_call x5 -> x7, Pallas kernels: 11.9 us -> 14.2 us  [call(): pl.pallas_call(kernel, out_shape=[jax.ShapeDtypeStruct(shape, dtype) for...]
  transfers between devices with their start and end apart: 23 -> 23, of which waited for: 9 -> 8; matrix products, arithmetic and copies ran while one was open for 1% -> 1% of each run, Pallas kernels for 0% -> 5%
where the time goes in v7:
time: 160 us; the launch traced here: 159 us
  starting transfers between devices  81.5 us (51%)
  waiting for transfers between devices  48.6 us (30%)
  Pallas kernels  14.2 us (9%)
  blocking collectives  8.36 us (5%)
  local copies, waits for them, and re-layouts  4.47 us (3%)
    ppermute x20, starting transfers between devices, passed(): return lax.ppermute(value, SEQ + ('c',), pairs)  51.8 us
    ppermute x20, waiting for transfers between devices, passed(): return lax.ppermute(value, SEQ + ('c',), pairs)  39.1 us
    ppermute x2, starting transfers between devices, half_round(): lax.ppermute(value, SEQ, [(i, (i + count // 2) % count) for i in range(co...  19.5 us
    pallas_call x7, Pallas kernels, call(): pl.pallas_call(kernel, out_shape=[jax.ShapeDtypeStruct(shape, dtype) for...  14.2 us
    all_to_all x1, starting transfers between devices, per_device(): sums = lax.all_to_all(squares, HEAD, 0, 0, tiled=True)  10.1 us
    all_to_all x1, blocking collectives, per_device(): terms = lax.all_to_all(terms, HEAD, 0, 0, tiled=True)  8.36 us
    ppermute x2, waiting for transfers between devices, half_round(): lax.ppermute(value, SEQ, [(i, (i + count // 2) % count) for i in range(co...  5.47 us
    unnamed x16, local copies, waits for them, and re-layouts  4.47 us
  transfers between devices with their start and end apart: 23, of which 8 were waited for; matrix products, arithmetic and copies ran while one was open for 1% of the time, Pallas kernels for 5%

profile of v7, /device:TPU:1, one launch (start us, length us, event | category | flops | bytes accessed | tf_op | source)
XLA Modules:
  0.0 159.0 jit_solution(3513001927979981055)
XLA Ops:
  0.6 0.0 copy-start
  0.6 0.9 copy-done
  1.5 0.9 copy-done.3
  2.4 0.8 squares.1
  3.2 10.1 %all-to-all-start = ((f32[8,8,128]{2,1,0:T(8,128)}), f32[8,8,128]{2,1,0:T(8,128)S(1)}, u32[]{:S(2)}, u32[]{:S(2)}) async-start(f32[8,8,128]{2,1,0:T(8,128)} %squares.1), calls=%async_computation | async-start | bytes 65536 | tf_op jit(solution)/shard_map/all_to_all | solution.py:309
  13.4 0.7 pad_maximum_fusion.gain_ref
  14.1 4.0 %all-to-all-done.sums_ref = f32[8,8,128]{2,1,0:T(8,128)S(1)} async-done(((f32[8,8,128]{2,1,0:T(8,128)}), f32[8,8,128]{2,1,0:T(8,128)S(1)}, u32[]{:S(2)}, u32[]{:S(2)}) %all-to-all-start) | async-done | bytes 32800 | tf_op jit(solution)/shard_map/all_to_all | solution.py:309
  18.1 0.9 copy-done.1
  19.0 0.9 copy-done.4
  19.9 0.9 copy-done.7
  20.8 0.2 norm.1
  21.0 1.3 collective-permute-start.3
  22.3 1.3 collective-permute-start.2
  23.6 11.3 %collective-permute-start.8 = (bf16[6,128,128]{2,1,0:T(8,128)(2,1)S(1)}, bf16[6,128,128]{2,1,0:T(8,128)(2,1)S(1)}, u32[]{:S(2)}, u32[]{:S(2)}) collective-permute-start(bf16[6,128,128]{2,1,0:T(8,128)(2,1)S(1)} %get-tuple-element.42.refs_0_), channel_id=1, source_target_pairs={{0,256},{8,264},{16,272},{24,280},{32,288},{40,296},{48,304},{56,3... | collective-permute-start | bytes 589832 | tf_op jit(solution)/shard_map/ppermute | solution.py:242
  35.0 2.5 %collective-permute-start.7 = (bf16[6,128,128]{2,1,0:T(8,128)(2,1)S(1)}, bf16[6,128,128]{2,1,0:T(8,128)(2,1)S(1)}, u32[]{:S(2)}, u32[]{:S(2)}) collective-permute-start(bf16[6,128,128]{2,1,0:T(8,128)(2,1)S(1)} %get-tuple-element.42.refs_0_), channel_id=1, source_target_pairs={{1,129},{9,137},{17,145},{25,153},{33,161},{41,169},{49,177},{57,1... | collective-permute-start | bytes 589832 | tf_op jit(solution)/shard_map/ppermute | solution.py:237
  37.5 1.3 collective-permute-start.5
  38.8 1.3 collective-permute-start.4
  40.1 1.3 collective-permute-start.6
  41.4 2.7 %collective-permute-start.1 = (bf16[6,128,128]{2,1,0:T(8,128)(2,1)S(1)}, bf16[6,128,128]{2,1,0:T(8,128)(2,1)S(1)}, u32[]{:S(2)}, u32[]{:S(2)}) collective-permute-start(bf16[6,128,128]{2,1,0:T(8,128)(2,1)S(1)} %get-tuple-element.42.refs_0_), channel_id=1, source_target_pairs={{1,9},{8,0},{9,17},{16,8},{17,25},{24,16},{25,33},{32,24},{33,41},... | collective-permute-start | bytes 589832 | tf_op jit(solution)/shard_map/ppermute | solution.py:237
  44.1 1.9 %collective-permute-done.7.refs_8_ = bf16[6,128,128]{2,1,0:T(8,128)(2,1)S(1)} collective-permute-done((bf16[6,128,128]{2,1,0:T(8,128)(2,1)S(1)}, bf16[6,128,128]{2,1,0:T(8,128)(2,1)S(1)}, u32[]{:S(2)}, u32[]{:S(2)}) %collective-permute-start.7) | collective-permute-done | bytes 196640 | tf_op jit(solution)/shard_map/ppermute | solution.py:237
  46.0 1.3 collective-permute-start
  47.3 8.0 %collective-permute-start.10 = (bf16[6,128,128]{2,1,0:T(8,128)(2,1)S(1)}, bf16[6,128,128]{2,1,0:T(8,128)(2,1)S(1)}, u32[]{:S(2)}, u32[]{:S(2)}) collective-permute-start(bf16[6,128,128]{2,1,0:T(8,128)(2,1)S(1)} %collective-permute-done.5.refs_6_), channel_id=1, source_target_pairs={{1,33},{9,41},{17,49},{25,57},{32,0},{33,65},{40,8},{41,73},{48,16... | collective-permute-start | bytes 589832 | tf_op jit(solution)/shard_map/ppermute | solution.py:237
  55.3 1.3 collective-permute-start.9
  56.7 1.4 early.1
  58.0 6.2 %collective-permute-done.10.refs_1_ = bf16[6,128,128]{2,1,0:T(8,128)(2,1)S(1)} collective-permute-done((bf16[6,128,128]{2,1,0:T(8,128)(2,1)S(1)}, bf16[6,128,128]{2,1,0:T(8,128)(2,1)S(1)}, u32[]{:S(2)}, u32[]{:S(2)}) %collective-permute-start.10) | collective-permute-done | bytes 196640 | tf_op jit(solution)/shard_map/ppermute | solution.py:237
  64.3 16.8 %collective-permute-done.9.refs_0_ = bf16[6,128,128]{2,1,0:T(8,128)(2,1)S(1)} collective-permute-done((bf16[6,128,128]{2,1,0:T(8,128)(2,1)S(1)}, bf16[6,128,128]{2,1,0:T(8,128)(2,1)S(1)}, u32[]{:S(2)}, u32[]{:S(2)}) %collective-permute-start.9) | collective-permute-done | bytes 196640 | tf_op jit(solution)/shard_map/ppermute | solution.py:237
  81.0 2.8 %late.1 = (bf16[3,128,128]{2,1,0:T(8,128)(2,1)}, f32[3,128,128]{2,1,0:T(8,128)S(1)}, f32[128,128]{1,0:T(8,128)S(1)}, bf16[6,128,128]{2,1,0:T(8,128)(2,1)S(1)}, bf16[6,128,128]{2,1,0:T(8,128)(2,1)S(1)}) custom-call(bf16[3,128,128]{2,1,0:T(8,128)(2,1)S(1)} %get-tuple-element.41.q_ref, bf16[3,128,128]{2,1,0:T(8,128)(2,1)S(1)} %bitcast.16, ...), custom_call_target="tpu_custom_call" | custom-call | tf_op jit(solution)/shard_map/late/pallas_call | solution.py:297
  83.8 3.2 %collective-permute-start.11 = (bf16[6,128,128]{2,1,0:T(8,128)(2,1)S(1)}, bf16[6,128,128]{2,1,0:T(8,128)(2,1)S(1)}, u32[]{:S(2)}, u32[]{:S(2)}) collective-permute-start(bf16[6,128,128]{2,1,0:T(8,128)(2,1)S(1)} %get-tuple-element.52), channel_id=1, source_target_pairs={{1,33},{9,41},{17,49},{25,57},{32,0},{33,65},{40,8},{41,73},{48,16... | collective-permute-start | bytes 589832 | tf_op jit(solution)/shard_map/ppermute | solution.py:237
  87.0 1.3 collective-permute-start.12
  88.3 7.2 %rest.1 = (f32[3,128,128]{2,1,0:T(8,128)S(1)}, f32[6,128,128]{2,1,0:T(8,128)S(1)}, bf16[6,128,128]{2,1,0:T(8,128)(2,1)S(1)}, bf16[6,128,128]{2,1,0:T(8,128)(2,1)...) custom-call(bf16[3,128,128]{2,1,0:T(8,128)(2,1)S(1)} %get-tuple-elem, ...), custom_call_target="tpu_custom_call" | custom-call | tf_op jit(solution)/shard_map/rest/pallas_call | solution.py:297
  95.5 0.0 copy-start.2
  95.5 0.0 copy-start.5
  95.5 6.0 %collective-permute-done.11 = bf16[6,128,128]{2,1,0:T(8,128)(2,1)S(1)} collective-permute-done((bf16[6,128,128]{2,1,0:T(8,128)(2,1)S(1)}, bf16[6,128,128]{2,1,0:T(8,128)(2,1)S(1)}, u32[]{:S(2)}, u32[]{:S(2)}) %collective-permute-start.11) | collective-permute-done | bytes 196640 | tf_op jit(solution)/shard_map/ppermute | solution.py:237
  101.5 2.7 %collective-permute-done.12 = bf16[6,128,128]{2,1,0:T(8,128)(2,1)S(1)} collective-permute-done((bf16[6,128,128]{2,1,0:T(8,128)(2,1)S(1)}, bf16[6,128,128]{2,1,0:T(8,128)(2,1)S(1)}, u32[]{:S(2)}, u32[]{:S(2)}) %collective-permute-start.12) | collective-permute-done | bytes 196640 | tf_op jit(solution)/shard_map/ppermute | solution.py:237
  104.2 1.3 collective-permute-start.13
  105.6 1.3 collective-permute-start.14
  106.9 1.3 collective-permute-start.17
  108.2 1.3 collective-permute-start.18
  109.5 5.5 %collective-permute-done.14 = bf16[6,128,128]{2,1,0:T(8,128)(2,1)S(1)} collective-permute-done((bf16[6,128,128]{2,1,0:T(8,128)(2,1)S(1)}, bf16[6,128,128]{2,1,0:T(8,128)(2,1)S(1)}, u32[]{:S(2)}, u32[]{:S(2)}) %collective-permute-start.14) | collective-permute-done | bytes 196640 | tf_op jit(solution)/shard_map/ppermute | solution.py:237
  115.0 5.5 %collective-permute-start.15 = (bf16[6,128,128]{2,1,0:T(8,128)(2,1)S(1)}, bf16[6,128,128]{2,1,0:T(8,128)(2,1)S(1)}, u32[]{:S(2)}, u32[]{:S(2)}) collective-permute-start(bf16[6,128,128]{2,1,0:T(8,128)(2,1)S(1)} %add_convert_fusion.1), channel_id=1, source_target_pairs={{1,17},{9,25},{16,0},{17,33},{24,8},{25,41},{32,16},{33,49},{40,24... | collective-permute-start | bytes 589832 | tf_op jit(solution)/shard_map/ppermute | solution.py:237
  120.6 1.3 collective-permute-start.16
  121.9 11.8 %collective-permute-start.19 = (bf16[6,128,128]{2,1,0:T(8,128)(2,1)S(1)}, bf16[6,128,128]{2,1,0:T(8,128)(2,1)S(1)}, u32[]{:S(2)}, u32[]{:S(2)}) collective-permute-start(bf16[6,128,128]{2,1,0:T(8,128)(2,1)S(1)} %get-tuple-element.70), channel_id=1, source_target_pairs={{1,129},{9,137},{17,145},{25,153},{33,161},{41,169},{49,177},{57,1... | collective-permute-start | bytes 589832 | tf_op jit(solution)/shard_map/ppermute | solution.py:237
  133.7 1.3 collective-permute-start.20
  135.0 8.1 %collective-permute-start.21 = (bf16[6,128,128]{2,1,0:T(8,128)(2,1)S(1)}, bf16[6,128,128]{2,1,0:T(8,128)(2,1)S(1)}, u32[]{:S(2)}, u32[]{:S(2)}) collective-permute-start(bf16[6,128,128]{2,1,0:T(8,128)(2,1)S(1)} %get-tuple-element.72), channel_id=1, source_target_pairs={{0,256},{8,264},{16,272},{24,280},{32,288},{40,296},{48,304},{56,3... | collective-permute-start | bytes 589832 | tf_op jit(solution)/shard_map/ppermute | solution.py:242
  143.2 5.5 %collective-permute-done.21.refs_7_ = bf16[6,128,128]{2,1,0:T(8,128)(2,1)S(1)} collective-permute-done((bf16[6,128,128]{2,1,0:T(8,128)(2,1)S(1)}, bf16[6,128,128]{2,1,0:T(8,128)(2,1)S(1)}, u32[]{:S(2)}, u32[]{:S(2)}) %collective-permute-start.21) | collective-permute-done | bytes 196640 | tf_op jit(solution)/shard_map/ppermute | solution.py:242
  148.7 1.0 terms.1
  149.7 8.4 %all_to_all.10.terms_ref = f32[8,8,128]{2,1,0:T(8,128)S(1)} all-to-all(f32[8,8,128]{2,1,0:T(8,128)S(1)} %get-tuple-element.73), channel_id=1, replica_groups=mesh['x'=4,'z'=16,'y'=4,'c'=2] {'y','c'}, dimensions={0} | all-to-all | bytes 65536 | tf_op jit(solution)/shard_map/all_to_all | solution.py:347
  158.0 0.9 final.1
  (27 shorter events, 0.2 us)
Async XLA Ops:
  0.6 0.9 copy-start
  1.5 0.9 copy-start.3
  2.4 78.6 %copy-start.6 = (bf16[128,3,128]{2,0,1:T(8,128)(2,1)S(1)}, bf16[128,3,128]{2,0,1:T(8,128)(2,1)}, u32[]{:S(2)}) copy-start(bf16[128,3,128]{2,0,1:T(8,128)(2,1)} %param.10) | copy-start | bytes 294916
  3.2 14.9 %all-to-all-start = ((f32[8,8,128]{2,1,0:T(8,128)}), f32[8,8,128]{2,1,0:T(8,128)S(1)}, u32[]{:S(2)}, u32[]{:S(2)}) async-start(f32[8,8,128]{2,1,0:T(8,128)} %squares.1), calls=%async_computation | async-start | bytes 65536 | tf_op jit(solution)/shard_map/all_to_all | solution.py:309
  18.1 0.9 copy-start.1
  19.0 0.9 copy-start.4
  19.9 0.9 copy-start.7
  21.0 16.5 %collective-permute-start.3 = (bf16[6,128,128]{2,1,0:T(8,128)(2,1)S(1)}, bf16[6,128,128]{2,1,0:T(8,128)(2,1)S(1)}, u32[]{:S(2)}, u32[]{:S(2)}) collective-permute-start(bf16[6,128,128]{2,1,0:T(8,128)(2,1)S(1)} %get-tuple-element.42.refs_0_), channel_id=1, source_target_pairs={{1,17},{9,25},{16,0},{17,33},{24,8},{25,41},{32,16},{33,49},{40,24... | collective-permute-start | bytes 589832 | tf_op jit(solution)/shard_map/ppermute | solution.py:237
  22.3 16.5 %collective-permute-start.2 = (bf16[6,128,128]{2,1,0:T(8,128)(2,1)S(1)}, bf16[6,128,128]{2,1,0:T(8,128)(2,1)S(1)}, u32[]{:S(2)}, u32[]{:S(2)}) collective-permute-start(bf16[6,128,128]{2,1,0:T(8,128)(2,1)S(1)} %get-tuple-element.42.refs_0_), channel_id=1, source_target_pairs={{0,16},{8,24},{16,32},{17,1},{24,40},{25,9},{32,48},{33,17},{40,56... | collective-permute-start | bytes 589832 | tf_op jit(solution)/shard_map/ppermute | solution.py:237
  23.6 17.8 %collective-permute-start.8 = (bf16[6,128,128]{2,1,0:T(8,128)(2,1)S(1)}, bf16[6,128,128]{2,1,0:T(8,128)(2,1)S(1)}, u32[]{:S(2)}, u32[]{:S(2)}) collective-permute-start(bf16[6,128,128]{2,1,0:T(8,128)(2,1)S(1)} %get-tuple-element.42.refs_0_), channel_id=1, source_target_pairs={{0,256},{8,264},{16,272},{24,280},{32,288},{40,296},{48,304},{56,3... | collective-permute-start | bytes 589832 | tf_op jit(solution)/shard_map/ppermute | solution.py:242
  35.0 11.0 %collective-permute-start.7 = (bf16[6,128,128]{2,1,0:T(8,128)(2,1)S(1)}, bf16[6,128,128]{2,1,0:T(8,128)(2,1)S(1)}, u32[]{:S(2)}, u32[]{:S(2)}) collective-permute-start(bf16[6,128,128]{2,1,0:T(8,128)(2,1)S(1)} %get-tuple-element.42.refs_0_), channel_id=1, source_target_pairs={{1,129},{9,137},{17,145},{25,153},{33,161},{41,169},{49,177},{57,1... | collective-permute-start | bytes 589832 | tf_op jit(solution)/shard_map/ppermute | solution.py:237
  37.5 9.8 %collective-permute-start.5 = (bf16[6,128,128]{2,1,0:T(8,128)(2,1)S(1)}, bf16[6,128,128]{2,1,0:T(8,128)(2,1)S(1)}, u32[]{:S(2)}, u32[]{:S(2)}) collective-permute-start(bf16[6,128,128]{2,1,0:T(8,128)(2,1)S(1)} %collective-permute-done.3.refs_4_), channel_id=1, source_target_pairs={{1,17},{9,25},{16,0},{17,33},{24,8},{25,41},{32,16},{33,49},{40,24... | collective-permute-start | bytes 589832 | tf_op jit(solution)/shard_map/ppermute | solution.py:237
  38.8 16.5 %collective-permute-start.4 = (bf16[6,128,128]{2,1,0:T(8,128)(2,1)S(1)}, bf16[6,128,128]{2,1,0:T(8,128)(2,1)S(1)}, u32[]{:S(2)}, u32[]{:S(2)}) collective-permute-start(bf16[6,128,128]{2,1,0:T(8,128)(2,1)S(1)} %collective-permute-done.2.refs_3_), channel_id=1, source_target_pairs={{0,16},{8,24},{16,32},{17,1},{24,40},{25,9},{32,48},{33,17},{40,56... | collective-permute-start | bytes 589832 | tf_op jit(solution)/shard_map/ppermute | solution.py:237
  40.1 16.5 %collective-permute-start.6 = (bf16[6,128,128]{2,1,0:T(8,128)(2,1)S(1)}, bf16[6,128,128]{2,1,0:T(8,128)(2,1)S(1)}, u32[]{:S(2)}, u32[]{:S(2)}) collective-permute-start(bf16[6,128,128]{2,1,0:T(8,128)(2,1)S(1)} %get-tuple-element.42.refs_0_), channel_id=1, source_target_pairs={{0,128},{8,136},{16,144},{24,152},{32,160},{40,168},{48,176},{56,1... | collective-permute-start | bytes 589832 | tf_op jit(solution)/shard_map/ppermute | solution.py:237
  41.4 15.2 %collective-permute-start.1 = (bf16[6,128,128]{2,1,0:T(8,128)(2,1)S(1)}, bf16[6,128,128]{2,1,0:T(8,128)(2,1)S(1)}, u32[]{:S(2)}, u32[]{:S(2)}) collective-permute-start(bf16[6,128,128]{2,1,0:T(8,128)(2,1)S(1)} %get-tuple-element.42.refs_0_), channel_id=1, source_target_pairs={{1,9},{8,0},{9,17},{16,8},{17,25},{24,16},{25,33},{32,24},{33,41},... | collective-permute-start | bytes 589832 | tf_op jit(solution)/shard_map/ppermute | solution.py:237
  46.0 10.6 %collective-permute-start = (bf16[6,128,128]{2,1,0:T(8,128)(2,1)S(1)}, bf16[6,128,128]{2,1,0:T(8,128)(2,1)S(1)}, u32[]{:S(2)}, u32[]{:S(2)}) collective-permute-start(bf16[6,128,128]{2,1,0:T(8,128)(2,1)S(1)} %get-tuple-element.42.refs_0_), channel_id=1, source_target_pairs={{0,8},{8,16},{9,1},{16,24},{17,9},{24,32},{25,17},{32,40},{33,25},... | collective-permute-start | bytes 589832 | tf_op jit(solution)/shard_map/ppermute | solution.py:237
  47.3 17.0 %collective-permute-start.10 = (bf16[6,128,128]{2,1,0:T(8,128)(2,1)S(1)}, bf16[6,128,128]{2,1,0:T(8,128)(2,1)S(1)}, u32[]{:S(2)}, u32[]{:S(2)}) collective-permute-start(bf16[6,128,128]{2,1,0:T(8,128)(2,1)S(1)} %collective-permute-done.5.refs_6_), channel_id=1, source_target_pairs={{1,33},{9,41},{17,49},{25,57},{32,0},{33,65},{40,8},{41,73},{48,16... | collective-permute-start | bytes 589832 | tf_op jit(solution)/shard_map/ppermute | solution.py:237
  55.3 25.7 %collective-permute-start.9 = (bf16[6,128,128]{2,1,0:T(8,128)(2,1)S(1)}, bf16[6,128,128]{2,1,0:T(8,128)(2,1)S(1)}, u32[]{:S(2)}, u32[]{:S(2)}) collective-permute-start(bf16[6,128,128]{2,1,0:T(8,128)(2,1)S(1)} %collective-permute-done.4.refs_5_), channel_id=1, source_target_pairs={{0,32},{8,40},{16,48},{24,56},{32,64},{33,1},{40,72},{41,9},{48,80... | collective-permute-start | bytes 589832 | tf_op jit(solution)/shard_map/ppermute | solution.py:237
  83.8 17.7 %collective-permute-start.11 = (bf16[6,128,128]{2,1,0:T(8,128)(2,1)S(1)}, bf16[6,128,128]{2,1,0:T(8,128)(2,1)S(1)}, u32[]{:S(2)}, u32[]{:S(2)}) collective-permute-start(bf16[6,128,128]{2,1,0:T(8,128)(2,1)S(1)} %get-tuple-element.52), channel_id=1, source_target_pairs={{1,33},{9,41},{17,49},{25,57},{32,0},{33,65},{40,8},{41,73},{48,16... | collective-permute-start | bytes 589832 | tf_op jit(solution)/shard_map/ppermute | solution.py:237
  87.0 17.1 %collective-permute-start.12 = (bf16[6,128,128]{2,1,0:T(8,128)(2,1)S(1)}, bf16[6,128,128]{2,1,0:T(8,128)(2,1)S(1)}, u32[]{:S(2)}, u32[]{:S(2)}) collective-permute-start(bf16[6,128,128]{2,1,0:T(8,128)(2,1)S(1)} %get-tuple-element.53), channel_id=1, source_target_pairs={{0,32},{8,40},{16,48},{24,56},{32,64},{33,1},{40,72},{41,9},{48,80... | collective-permute-start | bytes 589832 | tf_op jit(solution)/shard_map/ppermute | solution.py:237
  95.5 53.2 %copy-start.2 = (bf16[128,3,128]{2,0,1:T(8,128)(2,1)S(1)}, bf16[128,3,128]{2,0,1:T(8,128)(2,1)}, u32[]{:S(2)}) copy-start(bf16[128,3,128]{2,0,1:T(8,128)(2,1)} %param.7) | copy-start | bytes 294916
  95.5 53.2 %copy-start.5 = (bf16[128,3,128]{2,0,1:T(8,128)(2,1)S(1)}, bf16[128,3,128]{2,0,1:T(8,128)(2,1)}, u32[]{:S(2)}) copy-start(bf16[128,3,128]{2,0,1:T(8,128)(2,1)} %param.8) | copy-start | bytes 294916
  104.2 5.3 %collective-permute-start.13 = (bf16[6,128,128]{2,1,0:T(8,128)(2,1)S(1)}, bf16[6,128,128]{2,1,0:T(8,128)(2,1)S(1)}, u32[]{:S(2)}, u32[]{:S(2)}) collective-permute-start(bf16[6,128,128]{2,1,0:T(8,128)(2,1)S(1)} %add_convert_fusion.3), channel_id=1, source_target_pairs={{1,17},{9,25},{16,0},{17,33},{24,8},{25,41},{32,16},{33,49},{40,24... | collective-permute-start | bytes 589832 | tf_op jit(solution)/shard_map/ppermute | solution.py:237
  105.6 9.4 %collective-permute-start.14 = (bf16[6,128,128]{2,1,0:T(8,128)(2,1)S(1)}, bf16[6,128,128]{2,1,0:T(8,128)(2,1)S(1)}, u32[]{:S(2)}, u32[]{:S(2)}) collective-permute-start(bf16[6,128,128]{2,1,0:T(8,128)(2,1)S(1)} %add_convert_fusion.2), channel_id=1, source_target_pairs={{0,16},{8,24},{16,32},{17,1},{24,40},{25,9},{32,48},{33,17},{40,56... | collective-permute-start | bytes 589832 | tf_op jit(solution)/shard_map/ppermute | solution.py:237
  106.9 26.8 %collective-permute-start.17 = (bf16[6,128,128]{2,1,0:T(8,128)(2,1)S(1)}, bf16[6,128,128]{2,1,0:T(8,128)(2,1)S(1)}, u32[]{:S(2)}, u32[]{:S(2)}) collective-permute-start(bf16[6,128,128]{2,1,0:T(8,128)(2,1)S(1)} %get-tuple-element.68), channel_id=1, source_target_pairs={{1,9},{8,0},{9,17},{16,8},{17,25},{24,16},{25,33},{32,24},{33,41},... | collective-permute-start | bytes 589832 | tf_op jit(solution)/shard_map/ppermute | solution.py:237
  108.2 26.8 %collective-permute-start.18 = (bf16[6,128,128]{2,1,0:T(8,128)(2,1)S(1)}, bf16[6,128,128]{2,1,0:T(8,128)(2,1)S(1)}, u32[]{:S(2)}, u32[]{:S(2)}) collective-permute-start(bf16[6,128,128]{2,1,0:T(8,128)(2,1)S(1)} %get-tuple-element.69), channel_id=1, source_target_pairs={{0,8},{8,16},{9,1},{16,24},{17,9},{24,32},{25,17},{32,40},{33,25},... | collective-permute-start | bytes 589832 | tf_op jit(solution)/shard_map/ppermute | solution.py:237
  115.0 28.2 %collective-permute-start.15 = (bf16[6,128,128]{2,1,0:T(8,128)(2,1)S(1)}, bf16[6,128,128]{2,1,0:T(8,128)(2,1)S(1)}, u32[]{:S(2)}, u32[]{:S(2)}) collective-permute-start(bf16[6,128,128]{2,1,0:T(8,128)(2,1)S(1)} %add_convert_fusion.1), channel_id=1, source_target_pairs={{1,17},{9,25},{16,0},{17,33},{24,8},{25,41},{32,16},{33,49},{40,24... | collective-permute-start | bytes 589832 | tf_op jit(solution)/shard_map/ppermute | solution.py:237
  120.6 22.6 %collective-permute-start.16 = (bf16[6,128,128]{2,1,0:T(8,128)(2,1)S(1)}, bf16[6,128,128]{2,1,0:T(8,128)(2,1)S(1)}, u32[]{:S(2)}, u32[]{:S(2)}) collective-permute-start(bf16[6,128,128]{2,1,0:T(8,128)(2,1)S(1)} %add_convert_fusion), channel_id=1, source_target_pairs={{0,16},{8,24},{16,32},{17,1},{24,40},{25,9},{32,48},{33,17},{40,56... | collective-permute-start | bytes 589832 | tf_op jit(solution)/shard_map/ppermute | solution.py:237
  121.9 21.4 %collective-permute-start.19 = (bf16[6,128,128]{2,1,0:T(8,128)(2,1)S(1)}, bf16[6,128,128]{2,1,0:T(8,128)(2,1)S(1)}, u32[]{:S(2)}, u32[]{:S(2)}) collective-permute-start(bf16[6,128,128]{2,1,0:T(8,128)(2,1)S(1)} %get-tuple-element.70), channel_id=1, source_target_pairs={{1,129},{9,137},{17,145},{25,153},{33,161},{41,169},{49,177},{57,1... | collective-permute-start | bytes 589832 | tf_op jit(solution)/shard_map/ppermute | solution.py:237
  133.7 9.5 %collective-permute-start.20 = (bf16[6,128,128]{2,1,0:T(8,128)(2,1)S(1)}, bf16[6,128,128]{2,1,0:T(8,128)(2,1)S(1)}, u32[]{:S(2)}, u32[]{:S(2)}) collective-permute-start(bf16[6,128,128]{2,1,0:T(8,128)(2,1)S(1)} %get-tuple-element.71), channel_id=1, source_target_pairs={{0,128},{8,136},{16,144},{24,152},{32,160},{40,168},{48,176},{56,1... | collective-permute-start | bytes 589832 | tf_op jit(solution)/shard_map/ppermute | solution.py:237
  135.0 13.7 %collective-permute-start.21 = (bf16[6,128,128]{2,1,0:T(8,128)(2,1)S(1)}, bf16[6,128,128]{2,1,0:T(8,128)(2,1)S(1)}, u32[]{:S(2)}, u32[]{:S(2)}) collective-permute-start(bf16[6,128,128]{2,1,0:T(8,128)(2,1)S(1)} %get-tuple-element.72), channel_id=1, source_target_pairs={{0,256},{8,264},{16,272},{24,280},{32,288},{40,296},{48,304},{56,3... | collective-permute-start | bytes 589832 | tf_op jit(solution)/shard_map/ppermute | solution.py:242

commit v8 on v7

--- a/solution.py
+++ b/solution.py
@@ -53,7 +53,19 @@
     return (at >= 0) & (at < line * lines)
 
 
-def squares_kernel(heads, q_ref, k_ref, out_ref):
+def fetch(sources, targets, sems):
+    copies = [
+        pltpu.make_async_copy(source, target, sems.at[at])
+        for at, (source, target) in enumerate(zip(sources, targets))
+    ]
+    for copy in copies:
+        copy.start()
+    for copy in copies:
+        copy.wait()
+
+
+def squares_kernel(heads, q_hbm, k_hbm, out_ref, q_ref, k_ref, sems):
+    fetch((q_hbm, k_hbm), (q_ref, k_ref), sems)
     out_ref[...] = jnp.zeros(out_ref.shape, F32)
     for row, ref in enumerate((q_ref, k_ref)):
         total = jnp.zeros((TILE, TILE), F32)
@@ -72,7 +84,10 @@
     return total
 
 
-def norm_kernel(heads, channels, sums_ref, q_ref, k_ref, v_ref, gain_ref, qn_ref, kv_ref, inverse_ref):
+def norm_kernel(
+    heads, channels, sums_ref, gain_ref, q_hbm, k_hbm, v_hbm, qn_ref, kv_ref, inverse_ref, q_ref, k_ref, sems
+):
+    fetch((q_hbm, k_hbm, v_hbm), (q_ref, k_ref, kv_ref.at[pl.ds(heads, heads)]), sems)
     inverse = lax.rsqrt(group_sum(sums_ref) / channels + EPS)
     inverse_ref[...] = inverse
     turned = columns(inverse)
@@ -83,7 +98,6 @@
         kv_ref[head] = (
             k_ref[head].astype(F32) * turned[:, 1:2] * gain_ref[heads + head : heads + head + 1]
         ).astype(BF16)
-        kv_ref[heads + head] = v_ref[head]
 
 
 def early_kernel(heads, places, q_ref, *refs):
@@ -125,41 +139,53 @@
     usable = [inside(place) for place in places]
     lane = lax.broadcasted_iota(jnp.int32, (TILE, TILE), 1)
     rows = jnp.zeros((TILE, TILE), F32)
-    for head in range(heads):
-        query, upstream = q_ref[head], do_ref[head]
+    every = range(heads)
+    scores = [
+        [jnp.where(use, dot(q_ref[head], tile[head], NT) * scale, -1e30) for use, tile in zip(usable, tiles)]
+        for head in every
+    ]
+    dprobs = [[dot(do_ref[head], tile[heads + head], NT) for tile in tiles] for head in every]
+    weights, keeps, shares, outs, deltas = [], [], [], [], []
+    for head in every:
         early_top = rows_ref[:, head : head + 1]
-        scores = []
-        top = jnp.full((TILE, TILE), -1e30, F32)
-        for t, tile in enumerate(tiles):
-            score = dot(query, tile[head], NT) * scale
-            score = jnp.where(usable[t], score, -1e30)
-            scores.append(score)
+        top = scores[head][0]
+        for score in scores[head][1:]:
             top = jnp.maximum(top, score)
         top = jnp.maximum(early_top, jnp.max(top, axis=1, keepdims=True))
-        keep = jnp.exp(early_top - top)
-        out = early_ref[head] * keep
-        weights = [jnp.exp(score - top) for score in scores]
-        total = weights[0]
-        for weight in weights[1:]:
+        keeps.append(jnp.exp(early_top - top))
+        weights.append([jnp.exp(score - top) for score in scores[head]])
+        total = weights[head][0]
+        for weight in weights[head][1:]:
             total = total + weight
         total = jnp.sum(total, axis=1, keepdims=True)
-        for t, tile in enumerate(tiles):
-            out = out + dot(weights[t].astype(BF16), tile[heads + head], NN)
-        share = 1.0 / (total + rows_ref[:, heads + head : heads + head + 1] * keep)
-        out = (out * share).astype(BF16)
-        out_ref[head] = out
-        delta = jnp.sum(upstream.astype(F32) * out.astype(F32), axis=1, keepdims=True)
+        total = total + rows_ref[:, heads + head : heads + head + 1] * keeps[head]
+        shares.append(1.0 / total)
+    for head in every:
+        out = early_ref[head] * keeps[head]
+        for weight, tile in zip(weights[head], tiles):
+            out = out + dot(weight.astype(BF16), tile[heads + head], NN)
+        outs.append((out * shares[head]).astype(BF16))
+        deltas.append(
+            jnp.sum(do_ref[head].astype(F32) * outs[head].astype(F32), axis=1, keepdims=True)
+        )
+    probs = [[weight * shares[head] for weight in weights[head]] for head in every]
+    dscores = [
+        [(prob * (dprob - deltas[head])).astype(BF16) for prob, dprob in zip(probs[head], dprobs[head])]
+        for head in every
+    ]
+    value_parts = [[dot(prob.astype(BF16), do_ref[head], TN) for prob in probs[head]] for head in every]
+    key_parts = [[dot(dscore, q_ref[head], TN) * scale for dscore in dscores[head]] for head in every]
+    for head in every:
         query_grad = jnp.zeros((TILE, TILE), F32)
-        for t, tile in enumerate(tiles):
-            prob = weights[t] * share
-            part = part_refs[t]
-            part[heads + head] = dot(prob.astype(BF16), upstream, TN).astype(part.dtype)
-            dscore = (prob * (dot(upstream, tile[heads + head], NT) - delta)).astype(BF16)
-            part[head] = (dot(dscore, query, TN) * scale).astype(part.dtype)
+        for dscore, tile in zip(dscores[head], tiles):
             query_grad = query_grad + dot(dscore, tile[head], NN)
+        rows = jnp.where(lane == head, keeps[head] * shares[head], rows)
+        rows = jnp.where(lane == heads + head, deltas[head], rows)
+        for t, part in enumerate(part_refs):
+            part[head] = key_parts[head][t].astype(part.dtype)
+            part[heads + head] = value_parts[head][t].astype(part.dtype)
+        out_ref[head] = outs[head]
         dq_ref[head] = query_grad
-        rows = jnp.where(lane == head, keep * share, rows)
-        rows = jnp.where(lane == heads + head, delta, rows)
     late_rows_ref[...] = rows
 
 
@@ -171,14 +197,17 @@
         query, upstream = q_ref[head], do_ref[head]
         share = rows_ref[:, head : head + 1]
         delta = rows_ref[:, heads + head : heads + head + 1]
+        dprobs = [dot(upstream, tile[heads + head], NT) for tile in tiles]
+        probs = [weight_ref[head, t] * share for t in range(count)]
+        dscores = [(prob * (dprob - delta)).astype(BF16) for prob, dprob in zip(probs, dprobs)]
         query_grad = late_dq_ref[head]
-        for t, tile in enumerate(tiles):
-            prob = weight_ref[head, t] * share
-            part = part_refs[t]
-            part[heads + head] = dot(prob.astype(BF16), upstream, TN).astype(part.dtype)
-            dscore = (prob * (dot(upstream, tile[heads + head], NT) - delta)).astype(BF16)
-            part[head] = (dot(dscore, query, TN) * scale).astype(part.dtype)
+        for dscore, tile in zip(dscores, tiles):
             query_grad = query_grad + dot(dscore, tile[head], NN)
+        value_parts = [dot(prob.astype(BF16), upstream, TN) for prob in probs]
+        key_parts = [dot(dscore, query, TN) * scale for dscore in dscores]
+        for part, key_part, value_part in zip(part_refs, key_parts, value_parts):
+            part[head] = key_part.astype(part.dtype)
+            part[heads + head] = value_part.astype(part.dtype)
         dq_ref[head] = query_grad * scale
 
 
@@ -254,9 +283,17 @@
 
 
 def collect(parts):
+    line = lax.axis_size("z")
     places = [len(NEAR) - 2, len(NEAR) - 1]
     carried = [parts[place] for place in places]
-    far = [parts[len(NEAR) + place] for place in range(FAR)]
+    others = [
+        lambda: passed(parts[1], NEAR[1]),
+        lambda: passed(parts[2], NEAR[2]),
+        lambda: half_round(parts[len(NEAR) + 2]),
+        lambda: passed(parts[len(NEAR)], -line),
+        lambda: passed(parts[len(NEAR) + 1], line),
+    ]
+    arrived = []
     while True:
         steps = [NEAR[place] - relay(NEAR[place]) for place in places]
         through = relay(NEAR[places[0]])
@@ -264,18 +301,14 @@
         if not through:
             break
         places = [place - 2 for place in places]
-        carried, far = lax.optimization_barrier((carried, far))
+        carried = lax.optimization_barrier(carried)
         carried = [
             (part.astype(F32) + parts[place]).astype(BF16) for part, place in zip(carried, places)
         ]
-    line = lax.axis_size("z")
-    return [
-        *carried,
-        *(passed(parts[place], NEAR[place]) for place in (1, 2)),
-        passed(far[0], -line),
-        passed(far[1], line),
-        half_round(far[2]),
-    ]
+        arrived += [send() for send in others[:3]]
+        others = others[3:]
+        carried, arrived = lax.optimization_barrier((carried, arrived))
+    return carried + arrived + [send() for send in others]
 
 
 def per_device(total_heads, q_raw, k_raw, values, grad_out, q_gain, k_gain, key_tiles):
@@ -293,11 +326,11 @@
     params = pltpu.CompilerParams(vmem_limit_bytes=VMEM_LIMIT)
     whole, pair = (heads, TILE, TILE), (2 * heads, TILE, TILE)
 
-    def call(kernel, name, out_shape, *operands, scratch=()):
+    def call(kernel, name, out_shape, *operands, scratch=(), raw=0):
         return pl.pallas_call(
             kernel,
             out_shape=[jax.ShapeDtypeStruct(shape, dtype) for shape, dtype in out_shape],
-            in_specs=[vmem] * len(operands),
+            in_specs=[vmem] * (len(operands) - raw) + [pl.BlockSpec(memory_space=pltpu.HBM)] * raw,
             out_specs=[vmem] * len(out_shape),
             scratch_shapes=list(scratch),
             compiler_params=params,
@@ -305,13 +338,23 @@
         )(*operands)
 
     rows = ((groups, 8, TILE), F32)
-    (squares,) = call(functools.partial(squares_kernel, heads), "squares", [rows], q_raw, k_raw)
+    held = [pltpu.VMEM(whole, BF16)] * 2
+    (squares,) = call(
+        functools.partial(squares_kernel, heads),
+        "squares",
+        [rows],
+        q_raw, k_raw,
+        scratch=held + [pltpu.SemaphoreType.DMA((2,))],
+        raw=2,
+    )
     sums = lax.all_to_all(squares, HEAD, 0, 0, tiled=True)
     q_norm, pairs, inverse = call(
         functools.partial(norm_kernel, heads, channels),
         "norm",
         [(whole, BF16), (pair, BF16), ((8, TILE), F32)],
-        sums, q_raw, k_raw, values, gains,
+        sums, gains, q_raw, k_raw, values,
+        scratch=held + [pltpu.SemaphoreType.DMA((3,))],
+        raw=3,
     )
     tiles = spread(pairs) + [passed(pairs, line), passed(pairs, -line), half_round(pairs)]
     late = [near - 2, near - 1]

time: 160 us -> 160 us (level)
  the two profiles are of different devices: /device:TPU:1 before, /device:TPU:7 now
where the time goes in v8:
time: 160 us; the launch traced here: 158 us
  starting transfers between devices  101 us (63%)
  waiting for transfers between devices  32 us (20%)
  blocking collectives  10.3 us (6%)
  Pallas kernels  8.24 us (5%)
  local copies, waits for them, and re-layouts  4.47 us (3%)
    ppermute x20, starting transfers between devices, passed(): return lax.ppermute(value, SEQ + ('c',), pairs)  87 us
    ppermute x20, waiting for transfers between devices, passed(): return lax.ppermute(value, SEQ + ('c',), pairs)  27.6 us
    all_to_all x1, blocking collectives, per_device(): terms = lax.all_to_all(terms, HEAD, 0, 0, tiled=True)  10.3 us
    ppermute x2, starting transfers between devices, half_round(): lax.ppermute(value, SEQ, [(i, (i + count // 2) % count) for i in range(co...  8.5 us
    pallas_call x7, Pallas kernels, call(): pl.pallas_call(kernel, out_shape=[jax.ShapeDtypeStruct(shape, dtype) for...  8.24 us
    all_to_all x1, starting transfers between devices, per_device(): sums = lax.all_to_all(squares, HEAD, 0, 0, tiled=True)  5.15 us
    unnamed x16, local copies, waits for them, and re-layouts  4.47 us
    all_to_all x1, waiting for transfers between devices, per_device(): sums = lax.all_to_all(squares, HEAD, 0, 0, tiled=True)  4.01 us
  transfers between devices with their start and end apart: 23, of which 10 were waited for; matrix products, arithmetic and copies ran while one was open for 1% of the time, Pallas kernels for 2%

profile of v8, /device:TPU:7, one launch (start us, length us, event | category | flops | bytes accessed | tf_op | source)
XLA Modules:
  0.0 157.5 jit_solution(2794897614667438314)
XLA Ops:
  0.6 0.9 copy-done
  1.5 0.9 copy-done.3
  2.4 1.1 squares.1
  3.5 5.2 %all-to-all-start = ((f32[8,8,128]{2,1,0:T(8,128)}), f32[8,8,128]{2,1,0:T(8,128)S(1)}, u32[]{:S(2)}, u32[]{:S(2)}) async-start(f32[8,8,128]{2,1,0:T(8,128)} %squares.1), calls=%async_computation | async-start | bytes 65536 | tf_op jit(solution)/shard_map/all_to_all | solution.py:350
  8.7 0.7 pad_maximum_fusion.gain_ref
  9.4 4.0 %all-to-all-done.sums_ref = f32[8,8,128]{2,1,0:T(8,128)S(1)} async-done(((f32[8,8,128]{2,1,0:T(8,128)}), f32[8,8,128]{2,1,0:T(8,128)S(1)}, u32[]{:S(2)}, u32[]{:S(2)}) %all-to-all-start) | async-done | bytes 32800 | tf_op jit(solution)/shard_map/all_to_all | solution.py:350
  13.4 0.9 copy-done.1
  14.3 0.9 copy-done.4
  15.2 0.9 copy-done.7
  16.1 0.6 norm.1
  16.7 4.9 %collective-permute-start.3 = (bf16[6,128,128]{2,1,0:T(8,128)(2,1)S(1)}, bf16[6,128,128]{2,1,0:T(8,128)(2,1)S(1)}, u32[]{:S(2)}, u32[]{:S(2)}) collective-permute-start(bf16[6,128,128]{2,1,0:T(8,128)(2,1)S(1)} %get-tuple-element.48.refs_0_), channel_id=1, source_target_pairs={{1,17},{9,25},{16,0},{17,33},{24,8},{25,41},{32,16},{33,49},{40,24... | collective-permute-start | bytes 589832 | tf_op jit(solution)/shard_map/ppermute | solution.py:266
  21.6 8.9 %collective-permute-start.2 = (bf16[6,128,128]{2,1,0:T(8,128)(2,1)S(1)}, bf16[6,128,128]{2,1,0:T(8,128)(2,1)S(1)}, u32[]{:S(2)}, u32[]{:S(2)}) collective-permute-start(bf16[6,128,128]{2,1,0:T(8,128)(2,1)S(1)} %get-tuple-element.48.refs_0_), channel_id=1, source_target_pairs={{0,16},{8,24},{16,32},{17,1},{24,40},{25,9},{32,48},{33,17},{40,56... | collective-permute-start | bytes 589832 | tf_op jit(solution)/shard_map/ppermute | solution.py:266
  30.4 2.7 %collective-permute-start.8 = (bf16[6,128,128]{2,1,0:T(8,128)(2,1)S(1)}, bf16[6,128,128]{2,1,0:T(8,128)(2,1)S(1)}, u32[]{:S(2)}, u32[]{:S(2)}) collective-permute-start(bf16[6,128,128]{2,1,0:T(8,128)(2,1)S(1)} %get-tuple-element.48.refs_0_), channel_id=1, source_target_pairs={{0,256},{8,264},{16,272},{24,280},{32,288},{40,296},{48,304},{56,3... | collective-permute-start | bytes 589832 | tf_op jit(solution)/shard_map/ppermute | solution.py:271
  33.2 1.3 collective-permute-start.7
  34.5 1.9 %collective-permute-start.5 = (bf16[6,128,128]{2,1,0:T(8,128)(2,1)S(1)}, bf16[6,128,128]{2,1,0:T(8,128)(2,1)S(1)}, u32[]{:S(2)}, u32[]{:S(2)}) collective-permute-start(bf16[6,128,128]{2,1,0:T(8,128)(2,1)S(1)} %collective-permute-done.3.refs_4_), channel_id=1, source_target_pairs={{1,17},{9,25},{16,0},{17,33},{24,8},{25,41},{32,16},{33,49},{40,24... | collective-permute-start | bytes 589832 | tf_op jit(solution)/shard_map/ppermute | solution.py:266
  36.4 2.2 %collective-permute-done.2.refs_3_ = bf16[6,128,128]{2,1,0:T(8,128)(2,1)S(1)} collective-permute-done((bf16[6,128,128]{2,1,0:T(8,128)(2,1)S(1)}, bf16[6,128,128]{2,1,0:T(8,128)(2,1)S(1)}, u32[]{:S(2)}, u32[]{:S(2)}) %collective-permute-start.2) | collective-permute-done | bytes 196640 | tf_op jit(solution)/shard_map/ppermute | solution.py:266
  38.6 6.9 %collective-permute-start.4 = (bf16[6,128,128]{2,1,0:T(8,128)(2,1)S(1)}, bf16[6,128,128]{2,1,0:T(8,128)(2,1)S(1)}, u32[]{:S(2)}, u32[]{:S(2)}) collective-permute-start(bf16[6,128,128]{2,1,0:T(8,128)(2,1)S(1)} %collective-permute-done.2.refs_3_), channel_id=1, source_target_pairs={{0,16},{8,24},{16,32},{17,1},{24,40},{25,9},{32,48},{33,17},{40,56... | collective-permute-start | bytes 589832 | tf_op jit(solution)/shard_map/ppermute | solution.py:266
  45.5 3.1 %collective-permute-start.6 = (bf16[6,128,128]{2,1,0:T(8,128)(2,1)S(1)}, bf16[6,128,128]{2,1,0:T(8,128)(2,1)S(1)}, u32[]{:S(2)}, u32[]{:S(2)}) collective-permute-start(bf16[6,128,128]{2,1,0:T(8,128)(2,1)S(1)} %get-tuple-element.48.refs_0_), channel_id=1, source_target_pairs={{0,128},{8,136},{16,144},{24,152},{32,160},{40,168},{48,176},{56,1... | collective-permute-start | bytes 589832 | tf_op jit(solution)/shard_map/ppermute | solution.py:266
  48.7 1.9 %collective-permute-start.1 = (bf16[6,128,128]{2,1,0:T(8,128)(2,1)S(1)}, bf16[6,128,128]{2,1,0:T(8,128)(2,1)S(1)}, u32[]{:S(2)}, u32[]{:S(2)}) collective-permute-start(bf16[6,128,128]{2,1,0:T(8,128)(2,1)S(1)} %get-tuple-element.48.refs_0_), channel_id=1, source_target_pairs={{1,9},{8,0},{9,17},{16,8},{17,25},{24,16},{25,33},{32,24},{33,41},... | collective-permute-start | bytes 589832 | tf_op jit(solution)/shard_map/ppermute | solution.py:266
  50.6 5.5 %collective-permute-start = (bf16[6,128,128]{2,1,0:T(8,128)(2,1)S(1)}, bf16[6,128,128]{2,1,0:T(8,128)(2,1)S(1)}, u32[]{:S(2)}, u32[]{:S(2)}) collective-permute-start(bf16[6,128,128]{2,1,0:T(8,128)(2,1)S(1)} %get-tuple-element.48.refs_0_), channel_id=1, source_target_pairs={{0,8},{8,16},{9,1},{16,24},{17,9},{24,32},{25,17},{32,40},{33,25},... | collective-permute-start | bytes 589832 | tf_op jit(solution)/shard_map/ppermute | solution.py:266
  56.1 1.9 %collective-permute-start.10 = (bf16[6,128,128]{2,1,0:T(8,128)(2,1)S(1)}, bf16[6,128,128]{2,1,0:T(8,128)(2,1)S(1)}, u32[]{:S(2)}, u32[]{:S(2)}) collective-permute-start(bf16[6,128,128]{2,1,0:T(8,128)(2,1)S(1)} %collective-permute-done.5.refs_6_), channel_id=1, source_target_pairs={{1,33},{9,41},{17,49},{25,57},{32,0},{33,65},{40,8},{41,73},{48,16... | collective-permute-start | bytes 589832 | tf_op jit(solution)/shard_map/ppermute | solution.py:266
  58.0 8.2 %collective-permute-start.9 = (bf16[6,128,128]{2,1,0:T(8,128)(2,1)S(1)}, bf16[6,128,128]{2,1,0:T(8,128)(2,1)S(1)}, u32[]{:S(2)}, u32[]{:S(2)}) collective-permute-start(bf16[6,128,128]{2,1,0:T(8,128)(2,1)S(1)} %collective-permute-done.4.refs_5_), channel_id=1, source_target_pairs={{0,32},{8,40},{16,48},{24,56},{32,64},{33,1},{40,72},{41,9},{48,80... | collective-permute-start | bytes 589832 | tf_op jit(solution)/shard_map/ppermute | solution.py:266
  66.2 1.4 early.1
  67.6 2.4 %collective-permute-done.10.refs_1_ = bf16[6,128,128]{2,1,0:T(8,128)(2,1)S(1)} collective-permute-done((bf16[6,128,128]{2,1,0:T(8,128)(2,1)S(1)}, bf16[6,128,128]{2,1,0:T(8,128)(2,1)S(1)}, u32[]{:S(2)}, u32[]{:S(2)}) %collective-permute-start.10) | collective-permute-done | bytes 196640 | tf_op jit(solution)/shard_map/ppermute | solution.py:266
  70.0 8.4 %collective-permute-done.9.refs_0_ = bf16[6,128,128]{2,1,0:T(8,128)(2,1)S(1)} collective-permute-done((bf16[6,128,128]{2,1,0:T(8,128)(2,1)S(1)}, bf16[6,128,128]{2,1,0:T(8,128)(2,1)S(1)}, u32[]{:S(2)}, u32[]{:S(2)}) %collective-permute-start.9) | collective-permute-done | bytes 196640 | tf_op jit(solution)/shard_map/ppermute | solution.py:266
  78.4 1.7 %late.1 = (bf16[3,128,128]{2,1,0:T(8,128)(2,1)}, f32[3,128,128]{2,1,0:T(8,128)S(1)}, f32[128,128]{1,0:T(8,128)S(1)}, bf16[6,128,128]{2,1,0:T(8,128)(2,1)S(1)}, bf16[6,128,128]{2,1,0:T(8,128)(2,1)S(1)}) custom-call(bf16[3,128,128]{2,1,0:T(8,128)(2,1)S(1)} %get-tuple-element.47.q_ref, bf16[3,128,128]{2,1,0:T(8,128)(2,1)S(1)} %bitcast.16, ...), custom_call_target="tpu_custom_call" | custom-call | tf_op jit(solution)/shard_map/late/pallas_call | solution.py:330
  80.1 2.3 %collective-permute-start.11 = (bf16[6,128,128]{2,1,0:T(8,128)(2,1)S(1)}, bf16[6,128,128]{2,1,0:T(8,128)(2,1)S(1)}, u32[]{:S(2)}, u32[]{:S(2)}) collective-permute-start(bf16[6,128,128]{2,1,0:T(8,128)(2,1)S(1)} %get-tuple-element.58), channel_id=1, source_target_pairs={{1,33},{9,41},{17,49},{25,57},{32,0},{33,65},{40,8},{41,73},{48,16... | collective-permute-start | bytes 589832 | tf_op jit(solution)/shard_map/ppermute | solution.py:266
  82.4 7.8 %collective-permute-start.12 = (bf16[6,128,128]{2,1,0:T(8,128)(2,1)S(1)}, bf16[6,128,128]{2,1,0:T(8,128)(2,1)S(1)}, u32[]{:S(2)}, u32[]{:S(2)}) collective-permute-start(bf16[6,128,128]{2,1,0:T(8,128)(2,1)S(1)} %get-tuple-element.59), channel_id=1, source_target_pairs={{0,32},{8,40},{16,48},{24,56},{32,64},{33,1},{40,72},{41,9},{48,80... | collective-permute-start | bytes 589832 | tf_op jit(solution)/shard_map/ppermute | solution.py:266
  90.2 1.6 %rest.1 = (f32[3,128,128]{2,1,0:T(8,128)S(1)}, f32[6,128,128]{2,1,0:T(8,128)S(1)}, bf16[6,128,128]{2,1,0:T(8,128)(2,1)S(1)}, bf16[6,128,128]{2,1,0:T(8,128)(2,1)...) custom-call(bf16[3,128,128]{2,1,0:T(8,128)(2,1)S(1)} %get-tuple-elem, ...), custom_call_target="tpu_custom_call" | custom-call | tf_op jit(solution)/shard_map/rest/pallas_call | solution.py:330
  91.9 4.4 %collective-permute-start.13 = (bf16[6,128,128]{2,1,0:T(8,128)(2,1)S(1)}, bf16[6,128,128]{2,1,0:T(8,128)(2,1)S(1)}, u32[]{:S(2)}, u32[]{:S(2)}) collective-permute-start(bf16[6,128,128]{2,1,0:T(8,128)(2,1)S(1)} %get-tuple-element.64), channel_id=1, source_target_pairs={{1,9},{8,0},{9,17},{16,8},{17,25},{24,16},{25,33},{32,24},{33,41},... | collective-permute-start | bytes 589832 | tf_op jit(solution)/shard_map/ppermute | solution.py:266
  96.3 4.0 %collective-permute-start.14 = (bf16[6,128,128]{2,1,0:T(8,128)(2,1)S(1)}, bf16[6,128,128]{2,1,0:T(8,128)(2,1)S(1)}, u32[]{:S(2)}, u32[]{:S(2)}) collective-permute-start(bf16[6,128,128]{2,1,0:T(8,128)(2,1)S(1)} %get-tuple-element.65), channel_id=1, source_target_pairs={{0,8},{8,16},{9,1},{16,24},{17,9},{24,32},{25,17},{32,40},{33,25},... | collective-permute-start | bytes 589832 | tf_op jit(solution)/shard_map/ppermute | solution.py:266
  100.2 5.8 %collective-permute-start.15 = (bf16[6,128,128]{2,1,0:T(8,128)(2,1)S(1)}, bf16[6,128,128]{2,1,0:T(8,128)(2,1)S(1)}, u32[]{:S(2)}, u32[]{:S(2)}) collective-permute-start(bf16[6,128,128]{2,1,0:T(8,128)(2,1)S(1)} %get-tuple-element.66), channel_id=1, source_target_pairs={{0,256},{8,264},{16,272},{24,280},{32,288},{40,296},{48,304},{56,3... | collective-permute-start | bytes 589832 | tf_op jit(solution)/shard_map/ppermute | solution.py:271
  106.0 1.1 collective-permute-done.12
  107.2 2.8 %collective-permute-done.14.refs_4_ = bf16[6,128,128]{2,1,0:T(8,128)(2,1)S(1)} collective-permute-done((bf16[6,128,128]{2,1,0:T(8,128)(2,1)S(1)}, bf16[6,128,128]{2,1,0:T(8,128)(2,1)S(1)}, u32[]{:S(2)}, u32[]{:S(2)}) %collective-permute-start.14) | collective-permute-done | bytes 196640 | tf_op jit(solution)/shard_map/ppermute | solution.py:266
  110.0 0.4 collective-permute-done.15.refs_5_
  110.4 2.3 %collective-permute-start.16 = (bf16[6,128,128]{2,1,0:T(8,128)(2,1)S(1)}, bf16[6,128,128]{2,1,0:T(8,128)(2,1)S(1)}, u32[]{:S(2)}, u32[]{:S(2)}) collective-permute-start(bf16[6,128,128]{2,1,0:T(8,128)(2,1)S(1)} %add_convert_fusion.3), channel_id=1, source_target_pairs={{1,17},{9,25},{16,0},{17,33},{24,8},{25,41},{32,16},{33,49},{40,24... | collective-permute-start | bytes 589832 | tf_op jit(solution)/shard_map/ppermute | solution.py:266
  112.7 5.9 %collective-permute-start.17 = (bf16[6,128,128]{2,1,0:T(8,128)(2,1)S(1)}, bf16[6,128,128]{2,1,0:T(8,128)(2,1)S(1)}, u32[]{:S(2)}, u32[]{:S(2)}) collective-permute-start(bf16[6,128,128]{2,1,0:T(8,128)(2,1)S(1)} %add_convert_fusion.2), channel_id=1, source_target_pairs={{0,16},{8,24},{16,32},{17,1},{24,40},{25,9},{32,48},{33,17},{40,56... | collective-permute-start | bytes 589832 | tf_op jit(solution)/shard_map/ppermute | solution.py:266
  118.7 1.3 collective-permute-start.18
  120.0 6.2 %collective-permute-start.19 = (bf16[6,128,128]{2,1,0:T(8,128)(2,1)S(1)}, bf16[6,128,128]{2,1,0:T(8,128)(2,1)S(1)}, u32[]{:S(2)}, u32[]{:S(2)}) collective-permute-start(bf16[6,128,128]{2,1,0:T(8,128)(2,1)S(1)} %get-tuple-element.77), channel_id=1, source_target_pairs={{0,128},{8,136},{16,144},{24,152},{32,160},{40,168},{48,176},{56,1... | collective-permute-start | bytes 589832 | tf_op jit(solution)/shard_map/ppermute | solution.py:266
  126.2 0.1 add_convert_fusion
  126.3 4.0 %collective-permute-done.18.refs_6_ = bf16[6,128,128]{2,1,0:T(8,128)(2,1)S(1)} collective-permute-done((bf16[6,128,128]{2,1,0:T(8,128)(2,1)S(1)}, bf16[6,128,128]{2,1,0:T(8,128)(2,1)S(1)}, u32[]{:S(2)}, u32[]{:S(2)}) %collective-permute-start.18) | collective-permute-done | bytes 196640 | tf_op jit(solution)/shard_map/ppermute | solution.py:266
  130.3 1.9 %collective-permute-start.20 = (bf16[6,128,128]{2,1,0:T(8,128)(2,1)S(1)}, bf16[6,128,128]{2,1,0:T(8,128)(2,1)S(1)}, u32[]{:S(2)}, u32[]{:S(2)}) collective-permute-start(bf16[6,128,128]{2,1,0:T(8,128)(2,1)S(1)} %get-tuple-element.78), channel_id=1, source_target_pairs={{1,17},{9,25},{16,0},{17,33},{24,8},{25,41},{32,16},{33,49},{40,24... | collective-permute-start | bytes 589832 | tf_op jit(solution)/shard_map/ppermute | solution.py:266
  132.2 6.4 %collective-permute-start.21 = (bf16[6,128,128]{2,1,0:T(8,128)(2,1)S(1)}, bf16[6,128,128]{2,1,0:T(8,128)(2,1)S(1)}, u32[]{:S(2)}, u32[]{:S(2)}) collective-permute-start(bf16[6,128,128]{2,1,0:T(8,128)(2,1)S(1)} %get-tuple-element.79), channel_id=1, source_target_pairs={{0,16},{8,24},{16,32},{17,1},{24,40},{25,9},{32,48},{33,17},{40,56... | collective-permute-start | bytes 589832 | tf_op jit(solution)/shard_map/ppermute | solution.py:266
  138.6 2.6 %collective-permute-done.20.refs_1_ = bf16[6,128,128]{2,1,0:T(8,128)(2,1)S(1)} collective-permute-done((bf16[6,128,128]{2,1,0:T(8,128)(2,1)S(1)}, bf16[6,128,128]{2,1,0:T(8,128)(2,1)S(1)}, u32[]{:S(2)}, u32[]{:S(2)}) %collective-permute-start.20) | collective-permute-done | bytes 196640 | tf_op jit(solution)/shard_map/ppermute | solution.py:266
  141.1 4.1 %collective-permute-done.21.refs_2_ = bf16[6,128,128]{2,1,0:T(8,128)(2,1)S(1)} collective-permute-done((bf16[6,128,128]{2,1,0:T(8,128)(2,1)S(1)}, bf16[6,128,128]{2,1,0:T(8,128)(2,1)S(1)}, u32[]{:S(2)}, u32[]{:S(2)}) %collective-permute-start.21) | collective-permute-done | bytes 196640 | tf_op jit(solution)/shard_map/ppermute | solution.py:266
  145.3 1.0 terms.1
  146.3 10.3 %all_to_all.10.terms_ref = f32[8,8,128]{2,1,0:T(8,128)S(1)} all-to-all(f32[8,8,128]{2,1,0:T(8,128)S(1)} %get-tuple-element.85), channel_id=1, replica_groups=mesh['x'=4,'z'=16,'y'=4,'c'=2] {'y','c'}, dimensions={0} | all-to-all | bytes 65536 | tf_op jit(solution)/shard_map/all_to_all | solution.py:390
  156.6 0.9 final.1
  (26 shorter events, 0.1 us)
Async XLA Ops:
  0.6 0.9 copy-start
  1.5 0.9 copy-start.3
  2.4 76.0 %copy-start.6 = (bf16[128,3,128]{2,0,1:T(8,128)(2,1)S(1)}, bf16[128,3,128]{2,0,1:T(8,128)(2,1)}, u32[]{:S(2)}) copy-start(bf16[128,3,128]{2,0,1:T(8,128)(2,1)} %param.10) | copy-start | bytes 294916
  3.5 9.9 %all-to-all-start = ((f32[8,8,128]{2,1,0:T(8,128)}), f32[8,8,128]{2,1,0:T(8,128)S(1)}, u32[]{:S(2)}, u32[]{:S(2)}) async-start(f32[8,8,128]{2,1,0:T(8,128)} %squares.1), calls=%async_computation | async-start | bytes 65536 | tf_op jit(solution)/shard_map/all_to_all | solution.py:350
  13.4 0.9 copy-start.1
  14.3 0.9 copy-start.4
  15.2 0.9 copy-start.7
  16.7 17.8 %collective-permute-start.3 = (bf16[6,128,128]{2,1,0:T(8,128)(2,1)S(1)}, bf16[6,128,128]{2,1,0:T(8,128)(2,1)S(1)}, u32[]{:S(2)}, u32[]{:S(2)}) collective-permute-start(bf16[6,128,128]{2,1,0:T(8,128)(2,1)S(1)} %get-tuple-element.48.refs_0_), channel_id=1, source_target_pairs={{1,17},{9,25},{16,0},{17,33},{24,8},{25,41},{32,16},{33,49},{40,24... | collective-permute-start | bytes 589832 | tf_op jit(solution)/shard_map/ppermute | solution.py:266
  21.6 17.0 %collective-permute-start.2 = (bf16[6,128,128]{2,1,0:T(8,128)(2,1)S(1)}, bf16[6,128,128]{2,1,0:T(8,128)(2,1)S(1)}, u32[]{:S(2)}, u32[]{:S(2)}) collective-permute-start(bf16[6,128,128]{2,1,0:T(8,128)(2,1)S(1)} %get-tuple-element.48.refs_0_), channel_id=1, source_target_pairs={{0,16},{8,24},{16,32},{17,1},{24,40},{25,9},{32,48},{33,17},{40,56... | collective-permute-start | bytes 589832 | tf_op jit(solution)/shard_map/ppermute | solution.py:266
  30.4 18.2 %collective-permute-start.8 = (bf16[6,128,128]{2,1,0:T(8,128)(2,1)S(1)}, bf16[6,128,128]{2,1,0:T(8,128)(2,1)S(1)}, u32[]{:S(2)}, u32[]{:S(2)}) collective-permute-start(bf16[6,128,128]{2,1,0:T(8,128)(2,1)S(1)} %get-tuple-element.48.refs_0_), channel_id=1, source_target_pairs={{0,256},{8,264},{16,272},{24,280},{32,288},{40,296},{48,304},{56,3... | collective-permute-start | bytes 589832 | tf_op jit(solution)/shard_map/ppermute | solution.py:271
  33.2 17.4 %collective-permute-start.7 = (bf16[6,128,128]{2,1,0:T(8,128)(2,1)S(1)}, bf16[6,128,128]{2,1,0:T(8,128)(2,1)S(1)}, u32[]{:S(2)}, u32[]{:S(2)}) collective-permute-start(bf16[6,128,128]{2,1,0:T(8,128)(2,1)S(1)} %get-tuple-element.48.refs_0_), channel_id=1, source_target_pairs={{1,129},{9,137},{17,145},{25,153},{33,161},{41,169},{49,177},{57,1... | collective-permute-start | bytes 589832 | tf_op jit(solution)/shard_map/ppermute | solution.py:266
  34.5 21.6 %collective-permute-start.5 = (bf16[6,128,128]{2,1,0:T(8,128)(2,1)S(1)}, bf16[6,128,128]{2,1,0:T(8,128)(2,1)S(1)}, u32[]{:S(2)}, u32[]{:S(2)}) collective-permute-start(bf16[6,128,128]{2,1,0:T(8,128)(2,1)S(1)} %collective-permute-done.3.refs_4_), channel_id=1, source_target_pairs={{1,17},{9,25},{16,0},{17,33},{24,8},{25,41},{32,16},{33,49},{40,24... | collective-permute-start | bytes 589832 | tf_op jit(solution)/shard_map/ppermute | solution.py:266
  38.6 19.4 %collective-permute-start.4 = (bf16[6,128,128]{2,1,0:T(8,128)(2,1)S(1)}, bf16[6,128,128]{2,1,0:T(8,128)(2,1)S(1)}, u32[]{:S(2)}, u32[]{:S(2)}) collective-permute-start(bf16[6,128,128]{2,1,0:T(8,128)(2,1)S(1)} %collective-permute-done.2.refs_3_), channel_id=1, source_target_pairs={{0,16},{8,24},{16,32},{17,1},{24,40},{25,9},{32,48},{33,17},{40,56... | collective-permute-start | bytes 589832 | tf_op jit(solution)/shard_map/ppermute | solution.py:266
  45.5 20.7 %collective-permute-start.6 = (bf16[6,128,128]{2,1,0:T(8,128)(2,1)S(1)}, bf16[6,128,128]{2,1,0:T(8,128)(2,1)S(1)}, u32[]{:S(2)}, u32[]{:S(2)}) collective-permute-start(bf16[6,128,128]{2,1,0:T(8,128)(2,1)S(1)} %get-tuple-element.48.refs_0_), channel_id=1, source_target_pairs={{0,128},{8,136},{16,144},{24,152},{32,160},{40,168},{48,176},{56,1... | collective-permute-start | bytes 589832 | tf_op jit(solution)/shard_map/ppermute | solution.py:266
  48.7 17.6 %collective-permute-start.1 = (bf16[6,128,128]{2,1,0:T(8,128)(2,1)S(1)}, bf16[6,128,128]{2,1,0:T(8,128)(2,1)S(1)}, u32[]{:S(2)}, u32[]{:S(2)}) collective-permute-start(bf16[6,128,128]{2,1,0:T(8,128)(2,1)S(1)} %get-tuple-element.48.refs_0_), channel_id=1, source_target_pairs={{1,9},{8,0},{9,17},{16,8},{17,25},{24,16},{25,33},{32,24},{33,41},... | collective-permute-start | bytes 589832 | tf_op jit(solution)/shard_map/ppermute | solution.py:266
  50.6 15.6 %collective-permute-start = (bf16[6,128,128]{2,1,0:T(8,128)(2,1)S(1)}, bf16[6,128,128]{2,1,0:T(8,128)(2,1)S(1)}, u32[]{:S(2)}, u32[]{:S(2)}) collective-permute-start(bf16[6,128,128]{2,1,0:T(8,128)(2,1)S(1)} %get-tuple-element.48.refs_0_), channel_id=1, source_target_pairs={{0,8},{8,16},{9,1},{16,24},{17,9},{24,32},{25,17},{32,40},{33,25},... | collective-permute-start | bytes 589832 | tf_op jit(solution)/shard_map/ppermute | solution.py:266
  56.1 13.9 %collective-permute-start.10 = (bf16[6,128,128]{2,1,0:T(8,128)(2,1)S(1)}, bf16[6,128,128]{2,1,0:T(8,128)(2,1)S(1)}, u32[]{:S(2)}, u32[]{:S(2)}) collective-permute-start(bf16[6,128,128]{2,1,0:T(8,128)(2,1)S(1)} %collective-permute-done.5.refs_6_), channel_id=1, source_target_pairs={{1,33},{9,41},{17,49},{25,57},{32,0},{33,65},{40,8},{41,73},{48,16... | collective-permute-start | bytes 589832 | tf_op jit(solution)/shard_map/ppermute | solution.py:266
  58.0 20.4 %collective-permute-start.9 = (bf16[6,128,128]{2,1,0:T(8,128)(2,1)S(1)}, bf16[6,128,128]{2,1,0:T(8,128)(2,1)S(1)}, u32[]{:S(2)}, u32[]{:S(2)}) collective-permute-start(bf16[6,128,128]{2,1,0:T(8,128)(2,1)S(1)} %collective-permute-done.4.refs_5_), channel_id=1, source_target_pairs={{0,32},{8,40},{16,48},{24,56},{32,64},{33,1},{40,72},{41,9},{48,80... | collective-permute-start | bytes 589832 | tf_op jit(solution)/shard_map/ppermute | solution.py:266
  80.1 25.9 %collective-permute-start.11 = (bf16[6,128,128]{2,1,0:T(8,128)(2,1)S(1)}, bf16[6,128,128]{2,1,0:T(8,128)(2,1)S(1)}, u32[]{:S(2)}, u32[]{:S(2)}) collective-permute-start(bf16[6,128,128]{2,1,0:T(8,128)(2,1)S(1)} %get-tuple-element.58), channel_id=1, source_target_pairs={{1,33},{9,41},{17,49},{25,57},{32,0},{33,65},{40,8},{41,73},{48,16... | collective-permute-start | bytes 589832 | tf_op jit(solution)/shard_map/ppermute | solution.py:266
  82.4 24.7 %collective-permute-start.12 = (bf16[6,128,128]{2,1,0:T(8,128)(2,1)S(1)}, bf16[6,128,128]{2,1,0:T(8,128)(2,1)S(1)}, u32[]{:S(2)}, u32[]{:S(2)}) collective-permute-start(bf16[6,128,128]{2,1,0:T(8,128)(2,1)S(1)} %get-tuple-element.59), channel_id=1, source_target_pairs={{0,32},{8,40},{16,48},{24,56},{32,64},{33,1},{40,72},{41,9},{48,80... | collective-permute-start | bytes 589832 | tf_op jit(solution)/shard_map/ppermute | solution.py:266
  91.8 53.5 %copy-start.2 = (bf16[128,3,128]{2,0,1:T(8,128)(2,1)S(1)}, bf16[128,3,128]{2,0,1:T(8,128)(2,1)}, u32[]{:S(2)}) copy-start(bf16[128,3,128]{2,0,1:T(8,128)(2,1)} %param.7) | copy-start | bytes 294916
  91.8 53.4 %copy-start.5 = (bf16[128,3,128]{2,0,1:T(8,128)(2,1)S(1)}, bf16[128,3,128]{2,0,1:T(8,128)(2,1)}, u32[]{:S(2)}) copy-start(bf16[128,3,128]{2,0,1:T(8,128)(2,1)} %param.8) | copy-start | bytes 294916
  91.9 15.4 %collective-permute-start.13 = (bf16[6,128,128]{2,1,0:T(8,128)(2,1)S(1)}, bf16[6,128,128]{2,1,0:T(8,128)(2,1)S(1)}, u32[]{:S(2)}, u32[]{:S(2)}) collective-permute-start(bf16[6,128,128]{2,1,0:T(8,128)(2,1)S(1)} %get-tuple-element.64), channel_id=1, source_target_pairs={{1,9},{8,0},{9,17},{16,8},{17,25},{24,16},{25,33},{32,24},{33,41},... | collective-permute-start | bytes 589832 | tf_op jit(solution)/shard_map/ppermute | solution.py:266
  96.3 13.8 %collective-permute-start.14 = (bf16[6,128,128]{2,1,0:T(8,128)(2,1)S(1)}, bf16[6,128,128]{2,1,0:T(8,128)(2,1)S(1)}, u32[]{:S(2)}, u32[]{:S(2)}) collective-permute-start(bf16[6,128,128]{2,1,0:T(8,128)(2,1)S(1)} %get-tuple-element.65), channel_id=1, source_target_pairs={{0,8},{8,16},{9,1},{16,24},{17,9},{24,32},{25,17},{32,40},{33,25},... | collective-permute-start | bytes 589832 | tf_op jit(solution)/shard_map/ppermute | solution.py:266
  100.2 10.1 %collective-permute-start.15 = (bf16[6,128,128]{2,1,0:T(8,128)(2,1)S(1)}, bf16[6,128,128]{2,1,0:T(8,128)(2,1)S(1)}, u32[]{:S(2)}, u32[]{:S(2)}) collective-permute-start(bf16[6,128,128]{2,1,0:T(8,128)(2,1)S(1)} %get-tuple-element.66), channel_id=1, source_target_pairs={{0,256},{8,264},{16,272},{24,280},{32,288},{40,296},{48,304},{56,3... | collective-permute-start | bytes 589832 | tf_op jit(solution)/shard_map/ppermute | solution.py:271
  110.4 15.8 %collective-permute-start.16 = (bf16[6,128,128]{2,1,0:T(8,128)(2,1)S(1)}, bf16[6,128,128]{2,1,0:T(8,128)(2,1)S(1)}, u32[]{:S(2)}, u32[]{:S(2)}) collective-permute-start(bf16[6,128,128]{2,1,0:T(8,128)(2,1)S(1)} %add_convert_fusion.3), channel_id=1, source_target_pairs={{1,17},{9,25},{16,0},{17,33},{24,8},{25,41},{32,16},{33,49},{40,24... | collective-permute-start | bytes 589832 | tf_op jit(solution)/shard_map/ppermute | solution.py:266
  112.7 13.5 %collective-permute-start.17 = (bf16[6,128,128]{2,1,0:T(8,128)(2,1)S(1)}, bf16[6,128,128]{2,1,0:T(8,128)(2,1)S(1)}, u32[]{:S(2)}, u32[]{:S(2)}) collective-permute-start(bf16[6,128,128]{2,1,0:T(8,128)(2,1)S(1)} %add_convert_fusion.2), channel_id=1, source_target_pairs={{0,16},{8,24},{16,32},{17,1},{24,40},{25,9},{32,48},{33,17},{40,56... | collective-permute-start | bytes 589832 | tf_op jit(solution)/shard_map/ppermute | solution.py:266
  118.7 11.6 %collective-permute-start.18 = (bf16[6,128,128]{2,1,0:T(8,128)(2,1)S(1)}, bf16[6,128,128]{2,1,0:T(8,128)(2,1)S(1)}, u32[]{:S(2)}, u32[]{:S(2)}) collective-permute-start(bf16[6,128,128]{2,1,0:T(8,128)(2,1)S(1)} %get-tuple-element.76), channel_id=1, source_target_pairs={{1,129},{9,137},{17,145},{25,153},{33,161},{41,169},{49,177},{57,1... | collective-permute-start | bytes 589832 | tf_op jit(solution)/shard_map/ppermute | solution.py:266
  120.0 10.3 %collective-permute-start.19 = (bf16[6,128,128]{2,1,0:T(8,128)(2,1)S(1)}, bf16[6,128,128]{2,1,0:T(8,128)(2,1)S(1)}, u32[]{:S(2)}, u32[]{:S(2)}) collective-permute-start(bf16[6,128,128]{2,1,0:T(8,128)(2,1)S(1)} %get-tuple-element.77), channel_id=1, source_target_pairs={{0,128},{8,136},{16,144},{24,152},{32,160},{40,168},{48,176},{56,1... | collective-permute-start | bytes 589832 | tf_op jit(solution)/shard_map/ppermute | solution.py:266
  130.3 10.9 %collective-permute-start.20 = (bf16[6,128,128]{2,1,0:T(8,128)(2,1)S(1)}, bf16[6,128,128]{2,1,0:T(8,128)(2,1)S(1)}, u32[]{:S(2)}, u32[]{:S(2)}) collective-permute-start(bf16[6,128,128]{2,1,0:T(8,128)(2,1)S(1)} %get-tuple-element.78), channel_id=1, source_target_pairs={{1,17},{9,25},{16,0},{17,33},{24,8},{25,41},{32,16},{33,49},{40,24... | collective-permute-start | bytes 589832 | tf_op jit(solution)/shard_map/ppermute | solution.py:266
  132.2 13.1 %collective-permute-start.21 = (bf16[6,128,128]{2,1,0:T(8,128)(2,1)S(1)}, bf16[6,128,128]{2,1,0:T(8,128)(2,1)S(1)}, u32[]{:S(2)}, u32[]{:S(2)}) collective-permute-start(bf16[6,128,128]{2,1,0:T(8,128)(2,1)S(1)} %get-tuple-element.79), channel_id=1, source_target_pairs={{0,16},{8,24},{16,32},{17,1},{24,40},{25,9},{32,48},{33,17},{40,56... | collective-permute-start | bytes 589832 | tf_op jit(solution)/shard_map/ppermute | solution.py:266

commit v9 on v8

--- a/solution.py
+++ b/solution.py
@@ -53,24 +53,12 @@
     return (at >= 0) & (at < line * lines)
 
 
-def fetch(sources, targets, sems):
-    copies = [
-        pltpu.make_async_copy(source, target, sems.at[at])
-        for at, (source, target) in enumerate(zip(sources, targets))
-    ]
-    for copy in copies:
-        copy.start()
-    for copy in copies:
-        copy.wait()
-
-
-def squares_kernel(heads, q_hbm, k_hbm, out_ref, q_ref, k_ref, sems):
-    fetch((q_hbm, k_hbm), (q_ref, k_ref), sems)
+def squares_kernel(heads, raw_ref, out_ref):
     out_ref[...] = jnp.zeros(out_ref.shape, F32)
-    for row, ref in enumerate((q_ref, k_ref)):
+    for row in range(2):
         total = jnp.zeros((TILE, TILE), F32)
         for head in range(heads):
-            floats = ref[head].astype(F32)
+            floats = raw_ref[row * heads + head].astype(F32)
             total = total + floats * floats
         total = row_sums(total)[0:1]
         for group in range(out_ref.shape[0]):
@@ -84,19 +72,17 @@
     return total
 
 
-def norm_kernel(
-    heads, channels, sums_ref, gain_ref, q_hbm, k_hbm, v_hbm, qn_ref, kv_ref, inverse_ref, q_ref, k_ref, sems
-):
-    fetch((q_hbm, k_hbm, v_hbm), (q_ref, k_ref, kv_ref.at[pl.ds(heads, heads)]), sems)
+def norm_kernel(heads, channels, sums_ref, gain_ref, raw_ref, qn_ref, kv_ref, inverse_ref):
     inverse = lax.rsqrt(group_sum(sums_ref) / channels + EPS)
     inverse_ref[...] = inverse
     turned = columns(inverse)
     for head in range(heads):
         qn_ref[head] = (
-            q_ref[head].astype(F32) * turned[:, 0:1] * gain_ref[head : head + 1]
+            raw_ref[head].astype(F32) * turned[:, 0:1] * gain_ref[head : head + 1]
         ).astype(BF16)
+        kv_ref[heads + head] = raw_ref[2 * heads + head]
         kv_ref[head] = (
-            k_ref[head].astype(F32) * turned[:, 1:2] * gain_ref[heads + head : heads + head + 1]
+            raw_ref[heads + head].astype(F32) * turned[:, 1:2] * gain_ref[heads + head : heads + head + 1]
         ).astype(BF16)
 
 
@@ -141,8 +127,11 @@
     rows = jnp.zeros((TILE, TILE), F32)
     every = range(heads)
     scores = [
-        [jnp.where(use, dot(q_ref[head], tile[head], NT) * scale, -1e30) for use, tile in zip(usable, tiles)]
-        for head in every
+        [dot(q_ref[head], tile[head], NT) * scale for tile in tiles] for head in every
+    ]
+    scores = [
+        [score if use is None else jnp.where(use, score, -1e30) for use, score in zip(usable, row)]
+        for row in scores
     ]
     dprobs = [[dot(do_ref[head], tile[heads + head], NT) for tile in tiles] for head in every]
     weights, keeps, shares, outs, deltas = [], [], [], [], []
@@ -211,7 +200,7 @@
         dq_ref[head] = query_grad * scale
 
 
-def terms_kernel(heads, q_ref, k_ref, dq_ref, gain_ref, *refs):
+def terms_kernel(heads, raw_ref, dq_ref, gain_ref, *refs):
     parts, (dk_ref, dv_ref, terms_ref) = refs[:-3], refs[-3:]
     query_total = jnp.zeros((TILE, TILE), F32)
     key_total = jnp.zeros((TILE, TILE), F32)
@@ -222,10 +211,10 @@
             value_grad = value_grad + part[heads + head].astype(F32)
         dk_ref[head] = key_grad
         dv_ref[head] = value_grad.astype(BF16)
-        query_total = query_total + q_ref[head].astype(F32) * (
+        query_total = query_total + raw_ref[head].astype(F32) * (
             dq_ref[head] * gain_ref[head : head + 1]
         )
-        key_total = key_total + k_ref[head].astype(F32) * (
+        key_total = key_total + raw_ref[heads + head].astype(F32) * (
             key_grad * gain_ref[heads + head : heads + head + 1]
         )
     terms_ref[...] = jnp.zeros(terms_ref.shape, F32)
@@ -236,7 +225,7 @@
 
 
 def final_kernel(
-    heads, channels, inverse_ref, terms_ref, q_ref, k_ref, dq_ref, dk_ref, gain_ref, gq_ref, gk_ref
+    heads, channels, inverse_ref, terms_ref, raw_ref, dq_ref, dk_ref, gain_ref, gq_ref, gk_ref
 ):
     inverse = inverse_ref[0:2]
     cubes = inverse * inverse * inverse * group_sum(terms_ref)[0:2] / channels
@@ -244,11 +233,11 @@
     for head in range(heads):
         gq_ref[head] = (
             turned[:, 0:1] * (gain_ref[head : head + 1] * dq_ref[head])
-            - q_ref[head].astype(F32) * turned[:, 2:3]
+            - raw_ref[head].astype(F32) * turned[:, 2:3]
         ).astype(BF16)
         gk_ref[head] = (
             turned[:, 1:2] * (gain_ref[heads + head : heads + head + 1] * dk_ref[head])
-            - k_ref[head].astype(F32) * turned[:, 3:4]
+            - raw_ref[heads + head].astype(F32) * turned[:, 3:4]
         ).astype(BF16)
 
 
@@ -287,9 +276,9 @@
     places = [len(NEAR) - 2, len(NEAR) - 1]
     carried = [parts[place] for place in places]
     others = [
+        lambda: parts[0] + half_round(parts[len(NEAR) + 2]).astype(F32),
         lambda: passed(parts[1], NEAR[1]),
         lambda: passed(parts[2], NEAR[2]),
-        lambda: half_round(parts[len(NEAR) + 2]),
         lambda: passed(parts[len(NEAR)], -line),
         lambda: passed(parts[len(NEAR) + 1], line),
     ]
@@ -308,7 +297,7 @@
         arrived += [send() for send in others[:3]]
         others = others[3:]
         carried, arrived = lax.optimization_barrier((carried, arrived))
-    return carried + arrived + [send() for send in others]
+    return arrived + carried + [send() for send in others]
 
 
 def per_device(total_heads, q_raw, k_raw, values, grad_out, q_gain, k_gain, key_tiles):
@@ -326,37 +315,29 @@
     params = pltpu.CompilerParams(vmem_limit_bytes=VMEM_LIMIT)
     whole, pair = (heads, TILE, TILE), (2 * heads, TILE, TILE)
 
-    def call(kernel, name, out_shape, *operands, scratch=(), raw=0):
+    def call(kernel, name, out_shape, *operands):
         return pl.pallas_call(
             kernel,
             out_shape=[jax.ShapeDtypeStruct(shape, dtype) for shape, dtype in out_shape],
-            in_specs=[vmem] * (len(operands) - raw) + [pl.BlockSpec(memory_space=pltpu.HBM)] * raw,
+            in_specs=[vmem] * len(operands),
             out_specs=[vmem] * len(out_shape),
-            scratch_shapes=list(scratch),
             compiler_params=params,
             name=name,
         )(*operands)
 
     rows = ((groups, 8, TILE), F32)
-    held = [pltpu.VMEM(whole, BF16)] * 2
-    (squares,) = call(
-        functools.partial(squares_kernel, heads),
-        "squares",
-        [rows],
-        q_raw, k_raw,
-        scratch=held + [pltpu.SemaphoreType.DMA((2,))],
-        raw=2,
-    )
+    raw = jnp.concatenate([q_raw, k_raw, values], axis=0)
+    (squares,) = call(functools.partial(squares_kernel, heads), "squares", [rows], raw)
     sums = lax.all_to_all(squares, HEAD, 0, 0, tiled=True)
     q_norm, pairs, inverse = call(
         functools.partial(norm_kernel, heads, channels),
         "norm",
         [(whole, BF16), (pair, BF16), ((8, TILE), F32)],
-        sums, gains, q_raw, k_raw, values,
-        scratch=held + [pltpu.SemaphoreType.DMA((3,))],
-        raw=3,
-    )
-    tiles = spread(pairs) + [passed(pairs, line), passed(pairs, -line), half_round(pairs)]
+        sums, gains, raw,
+    )
+    half = half_round(pairs)
+    tiles = spread(pairs)
+    tiles += [passed(pairs, line), passed(pairs, -line), half]
     late = [near - 2, near - 1]
     early = [t for t in range(count) if t not in late]
     early_tiles, late_tiles = [tiles[t] for t in early], [tiles[t] for t in late]
@@ -385,14 +366,14 @@
         functools.partial(terms_kernel, heads),
         "terms",
         [(whole, F32), (whole, BF16), rows],
-        q_raw, k_raw, dq, gains, parts[0], *arrived,
+        raw, dq, gains, *arrived,
     )
     terms = lax.all_to_all(terms, HEAD, 0, 0, tiled=True)
     grad_q, grad_k = call(
         functools.partial(final_kernel, heads, channels),
         "final",
         [(whole, BF16)] * 2,
-        inverse, terms, q_raw, k_raw, dq, dk, gains,
+        inverse, terms, raw, dq, dk, gains,
     )
     return tuple(
         jnp.transpose(array, (1, 0, 2)) for array in (attended, grad_q, grad_k, grad_v)

time: 160 us -> 155 us (0.969)
  local copies, waits for them, and re-layouts: 4.47 us -> 0.01 us
    unnamed x16 -> x2, local copies, waits for them, and re-layouts: 4.47 us -> 0.01 us
  transfers between devices with their start and end apart: 23 -> 23, of which waited for: 10 -> 11; matrix products, arithmetic and copies ran while one was open for 1% -> 1% of each run, Pallas kernels for 2% -> 2%
where the time goes in v9:
time: 155 us; the launch traced here: 153 us
  starting transfers between devices  99.9 us (64%)
  waiting for transfers between devices  30.7 us (20%)
  blocking collectives  11.9 us (8%)
  Pallas kernels  7.59 us (5%)
  other arithmetic  2 us (1%)
    ppermute x20, starting transfers between devices, passed(): return lax.ppermute(value, SEQ + ('c',), pairs)  85.4 us
    ppermute x20, waiting for transfers between devices, passed(): return lax.ppermute(value, SEQ + ('c',), pairs)  26.7 us
    all_to_all x1, blocking collectives, per_device(): terms = lax.all_to_all(terms, HEAD, 0, 0, tiled=True)  11.9 us
    ppermute x2, starting transfers between devices, half_round(): lax.ppermute(value, SEQ, [(i, (i + count // 2) % count) for i in range(co...  9.35 us
    pallas_call x7, Pallas kernels, call(): pl.pallas_call(kernel, out_shape=[jax.ShapeDtypeStruct(shape, dtype) for...  7.59 us
    all_to_all x1, starting transfers between devices, per_device(): sums = lax.all_to_all(squares, HEAD, 0, 0, tiled=True)  5.14 us
    all_to_all x1, waiting for transfers between devices, per_device(): sums = lax.all_to_all(squares, HEAD, 0, 0, tiled=True)  4.01 us
  transfers between devices with their start and end apart: 23, of which 11 were waited for; matrix products, arithmetic and copies ran while one was open for 1% of the time, Pallas kernels for 2%

profile of v9, /device:TPU:7, one launch (start us, length us, event | category | flops | bytes accessed | tf_op | source)
XLA Modules:
  0.0 153.1 jit_solution(13212067484453081126)
XLA Ops:
  0.6 1.1 pad_maximum_fusion.raw_ref
  1.7 0.8 squares.1
  2.5 5.1 %all-to-all-start = ((f32[8,8,128]{2,1,0:T(8,128)}), f32[8,8,128]{2,1,0:T(8,128)S(1)}, u32[]{:S(2)}, u32[]{:S(2)}) async-start(f32[8,8,128]{2,1,0:T(8,128)} %squares.1), calls=%async_computation | async-start | bytes 65536 | tf_op jit(solution)/shard_map/all_to_all | solution.py:331
  7.7 0.7 pad_maximum_fusion.1.gain_ref
  8.4 4.0 %all-to-all-done.sums_ref = f32[8,8,128]{2,1,0:T(8,128)S(1)} async-done(((f32[8,8,128]{2,1,0:T(8,128)}), f32[8,8,128]{2,1,0:T(8,128)S(1)}, u32[]{:S(2)}, u32[]{:S(2)}) %all-to-all-start) | async-done | bytes 32800 | tf_op jit(solution)/shard_map/all_to_all | solution.py:331
  12.4 0.2 norm.1
  12.6 4.9 %collective-permute-start.3 = (bf16[6,128,128]{2,1,0:T(8,128)(2,1)S(1)}, bf16[6,128,128]{2,1,0:T(8,128)(2,1)S(1)}, u32[]{:S(2)}, u32[]{:S(2)}) collective-permute-start(bf16[6,128,128]{2,1,0:T(8,128)(2,1)S(1)} %get-tuple-element.48.refs_0_), channel_id=1, source_target_pairs={{1,17},{9,25},{16,0},{17,33},{24,8},{25,41},{32,16},{33,49},{40,24... | collective-permute-start | bytes 589832 | tf_op jit(solution)/shard_map/ppermute | solution.py:255
  17.5 8.9 %collective-permute-start.2 = (bf16[6,128,128]{2,1,0:T(8,128)(2,1)S(1)}, bf16[6,128,128]{2,1,0:T(8,128)(2,1)S(1)}, u32[]{:S(2)}, u32[]{:S(2)}) collective-permute-start(bf16[6,128,128]{2,1,0:T(8,128)(2,1)S(1)} %get-tuple-element.48.refs_0_), channel_id=1, source_target_pairs={{0,16},{8,24},{16,32},{17,1},{24,40},{25,9},{32,48},{33,17},{40,56... | collective-permute-start | bytes 589832 | tf_op jit(solution)/shard_map/ppermute | solution.py:255
  26.4 2.7 %collective-permute-start.8 = (bf16[6,128,128]{2,1,0:T(8,128)(2,1)S(1)}, bf16[6,128,128]{2,1,0:T(8,128)(2,1)S(1)}, u32[]{:S(2)}, u32[]{:S(2)}) collective-permute-start(bf16[6,128,128]{2,1,0:T(8,128)(2,1)S(1)} %get-tuple-element.48.refs_0_), channel_id=1, source_target_pairs={{0,256},{8,264},{16,272},{24,280},{32,288},{40,296},{48,304},{56,3... | collective-permute-start | bytes 589832 | tf_op jit(solution)/shard_map/ppermute | solution.py:260
  29.1 1.3 collective-permute-start.7
  30.4 0.0 collective-permute-done.3.refs_4_
  30.4 1.9 %collective-permute-start.5 = (bf16[6,128,128]{2,1,0:T(8,128)(2,1)S(1)}, bf16[6,128,128]{2,1,0:T(8,128)(2,1)S(1)}, u32[]{:S(2)}, u32[]{:S(2)}) collective-permute-start(bf16[6,128,128]{2,1,0:T(8,128)(2,1)S(1)} %collective-permute-done.3.refs_4_), channel_id=1, source_target_pairs={{1,17},{9,25},{16,0},{17,33},{24,8},{25,41},{32,16},{33,49},{40,24... | collective-permute-start | bytes 589832 | tf_op jit(solution)/shard_map/ppermute | solution.py:255
  32.4 2.2 %collective-permute-done.2.refs_3_ = bf16[6,128,128]{2,1,0:T(8,128)(2,1)S(1)} collective-permute-done((bf16[6,128,128]{2,1,0:T(8,128)(2,1)S(1)}, bf16[6,128,128]{2,1,0:T(8,128)(2,1)S(1)}, u32[]{:S(2)}, u32[]{:S(2)}) %collective-permute-start.2) | collective-permute-done | bytes 196640 | tf_op jit(solution)/shard_map/ppermute | solution.py:255
  34.6 6.9 %collective-permute-start.4 = (bf16[6,128,128]{2,1,0:T(8,128)(2,1)S(1)}, bf16[6,128,128]{2,1,0:T(8,128)(2,1)S(1)}, u32[]{:S(2)}, u32[]{:S(2)}) collective-permute-start(bf16[6,128,128]{2,1,0:T(8,128)(2,1)S(1)} %collective-permute-done.2.refs_3_), channel_id=1, source_target_pairs={{0,16},{8,24},{16,32},{17,1},{24,40},{25,9},{32,48},{33,17},{40,56... | collective-permute-start | bytes 589832 | tf_op jit(solution)/shard_map/ppermute | solution.py:255
  41.5 3.1 %collective-permute-start.6 = (bf16[6,128,128]{2,1,0:T(8,128)(2,1)S(1)}, bf16[6,128,128]{2,1,0:T(8,128)(2,1)S(1)}, u32[]{:S(2)}, u32[]{:S(2)}) collective-permute-start(bf16[6,128,128]{2,1,0:T(8,128)(2,1)S(1)} %get-tuple-element.48.refs_0_), channel_id=1, source_target_pairs={{0,128},{8,136},{16,144},{24,152},{32,160},{40,168},{48,176},{56,1... | collective-permute-start | bytes 589832 | tf_op jit(solution)/shard_map/ppermute | solution.py:255
  44.6 0.0 collective-permute-done.8.refs_9_
  44.6 1.9 %collective-permute-start.1 = (bf16[6,128,128]{2,1,0:T(8,128)(2,1)S(1)}, bf16[6,128,128]{2,1,0:T(8,128)(2,1)S(1)}, u32[]{:S(2)}, u32[]{:S(2)}) collective-permute-start(bf16[6,128,128]{2,1,0:T(8,128)(2,1)S(1)} %get-tuple-element.48.refs_0_), channel_id=1, source_target_pairs={{1,9},{8,0},{9,17},{16,8},{17,25},{24,16},{25,33},{32,24},{33,41},... | collective-permute-start | bytes 589832 | tf_op jit(solution)/shard_map/ppermute | solution.py:255
  46.5 5.5 %collective-permute-start = (bf16[6,128,128]{2,1,0:T(8,128)(2,1)S(1)}, bf16[6,128,128]{2,1,0:T(8,128)(2,1)S(1)}, u32[]{:S(2)}, u32[]{:S(2)}) collective-permute-start(bf16[6,128,128]{2,1,0:T(8,128)(2,1)S(1)} %get-tuple-element.48.refs_0_), channel_id=1, source_target_pairs={{0,8},{8,16},{9,1},{16,24},{17,9},{24,32},{25,17},{32,40},{33,25},... | collective-permute-start | bytes 589832 | tf_op jit(solution)/shard_map/ppermute | solution.py:255
  52.0 1.9 %collective-permute-start.10 = (bf16[6,128,128]{2,1,0:T(8,128)(2,1)S(1)}, bf16[6,128,128]{2,1,0:T(8,128)(2,1)S(1)}, u32[]{:S(2)}, u32[]{:S(2)}) collective-permute-start(bf16[6,128,128]{2,1,0:T(8,128)(2,1)S(1)} %collective-permute-done.5.refs_6_), channel_id=1, source_target_pairs={{1,33},{9,41},{17,49},{25,57},{32,0},{33,65},{40,8},{41,73},{48,16... | collective-permute-start | bytes 589832 | tf_op jit(solution)/shard_map/ppermute | solution.py:255
  54.0 8.2 %collective-permute-start.9 = (bf16[6,128,128]{2,1,0:T(8,128)(2,1)S(1)}, bf16[6,128,128]{2,1,0:T(8,128)(2,1)S(1)}, u32[]{:S(2)}, u32[]{:S(2)}) collective-permute-start(bf16[6,128,128]{2,1,0:T(8,128)(2,1)S(1)} %collective-permute-done.4.refs_5_), channel_id=1, source_target_pairs={{0,32},{8,40},{16,48},{24,56},{32,64},{33,1},{40,72},{41,9},{48,80... | collective-permute-start | bytes 589832 | tf_op jit(solution)/shard_map/ppermute | solution.py:255
  62.2 1.4 early.1
  63.5 2.4 %collective-permute-done.10.refs_1_ = bf16[6,128,128]{2,1,0:T(8,128)(2,1)S(1)} collective-permute-done((bf16[6,128,128]{2,1,0:T(8,128)(2,1)S(1)}, bf16[6,128,128]{2,1,0:T(8,128)(2,1)S(1)}, u32[]{:S(2)}, u32[]{:S(2)}) %collective-permute-start.10) | collective-permute-done | bytes 196640 | tf_op jit(solution)/shard_map/ppermute | solution.py:255
  65.9 8.4 %collective-permute-done.9.refs_0_ = bf16[6,128,128]{2,1,0:T(8,128)(2,1)S(1)} collective-permute-done((bf16[6,128,128]{2,1,0:T(8,128)(2,1)S(1)}, bf16[6,128,128]{2,1,0:T(8,128)(2,1)S(1)}, u32[]{:S(2)}, u32[]{:S(2)}) %collective-permute-start.9) | collective-permute-done | bytes 196640 | tf_op jit(solution)/shard_map/ppermute | solution.py:255
  74.4 1.7 %late.1 = (bf16[3,128,128]{2,1,0:T(8,128)(2,1)}, f32[3,128,128]{2,1,0:T(8,128)S(1)}, f32[128,128]{1,0:T(8,128)S(1)}, bf16[6,128,128]{2,1,0:T(8,128)(2,1)S(1)}, bf16[6,128,128]{2,1,0:T(8,128)(2,1)S(1)}) custom-call(bf16[3,128,128]{2,1,0:T(8,128)(2,1)S(1)} %get-tuple-element.47.q_ref, bf16[3,128,128]{2,1,0:T(8,128)(2,1)S(1)} %bitcast.8, ...), custom_call_target="tpu_custom_call" | custom-call | tf_op jit(solution)/shard_map/late/pallas_call | solution.py:319
  76.0 2.3 %collective-permute-start.11 = (bf16[6,128,128]{2,1,0:T(8,128)(2,1)S(1)}, bf16[6,128,128]{2,1,0:T(8,128)(2,1)S(1)}, u32[]{:S(2)}, u32[]{:S(2)}) collective-permute-start(bf16[6,128,128]{2,1,0:T(8,128)(2,1)S(1)} %get-tuple-element.57), channel_id=1, source_target_pairs={{1,33},{9,41},{17,49},{25,57},{32,0},{33,65},{40,8},{41,73},{48,16... | collective-permute-start | bytes 589832 | tf_op jit(solution)/shard_map/ppermute | solution.py:255
  78.4 7.8 %collective-permute-start.12 = (bf16[6,128,128]{2,1,0:T(8,128)(2,1)S(1)}, bf16[6,128,128]{2,1,0:T(8,128)(2,1)S(1)}, u32[]{:S(2)}, u32[]{:S(2)}) collective-permute-start(bf16[6,128,128]{2,1,0:T(8,128)(2,1)S(1)} %get-tuple-element.58), channel_id=1, source_target_pairs={{0,32},{8,40},{16,48},{24,56},{32,64},{33,1},{40,72},{41,9},{48,80... | collective-permute-start | bytes 589832 | tf_op jit(solution)/shard_map/ppermute | solution.py:255
  86.1 1.6 %rest.1 = (f32[3,128,128]{2,1,0:T(8,128)S(1)}, f32[6,128,128]{2,1,0:T(8,128)S(1)}, bf16[6,128,128]{2,1,0:T(8,128)(2,1)S(1)}, bf16[6,128,128]{2,1,0:T(8,128)(2,1)...) custom-call(bf16[3,128,128]{2,1,0:T(8,128)(2,1)S(1)} %get-tuple-elem, ...), custom_call_target="tpu_custom_call" | custom-call | tf_op jit(solution)/shard_map/rest/pallas_call | solution.py:319
  87.8 6.6 %collective-permute-start.13 = (bf16[6,128,128]{2,1,0:T(8,128)(2,1)S(1)}, bf16[6,128,128]{2,1,0:T(8,128)(2,1)S(1)}, u32[]{:S(2)}, u32[]{:S(2)}) collective-permute-start(bf16[6,128,128]{2,1,0:T(8,128)(2,1)S(1)} %get-tuple-element.64), channel_id=1, source_target_pairs={{0,256},{8,264},{16,272},{24,280},{32,288},{40,296},{48,304},{56,3... | collective-permute-start | bytes 589832 | tf_op jit(solution)/shard_map/ppermute | solution.py:260
  94.4 1.9 %collective-permute-start.14 = (bf16[6,128,128]{2,1,0:T(8,128)(2,1)S(1)}, bf16[6,128,128]{2,1,0:T(8,128)(2,1)S(1)}, u32[]{:S(2)}, u32[]{:S(2)}) collective-permute-start(bf16[6,128,128]{2,1,0:T(8,128)(2,1)S(1)} %get-tuple-element.65), channel_id=1, source_target_pairs={{1,9},{8,0},{9,17},{16,8},{17,25},{24,16},{25,33},{32,24},{33,41},... | collective-permute-start | bytes 589832 | tf_op jit(solution)/shard_map/ppermute | solution.py:255
  96.3 5.5 %collective-permute-start.15 = (bf16[6,128,128]{2,1,0:T(8,128)(2,1)S(1)}, bf16[6,128,128]{2,1,0:T(8,128)(2,1)S(1)}, u32[]{:S(2)}, u32[]{:S(2)}) collective-permute-start(bf16[6,128,128]{2,1,0:T(8,128)(2,1)S(1)} %get-tuple-element.66), channel_id=1, source_target_pairs={{0,8},{8,16},{9,1},{16,24},{17,9},{24,32},{25,17},{32,40},{33,25},... | collective-permute-start | bytes 589832 | tf_op jit(solution)/shard_map/ppermute | solution.py:255
  101.8 0.3 collective-permute-done.12
  102.1 0.1 add_convert_fusion.2
  102.3 0.6 collective-permute-done.14.refs_1_
  102.9 3.1 %collective-permute-done.15.refs_2_ = bf16[6,128,128]{2,1,0:T(8,128)(2,1)S(1)} collective-permute-done((bf16[6,128,128]{2,1,0:T(8,128)(2,1)S(1)}, bf16[6,128,128]{2,1,0:T(8,128)(2,1)S(1)}, u32[]{:S(2)}, u32[]{:S(2)}) %collective-permute-start.15) | collective-permute-done | bytes 196640 | tf_op jit(solution)/shard_map/ppermute | solution.py:255
  106.0 2.7 %collective-permute-start.16 = (bf16[6,128,128]{2,1,0:T(8,128)(2,1)S(1)}, bf16[6,128,128]{2,1,0:T(8,128)(2,1)S(1)}, u32[]{:S(2)}, u32[]{:S(2)}) collective-permute-start(bf16[6,128,128]{2,1,0:T(8,128)(2,1)S(1)} %add_convert_fusion.3), channel_id=1, source_target_pairs={{1,17},{9,25},{16,0},{17,33},{24,8},{25,41},{32,16},{33,49},{40,24... | collective-permute-start | bytes 589832 | tf_op jit(solution)/shard_map/ppermute | solution.py:255
  108.7 6.1 %collective-permute-start.17 = (bf16[6,128,128]{2,1,0:T(8,128)(2,1)S(1)}, bf16[6,128,128]{2,1,0:T(8,128)(2,1)S(1)}, u32[]{:S(2)}, u32[]{:S(2)}) collective-permute-start(bf16[6,128,128]{2,1,0:T(8,128)(2,1)S(1)} %add_convert_fusion.2), channel_id=1, source_target_pairs={{0,16},{8,24},{16,32},{17,1},{24,40},{25,9},{32,48},{33,17},{40,56... | collective-permute-start | bytes 589832 | tf_op jit(solution)/shard_map/ppermute | solution.py:255
  114.8 1.3 collective-permute-start.18
  116.1 5.1 %collective-permute-start.19 = (bf16[6,128,128]{2,1,0:T(8,128)(2,1)S(1)}, bf16[6,128,128]{2,1,0:T(8,128)(2,1)S(1)}, u32[]{:S(2)}, u32[]{:S(2)}) collective-permute-start(bf16[6,128,128]{2,1,0:T(8,128)(2,1)S(1)} %get-tuple-element.77), channel_id=1, source_target_pairs={{0,128},{8,136},{16,144},{24,152},{32,160},{40,168},{48,176},{56,1... | collective-permute-start | bytes 589832 | tf_op jit(solution)/shard_map/ppermute | solution.py:255
  121.2 0.7 collective-permute-done.17
  121.9 0.1 add_convert_fusion
  122.1 3.5 %collective-permute-done.18.refs_3_ = bf16[6,128,128]{2,1,0:T(8,128)(2,1)S(1)} collective-permute-done((bf16[6,128,128]{2,1,0:T(8,128)(2,1)S(1)}, bf16[6,128,128]{2,1,0:T(8,128)(2,1)S(1)}, u32[]{:S(2)}, u32[]{:S(2)}) %collective-permute-start.18) | collective-permute-done | bytes 196640 | tf_op jit(solution)/shard_map/ppermute | solution.py:255
  125.5 1.9 %collective-permute-start.20 = (bf16[6,128,128]{2,1,0:T(8,128)(2,1)S(1)}, bf16[6,128,128]{2,1,0:T(8,128)(2,1)S(1)}, u32[]{:S(2)}, u32[]{:S(2)}) collective-permute-start(bf16[6,128,128]{2,1,0:T(8,128)(2,1)S(1)} %get-tuple-element.83), channel_id=1, source_target_pairs={{1,17},{9,25},{16,0},{17,33},{24,8},{25,41},{32,16},{33,49},{40,24... | collective-permute-start | bytes 589832 | tf_op jit(solution)/shard_map/ppermute | solution.py:255
  127.5 6.4 %collective-permute-start.21 = (bf16[6,128,128]{2,1,0:T(8,128)(2,1)S(1)}, bf16[6,128,128]{2,1,0:T(8,128)(2,1)S(1)}, u32[]{:S(2)}, u32[]{:S(2)}) collective-permute-start(bf16[6,128,128]{2,1,0:T(8,128)(2,1)S(1)} %get-tuple-element.84), channel_id=1, source_target_pairs={{0,16},{8,24},{16,32},{17,1},{24,40},{25,9},{32,48},{33,17},{40,56... | collective-permute-start | bytes 589832 | tf_op jit(solution)/shard_map/ppermute | solution.py:255
  133.9 1.7 %collective-permute-done.20.refs_5_ = bf16[6,128,128]{2,1,0:T(8,128)(2,1)S(1)} collective-permute-done((bf16[6,128,128]{2,1,0:T(8,128)(2,1)S(1)}, bf16[6,128,128]{2,1,0:T(8,128)(2,1)S(1)}, u32[]{:S(2)}, u32[]{:S(2)}) %collective-permute-start.20) | collective-permute-done | bytes 196640 | tf_op jit(solution)/shard_map/ppermute | solution.py:255
  135.6 3.7 %collective-permute-done.21.refs_6_ = bf16[6,128,128]{2,1,0:T(8,128)(2,1)S(1)} collective-permute-done((bf16[6,128,128]{2,1,0:T(8,128)(2,1)S(1)}, bf16[6,128,128]{2,1,0:T(8,128)(2,1)S(1)}, u32[]{:S(2)}, u32[]{:S(2)}) %collective-permute-start.21) | collective-permute-done | bytes 196640 | tf_op jit(solution)/shard_map/ppermute | solution.py:255
  139.3 0.9 terms.1
  140.2 11.9 %all_to_all.10.terms_ref = f32[8,8,128]{2,1,0:T(8,128)S(1)} all-to-all(f32[8,8,128]{2,1,0:T(8,128)S(1)} %get-tuple-element.85), channel_id=1, replica_groups=mesh['x'=4,'z'=16,'y'=4,'c'=2] {'y','c'}, dimensions={0} | all-to-all | bytes 65536 | tf_op jit(solution)/shard_map/all_to_all | solution.py:371
  152.1 0.9 final.1
  (14 shorter events, 0.1 us)
Async XLA Ops:
  0.6 73.7 %copy-start = (bf16[128,3,128]{2,0,1:T(8,128)(2,1)S(1)}, bf16[128,3,128]{2,0,1:T(8,128)(2,1)}, u32[]{:S(2)}) copy-start(bf16[128,3,128]{2,0,1:T(8,128)(2,1)} %param.10) | copy-start | bytes 294916
  2.5 9.9 %all-to-all-start = ((f32[8,8,128]{2,1,0:T(8,128)}), f32[8,8,128]{2,1,0:T(8,128)S(1)}, u32[]{:S(2)}, u32[]{:S(2)}) async-start(f32[8,8,128]{2,1,0:T(8,128)} %squares.1), calls=%async_computation | async-start | bytes 65536 | tf_op jit(solution)/shard_map/all_to_all | solution.py:331
  12.6 17.8 %collective-permute-start.3 = (bf16[6,128,128]{2,1,0:T(8,128)(2,1)S(1)}, bf16[6,128,128]{2,1,0:T(8,128)(2,1)S(1)}, u32[]{:S(2)}, u32[]{:S(2)}) collective-permute-start(bf16[6,128,128]{2,1,0:T(8,128)(2,1)S(1)} %get-tuple-element.48.refs_0_), channel_id=1, source_target_pairs={{1,17},{9,25},{16,0},{17,33},{24,8},{25,41},{32,16},{33,49},{40,24... | collective-permute-start | bytes 589832 | tf_op jit(solution)/shard_map/ppermute | solution.py:255
  17.5 17.0 %collective-permute-start.2 = (bf16[6,128,128]{2,1,0:T(8,128)(2,1)S(1)}, bf16[6,128,128]{2,1,0:T(8,128)(2,1)S(1)}, u32[]{:S(2)}, u32[]{:S(2)}) collective-permute-start(bf16[6,128,128]{2,1,0:T(8,128)(2,1)S(1)} %get-tuple-element.48.refs_0_), channel_id=1, source_target_pairs={{0,16},{8,24},{16,32},{17,1},{24,40},{25,9},{32,48},{33,17},{40,56... | collective-permute-start | bytes 589832 | tf_op jit(solution)/shard_map/ppermute | solution.py:255
  26.4 18.2 %collective-permute-start.8 = (bf16[6,128,128]{2,1,0:T(8,128)(2,1)S(1)}, bf16[6,128,128]{2,1,0:T(8,128)(2,1)S(1)}, u32[]{:S(2)}, u32[]{:S(2)}) collective-permute-start(bf16[6,128,128]{2,1,0:T(8,128)(2,1)S(1)} %get-tuple-element.48.refs_0_), channel_id=1, source_target_pairs={{0,256},{8,264},{16,272},{24,280},{32,288},{40,296},{48,304},{56,3... | collective-permute-start | bytes 589832 | tf_op jit(solution)/shard_map/ppermute | solution.py:260
  29.1 17.4 %collective-permute-start.7 = (bf16[6,128,128]{2,1,0:T(8,128)(2,1)S(1)}, bf16[6,128,128]{2,1,0:T(8,128)(2,1)S(1)}, u32[]{:S(2)}, u32[]{:S(2)}) collective-permute-start(bf16[6,128,128]{2,1,0:T(8,128)(2,1)S(1)} %get-tuple-element.48.refs_0_), channel_id=1, source_target_pairs={{1,129},{9,137},{17,145},{25,153},{33,161},{41,169},{49,177},{57,1... | collective-permute-start | bytes 589832 | tf_op jit(solution)/shard_map/ppermute | solution.py:255
  30.4 21.6 %collective-permute-start.5 = (bf16[6,128,128]{2,1,0:T(8,128)(2,1)S(1)}, bf16[6,128,128]{2,1,0:T(8,128)(2,1)S(1)}, u32[]{:S(2)}, u32[]{:S(2)}) collective-permute-start(bf16[6,128,128]{2,1,0:T(8,128)(2,1)S(1)} %collective-permute-done.3.refs_4_), channel_id=1, source_target_pairs={{1,17},{9,25},{16,0},{17,33},{24,8},{25,41},{32,16},{33,49},{40,24... | collective-permute-start | bytes 589832 | tf_op jit(solution)/shard_map/ppermute | solution.py:255
  34.6 19.4 %collective-permute-start.4 = (bf16[6,128,128]{2,1,0:T(8,128)(2,1)S(1)}, bf16[6,128,128]{2,1,0:T(8,128)(2,1)S(1)}, u32[]{:S(2)}, u32[]{:S(2)}) collective-permute-start(bf16[6,128,128]{2,1,0:T(8,128)(2,1)S(1)} %collective-permute-done.2.refs_3_), channel_id=1, source_target_pairs={{0,16},{8,24},{16,32},{17,1},{24,40},{25,9},{32,48},{33,17},{40,56... | collective-permute-start | bytes 589832 | tf_op jit(solution)/shard_map/ppermute | solution.py:255
  41.5 20.7 %collective-permute-start.6 = (bf16[6,128,128]{2,1,0:T(8,128)(2,1)S(1)}, bf16[6,128,128]{2,1,0:T(8,128)(2,1)S(1)}, u32[]{:S(2)}, u32[]{:S(2)}) collective-permute-start(bf16[6,128,128]{2,1,0:T(8,128)(2,1)S(1)} %get-tuple-element.48.refs_0_), channel_id=1, source_target_pairs={{0,128},{8,136},{16,144},{24,152},{32,160},{40,168},{48,176},{56,1... | collective-permute-start | bytes 589832 | tf_op jit(solution)/shard_map/ppermute | solution.py:255
  44.6 17.6 %collective-permute-start.1 = (bf16[6,128,128]{2,1,0:T(8,128)(2,1)S(1)}, bf16[6,128,128]{2,1,0:T(8,128)(2,1)S(1)}, u32[]{:S(2)}, u32[]{:S(2)}) collective-permute-start(bf16[6,128,128]{2,1,0:T(8,128)(2,1)S(1)} %get-tuple-element.48.refs_0_), channel_id=1, source_target_pairs={{1,9},{8,0},{9,17},{16,8},{17,25},{24,16},{25,33},{32,24},{33,41},... | collective-permute-start | bytes 589832 | tf_op jit(solution)/shard_map/ppermute | solution.py:255
  46.5 15.6 %collective-permute-start = (bf16[6,128,128]{2,1,0:T(8,128)(2,1)S(1)}, bf16[6,128,128]{2,1,0:T(8,128)(2,1)S(1)}, u32[]{:S(2)}, u32[]{:S(2)}) collective-permute-start(bf16[6,128,128]{2,1,0:T(8,128)(2,1)S(1)} %get-tuple-element.48.refs_0_), channel_id=1, source_target_pairs={{0,8},{8,16},{9,1},{16,24},{17,9},{24,32},{25,17},{32,40},{33,25},... | collective-permute-start | bytes 589832 | tf_op jit(solution)/shard_map/ppermute | solution.py:255
  52.0 13.9 %collective-permute-start.10 = (bf16[6,128,128]{2,1,0:T(8,128)(2,1)S(1)}, bf16[6,128,128]{2,1,0:T(8,128)(2,1)S(1)}, u32[]{:S(2)}, u32[]{:S(2)}) collective-permute-start(bf16[6,128,128]{2,1,0:T(8,128)(2,1)S(1)} %collective-permute-done.5.refs_6_), channel_id=1, source_target_pairs={{1,33},{9,41},{17,49},{25,57},{32,0},{33,65},{40,8},{41,73},{48,16... | collective-permute-start | bytes 589832 | tf_op jit(solution)/shard_map/ppermute | solution.py:255
  54.0 20.4 %collective-permute-start.9 = (bf16[6,128,128]{2,1,0:T(8,128)(2,1)S(1)}, bf16[6,128,128]{2,1,0:T(8,128)(2,1)S(1)}, u32[]{:S(2)}, u32[]{:S(2)}) collective-permute-start(bf16[6,128,128]{2,1,0:T(8,128)(2,1)S(1)} %collective-permute-done.4.refs_5_), channel_id=1, source_target_pairs={{0,32},{8,40},{16,48},{24,56},{32,64},{33,1},{40,72},{41,9},{48,80... | collective-permute-start | bytes 589832 | tf_op jit(solution)/shard_map/ppermute | solution.py:255
  76.0 25.8 %collective-permute-start.11 = (bf16[6,128,128]{2,1,0:T(8,128)(2,1)S(1)}, bf16[6,128,128]{2,1,0:T(8,128)(2,1)S(1)}, u32[]{:S(2)}, u32[]{:S(2)}) collective-permute-start(bf16[6,128,128]{2,1,0:T(8,128)(2,1)S(1)} %get-tuple-element.57), channel_id=1, source_target_pairs={{1,33},{9,41},{17,49},{25,57},{32,0},{33,65},{40,8},{41,73},{48,16... | collective-permute-start | bytes 589832 | tf_op jit(solution)/shard_map/ppermute | solution.py:255
  78.4 23.8 %collective-permute-start.12 = (bf16[6,128,128]{2,1,0:T(8,128)(2,1)S(1)}, bf16[6,128,128]{2,1,0:T(8,128)(2,1)S(1)}, u32[]{:S(2)}, u32[]{:S(2)}) collective-permute-start(bf16[6,128,128]{2,1,0:T(8,128)(2,1)S(1)} %get-tuple-element.58), channel_id=1, source_target_pairs={{0,32},{8,40},{16,48},{24,56},{32,64},{33,1},{40,72},{41,9},{48,80... | collective-permute-start | bytes 589832 | tf_op jit(solution)/shard_map/ppermute | solution.py:255
  87.8 14.4 %collective-permute-start.13 = (bf16[6,128,128]{2,1,0:T(8,128)(2,1)S(1)}, bf16[6,128,128]{2,1,0:T(8,128)(2,1)S(1)}, u32[]{:S(2)}, u32[]{:S(2)}) collective-permute-start(bf16[6,128,128]{2,1,0:T(8,128)(2,1)S(1)} %get-tuple-element.64), channel_id=1, source_target_pairs={{0,256},{8,264},{16,272},{24,280},{32,288},{40,296},{48,304},{56,3... | collective-permute-start | bytes 589832 | tf_op jit(solution)/shard_map/ppermute | solution.py:260
  94.4 8.5 %collective-permute-start.14 = (bf16[6,128,128]{2,1,0:T(8,128)(2,1)S(1)}, bf16[6,128,128]{2,1,0:T(8,128)(2,1)S(1)}, u32[]{:S(2)}, u32[]{:S(2)}) collective-permute-start(bf16[6,128,128]{2,1,0:T(8,128)(2,1)S(1)} %get-tuple-element.65), channel_id=1, source_target_pairs={{1,9},{8,0},{9,17},{16,8},{17,25},{24,16},{25,33},{32,24},{33,41},... | collective-permute-start | bytes 589832 | tf_op jit(solution)/shard_map/ppermute | solution.py:255
  96.3 9.7 %collective-permute-start.15 = (bf16[6,128,128]{2,1,0:T(8,128)(2,1)S(1)}, bf16[6,128,128]{2,1,0:T(8,128)(2,1)S(1)}, u32[]{:S(2)}, u32[]{:S(2)}) collective-permute-start(bf16[6,128,128]{2,1,0:T(8,128)(2,1)S(1)} %get-tuple-element.66), channel_id=1, source_target_pairs={{0,8},{8,16},{9,1},{16,24},{17,9},{24,32},{25,17},{32,40},{33,25},... | collective-permute-start | bytes 589832 | tf_op jit(solution)/shard_map/ppermute | solution.py:255
  106.0 15.2 %collective-permute-start.16 = (bf16[6,128,128]{2,1,0:T(8,128)(2,1)S(1)}, bf16[6,128,128]{2,1,0:T(8,128)(2,1)S(1)}, u32[]{:S(2)}, u32[]{:S(2)}) collective-permute-start(bf16[6,128,128]{2,1,0:T(8,128)(2,1)S(1)} %add_convert_fusion.3), channel_id=1, source_target_pairs={{1,17},{9,25},{16,0},{17,33},{24,8},{25,41},{32,16},{33,49},{40,24... | collective-permute-start | bytes 589832 | tf_op jit(solution)/shard_map/ppermute | solution.py:255
  108.7 13.2 %collective-permute-start.17 = (bf16[6,128,128]{2,1,0:T(8,128)(2,1)S(1)}, bf16[6,128,128]{2,1,0:T(8,128)(2,1)S(1)}, u32[]{:S(2)}, u32[]{:S(2)}) collective-permute-start(bf16[6,128,128]{2,1,0:T(8,128)(2,1)S(1)} %add_convert_fusion.2), channel_id=1, source_target_pairs={{0,16},{8,24},{16,32},{17,1},{24,40},{25,9},{32,48},{33,17},{40,56... | collective-permute-start | bytes 589832 | tf_op jit(solution)/shard_map/ppermute | solution.py:255
  114.8 10.7 %collective-permute-start.18 = (bf16[6,128,128]{2,1,0:T(8,128)(2,1)S(1)}, bf16[6,128,128]{2,1,0:T(8,128)(2,1)S(1)}, u32[]{:S(2)}, u32[]{:S(2)}) collective-permute-start(bf16[6,128,128]{2,1,0:T(8,128)(2,1)S(1)} %get-tuple-element.76), channel_id=1, source_target_pairs={{1,129},{9,137},{17,145},{25,153},{33,161},{41,169},{49,177},{57,1... | collective-permute-start | bytes 589832 | tf_op jit(solution)/shard_map/ppermute | solution.py:255
  116.1 9.4 %collective-permute-start.19 = (bf16[6,128,128]{2,1,0:T(8,128)(2,1)S(1)}, bf16[6,128,128]{2,1,0:T(8,128)(2,1)S(1)}, u32[]{:S(2)}, u32[]{:S(2)}) collective-permute-start(bf16[6,128,128]{2,1,0:T(8,128)(2,1)S(1)} %get-tuple-element.77), channel_id=1, source_target_pairs={{0,128},{8,136},{16,144},{24,152},{32,160},{40,168},{48,176},{56,1... | collective-permute-start | bytes 589832 | tf_op jit(solution)/shard_map/ppermute | solution.py:255
  125.5 10.0 %collective-permute-start.20 = (bf16[6,128,128]{2,1,0:T(8,128)(2,1)S(1)}, bf16[6,128,128]{2,1,0:T(8,128)(2,1)S(1)}, u32[]{:S(2)}, u32[]{:S(2)}) collective-permute-start(bf16[6,128,128]{2,1,0:T(8,128)(2,1)S(1)} %get-tuple-element.83), channel_id=1, source_target_pairs={{1,17},{9,25},{16,0},{17,33},{24,8},{25,41},{32,16},{33,49},{40,24... | collective-permute-start | bytes 589832 | tf_op jit(solution)/shard_map/ppermute | solution.py:255
  127.5 11.8 %collective-permute-start.21 = (bf16[6,128,128]{2,1,0:T(8,128)(2,1)S(1)}, bf16[6,128,128]{2,1,0:T(8,128)(2,1)S(1)}, u32[]{:S(2)}, u32[]{:S(2)}) collective-permute-start(bf16[6,128,128]{2,1,0:T(8,128)(2,1)S(1)} %get-tuple-element.84), channel_id=1, source_target_pairs={{0,16},{8,24},{16,32},{17,1},{24,40},{25,9},{32,48},{33,17},{40,56... | collective-permute-start | bytes 589832 | tf_op jit(solution)/shard_map/ppermute | solution.py:255

commit v10 on v9

--- a/solution.py
+++ b/solution.py
@@ -255,9 +255,14 @@
     return lax.ppermute(value, SEQ + ("c",), pairs)
 
 
-def half_round(value):
+def around(value, steps):
     count = lax.axis_size("x") * lax.axis_size("z")
-    return lax.ppermute(value, SEQ, [(i, (i + count // 2) % count) for i in range(count)])
+    pairs = [
+        (2 * i + core, 2 * ((i + way * steps) % count) + core)
+        for i in range(count)
+        for core, way in enumerate((1, -1))
+    ]
+    return lax.ppermute(value, SEQ + ("c",), pairs)
 
 
 def relay(offset):
@@ -272,15 +277,18 @@
 
 
 def collect(parts):
-    line = lax.axis_size("z")
-    places = [len(NEAR) - 2, len(NEAR) - 1]
+    near, line = len(NEAR), lax.axis_size("z")
+    places = [near - 2, near - 1]
     carried = [parts[place] for place in places]
-    others = [
-        lambda: parts[0] + half_round(parts[len(NEAR) + 2]).astype(F32),
-        lambda: passed(parts[1], NEAR[1]),
-        lambda: passed(parts[2], NEAR[2]),
-        lambda: passed(parts[len(NEAR)], -line),
-        lambda: passed(parts[len(NEAR) + 1], line),
+    stages = [
+        lambda got: [
+            passed(parts[1], NEAR[1]), passed(parts[2], NEAR[2]), around(parts[near + 2], -line)
+        ],
+        lambda got: [
+            *got[:2],
+            around((got[2].astype(F32) + parts[near]).astype(BF16), -line),
+            passed(parts[near + 1], line),
+        ],
     ]
     arrived = []
     while True:
@@ -294,10 +302,11 @@
         carried = [
             (part.astype(F32) + parts[place]).astype(BF16) for part, place in zip(carried, places)
         ]
-        arrived += [send() for send in others[:3]]
-        others = others[3:]
+        arrived = stages.pop(0)(arrived)
         carried, arrived = lax.optimization_barrier((carried, arrived))
-    return arrived + carried + [send() for send in others]
+    for stage in stages:
+        arrived = stage(arrived)
+    return arrived + carried
 
 
 def per_device(total_heads, q_raw, k_raw, values, grad_out, q_gain, k_gain, key_tiles):
@@ -335,9 +344,9 @@
         [(whole, BF16), (pair, BF16), ((8, TILE), F32)],
         sums, gains, raw,
     )
-    half = half_round(pairs)
+    before = around(pairs, line)
     tiles = spread(pairs)
-    tiles += [passed(pairs, line), passed(pairs, -line), half]
+    tiles += [before, passed(pairs, -line), around(before, line)]
     late = [near - 2, near - 1]
     early = [t for t in range(count) if t not in late]
     early_tiles, late_tiles = [tiles[t] for t in early], [tiles[t] for t in late]
@@ -357,7 +366,7 @@
     dq, *early_parts = call(
         functools.partial(rest_kernel, heads),
         "rest",
-        [(whole, F32)] + [(pair, F32 if t == 0 or 2 < t < near else BF16) for t in early],
+        [(whole, F32)] + [(pair, F32 if t == 0 or 2 < t <= near else BF16) for t in early],
         q_norm, grad_out, weights, late_dq, late_rows, *early_tiles,
     )
     parts = dict(zip(early + late, early_parts + late_parts))
@@ -366,7 +375,7 @@
         functools.partial(terms_kernel, heads),
         "terms",
         [(whole, F32), (whole, BF16), rows],
-        raw, dq, gains, *arrived,
+        raw, dq, gains, parts[0], *arrived,
     )
     terms = lax.all_to_all(terms, HEAD, 0, 0, tiled=True)
     grad_q, grad_k = call(

time: 155 us -> 154 us (level)
  the two profiles are of different devices: /device:TPU:7 before, /device:TPU:34 now
where the time goes in v10:
time: 154 us; the launch traced here: 153 us
  starting transfers between devices  96 us (62%)
  waiting for transfers between devices  39 us (25%)
  blocking collectives  7.8 us (5%)
  Pallas kernels  7.59 us (5%)
  other arithmetic  2.01 us (1%)
    ppermute x18, starting transfers between devices, passed(): return lax.ppermute(value, SEQ + ('c',), pairs)  78.5 us
    ppermute x18, waiting for transfers between devices, passed(): return lax.ppermute(value, SEQ + ('c',), pairs)  34.2 us
    ppermute x4, starting transfers between devices, around(): return lax.ppermute(value, SEQ + ('c',), pairs)  13 us
    all_to_all x1, blocking collectives, per_device(): terms = lax.all_to_all(terms, HEAD, 0, 0, tiled=True)  7.8 us
    pallas_call x7, Pallas kernels, call(): pl.pallas_call(kernel, out_shape=[jax.ShapeDtypeStruct(shape, dtype) for...  7.59 us
    all_to_all x1, waiting for transfers between devices, per_device(): sums = lax.all_to_all(squares, HEAD, 0, 0, tiled=True)  4.74 us
    all_to_all x1, starting transfers between devices, per_device(): sums = lax.all_to_all(squares, HEAD, 0, 0, tiled=True)  4.47 us
  transfers between devices with their start and end apart: 23, of which 9 were waited for; matrix products, arithmetic and copies ran while one was open for 1% of the time, Pallas kernels for 2%

profile of v10, /device:TPU:34, one launch (start us, length us, event | category | flops | bytes accessed | tf_op | source)
XLA Modules:
  0.0 153.4 jit_solution(12549662876770050350)
XLA Ops:
  0.6 1.1 pad_maximum_fusion.raw_ref
  1.7 0.8 squares.1
  2.5 4.5 %all-to-all-start = ((f32[8,8,128]{2,1,0:T(8,128)}), f32[8,8,128]{2,1,0:T(8,128)S(1)}, u32[]{:S(2)}, u32[]{:S(2)}) async-start(f32[8,8,128]{2,1,0:T(8,128)} %squares.1), calls=%async_computation | async-start | bytes 65536 | tf_op jit(solution)/shard_map/all_to_all | solution.py:340
  7.0 0.7 pad_maximum_fusion.1.gain_ref
  7.7 4.7 %all-to-all-done.sums_ref = f32[8,8,128]{2,1,0:T(8,128)S(1)} async-done(((f32[8,8,128]{2,1,0:T(8,128)}), f32[8,8,128]{2,1,0:T(8,128)S(1)}, u32[]{:S(2)}, u32[]{:S(2)}) %all-to-all-start) | async-done | bytes 32800 | tf_op jit(solution)/shard_map/all_to_all | solution.py:340
  12.4 0.2 norm.1
  12.7 10.9 %collective-permute-start.3 = (bf16[6,128,128]{2,1,0:T(8,128)(2,1)S(1)}, bf16[6,128,128]{2,1,0:T(8,128)(2,1)S(1)}, u32[]{:S(2)}, u32[]{:S(2)}) collective-permute-start(bf16[6,128,128]{2,1,0:T(8,128)(2,1)S(1)} %get-tuple-element.47.refs_0_), channel_id=1, source_target_pairs={{1,17},{9,25},{16,0},{17,33},{24,8},{25,41},{32,16},{33,49},{40,24... | collective-permute-start | bytes 589832 | tf_op jit(solution)/shard_map/ppermute | solution.py:255
  23.6 1.9 %collective-permute-start.2 = (bf16[6,128,128]{2,1,0:T(8,128)(2,1)S(1)}, bf16[6,128,128]{2,1,0:T(8,128)(2,1)S(1)}, u32[]{:S(2)}, u32[]{:S(2)}) collective-permute-start(bf16[6,128,128]{2,1,0:T(8,128)(2,1)S(1)} %get-tuple-element.47.refs_0_), channel_id=1, source_target_pairs={{0,16},{8,24},{16,32},{17,1},{24,40},{25,9},{32,48},{33,17},{40,56... | collective-permute-start | bytes 589832 | tf_op jit(solution)/shard_map/ppermute | solution.py:255
  25.5 1.9 %collective-permute-start.7 = (bf16[6,128,128]{2,1,0:T(8,128)(2,1)S(1)}, bf16[6,128,128]{2,1,0:T(8,128)(2,1)S(1)}, u32[]{:S(2)}, u32[]{:S(2)}) collective-permute-start(bf16[6,128,128]{2,1,0:T(8,128)(2,1)S(1)} %get-tuple-element.47.refs_0_), channel_id=1, source_target_pairs={{1,129},{9,137},{17,145},{25,153},{33,161},{41,169},{49,177},{57,1... | collective-permute-start | bytes 589832 | tf_op jit(solution)/shard_map/ppermute | solution.py:255
  27.5 3.9 %collective-permute-start.6 = (bf16[6,128,128]{2,1,0:T(8,128)(2,1)S(1)}, bf16[6,128,128]{2,1,0:T(8,128)(2,1)S(1)}, u32[]{:S(2)}, u32[]{:S(2)}) collective-permute-start(bf16[6,128,128]{2,1,0:T(8,128)(2,1)S(1)} %get-tuple-element.47.refs_0_), channel_id=1, source_target_pairs={{0,128},{1,385},{8,136},{9,393},{16,144},{17,401},{24,152},{25,409... | collective-permute-start | bytes 589832 | tf_op jit(solution)/shard_map/ppermute | solution.py:265
  31.4 6.9 %collective-permute-start.5 = (bf16[6,128,128]{2,1,0:T(8,128)(2,1)S(1)}, bf16[6,128,128]{2,1,0:T(8,128)(2,1)S(1)}, u32[]{:S(2)}, u32[]{:S(2)}) collective-permute-start(bf16[6,128,128]{2,1,0:T(8,128)(2,1)S(1)} %collective-permute-done.3.refs_4_), channel_id=1, source_target_pairs={{1,17},{9,25},{16,0},{17,33},{24,8},{25,41},{32,16},{33,49},{40,24... | collective-permute-start | bytes 589832 | tf_op jit(solution)/shard_map/ppermute | solution.py:255
  38.3 1.9 %collective-permute-start.4 = (bf16[6,128,128]{2,1,0:T(8,128)(2,1)S(1)}, bf16[6,128,128]{2,1,0:T(8,128)(2,1)S(1)}, u32[]{:S(2)}, u32[]{:S(2)}) collective-permute-start(bf16[6,128,128]{2,1,0:T(8,128)(2,1)S(1)} %collective-permute-done.2.refs_3_), channel_id=1, source_target_pairs={{0,16},{8,24},{16,32},{17,1},{24,40},{25,9},{32,48},{33,17},{40,56... | collective-permute-start | bytes 589832 | tf_op jit(solution)/shard_map/ppermute | solution.py:255
  40.3 4.6 %collective-permute-start.1 = (bf16[6,128,128]{2,1,0:T(8,128)(2,1)S(1)}, bf16[6,128,128]{2,1,0:T(8,128)(2,1)S(1)}, u32[]{:S(2)}, u32[]{:S(2)}) collective-permute-start(bf16[6,128,128]{2,1,0:T(8,128)(2,1)S(1)} %get-tuple-element.47.refs_0_), channel_id=1, source_target_pairs={{1,9},{8,0},{9,17},{16,8},{17,25},{24,16},{25,33},{32,24},{33,41},... | collective-permute-start | bytes 589832 | tf_op jit(solution)/shard_map/ppermute | solution.py:255
  44.9 0.0 collective-permute-done.7.refs_8_
  44.9 1.9 %collective-permute-start = (bf16[6,128,128]{2,1,0:T(8,128)(2,1)S(1)}, bf16[6,128,128]{2,1,0:T(8,128)(2,1)S(1)}, u32[]{:S(2)}, u32[]{:S(2)}) collective-permute-start(bf16[6,128,128]{2,1,0:T(8,128)(2,1)S(1)} %get-tuple-element.47.refs_0_), channel_id=1, source_target_pairs={{0,8},{8,16},{9,1},{16,24},{17,9},{24,32},{25,17},{32,40},{33,25},... | collective-permute-start | bytes 589832 | tf_op jit(solution)/shard_map/ppermute | solution.py:255
  46.9 0.0 collective-permute-done.6.refs_7_
  46.9 3.4 %collective-permute-start.8 = (bf16[6,128,128]{2,1,0:T(8,128)(2,1)S(1)}, bf16[6,128,128]{2,1,0:T(8,128)(2,1)S(1)}, u32[]{:S(2)}, u32[]{:S(2)}) collective-permute-start(bf16[6,128,128]{2,1,0:T(8,128)(2,1)S(1)} %collective-permute-done.6.refs_7_), channel_id=1, source_target_pairs={{0,128},{1,385},{8,136},{9,393},{16,144},{17,401},{24,152},{25,409... | collective-permute-start | bytes 589832 | tf_op jit(solution)/shard_map/ppermute | solution.py:265
  50.3 0.0 collective-permute-done.5.refs_6_
  50.3 7.8 %collective-permute-start.10 = (bf16[6,128,128]{2,1,0:T(8,128)(2,1)S(1)}, bf16[6,128,128]{2,1,0:T(8,128)(2,1)S(1)}, u32[]{:S(2)}, u32[]{:S(2)}) collective-permute-start(bf16[6,128,128]{2,1,0:T(8,128)(2,1)S(1)} %collective-permute-done.5.refs_6_), channel_id=1, source_target_pairs={{1,33},{9,41},{17,49},{25,57},{32,0},{33,65},{40,8},{41,73},{48,16... | collective-permute-start | bytes 589832 | tf_op jit(solution)/shard_map/ppermute | solution.py:255
  58.1 0.0 collective-permute-done.4.refs_5_
  58.1 1.9 %collective-permute-start.9 = (bf16[6,128,128]{2,1,0:T(8,128)(2,1)S(1)}, bf16[6,128,128]{2,1,0:T(8,128)(2,1)S(1)}, u32[]{:S(2)}, u32[]{:S(2)}) collective-permute-start(bf16[6,128,128]{2,1,0:T(8,128)(2,1)S(1)} %collective-permute-done.4.refs_5_), channel_id=1, source_target_pairs={{0,32},{8,40},{16,48},{24,56},{32,64},{33,1},{40,72},{41,9},{48,80... | collective-permute-start | bytes 589832 | tf_op jit(solution)/shard_map/ppermute | solution.py:255
  60.1 1.3 collective-permute-done.refs_1_
  61.3 1.4 early.1
  62.7 11.3 %collective-permute-done.10.refs_1_ = bf16[6,128,128]{2,1,0:T(8,128)(2,1)S(1)} collective-permute-done((bf16[6,128,128]{2,1,0:T(8,128)(2,1)S(1)}, bf16[6,128,128]{2,1,0:T(8,128)(2,1)S(1)}, u32[]{:S(2)}, u32[]{:S(2)}) %collective-permute-start.10) | collective-permute-done | bytes 196640 | tf_op jit(solution)/shard_map/ppermute | solution.py:255
  74.0 1.7 %late.1 = (bf16[3,128,128]{2,1,0:T(8,128)(2,1)}, f32[3,128,128]{2,1,0:T(8,128)S(1)}, f32[128,128]{1,0:T(8,128)S(1)}, bf16[6,128,128]{2,1,0:T(8,128)(2,1)S(1)}, bf16[6,128,128]{2,1,0:T(8,128)(2,1)S(1)}) custom-call(bf16[3,128,128]{2,1,0:T(8,128)(2,1)S(1)} %get-tuple-element.46.q_ref, bf16[3,128,128]{2,1,0:T(8,128)(2,1)S(1)} %bitcast.8, ...), custom_call_target="tpu_custom_call" | custom-call | tf_op jit(solution)/shard_map/late/pallas_call | solution.py:328
  75.7 8.0 %collective-permute-start.11 = (bf16[6,128,128]{2,1,0:T(8,128)(2,1)S(1)}, bf16[6,128,128]{2,1,0:T(8,128)(2,1)S(1)}, u32[]{:S(2)}, u32[]{:S(2)}) collective-permute-start(bf16[6,128,128]{2,1,0:T(8,128)(2,1)S(1)} %get-tuple-element.57), channel_id=1, source_target_pairs={{1,33},{9,41},{17,49},{25,57},{32,0},{33,65},{40,8},{41,73},{48,16... | collective-permute-start | bytes 589832 | tf_op jit(solution)/shard_map/ppermute | solution.py:255
  83.7 1.9 %collective-permute-start.12 = (bf16[6,128,128]{2,1,0:T(8,128)(2,1)S(1)}, bf16[6,128,128]{2,1,0:T(8,128)(2,1)S(1)}, u32[]{:S(2)}, u32[]{:S(2)}) collective-permute-start(bf16[6,128,128]{2,1,0:T(8,128)(2,1)S(1)} %get-tuple-element.58), channel_id=1, source_target_pairs={{0,32},{8,40},{16,48},{24,56},{32,64},{33,1},{40,72},{41,9},{48,80... | collective-permute-start | bytes 589832 | tf_op jit(solution)/shard_map/ppermute | solution.py:255
  85.6 1.6 %rest.1 = (f32[3,128,128]{2,1,0:T(8,128)S(1)}, f32[6,128,128]{2,1,0:T(8,128)S(1)}, bf16[6,128,128]{2,1,0:T(8,128)(2,1)S(1)}, bf16[6,128,128]{2,1,0:T(8,128)(2,1)...) custom-call(bf16[3,128,128]{2,1,0:T(8,128)(2,1)S(1)} %get-tuple-elem, ...), custom_call_target="tpu_custom_call" | custom-call | tf_op jit(solution)/shard_map/rest/pallas_call | solution.py:328
  87.3 4.8 %collective-permute-start.13 = (bf16[6,128,128]{2,1,0:T(8,128)(2,1)S(1)}, bf16[6,128,128]{2,1,0:T(8,128)(2,1)S(1)}, u32[]{:S(2)}, u32[]{:S(2)}) collective-permute-start(bf16[6,128,128]{2,1,0:T(8,128)(2,1)S(1)} %get-tuple-element.63), channel_id=1, source_target_pairs={{1,9},{8,0},{9,17},{16,8},{17,25},{24,16},{25,33},{32,24},{33,41},... | collective-permute-start | bytes 589832 | tf_op jit(solution)/shard_map/ppermute | solution.py:255
  92.1 1.9 %collective-permute-start.14 = (bf16[6,128,128]{2,1,0:T(8,128)(2,1)S(1)}, bf16[6,128,128]{2,1,0:T(8,128)(2,1)S(1)}, u32[]{:S(2)}, u32[]{:S(2)}) collective-permute-start(bf16[6,128,128]{2,1,0:T(8,128)(2,1)S(1)} %get-tuple-element.64), channel_id=1, source_target_pairs={{0,8},{8,16},{9,1},{16,24},{17,9},{24,32},{25,17},{32,40},{33,25},... | collective-permute-start | bytes 589832 | tf_op jit(solution)/shard_map/ppermute | solution.py:255
  94.1 3.8 %collective-permute-start.15 = (bf16[6,128,128]{2,1,0:T(8,128)(2,1)S(1)}, bf16[6,128,128]{2,1,0:T(8,128)(2,1)S(1)}, u32[]{:S(2)}, u32[]{:S(2)}) collective-permute-start(bf16[6,128,128]{2,1,0:T(8,128)(2,1)S(1)} %get-tuple-element.65), channel_id=1, source_target_pairs={{0,384},{1,129},{8,392},{9,137},{16,400},{17,145},{24,408},{25,153... | collective-permute-start | bytes 589832 | tf_op jit(solution)/shard_map/ppermute | solution.py:265
  97.8 2.3 %collective-permute-done.11 = bf16[6,128,128]{2,1,0:T(8,128)(2,1)S(1)} collective-permute-done((bf16[6,128,128]{2,1,0:T(8,128)(2,1)S(1)}, bf16[6,128,128]{2,1,0:T(8,128)(2,1)S(1)}, u32[]{:S(2)}, u32[]{:S(2)}) %collective-permute-start.11) | collective-permute-done | bytes 196640 | tf_op jit(solution)/shard_map/ppermute | solution.py:255
  100.1 1.9 %collective-permute-start.19 = (bf16[6,128,128]{2,1,0:T(8,128)(2,1)S(1)}, bf16[6,128,128]{2,1,0:T(8,128)(2,1)S(1)}, u32[]{:S(2)}, u32[]{:S(2)}) collective-permute-start(bf16[6,128,128]{2,1,0:T(8,128)(2,1)S(1)} %get-tuple-element.76), channel_id=1, source_target_pairs={{0,128},{8,136},{16,144},{24,152},{32,160},{40,168},{48,176},{56,1... | collective-permute-start | bytes 589832 | tf_op jit(solution)/shard_map/ppermute | solution.py:255
  102.0 0.1 add_convert_fusion.3
  102.1 3.5 %collective-permute-done.13.refs_1_ = bf16[6,128,128]{2,1,0:T(8,128)(2,1)S(1)} collective-permute-done((bf16[6,128,128]{2,1,0:T(8,128)(2,1)S(1)}, bf16[6,128,128]{2,1,0:T(8,128)(2,1)S(1)}, u32[]{:S(2)}, u32[]{:S(2)}) %collective-permute-start.13) | collective-permute-done | bytes 196640 | tf_op jit(solution)/shard_map/ppermute | solution.py:255
  105.7 8.6 %collective-permute-start.16 = (bf16[6,128,128]{2,1,0:T(8,128)(2,1)S(1)}, bf16[6,128,128]{2,1,0:T(8,128)(2,1)S(1)}, u32[]{:S(2)}, u32[]{:S(2)}) collective-permute-start(bf16[6,128,128]{2,1,0:T(8,128)(2,1)S(1)} %add_convert_fusion.4), channel_id=1, source_target_pairs={{1,17},{9,25},{16,0},{17,33},{24,8},{25,41},{32,16},{33,49},{40,24... | collective-permute-start | bytes 589832 | tf_op jit(solution)/shard_map/ppermute | solution.py:255
  114.3 1.9 %collective-permute-start.17 = (bf16[6,128,128]{2,1,0:T(8,128)(2,1)S(1)}, bf16[6,128,128]{2,1,0:T(8,128)(2,1)S(1)}, u32[]{:S(2)}, u32[]{:S(2)}) collective-permute-start(bf16[6,128,128]{2,1,0:T(8,128)(2,1)S(1)} %add_convert_fusion.3), channel_id=1, source_target_pairs={{0,16},{8,24},{16,32},{17,1},{24,40},{25,9},{32,48},{33,17},{40,56... | collective-permute-start | bytes 589832 | tf_op jit(solution)/shard_map/ppermute | solution.py:255
  116.3 1.9 %collective-permute-start.18 = (bf16[6,128,128]{2,1,0:T(8,128)(2,1)S(1)}, bf16[6,128,128]{2,1,0:T(8,128)(2,1)S(1)}, u32[]{:S(2)}, u32[]{:S(2)}) collective-permute-start(bf16[6,128,128]{2,1,0:T(8,128)(2,1)S(1)} %add_convert_fusion), channel_id=1, source_target_pairs={{0,384},{1,129},{8,392},{9,137},{16,400},{17,145},{24,408},{25,153... | collective-permute-start | bytes 589832 | tf_op jit(solution)/shard_map/ppermute | solution.py:265
  118.2 4.9 %collective-permute-done.16 = bf16[6,128,128]{2,1,0:T(8,128)(2,1)S(1)} collective-permute-done((bf16[6,128,128]{2,1,0:T(8,128)(2,1)S(1)}, bf16[6,128,128]{2,1,0:T(8,128)(2,1)S(1)}, u32[]{:S(2)}, u32[]{:S(2)}) %collective-permute-start.16) | collective-permute-done | bytes 196640 | tf_op jit(solution)/shard_map/ppermute | solution.py:255
  123.1 1.8 %collective-permute-done.17 = bf16[6,128,128]{2,1,0:T(8,128)(2,1)S(1)} collective-permute-done((bf16[6,128,128]{2,1,0:T(8,128)(2,1)S(1)}, bf16[6,128,128]{2,1,0:T(8,128)(2,1)S(1)}, u32[]{:S(2)}, u32[]{:S(2)}) %collective-permute-start.17) | collective-permute-done | bytes 196640 | tf_op jit(solution)/shard_map/ppermute | solution.py:255
  124.9 0.1 add_convert_fusion.1
  125.0 7.6 %collective-permute-start.20 = (bf16[6,128,128]{2,1,0:T(8,128)(2,1)S(1)}, bf16[6,128,128]{2,1,0:T(8,128)(2,1)S(1)}, u32[]{:S(2)}, u32[]{:S(2)}) collective-permute-start(bf16[6,128,128]{2,1,0:T(8,128)(2,1)S(1)} %get-tuple-element.81), channel_id=1, source_target_pairs={{1,17},{9,25},{16,0},{17,33},{24,8},{25,41},{32,16},{33,49},{40,24... | collective-permute-start | bytes 589832 | tf_op jit(solution)/shard_map/ppermute | solution.py:255
  132.6 1.9 %collective-permute-start.21 = (bf16[6,128,128]{2,1,0:T(8,128)(2,1)S(1)}, bf16[6,128,128]{2,1,0:T(8,128)(2,1)S(1)}, u32[]{:S(2)}, u32[]{:S(2)}) collective-permute-start(bf16[6,128,128]{2,1,0:T(8,128)(2,1)S(1)} %get-tuple-element.82), channel_id=1, source_target_pairs={{0,16},{8,24},{16,32},{17,1},{24,40},{25,9},{32,48},{33,17},{40,56... | collective-permute-start | bytes 589832 | tf_op jit(solution)/shard_map/ppermute | solution.py:255
  134.6 2.3 %collective-permute-done.20.refs_5_ = bf16[6,128,128]{2,1,0:T(8,128)(2,1)S(1)} collective-permute-done((bf16[6,128,128]{2,1,0:T(8,128)(2,1)S(1)}, bf16[6,128,128]{2,1,0:T(8,128)(2,1)S(1)}, u32[]{:S(2)}, u32[]{:S(2)}) %collective-permute-start.20) | collective-permute-done | bytes 196640 | tf_op jit(solution)/shard_map/ppermute | solution.py:255
  136.9 6.8 %collective-permute-done.21.refs_6_ = bf16[6,128,128]{2,1,0:T(8,128)(2,1)S(1)} collective-permute-done((bf16[6,128,128]{2,1,0:T(8,128)(2,1)S(1)}, bf16[6,128,128]{2,1,0:T(8,128)(2,1)S(1)}, u32[]{:S(2)}, u32[]{:S(2)}) %collective-permute-start.21) | collective-permute-done | bytes 196640 | tf_op jit(solution)/shard_map/ppermute | solution.py:255
  143.7 0.9 terms.1
  144.6 7.8 %all_to_all.10.terms_ref = f32[8,8,128]{2,1,0:T(8,128)S(1)} all-to-all(f32[8,8,128]{2,1,0:T(8,128)S(1)} %get-tuple-element.83), channel_id=1, replica_groups=mesh['x'=4,'z'=16,'y'=4,'c'=2] {'y','c'}, dimensions={0} | all-to-all | bytes 65536 | tf_op jit(solution)/shard_map/all_to_all | solution.py:380
  152.4 0.9 final.1
  (14 shorter events, 0.1 us)
Async XLA Ops:
  0.6 73.3 %copy-start = (bf16[128,3,128]{2,0,1:T(8,128)(2,1)S(1)}, bf16[128,3,128]{2,0,1:T(8,128)(2,1)}, u32[]{:S(2)}) copy-start(bf16[128,3,128]{2,0,1:T(8,128)(2,1)} %param.10) | copy-start | bytes 294916
  2.5 9.9 %all-to-all-start = ((f32[8,8,128]{2,1,0:T(8,128)}), f32[8,8,128]{2,1,0:T(8,128)S(1)}, u32[]{:S(2)}, u32[]{:S(2)}) async-start(f32[8,8,128]{2,1,0:T(8,128)} %squares.1), calls=%async_computation | async-start | bytes 65536 | tf_op jit(solution)/shard_map/all_to_all | solution.py:340
  12.7 18.7 %collective-permute-start.3 = (bf16[6,128,128]{2,1,0:T(8,128)(2,1)S(1)}, bf16[6,128,128]{2,1,0:T(8,128)(2,1)S(1)}, u32[]{:S(2)}, u32[]{:S(2)}) collective-permute-start(bf16[6,128,128]{2,1,0:T(8,128)(2,1)S(1)} %get-tuple-element.47.refs_0_), channel_id=1, source_target_pairs={{1,17},{9,25},{16,0},{17,33},{24,8},{25,41},{32,16},{33,49},{40,24... | collective-permute-start | bytes 589832 | tf_op jit(solution)/shard_map/ppermute | solution.py:255
  23.6 14.7 %collective-permute-start.2 = (bf16[6,128,128]{2,1,0:T(8,128)(2,1)S(1)}, bf16[6,128,128]{2,1,0:T(8,128)(2,1)S(1)}, u32[]{:S(2)}, u32[]{:S(2)}) collective-permute-start(bf16[6,128,128]{2,1,0:T(8,128)(2,1)S(1)} %get-tuple-element.47.refs_0_), channel_id=1, source_target_pairs={{0,16},{8,24},{16,32},{17,1},{24,40},{25,9},{32,48},{33,17},{40,56... | collective-permute-start | bytes 589832 | tf_op jit(solution)/shard_map/ppermute | solution.py:255
  25.5 19.4 %collective-permute-start.7 = (bf16[6,128,128]{2,1,0:T(8,128)(2,1)S(1)}, bf16[6,128,128]{2,1,0:T(8,128)(2,1)S(1)}, u32[]{:S(2)}, u32[]{:S(2)}) collective-permute-start(bf16[6,128,128]{2,1,0:T(8,128)(2,1)S(1)} %get-tuple-element.47.refs_0_), channel_id=1, source_target_pairs={{1,129},{9,137},{17,145},{25,153},{33,161},{41,169},{49,177},{57,1... | collective-permute-start | bytes 589832 | tf_op jit(solution)/shard_map/ppermute | solution.py:255
  27.5 19.4 %collective-permute-start.6 = (bf16[6,128,128]{2,1,0:T(8,128)(2,1)S(1)}, bf16[6,128,128]{2,1,0:T(8,128)(2,1)S(1)}, u32[]{:S(2)}, u32[]{:S(2)}) collective-permute-start(bf16[6,128,128]{2,1,0:T(8,128)(2,1)S(1)} %get-tuple-element.47.refs_0_), channel_id=1, source_target_pairs={{0,128},{1,385},{8,136},{9,393},{16,144},{17,401},{24,152},{25,409... | collective-permute-start | bytes 589832 | tf_op jit(solution)/shard_map/ppermute | solution.py:265
  31.4 18.9 %collective-permute-start.5 = (bf16[6,128,128]{2,1,0:T(8,128)(2,1)S(1)}, bf16[6,128,128]{2,1,0:T(8,128)(2,1)S(1)}, u32[]{:S(2)}, u32[]{:S(2)}) collective-permute-start(bf16[6,128,128]{2,1,0:T(8,128)(2,1)S(1)} %collective-permute-done.3.refs_4_), channel_id=1, source_target_pairs={{1,17},{9,25},{16,0},{17,33},{24,8},{25,41},{32,16},{33,49},{40,24... | collective-permute-start | bytes 589832 | tf_op jit(solution)/shard_map/ppermute | solution.py:255
  38.3 19.8 %collective-permute-start.4 = (bf16[6,128,128]{2,1,0:T(8,128)(2,1)S(1)}, bf16[6,128,128]{2,1,0:T(8,128)(2,1)S(1)}, u32[]{:S(2)}, u32[]{:S(2)}) collective-permute-start(bf16[6,128,128]{2,1,0:T(8,128)(2,1)S(1)} %collective-permute-done.2.refs_3_), channel_id=1, source_target_pairs={{0,16},{8,24},{16,32},{17,1},{24,40},{25,9},{32,48},{33,17},{40,56... | collective-permute-start | bytes 589832 | tf_op jit(solution)/shard_map/ppermute | solution.py:255
  40.3 19.8 %collective-permute-start.1 = (bf16[6,128,128]{2,1,0:T(8,128)(2,1)S(1)}, bf16[6,128,128]{2,1,0:T(8,128)(2,1)S(1)}, u32[]{:S(2)}, u32[]{:S(2)}) collective-permute-start(bf16[6,128,128]{2,1,0:T(8,128)(2,1)S(1)} %get-tuple-element.47.refs_0_), channel_id=1, source_target_pairs={{1,9},{8,0},{9,17},{16,8},{17,25},{24,16},{25,33},{32,24},{33,41},... | collective-permute-start | bytes 589832 | tf_op jit(solution)/shard_map/ppermute | solution.py:255
  44.9 16.4 %collective-permute-start = (bf16[6,128,128]{2,1,0:T(8,128)(2,1)S(1)}, bf16[6,128,128]{2,1,0:T(8,128)(2,1)S(1)}, u32[]{:S(2)}, u32[]{:S(2)}) collective-permute-start(bf16[6,128,128]{2,1,0:T(8,128)(2,1)S(1)} %get-tuple-element.47.refs_0_), channel_id=1, source_target_pairs={{0,8},{8,16},{9,1},{16,24},{17,9},{24,32},{25,17},{32,40},{33,25},... | collective-permute-start | bytes 589832 | tf_op jit(solution)/shard_map/ppermute | solution.py:255
  46.9 14.5 %collective-permute-start.8 = (bf16[6,128,128]{2,1,0:T(8,128)(2,1)S(1)}, bf16[6,128,128]{2,1,0:T(8,128)(2,1)S(1)}, u32[]{:S(2)}, u32[]{:S(2)}) collective-permute-start(bf16[6,128,128]{2,1,0:T(8,128)(2,1)S(1)} %collective-permute-done.6.refs_7_), channel_id=1, source_target_pairs={{0,128},{1,385},{8,136},{9,393},{16,144},{17,401},{24,152},{25,409... | collective-permute-start | bytes 589832 | tf_op jit(solution)/shard_map/ppermute | solution.py:265
  50.3 23.7 %collective-permute-start.10 = (bf16[6,128,128]{2,1,0:T(8,128)(2,1)S(1)}, bf16[6,128,128]{2,1,0:T(8,128)(2,1)S(1)}, u32[]{:S(2)}, u32[]{:S(2)}) collective-permute-start(bf16[6,128,128]{2,1,0:T(8,128)(2,1)S(1)} %collective-permute-done.5.refs_6_), channel_id=1, source_target_pairs={{1,33},{9,41},{17,49},{25,57},{32,0},{33,65},{40,8},{41,73},{48,16... | collective-permute-start | bytes 589832 | tf_op jit(solution)/shard_map/ppermute | solution.py:255
  58.1 15.8 %collective-permute-start.9 = (bf16[6,128,128]{2,1,0:T(8,128)(2,1)S(1)}, bf16[6,128,128]{2,1,0:T(8,128)(2,1)S(1)}, u32[]{:S(2)}, u32[]{:S(2)}) collective-permute-start(bf16[6,128,128]{2,1,0:T(8,128)(2,1)S(1)} %collective-permute-done.4.refs_5_), channel_id=1, source_target_pairs={{0,32},{8,40},{16,48},{24,56},{32,64},{33,1},{40,72},{41,9},{48,80... | collective-permute-start | bytes 589832 | tf_op jit(solution)/shard_map/ppermute | solution.py:255
  75.7 24.4 %collective-permute-start.11 = (bf16[6,128,128]{2,1,0:T(8,128)(2,1)S(1)}, bf16[6,128,128]{2,1,0:T(8,128)(2,1)S(1)}, u32[]{:S(2)}, u32[]{:S(2)}) collective-permute-start(bf16[6,128,128]{2,1,0:T(8,128)(2,1)S(1)} %get-tuple-element.57), channel_id=1, source_target_pairs={{1,33},{9,41},{17,49},{25,57},{32,0},{33,65},{40,8},{41,73},{48,16... | collective-permute-start | bytes 589832 | tf_op jit(solution)/shard_map/ppermute | solution.py:255
  83.7 18.3 %collective-permute-start.12 = (bf16[6,128,128]{2,1,0:T(8,128)(2,1)S(1)}, bf16[6,128,128]{2,1,0:T(8,128)(2,1)S(1)}, u32[]{:S(2)}, u32[]{:S(2)}) collective-permute-start(bf16[6,128,128]{2,1,0:T(8,128)(2,1)S(1)} %get-tuple-element.58), channel_id=1, source_target_pairs={{0,32},{8,40},{16,48},{24,56},{32,64},{33,1},{40,72},{41,9},{48,80... | collective-permute-start | bytes 589832 | tf_op jit(solution)/shard_map/ppermute | solution.py:255
  87.3 18.4 %collective-permute-start.13 = (bf16[6,128,128]{2,1,0:T(8,128)(2,1)S(1)}, bf16[6,128,128]{2,1,0:T(8,128)(2,1)S(1)}, u32[]{:S(2)}, u32[]{:S(2)}) collective-permute-start(bf16[6,128,128]{2,1,0:T(8,128)(2,1)S(1)} %get-tuple-element.63), channel_id=1, source_target_pairs={{1,9},{8,0},{9,17},{16,8},{17,25},{24,16},{25,33},{32,24},{33,41},... | collective-permute-start | bytes 589832 | tf_op jit(solution)/shard_map/ppermute | solution.py:255
  92.1 13.5 %collective-permute-start.14 = (bf16[6,128,128]{2,1,0:T(8,128)(2,1)S(1)}, bf16[6,128,128]{2,1,0:T(8,128)(2,1)S(1)}, u32[]{:S(2)}, u32[]{:S(2)}) collective-permute-start(bf16[6,128,128]{2,1,0:T(8,128)(2,1)S(1)} %get-tuple-element.64), channel_id=1, source_target_pairs={{0,8},{8,16},{9,1},{16,24},{17,9},{24,32},{25,17},{32,40},{33,25},... | collective-permute-start | bytes 589832 | tf_op jit(solution)/shard_map/ppermute | solution.py:255
  94.1 11.6 %collective-permute-start.15 = (bf16[6,128,128]{2,1,0:T(8,128)(2,1)S(1)}, bf16[6,128,128]{2,1,0:T(8,128)(2,1)S(1)}, u32[]{:S(2)}, u32[]{:S(2)}) collective-permute-start(bf16[6,128,128]{2,1,0:T(8,128)(2,1)S(1)} %get-tuple-element.65), channel_id=1, source_target_pairs={{0,384},{1,129},{8,392},{9,137},{16,400},{17,145},{24,408},{25,153... | collective-permute-start | bytes 589832 | tf_op jit(solution)/shard_map/ppermute | solution.py:265
  100.1 24.9 %collective-permute-start.19 = (bf16[6,128,128]{2,1,0:T(8,128)(2,1)S(1)}, bf16[6,128,128]{2,1,0:T(8,128)(2,1)S(1)}, u32[]{:S(2)}, u32[]{:S(2)}) collective-permute-start(bf16[6,128,128]{2,1,0:T(8,128)(2,1)S(1)} %get-tuple-element.76), channel_id=1, source_target_pairs={{0,128},{8,136},{16,144},{24,152},{32,160},{40,168},{48,176},{56,1... | collective-permute-start | bytes 589832 | tf_op jit(solution)/shard_map/ppermute | solution.py:255
  105.7 17.4 %collective-permute-start.16 = (bf16[6,128,128]{2,1,0:T(8,128)(2,1)S(1)}, bf16[6,128,128]{2,1,0:T(8,128)(2,1)S(1)}, u32[]{:S(2)}, u32[]{:S(2)}) collective-permute-start(bf16[6,128,128]{2,1,0:T(8,128)(2,1)S(1)} %add_convert_fusion.4), channel_id=1, source_target_pairs={{1,17},{9,25},{16,0},{17,33},{24,8},{25,41},{32,16},{33,49},{40,24... | collective-permute-start | bytes 589832 | tf_op jit(solution)/shard_map/ppermute | solution.py:255
  114.3 10.6 %collective-permute-start.17 = (bf16[6,128,128]{2,1,0:T(8,128)(2,1)S(1)}, bf16[6,128,128]{2,1,0:T(8,128)(2,1)S(1)}, u32[]{:S(2)}, u32[]{:S(2)}) collective-permute-start(bf16[6,128,128]{2,1,0:T(8,128)(2,1)S(1)} %add_convert_fusion.3), channel_id=1, source_target_pairs={{0,16},{8,24},{16,32},{17,1},{24,40},{25,9},{32,48},{33,17},{40,56... | collective-permute-start | bytes 589832 | tf_op jit(solution)/shard_map/ppermute | solution.py:255
  116.3 8.8 %collective-permute-start.18 = (bf16[6,128,128]{2,1,0:T(8,128)(2,1)S(1)}, bf16[6,128,128]{2,1,0:T(8,128)(2,1)S(1)}, u32[]{:S(2)}, u32[]{:S(2)}) collective-permute-start(bf16[6,128,128]{2,1,0:T(8,128)(2,1)S(1)} %add_convert_fusion), channel_id=1, source_target_pairs={{0,384},{1,129},{8,392},{9,137},{16,400},{17,145},{24,408},{25,153... | collective-permute-start | bytes 589832 | tf_op jit(solution)/shard_map/ppermute | solution.py:265
  125.0 11.9 %collective-permute-start.20 = (bf16[6,128,128]{2,1,0:T(8,128)(2,1)S(1)}, bf16[6,128,128]{2,1,0:T(8,128)(2,1)S(1)}, u32[]{:S(2)}, u32[]{:S(2)}) collective-permute-start(bf16[6,128,128]{2,1,0:T(8,128)(2,1)S(1)} %get-tuple-element.81), channel_id=1, source_target_pairs={{1,17},{9,25},{16,0},{17,33},{24,8},{25,41},{32,16},{33,49},{40,24... | collective-permute-start | bytes 589832 | tf_op jit(solution)/shard_map/ppermute | solution.py:255
  132.6 11.1 %collective-permute-start.21 = (bf16[6,128,128]{2,1,0:T(8,128)(2,1)S(1)}, bf16[6,128,128]{2,1,0:T(8,128)(2,1)S(1)}, u32[]{:S(2)}, u32[]{:S(2)}) collective-permute-start(bf16[6,128,128]{2,1,0:T(8,128)(2,1)S(1)} %get-tuple-element.82), channel_id=1, source_target_pairs={{0,16},{8,24},{16,32},{17,1},{24,40},{25,9},{32,48},{33,17},{40,56... | collective-permute-start | bytes 589832 | tf_op jit(solution)/shard_map/ppermute | solution.py:255

commit v11 on v10

--- a/solution.py
+++ b/solution.py
@@ -346,10 +346,10 @@
     )
     before = around(pairs, line)
     tiles = spread(pairs)
-    tiles += [before, passed(pairs, -line), around(before, line)]
-    late = [near - 2, near - 1]
+    tiles += [before, passed(pairs, -line), None]
+    late = [near - 2, near - 1, near + 2]
     early = [t for t in range(count) if t not in late]
-    early_tiles, late_tiles = [tiles[t] for t in early], [tiles[t] for t in late]
+    early_tiles = [tiles[t] for t in early]
     square = ((TILE, TILE), F32)
     weights, early_out, early_rows = call(
         functools.partial(early_kernel, heads, early),
@@ -357,6 +357,9 @@
         [((heads, len(early), TILE, TILE), F32), (whole, F32), square],
         q_norm, *early_tiles,
     )
+    before, early_rows = lax.optimization_barrier((before, early_rows))
+    tiles[near + 2] = around(before, line)
+    late_tiles = [tiles[t] for t in late]
     attended, late_dq, late_rows, *late_parts = call(
         functools.partial(late_kernel, heads, late),
         "late",

time: 154 us -> 160 us (1.039)
  the two profiles are of different devices: /device:TPU:34 before, /device:TPU:7 now
where the time goes in v11:
time: 160 us; the launch traced here: 159 us
  starting transfers between devices  96.2 us (60%)
  waiting for transfers between devices  39.5 us (25%)
  blocking collectives  13.1 us (8%)
  Pallas kernels  7.65 us (5%)
  other arithmetic  1.99 us (1%)
    ppermute x18, starting transfers between devices, passed(): return lax.ppermute(value, SEQ + ('c',), pairs)  80.8 us
    ppermute x18, waiting for transfers between devices, passed(): return lax.ppermute(value, SEQ + ('c',), pairs)  34.3 us
    all_to_all x1, blocking collectives, per_device(): terms = lax.all_to_all(terms, HEAD, 0, 0, tiled=True)  13.1 us
    ppermute x4, starting transfers between devices, around(): return lax.ppermute(value, SEQ + ('c',), pairs)  10.2 us
    pallas_call x7, Pallas kernels, call(): pl.pallas_call(kernel, out_shape=[jax.ShapeDtypeStruct(shape, dtype) for...  7.65 us
    all_to_all x1, starting transfers between devices, per_device(): sums = lax.all_to_all(squares, HEAD, 0, 0, tiled=True)  5.14 us
    all_to_all x1, waiting for transfers between devices, per_device(): sums = lax.all_to_all(squares, HEAD, 0, 0, tiled=True)  4.01 us
  transfers between devices with their start and end apart: 23, of which 12 were waited for; matrix products, arithmetic and copies ran while one was open for 1% of the time, Pallas kernels for 1%

profile of v11, /device:TPU:7, one launch (start us, length us, event | category | flops | bytes accessed | tf_op | source)
XLA Modules:
  0.0 159.4 jit_solution(17973331687015542484)
XLA Ops:
  0.6 1.1 pad_maximum_fusion.raw_ref
  1.7 0.8 squares.1
  2.5 5.1 %all-to-all-start = ((f32[8,8,128]{2,1,0:T(8,128)}), f32[8,8,128]{2,1,0:T(8,128)S(1)}, u32[]{:S(2)}, u32[]{:S(2)}) async-start(f32[8,8,128]{2,1,0:T(8,128)} %squares.1), calls=%async_computation | async-start | bytes 65536 | tf_op jit(solution)/shard_map/all_to_all | solution.py:340
  7.7 0.7 pad_maximum_fusion.1.gain_ref
  8.4 4.0 %all-to-all-done.sums_ref = f32[8,8,128]{2,1,0:T(8,128)S(1)} async-done(((f32[8,8,128]{2,1,0:T(8,128)}), f32[8,8,128]{2,1,0:T(8,128)S(1)}, u32[]{:S(2)}, u32[]{:S(2)}) %all-to-all-start) | async-done | bytes 32800 | tf_op jit(solution)/shard_map/all_to_all | solution.py:340
  12.4 0.2 norm.1
  12.6 1.3 collective-permute-start.7
  13.9 4.9 %collective-permute-start.3 = (bf16[6,128,128]{2,1,0:T(8,128)(2,1)S(1)}, bf16[6,128,128]{2,1,0:T(8,128)(2,1)S(1)}, u32[]{:S(2)}, u32[]{:S(2)}) collective-permute-start(bf16[6,128,128]{2,1,0:T(8,128)(2,1)S(1)} %get-tuple-element.49.refs_0_), channel_id=1, source_target_pairs={{1,17},{9,25},{16,0},{17,33},{24,8},{25,41},{32,16},{33,49},{40,24... | collective-permute-start | bytes 589832 | tf_op jit(solution)/shard_map/ppermute | solution.py:255
  18.8 10.4 %collective-permute-start.2 = (bf16[6,128,128]{2,1,0:T(8,128)(2,1)S(1)}, bf16[6,128,128]{2,1,0:T(8,128)(2,1)S(1)}, u32[]{:S(2)}, u32[]{:S(2)}) collective-permute-start(bf16[6,128,128]{2,1,0:T(8,128)(2,1)S(1)} %get-tuple-element.49.refs_0_), channel_id=1, source_target_pairs={{0,16},{8,24},{16,32},{17,1},{24,40},{25,9},{32,48},{33,17},{40,56... | collective-permute-start | bytes 589832 | tf_op jit(solution)/shard_map/ppermute | solution.py:255
  29.2 2.5 %collective-permute-start.6 = (bf16[6,128,128]{2,1,0:T(8,128)(2,1)S(1)}, bf16[6,128,128]{2,1,0:T(8,128)(2,1)S(1)}, u32[]{:S(2)}, u32[]{:S(2)}) collective-permute-start(bf16[6,128,128]{2,1,0:T(8,128)(2,1)S(1)} %get-tuple-element.49.refs_0_), channel_id=1, source_target_pairs={{0,128},{1,385},{8,136},{9,393},{16,144},{17,401},{24,152},{25,409... | collective-permute-start | bytes 589832 | tf_op jit(solution)/shard_map/ppermute | solution.py:265
  31.7 2.6 %collective-permute-start.1 = (bf16[6,128,128]{2,1,0:T(8,128)(2,1)S(1)}, bf16[6,128,128]{2,1,0:T(8,128)(2,1)S(1)}, u32[]{:S(2)}, u32[]{:S(2)}) collective-permute-start(bf16[6,128,128]{2,1,0:T(8,128)(2,1)S(1)} %get-tuple-element.49.refs_0_), channel_id=1, source_target_pairs={{1,9},{8,0},{9,17},{16,8},{17,25},{24,16},{25,33},{32,24},{33,41},... | collective-permute-start | bytes 589832 | tf_op jit(solution)/shard_map/ppermute | solution.py:255
  34.3 4.7 %collective-permute-start = (bf16[6,128,128]{2,1,0:T(8,128)(2,1)S(1)}, bf16[6,128,128]{2,1,0:T(8,128)(2,1)S(1)}, u32[]{:S(2)}, u32[]{:S(2)}) collective-permute-start(bf16[6,128,128]{2,1,0:T(8,128)(2,1)S(1)} %get-tuple-element.49.refs_0_), channel_id=1, source_target_pairs={{0,8},{8,16},{9,1},{16,24},{17,9},{24,32},{25,17},{32,40},{33,25},... | collective-permute-start | bytes 589832 | tf_op jit(solution)/shard_map/ppermute | solution.py:255
  39.1 1.9 %collective-permute-start.5 = (bf16[6,128,128]{2,1,0:T(8,128)(2,1)S(1)}, bf16[6,128,128]{2,1,0:T(8,128)(2,1)S(1)}, u32[]{:S(2)}, u32[]{:S(2)}) collective-permute-start(bf16[6,128,128]{2,1,0:T(8,128)(2,1)S(1)} %collective-permute-done.3.refs_4_), channel_id=1, source_target_pairs={{1,17},{9,25},{16,0},{17,33},{24,8},{25,41},{32,16},{33,49},{40,24... | collective-permute-start | bytes 589832 | tf_op jit(solution)/shard_map/ppermute | solution.py:255
  41.0 0.0 collective-permute-done.2.refs_3_
  41.0 6.4 %collective-permute-start.4 = (bf16[6,128,128]{2,1,0:T(8,128)(2,1)S(1)}, bf16[6,128,128]{2,1,0:T(8,128)(2,1)S(1)}, u32[]{:S(2)}, u32[]{:S(2)}) collective-permute-start(bf16[6,128,128]{2,1,0:T(8,128)(2,1)S(1)} %collective-permute-done.2.refs_3_), channel_id=1, source_target_pairs={{0,16},{8,24},{16,32},{17,1},{24,40},{25,9},{32,48},{33,17},{40,56... | collective-permute-start | bytes 589832 | tf_op jit(solution)/shard_map/ppermute | solution.py:255
  47.4 0.0 collective-permute-done.refs_1_
  47.5 2.4 %collective-permute-done.5.refs_6_ = bf16[6,128,128]{2,1,0:T(8,128)(2,1)S(1)} collective-permute-done((bf16[6,128,128]{2,1,0:T(8,128)(2,1)S(1)}, bf16[6,128,128]{2,1,0:T(8,128)(2,1)S(1)}, u32[]{:S(2)}, u32[]{:S(2)}) %collective-permute-start.5) | collective-permute-done | bytes 196640 | tf_op jit(solution)/shard_map/ppermute | solution.py:255
  49.8 3.5 %collective-permute-done.4.refs_5_ = bf16[6,128,128]{2,1,0:T(8,128)(2,1)S(1)} collective-permute-done((bf16[6,128,128]{2,1,0:T(8,128)(2,1)S(1)}, bf16[6,128,128]{2,1,0:T(8,128)(2,1)S(1)}, u32[]{:S(2)}, u32[]{:S(2)}) %collective-permute-start.4) | collective-permute-done | bytes 196640 | tf_op jit(solution)/shard_map/ppermute | solution.py:255
  53.3 1.3 early.1
  54.6 4.2 %collective-permute-start.9 = (bf16[6,128,128]{2,1,0:T(8,128)(2,1)S(1)}, bf16[6,128,128]{2,1,0:T(8,128)(2,1)S(1)}, u32[]{:S(2)}, u32[]{:S(2)}) collective-permute-start(bf16[6,128,128]{2,1,0:T(8,128)(2,1)S(1)} %collective-permute-done.5.refs_6_), channel_id=1, source_target_pairs={{1,33},{9,41},{17,49},{25,57},{32,0},{33,65},{40,8},{41,73},{48,16... | collective-permute-start | bytes 589832 | tf_op jit(solution)/shard_map/ppermute | solution.py:255
  58.8 5.9 %collective-permute-start.8 = (bf16[6,128,128]{2,1,0:T(8,128)(2,1)S(1)}, bf16[6,128,128]{2,1,0:T(8,128)(2,1)S(1)}, u32[]{:S(2)}, u32[]{:S(2)}) collective-permute-start(bf16[6,128,128]{2,1,0:T(8,128)(2,1)S(1)} %collective-permute-done.4.refs_5_), channel_id=1, source_target_pairs={{0,32},{8,40},{16,48},{24,56},{32,64},{33,1},{40,72},{41,9},{48,80... | collective-permute-start | bytes 589832 | tf_op jit(solution)/shard_map/ppermute | solution.py:255
  64.7 3.9 %collective-permute-start.10 = (bf16[6,128,128]{2,1,0:T(8,128)(2,1)S(1)}, bf16[6,128,128]{2,1,0:T(8,128)(2,1)S(1)}, u32[]{:S(2)}, u32[]{:S(2)}) collective-permute-start(bf16[6,128,128]{2,1,0:T(8,128)(2,1)S(1)} %collective-permute-done.6.refs_7_), channel_id=1, source_target_pairs={{0,128},{1,385},{8,136},{9,393},{16,144},{17,401},{24,152},{25,409... | collective-permute-start | bytes 589832 | tf_op jit(solution)/shard_map/ppermute | solution.py:265
  68.7 2.7 %collective-permute-done.9.refs_1_ = bf16[6,128,128]{2,1,0:T(8,128)(2,1)S(1)} collective-permute-done((bf16[6,128,128]{2,1,0:T(8,128)(2,1)S(1)}, bf16[6,128,128]{2,1,0:T(8,128)(2,1)S(1)}, u32[]{:S(2)}, u32[]{:S(2)}) %collective-permute-start.9) | collective-permute-done | bytes 196640 | tf_op jit(solution)/shard_map/ppermute | solution.py:255
  71.3 9.9 %collective-permute-done.8.refs_0_ = bf16[6,128,128]{2,1,0:T(8,128)(2,1)S(1)} collective-permute-done((bf16[6,128,128]{2,1,0:T(8,128)(2,1)S(1)}, bf16[6,128,128]{2,1,0:T(8,128)(2,1)S(1)}, u32[]{:S(2)}, u32[]{:S(2)}) %collective-permute-start.8) | collective-permute-done | bytes 196640 | tf_op jit(solution)/shard_map/ppermute | solution.py:255
  81.2 2.1 %late.1 = (bf16[3,128,128]{2,1,0:T(8,128)(2,1)}, f32[3,128,128]{2,1,0:T(8,128)S(1)}, f32[128,128]{1,0:T(8,128)S(1)}, bf16[6,128,128]{2,1,0:T(8,128)(2,1)S(1)}, b...) custom-call(bf16[3,128,128]{2,1,0:T(8,128)(2,1)S(1)} %get-tuple-element.48.q_ref, ...), custom_call_target="tpu_custom_call" | custom-call | tf_op jit(solution)/shard_map/late/pallas_call | solution.py:328
  83.3 2.1 %collective-permute-start.11 = (bf16[6,128,128]{2,1,0:T(8,128)(2,1)S(1)}, bf16[6,128,128]{2,1,0:T(8,128)(2,1)S(1)}, u32[]{:S(2)}, u32[]{:S(2)}) collective-permute-start(bf16[6,128,128]{2,1,0:T(8,128)(2,1)S(1)} %get-tuple-element.61), channel_id=1, source_target_pairs={{1,33},{9,41},{17,49},{25,57},{32,0},{33,65},{40,8},{41,73},{48,16... | collective-permute-start | bytes 589832 | tf_op jit(solution)/shard_map/ppermute | solution.py:255
  85.4 8.0 %collective-permute-start.12 = (bf16[6,128,128]{2,1,0:T(8,128)(2,1)S(1)}, bf16[6,128,128]{2,1,0:T(8,128)(2,1)S(1)}, u32[]{:S(2)}, u32[]{:S(2)}) collective-permute-start(bf16[6,128,128]{2,1,0:T(8,128)(2,1)S(1)} %get-tuple-element.62), channel_id=1, source_target_pairs={{0,32},{8,40},{16,48},{24,56},{32,64},{33,1},{40,72},{41,9},{48,80... | collective-permute-start | bytes 589832 | tf_op jit(solution)/shard_map/ppermute | solution.py:255
  93.4 1.4 rest.1
  94.8 1.9 %collective-permute-start.13 = (bf16[6,128,128]{2,1,0:T(8,128)(2,1)S(1)}, bf16[6,128,128]{2,1,0:T(8,128)(2,1)S(1)}, u32[]{:S(2)}, u32[]{:S(2)}) collective-permute-start(bf16[6,128,128]{2,1,0:T(8,128)(2,1)S(1)} %get-tuple-element.67), channel_id=1, source_target_pairs={{1,9},{8,0},{9,17},{16,8},{17,25},{24,16},{25,33},{32,24},{33,41},... | collective-permute-start | bytes 589832 | tf_op jit(solution)/shard_map/ppermute | solution.py:255
  96.7 5.5 %collective-permute-start.14 = (bf16[6,128,128]{2,1,0:T(8,128)(2,1)S(1)}, bf16[6,128,128]{2,1,0:T(8,128)(2,1)S(1)}, u32[]{:S(2)}, u32[]{:S(2)}) collective-permute-start(bf16[6,128,128]{2,1,0:T(8,128)(2,1)S(1)} %get-tuple-element.68), channel_id=1, source_target_pairs={{0,8},{8,16},{9,1},{16,24},{17,9},{24,32},{25,17},{32,40},{33,25},... | collective-permute-start | bytes 589832 | tf_op jit(solution)/shard_map/ppermute | solution.py:255
  102.2 3.7 %collective-permute-start.19 = (bf16[6,128,128]{2,1,0:T(8,128)(2,1)S(1)}, bf16[6,128,128]{2,1,0:T(8,128)(2,1)S(1)}, u32[]{:S(2)}, u32[]{:S(2)}) collective-permute-start(bf16[6,128,128]{2,1,0:T(8,128)(2,1)S(1)} %get-tuple-element.80), channel_id=1, source_target_pairs={{0,128},{8,136},{16,144},{24,152},{32,160},{40,168},{48,176},{56,1... | collective-permute-start | bytes 589832 | tf_op jit(solution)/shard_map/ppermute | solution.py:255
  105.9 1.9 %collective-permute-start.15 = (bf16[6,128,128]{2,1,0:T(8,128)(2,1)S(1)}, bf16[6,128,128]{2,1,0:T(8,128)(2,1)S(1)}, u32[]{:S(2)}, u32[]{:S(2)}) collective-permute-start(bf16[6,128,128]{2,1,0:T(8,128)(2,1)S(1)} %get-tuple-element.69), channel_id=1, source_target_pairs={{0,384},{1,129},{8,392},{9,137},{16,400},{17,145},{24,408},{25,153... | collective-permute-start | bytes 589832 | tf_op jit(solution)/shard_map/ppermute | solution.py:265
  108.0 0.5 collective-permute-done.13.refs_1_
  108.5 4.2 %collective-permute-done.14.refs_2_ = bf16[6,128,128]{2,1,0:T(8,128)(2,1)S(1)} collective-permute-done((bf16[6,128,128]{2,1,0:T(8,128)(2,1)S(1)}, bf16[6,128,128]{2,1,0:T(8,128)(2,1)S(1)}, u32[]{:S(2)}, u32[]{:S(2)}) %collective-permute-start.14) | collective-permute-done | bytes 196640 | tf_op jit(solution)/shard_map/ppermute | solution.py:255
  112.7 1.1 collective-permute-done.15
  113.8 1.9 %collective-permute-start.16 = (bf16[6,128,128]{2,1,0:T(8,128)(2,1)S(1)}, bf16[6,128,128]{2,1,0:T(8,128)(2,1)S(1)}, u32[]{:S(2)}, u32[]{:S(2)}) collective-permute-start(bf16[6,128,128]{2,1,0:T(8,128)(2,1)S(1)} %add_convert_fusion.4), channel_id=1, source_target_pairs={{1,17},{9,25},{16,0},{17,33},{24,8},{25,41},{32,16},{33,49},{40,24... | collective-permute-start | bytes 589832 | tf_op jit(solution)/shard_map/ppermute | solution.py:255
  115.7 6.4 %collective-permute-start.17 = (bf16[6,128,128]{2,1,0:T(8,128)(2,1)S(1)}, bf16[6,128,128]{2,1,0:T(8,128)(2,1)S(1)}, u32[]{:S(2)}, u32[]{:S(2)}) collective-permute-start(bf16[6,128,128]{2,1,0:T(8,128)(2,1)S(1)} %add_convert_fusion.3), channel_id=1, source_target_pairs={{0,16},{8,24},{16,32},{17,1},{24,40},{25,9},{32,48},{33,17},{40,56... | collective-permute-start | bytes 589832 | tf_op jit(solution)/shard_map/ppermute | solution.py:255
  122.1 1.9 %collective-permute-start.18 = (bf16[6,128,128]{2,1,0:T(8,128)(2,1)S(1)}, bf16[6,128,128]{2,1,0:T(8,128)(2,1)S(1)}, u32[]{:S(2)}, u32[]{:S(2)}) collective-permute-start(bf16[6,128,128]{2,1,0:T(8,128)(2,1)S(1)} %add_convert_fusion), channel_id=1, source_target_pairs={{0,384},{1,129},{8,392},{9,137},{16,400},{17,145},{24,408},{25,153... | collective-permute-start | bytes 589832 | tf_op jit(solution)/shard_map/ppermute | solution.py:265
  124.1 0.3 collective-permute-done.16
  124.3 5.5 %collective-permute-done.17 = bf16[6,128,128]{2,1,0:T(8,128)(2,1)S(1)} collective-permute-done((bf16[6,128,128]{2,1,0:T(8,128)(2,1)S(1)}, bf16[6,128,128]{2,1,0:T(8,128)(2,1)S(1)}, u32[]{:S(2)}, u32[]{:S(2)}) %collective-permute-start.17) | collective-permute-done | bytes 196640 | tf_op jit(solution)/shard_map/ppermute | solution.py:255
  129.9 0.1 add_convert_fusion.1
  130.0 1.9 %collective-permute-start.20 = (bf16[6,128,128]{2,1,0:T(8,128)(2,1)S(1)}, bf16[6,128,128]{2,1,0:T(8,128)(2,1)S(1)}, u32[]{:S(2)}, u32[]{:S(2)}) collective-permute-start(bf16[6,128,128]{2,1,0:T(8,128)(2,1)S(1)} %get-tuple-element.85), channel_id=1, source_target_pairs={{1,17},{9,25},{16,0},{17,33},{24,8},{25,41},{32,16},{33,49},{40,24... | collective-permute-start | bytes 589832 | tf_op jit(solution)/shard_map/ppermute | solution.py:255
  131.9 7.1 %collective-permute-start.21 = (bf16[6,128,128]{2,1,0:T(8,128)(2,1)S(1)}, bf16[6,128,128]{2,1,0:T(8,128)(2,1)S(1)}, u32[]{:S(2)}, u32[]{:S(2)}) collective-permute-start(bf16[6,128,128]{2,1,0:T(8,128)(2,1)S(1)} %get-tuple-element.86), channel_id=1, source_target_pairs={{0,16},{8,24},{16,32},{17,1},{24,40},{25,9},{32,48},{33,17},{40,56... | collective-permute-start | bytes 589832 | tf_op jit(solution)/shard_map/ppermute | solution.py:255
  139.1 2.2 %collective-permute-done.20.refs_5_ = bf16[6,128,128]{2,1,0:T(8,128)(2,1)S(1)} collective-permute-done((bf16[6,128,128]{2,1,0:T(8,128)(2,1)S(1)}, bf16[6,128,128]{2,1,0:T(8,128)(2,1)S(1)}, u32[]{:S(2)}, u32[]{:S(2)}) %collective-permute-start.20) | collective-permute-done | bytes 196640 | tf_op jit(solution)/shard_map/ppermute | solution.py:255
  141.3 3.1 %collective-permute-done.21.refs_6_ = bf16[6,128,128]{2,1,0:T(8,128)(2,1)S(1)} collective-permute-done((bf16[6,128,128]{2,1,0:T(8,128)(2,1)S(1)}, bf16[6,128,128]{2,1,0:T(8,128)(2,1)S(1)}, u32[]{:S(2)}, u32[]{:S(2)}) %collective-permute-start.21) | collective-permute-done | bytes 196640 | tf_op jit(solution)/shard_map/ppermute | solution.py:255
  144.4 0.9 terms.1
  145.4 13.1 %all_to_all.10.terms_ref = f32[8,8,128]{2,1,0:T(8,128)S(1)} all-to-all(f32[8,8,128]{2,1,0:T(8,128)S(1)} %get-tuple-element.87), channel_id=1, replica_groups=mesh['x'=4,'z'=16,'y'=4,'c'=2] {'y','c'}, dimensions={0} | all-to-all | bytes 65536 | tf_op jit(solution)/shard_map/all_to_all | solution.py:383
  158.4 0.9 final.1
  (14 shorter events, 0.2 us)
Async XLA Ops:
  0.6 80.6 %copy-start = (bf16[128,3,128]{2,0,1:T(8,128)(2,1)S(1)}, bf16[128,3,128]{2,0,1:T(8,128)(2,1)}, u32[]{:S(2)}) copy-start(bf16[128,3,128]{2,0,1:T(8,128)(2,1)} %param.10) | copy-start | bytes 294916
  2.5 9.9 %all-to-all-start = ((f32[8,8,128]{2,1,0:T(8,128)}), f32[8,8,128]{2,1,0:T(8,128)S(1)}, u32[]{:S(2)}, u32[]{:S(2)}) async-start(f32[8,8,128]{2,1,0:T(8,128)} %squares.1), calls=%async_computation | async-start | bytes 65536 | tf_op jit(solution)/shard_map/all_to_all | solution.py:340
  12.6 21.7 %collective-permute-start.7 = (bf16[6,128,128]{2,1,0:T(8,128)(2,1)S(1)}, bf16[6,128,128]{2,1,0:T(8,128)(2,1)S(1)}, u32[]{:S(2)}, u32[]{:S(2)}) collective-permute-start(bf16[6,128,128]{2,1,0:T(8,128)(2,1)S(1)} %get-tuple-element.49.refs_0_), channel_id=1, source_target_pairs={{1,129},{9,137},{17,145},{25,153},{33,161},{41,169},{49,177},{57,1... | collective-permute-start | bytes 589832 | tf_op jit(solution)/shard_map/ppermute | solution.py:255
  13.9 25.2 %collective-permute-start.3 = (bf16[6,128,128]{2,1,0:T(8,128)(2,1)S(1)}, bf16[6,128,128]{2,1,0:T(8,128)(2,1)S(1)}, u32[]{:S(2)}, u32[]{:S(2)}) collective-permute-start(bf16[6,128,128]{2,1,0:T(8,128)(2,1)S(1)} %get-tuple-element.49.refs_0_), channel_id=1, source_target_pairs={{1,17},{9,25},{16,0},{17,33},{24,8},{25,41},{32,16},{33,49},{40,24... | collective-permute-start | bytes 589832 | tf_op jit(solution)/shard_map/ppermute | solution.py:255
  18.8 22.2 %collective-permute-start.2 = (bf16[6,128,128]{2,1,0:T(8,128)(2,1)S(1)}, bf16[6,128,128]{2,1,0:T(8,128)(2,1)S(1)}, u32[]{:S(2)}, u32[]{:S(2)}) collective-permute-start(bf16[6,128,128]{2,1,0:T(8,128)(2,1)S(1)} %get-tuple-element.49.refs_0_), channel_id=1, source_target_pairs={{0,16},{8,24},{16,32},{17,1},{24,40},{25,9},{32,48},{33,17},{40,56... | collective-permute-start | bytes 589832 | tf_op jit(solution)/shard_map/ppermute | solution.py:255
  29.2 18.2 %collective-permute-start.6 = (bf16[6,128,128]{2,1,0:T(8,128)(2,1)S(1)}, bf16[6,128,128]{2,1,0:T(8,128)(2,1)S(1)}, u32[]{:S(2)}, u32[]{:S(2)}) collective-permute-start(bf16[6,128,128]{2,1,0:T(8,128)(2,1)S(1)} %get-tuple-element.49.refs_0_), channel_id=1, source_target_pairs={{0,128},{1,385},{8,136},{9,393},{16,144},{17,401},{24,152},{25,409... | collective-permute-start | bytes 589832 | tf_op jit(solution)/shard_map/ppermute | solution.py:265
  31.7 15.8 %collective-permute-start.1 = (bf16[6,128,128]{2,1,0:T(8,128)(2,1)S(1)}, bf16[6,128,128]{2,1,0:T(8,128)(2,1)S(1)}, u32[]{:S(2)}, u32[]{:S(2)}) collective-permute-start(bf16[6,128,128]{2,1,0:T(8,128)(2,1)S(1)} %get-tuple-element.49.refs_0_), channel_id=1, source_target_pairs={{1,9},{8,0},{9,17},{16,8},{17,25},{24,16},{25,33},{32,24},{33,41},... | collective-permute-start | bytes 589832 | tf_op jit(solution)/shard_map/ppermute | solution.py:255
  34.3 13.1 %collective-permute-start = (bf16[6,128,128]{2,1,0:T(8,128)(2,1)S(1)}, bf16[6,128,128]{2,1,0:T(8,128)(2,1)S(1)}, u32[]{:S(2)}, u32[]{:S(2)}) collective-permute-start(bf16[6,128,128]{2,1,0:T(8,128)(2,1)S(1)} %get-tuple-element.49.refs_0_), channel_id=1, source_target_pairs={{0,8},{8,16},{9,1},{16,24},{17,9},{24,32},{25,17},{32,40},{33,25},... | collective-permute-start | bytes 589832 | tf_op jit(solution)/shard_map/ppermute | solution.py:255
  39.1 10.7 %collective-permute-start.5 = (bf16[6,128,128]{2,1,0:T(8,128)(2,1)S(1)}, bf16[6,128,128]{2,1,0:T(8,128)(2,1)S(1)}, u32[]{:S(2)}, u32[]{:S(2)}) collective-permute-start(bf16[6,128,128]{2,1,0:T(8,128)(2,1)S(1)} %collective-permute-done.3.refs_4_), channel_id=1, source_target_pairs={{1,17},{9,25},{16,0},{17,33},{24,8},{25,41},{32,16},{33,49},{40,24... | collective-permute-start | bytes 589832 | tf_op jit(solution)/shard_map/ppermute | solution.py:255
  41.0 12.3 %collective-permute-start.4 = (bf16[6,128,128]{2,1,0:T(8,128)(2,1)S(1)}, bf16[6,128,128]{2,1,0:T(8,128)(2,1)S(1)}, u32[]{:S(2)}, u32[]{:S(2)}) collective-permute-start(bf16[6,128,128]{2,1,0:T(8,128)(2,1)S(1)} %collective-permute-done.2.refs_3_), channel_id=1, source_target_pairs={{0,16},{8,24},{16,32},{17,1},{24,40},{25,9},{32,48},{33,17},{40,56... | collective-permute-start | bytes 589832 | tf_op jit(solution)/shard_map/ppermute | solution.py:255
  54.6 16.7 %collective-permute-start.9 = (bf16[6,128,128]{2,1,0:T(8,128)(2,1)S(1)}, bf16[6,128,128]{2,1,0:T(8,128)(2,1)S(1)}, u32[]{:S(2)}, u32[]{:S(2)}) collective-permute-start(bf16[6,128,128]{2,1,0:T(8,128)(2,1)S(1)} %collective-permute-done.5.refs_6_), channel_id=1, source_target_pairs={{1,33},{9,41},{17,49},{25,57},{32,0},{33,65},{40,8},{41,73},{48,16... | collective-permute-start | bytes 589832 | tf_op jit(solution)/shard_map/ppermute | solution.py:255
  58.8 22.4 %collective-permute-start.8 = (bf16[6,128,128]{2,1,0:T(8,128)(2,1)S(1)}, bf16[6,128,128]{2,1,0:T(8,128)(2,1)S(1)}, u32[]{:S(2)}, u32[]{:S(2)}) collective-permute-start(bf16[6,128,128]{2,1,0:T(8,128)(2,1)S(1)} %collective-permute-done.4.refs_5_), channel_id=1, source_target_pairs={{0,32},{8,40},{16,48},{24,56},{32,64},{33,1},{40,72},{41,9},{48,80... | collective-permute-start | bytes 589832 | tf_op jit(solution)/shard_map/ppermute | solution.py:255
  64.7 16.5 %collective-permute-start.10 = (bf16[6,128,128]{2,1,0:T(8,128)(2,1)S(1)}, bf16[6,128,128]{2,1,0:T(8,128)(2,1)S(1)}, u32[]{:S(2)}, u32[]{:S(2)}) collective-permute-start(bf16[6,128,128]{2,1,0:T(8,128)(2,1)S(1)} %collective-permute-done.6.refs_7_), channel_id=1, source_target_pairs={{0,128},{1,385},{8,136},{9,393},{16,144},{17,401},{24,152},{25,409... | collective-permute-start | bytes 589832 | tf_op jit(solution)/shard_map/ppermute | solution.py:265
  83.3 22.6 %collective-permute-start.11 = (bf16[6,128,128]{2,1,0:T(8,128)(2,1)S(1)}, bf16[6,128,128]{2,1,0:T(8,128)(2,1)S(1)}, u32[]{:S(2)}, u32[]{:S(2)}) collective-permute-start(bf16[6,128,128]{2,1,0:T(8,128)(2,1)S(1)} %get-tuple-element.61), channel_id=1, source_target_pairs={{1,33},{9,41},{17,49},{25,57},{32,0},{33,65},{40,8},{41,73},{48,16... | collective-permute-start | bytes 589832 | tf_op jit(solution)/shard_map/ppermute | solution.py:255
  85.4 22.4 %collective-permute-start.12 = (bf16[6,128,128]{2,1,0:T(8,128)(2,1)S(1)}, bf16[6,128,128]{2,1,0:T(8,128)(2,1)S(1)}, u32[]{:S(2)}, u32[]{:S(2)}) collective-permute-start(bf16[6,128,128]{2,1,0:T(8,128)(2,1)S(1)} %get-tuple-element.62), channel_id=1, source_target_pairs={{0,32},{8,40},{16,48},{24,56},{32,64},{33,1},{40,72},{41,9},{48,80... | collective-permute-start | bytes 589832 | tf_op jit(solution)/shard_map/ppermute | solution.py:255
  94.8 13.6 %collective-permute-start.13 = (bf16[6,128,128]{2,1,0:T(8,128)(2,1)S(1)}, bf16[6,128,128]{2,1,0:T(8,128)(2,1)S(1)}, u32[]{:S(2)}, u32[]{:S(2)}) collective-permute-start(bf16[6,128,128]{2,1,0:T(8,128)(2,1)S(1)} %get-tuple-element.67), channel_id=1, source_target_pairs={{1,9},{8,0},{9,17},{16,8},{17,25},{24,16},{25,33},{32,24},{33,41},... | collective-permute-start | bytes 589832 | tf_op jit(solution)/shard_map/ppermute | solution.py:255
  96.7 15.9 %collective-permute-start.14 = (bf16[6,128,128]{2,1,0:T(8,128)(2,1)S(1)}, bf16[6,128,128]{2,1,0:T(8,128)(2,1)S(1)}, u32[]{:S(2)}, u32[]{:S(2)}) collective-permute-start(bf16[6,128,128]{2,1,0:T(8,128)(2,1)S(1)} %get-tuple-element.68), channel_id=1, source_target_pairs={{0,8},{8,16},{9,1},{16,24},{17,9},{24,32},{25,17},{32,40},{33,25},... | collective-permute-start | bytes 589832 | tf_op jit(solution)/shard_map/ppermute | solution.py:255
  102.2 27.8 %collective-permute-start.19 = (bf16[6,128,128]{2,1,0:T(8,128)(2,1)S(1)}, bf16[6,128,128]{2,1,0:T(8,128)(2,1)S(1)}, u32[]{:S(2)}, u32[]{:S(2)}) collective-permute-start(bf16[6,128,128]{2,1,0:T(8,128)(2,1)S(1)} %get-tuple-element.80), channel_id=1, source_target_pairs={{0,128},{8,136},{16,144},{24,152},{32,160},{40,168},{48,176},{56,1... | collective-permute-start | bytes 589832 | tf_op jit(solution)/shard_map/ppermute | solution.py:255
  105.9 7.9 %collective-permute-start.15 = (bf16[6,128,128]{2,1,0:T(8,128)(2,1)S(1)}, bf16[6,128,128]{2,1,0:T(8,128)(2,1)S(1)}, u32[]{:S(2)}, u32[]{:S(2)}) collective-permute-start(bf16[6,128,128]{2,1,0:T(8,128)(2,1)S(1)} %get-tuple-element.69), channel_id=1, source_target_pairs={{0,384},{1,129},{8,392},{9,137},{16,400},{17,145},{24,408},{25,153... | collective-permute-start | bytes 589832 | tf_op jit(solution)/shard_map/ppermute | solution.py:265
  113.8 10.5 %collective-permute-start.16 = (bf16[6,128,128]{2,1,0:T(8,128)(2,1)S(1)}, bf16[6,128,128]{2,1,0:T(8,128)(2,1)S(1)}, u32[]{:S(2)}, u32[]{:S(2)}) collective-permute-start(bf16[6,128,128]{2,1,0:T(8,128)(2,1)S(1)} %add_convert_fusion.4), channel_id=1, source_target_pairs={{1,17},{9,25},{16,0},{17,33},{24,8},{25,41},{32,16},{33,49},{40,24... | collective-permute-start | bytes 589832 | tf_op jit(solution)/shard_map/ppermute | solution.py:255
  115.7 14.2 %collective-permute-start.17 = (bf16[6,128,128]{2,1,0:T(8,128)(2,1)S(1)}, bf16[6,128,128]{2,1,0:T(8,128)(2,1)S(1)}, u32[]{:S(2)}, u32[]{:S(2)}) collective-permute-start(bf16[6,128,128]{2,1,0:T(8,128)(2,1)S(1)} %add_convert_fusion.3), channel_id=1, source_target_pairs={{0,16},{8,24},{16,32},{17,1},{24,40},{25,9},{32,48},{33,17},{40,56... | collective-permute-start | bytes 589832 | tf_op jit(solution)/shard_map/ppermute | solution.py:255
  122.1 7.8 %collective-permute-start.18 = (bf16[6,128,128]{2,1,0:T(8,128)(2,1)S(1)}, bf16[6,128,128]{2,1,0:T(8,128)(2,1)S(1)}, u32[]{:S(2)}, u32[]{:S(2)}) collective-permute-start(bf16[6,128,128]{2,1,0:T(8,128)(2,1)S(1)} %add_convert_fusion), channel_id=1, source_target_pairs={{0,384},{1,129},{8,392},{9,137},{16,400},{17,145},{24,408},{25,153... | collective-permute-start | bytes 589832 | tf_op jit(solution)/shard_map/ppermute | solution.py:265
  130.0 11.3 %collective-permute-start.20 = (bf16[6,128,128]{2,1,0:T(8,128)(2,1)S(1)}, bf16[6,128,128]{2,1,0:T(8,128)(2,1)S(1)}, u32[]{:S(2)}, u32[]{:S(2)}) collective-permute-start(bf16[6,128,128]{2,1,0:T(8,128)(2,1)S(1)} %get-tuple-element.85), channel_id=1, source_target_pairs={{1,17},{9,25},{16,0},{17,33},{24,8},{25,41},{32,16},{33,49},{40,24... | collective-permute-start | bytes 589832 | tf_op jit(solution)/shard_map/ppermute | solution.py:255
  131.9 12.5 %collective-permute-start.21 = (bf16[6,128,128]{2,1,0:T(8,128)(2,1)S(1)}, bf16[6,128,128]{2,1,0:T(8,128)(2,1)S(1)}, u32[]{:S(2)}, u32[]{:S(2)}) collective-permute-start(bf16[6,128,128]{2,1,0:T(8,128)(2,1)S(1)} %get-tuple-element.86), channel_id=1, source_target_pairs={{0,16},{8,24},{16,32},{17,1},{24,40},{25,9},{32,48},{33,17},{40,56... | collective-permute-start | bytes 589832 | tf_op jit(solution)/shard_map/ppermute | solution.py:255

commit v12 on v10

--- a/solution.py
+++ b/solution.py
@@ -348,7 +348,7 @@
     tiles = spread(pairs)
     tiles += [before, passed(pairs, -line), around(before, line)]
     late = [near - 2, near - 1]
-    early = [t for t in range(count) if t not in late]
+    early = [0, near, near + 1, *range(3, near - 2), 1, 2, near + 2]
     early_tiles, late_tiles = [tiles[t] for t in early], [tiles[t] for t in late]
     square = ((TILE, TILE), F32)
     weights, early_out, early_rows = call(

time: 154 us -> 151 us (0.981)
  the two profiles are of different devices: /device:TPU:34 before, /device:TPU:7 now
where the time goes in v12:
time: 151 us; the launch traced here: 148 us
  starting transfers between devices  91.1 us (60%)
  waiting for transfers between devices  37.5 us (25%)
  blocking collectives  9.21 us (6%)
  Pallas kernels  7.59 us (5%)
  other arithmetic  2.01 us (1%)
    ppermute x18, starting transfers between devices, passed(): return lax.ppermute(value, SEQ + ('c',), pairs)  75.9 us
    ppermute x18, waiting for transfers between devices, passed(): return lax.ppermute(value, SEQ + ('c',), pairs)  27.4 us
    ppermute x4, starting transfers between devices, around(): return lax.ppermute(value, SEQ + ('c',), pairs)  9.99 us
    all_to_all x1, blocking collectives, per_device(): terms = lax.all_to_all(terms, HEAD, 0, 0, tiled=True)  9.21 us
    pallas_call x7, Pallas kernels, call(): pl.pallas_call(kernel, out_shape=[jax.ShapeDtypeStruct(shape, dtype) for...  7.59 us
    ppermute x4, waiting for transfers between devices, around(): return lax.ppermute(value, SEQ + ('c',), pairs)  6.03 us
    all_to_all x1, starting transfers between devices, per_device(): sums = lax.all_to_all(squares, HEAD, 0, 0, tiled=True)  5.14 us
    all_to_all x1, waiting for transfers between devices, per_device(): sums = lax.all_to_all(squares, HEAD, 0, 0, tiled=True)  4.01 us
  transfers between devices with their start and end apart: 23, of which 10 were waited for; matrix products, arithmetic and copies ran while one was open for 1% of the time, Pallas kernels for 2%

profile of v12, /device:TPU:7, one launch (start us, length us, event | category | flops | bytes accessed | tf_op | source)
XLA Modules:
  0.0 148.3 jit_solution(1982060452776176280)
XLA Ops:
  0.6 1.1 pad_maximum_fusion.raw_ref
  1.7 0.8 squares.1
  2.5 5.1 %all-to-all-start = ((f32[8,8,128]{2,1,0:T(8,128)}), f32[8,8,128]{2,1,0:T(8,128)S(1)}, u32[]{:S(2)}, u32[]{:S(2)}) async-start(f32[8,8,128]{2,1,0:T(8,128)} %squares.1), calls=%async_computation | async-start | bytes 65536 | tf_op jit(solution)/shard_map/all_to_all | solution.py:340
  7.7 0.7 pad_maximum_fusion.1.gain_ref
  8.4 4.0 %all-to-all-done.sums_ref = f32[8,8,128]{2,1,0:T(8,128)S(1)} async-done(((f32[8,8,128]{2,1,0:T(8,128)}), f32[8,8,128]{2,1,0:T(8,128)S(1)}, u32[]{:S(2)}, u32[]{:S(2)}) %all-to-all-start) | async-done | bytes 32800 | tf_op jit(solution)/shard_map/all_to_all | solution.py:340
  12.4 0.2 norm.1
  12.6 4.9 %collective-permute-start.3 = (bf16[6,128,128]{2,1,0:T(8,128)(2,1)S(1)}, bf16[6,128,128]{2,1,0:T(8,128)(2,1)S(1)}, u32[]{:S(2)}, u32[]{:S(2)}) collective-permute-start(bf16[6,128,128]{2,1,0:T(8,128)(2,1)S(1)} %get-tuple-element.47.refs_0_), channel_id=1, source_target_pairs={{1,17},{9,25},{16,0},{17,33},{24,8},{25,41},{32,16},{33,49},{40,24... | collective-permute-start | bytes 589832 | tf_op jit(solution)/shard_map/ppermute | solution.py:255
  17.5 8.9 %collective-permute-start.2 = (bf16[6,128,128]{2,1,0:T(8,128)(2,1)S(1)}, bf16[6,128,128]{2,1,0:T(8,128)(2,1)S(1)}, u32[]{:S(2)}, u32[]{:S(2)}) collective-permute-start(bf16[6,128,128]{2,1,0:T(8,128)(2,1)S(1)} %get-tuple-element.47.refs_0_), channel_id=1, source_target_pairs={{0,16},{8,24},{16,32},{17,1},{24,40},{25,9},{32,48},{33,17},{40,56... | collective-permute-start | bytes 589832 | tf_op jit(solution)/shard_map/ppermute | solution.py:255
  26.4 2.6 %collective-permute-start.7 = (bf16[6,128,128]{2,1,0:T(8,128)(2,1)S(1)}, bf16[6,128,128]{2,1,0:T(8,128)(2,1)S(1)}, u32[]{:S(2)}, u32[]{:S(2)}) collective-permute-start(bf16[6,128,128]{2,1,0:T(8,128)(2,1)S(1)} %get-tuple-element.47.refs_0_), channel_id=1, source_target_pairs={{1,9},{8,0},{9,17},{16,8},{17,25},{24,16},{25,33},{32,24},{33,41},... | collective-permute-start | bytes 589832 | tf_op jit(solution)/shard_map/ppermute | solution.py:255
  29.0 2.2 %collective-permute-start = (bf16[6,128,128]{2,1,0:T(8,128)(2,1)S(1)}, bf16[6,128,128]{2,1,0:T(8,128)(2,1)S(1)}, u32[]{:S(2)}, u32[]{:S(2)}) collective-permute-start(bf16[6,128,128]{2,1,0:T(8,128)(2,1)S(1)} %get-tuple-element.47.refs_0_), channel_id=1, source_target_pairs={{0,128},{1,385},{8,136},{9,393},{16,144},{17,401},{24,152},{25,409... | collective-permute-start | bytes 589832 | tf_op jit(solution)/shard_map/ppermute | solution.py:265
  31.2 1.9 %collective-permute-start.5 = (bf16[6,128,128]{2,1,0:T(8,128)(2,1)S(1)}, bf16[6,128,128]{2,1,0:T(8,128)(2,1)S(1)}, u32[]{:S(2)}, u32[]{:S(2)}) collective-permute-start(bf16[6,128,128]{2,1,0:T(8,128)(2,1)S(1)} %collective-permute-done.3.refs_4_), channel_id=1, source_target_pairs={{1,17},{9,25},{16,0},{17,33},{24,8},{25,41},{32,16},{33,49},{40,24... | collective-permute-start | bytes 589832 | tf_op jit(solution)/shard_map/ppermute | solution.py:255
  33.1 1.5 collective-permute-done.2.refs_3_
  34.6 6.9 %collective-permute-start.4 = (bf16[6,128,128]{2,1,0:T(8,128)(2,1)S(1)}, bf16[6,128,128]{2,1,0:T(8,128)(2,1)S(1)}, u32[]{:S(2)}, u32[]{:S(2)}) collective-permute-start(bf16[6,128,128]{2,1,0:T(8,128)(2,1)S(1)} %collective-permute-done.2.refs_3_), channel_id=1, source_target_pairs={{0,16},{8,24},{16,32},{17,1},{24,40},{25,9},{32,48},{33,17},{40,56... | collective-permute-start | bytes 589832 | tf_op jit(solution)/shard_map/ppermute | solution.py:255
  41.5 1.9 %collective-permute-start.6 = (bf16[6,128,128]{2,1,0:T(8,128)(2,1)S(1)}, bf16[6,128,128]{2,1,0:T(8,128)(2,1)S(1)}, u32[]{:S(2)}, u32[]{:S(2)}) collective-permute-start(bf16[6,128,128]{2,1,0:T(8,128)(2,1)S(1)} %get-tuple-element.47.refs_0_), channel_id=1, source_target_pairs={{0,8},{8,16},{9,1},{16,24},{17,9},{24,32},{25,17},{32,40},{33,25},... | collective-permute-start | bytes 589832 | tf_op jit(solution)/shard_map/ppermute | solution.py:255
  43.5 1.3 collective-permute-start.1
  44.8 0.0 collective-permute-done.refs_1_
  44.8 4.0 %collective-permute-start.8 = (bf16[6,128,128]{2,1,0:T(8,128)(2,1)S(1)}, bf16[6,128,128]{2,1,0:T(8,128)(2,1)S(1)}, u32[]{:S(2)}, u32[]{:S(2)}) collective-permute-start(bf16[6,128,128]{2,1,0:T(8,128)(2,1)S(1)} %collective-permute-done.refs_1_), channel_id=1, source_target_pairs={{0,128},{1,385},{8,136},{9,393},{16,144},{17,401},{24,152},{25,409... | collective-permute-start | bytes 589832 | tf_op jit(solution)/shard_map/ppermute | solution.py:265
  48.8 1.9 %collective-permute-start.10 = (bf16[6,128,128]{2,1,0:T(8,128)(2,1)S(1)}, bf16[6,128,128]{2,1,0:T(8,128)(2,1)S(1)}, u32[]{:S(2)}, u32[]{:S(2)}) collective-permute-start(bf16[6,128,128]{2,1,0:T(8,128)(2,1)S(1)} %collective-permute-done.5.refs_6_), channel_id=1, source_target_pairs={{1,33},{9,41},{17,49},{25,57},{32,0},{33,65},{40,8},{41,73},{48,16... | collective-permute-start | bytes 589832 | tf_op jit(solution)/shard_map/ppermute | solution.py:255
  50.7 8.2 %collective-permute-start.9 = (bf16[6,128,128]{2,1,0:T(8,128)(2,1)S(1)}, bf16[6,128,128]{2,1,0:T(8,128)(2,1)S(1)}, u32[]{:S(2)}, u32[]{:S(2)}) collective-permute-start(bf16[6,128,128]{2,1,0:T(8,128)(2,1)S(1)} %collective-permute-done.4.refs_5_), channel_id=1, source_target_pairs={{0,32},{8,40},{16,48},{24,56},{32,64},{33,1},{40,72},{41,9},{48,80... | collective-permute-start | bytes 589832 | tf_op jit(solution)/shard_map/ppermute | solution.py:255
  58.9 0.0 collective-permute-done.6.refs_7_
  58.9 1.4 early.1
  60.3 3.4 %collective-permute-done.10.refs_1_ = bf16[6,128,128]{2,1,0:T(8,128)(2,1)S(1)} collective-permute-done((bf16[6,128,128]{2,1,0:T(8,128)(2,1)S(1)}, bf16[6,128,128]{2,1,0:T(8,128)(2,1)S(1)}, u32[]{:S(2)}, u32[]{:S(2)}) %collective-permute-start.10) | collective-permute-done | bytes 196640 | tf_op jit(solution)/shard_map/ppermute | solution.py:255
  63.7 12.0 %collective-permute-done.9.refs_0_ = bf16[6,128,128]{2,1,0:T(8,128)(2,1)S(1)} collective-permute-done((bf16[6,128,128]{2,1,0:T(8,128)(2,1)S(1)}, bf16[6,128,128]{2,1,0:T(8,128)(2,1)S(1)}, u32[]{:S(2)}, u32[]{:S(2)}) %collective-permute-start.9) | collective-permute-done | bytes 196640 | tf_op jit(solution)/shard_map/ppermute | solution.py:255
  75.7 1.7 %late.1 = (bf16[3,128,128]{2,1,0:T(8,128)(2,1)}, f32[3,128,128]{2,1,0:T(8,128)S(1)}, f32[128,128]{1,0:T(8,128)S(1)}, bf16[6,128,128]{2,1,0:T(8,128)(2,1)S(1)}, bf16[6,128,128]{2,1,0:T(8,128)(2,1)S(1)}) custom-call(bf16[3,128,128]{2,1,0:T(8,128)(2,1)S(1)} %get-tuple-element.46.q_ref, bf16[3,128,128]{2,1,0:T(8,128)(2,1)S(1)} %bitcast.8, ...), custom_call_target="tpu_custom_call" | custom-call | tf_op jit(solution)/shard_map/late/pallas_call | solution.py:328
  77.4 1.9 %collective-permute-start.11 = (bf16[6,128,128]{2,1,0:T(8,128)(2,1)S(1)}, bf16[6,128,128]{2,1,0:T(8,128)(2,1)S(1)}, u32[]{:S(2)}, u32[]{:S(2)}) collective-permute-start(bf16[6,128,128]{2,1,0:T(8,128)(2,1)S(1)} %get-tuple-element.57), channel_id=1, source_target_pairs={{1,33},{9,41},{17,49},{25,57},{32,0},{33,65},{40,8},{41,73},{48,16... | collective-permute-start | bytes 589832 | tf_op jit(solution)/shard_map/ppermute | solution.py:255
  79.3 8.2 %collective-permute-start.12 = (bf16[6,128,128]{2,1,0:T(8,128)(2,1)S(1)}, bf16[6,128,128]{2,1,0:T(8,128)(2,1)S(1)}, u32[]{:S(2)}, u32[]{:S(2)}) collective-permute-start(bf16[6,128,128]{2,1,0:T(8,128)(2,1)S(1)} %get-tuple-element.58), channel_id=1, source_target_pairs={{0,32},{8,40},{16,48},{24,56},{32,64},{33,1},{40,72},{41,9},{48,80... | collective-permute-start | bytes 589832 | tf_op jit(solution)/shard_map/ppermute | solution.py:255
  87.5 1.6 %rest.1 = (f32[3,128,128]{2,1,0:T(8,128)S(1)}, f32[6,128,128]{2,1,0:T(8,128)S(1)}, f32[6,128,128]{2,1,0:T(8,128)S(1)}, bf16[6,128,128]{2,1,0:T(8,128)(2,1)S(1)},...) custom-call(bf16[3,128,128]{2,1,0:T(8,128)(2,1)S(1)} %get-tuple-elem, ...), custom_call_target="tpu_custom_call" | custom-call | tf_op jit(solution)/shard_map/rest/pallas_call | solution.py:328
  89.2 1.9 %collective-permute-start.13 = (bf16[6,128,128]{2,1,0:T(8,128)(2,1)S(1)}, bf16[6,128,128]{2,1,0:T(8,128)(2,1)S(1)}, u32[]{:S(2)}, u32[]{:S(2)}) collective-permute-start(bf16[6,128,128]{2,1,0:T(8,128)(2,1)S(1)} %get-tuple-element.63), channel_id=1, source_target_pairs={{1,9},{8,0},{9,17},{16,8},{17,25},{24,16},{25,33},{32,24},{33,41},... | collective-permute-start | bytes 589832 | tf_op jit(solution)/shard_map/ppermute | solution.py:255
  91.1 5.5 %collective-permute-start.14 = (bf16[6,128,128]{2,1,0:T(8,128)(2,1)S(1)}, bf16[6,128,128]{2,1,0:T(8,128)(2,1)S(1)}, u32[]{:S(2)}, u32[]{:S(2)}) collective-permute-start(bf16[6,128,128]{2,1,0:T(8,128)(2,1)S(1)} %get-tuple-element.64), channel_id=1, source_target_pairs={{0,8},{8,16},{9,1},{16,24},{17,9},{24,32},{25,17},{32,40},{33,25},... | collective-permute-start | bytes 589832 | tf_op jit(solution)/shard_map/ppermute | solution.py:255
  96.6 1.9 %collective-permute-start.15 = (bf16[6,128,128]{2,1,0:T(8,128)(2,1)S(1)}, bf16[6,128,128]{2,1,0:T(8,128)(2,1)S(1)}, u32[]{:S(2)}, u32[]{:S(2)}) collective-permute-start(bf16[6,128,128]{2,1,0:T(8,128)(2,1)S(1)} %get-tuple-element.65), channel_id=1, source_target_pairs={{0,384},{1,129},{8,392},{9,137},{16,400},{17,145},{24,408},{25,153... | collective-permute-start | bytes 589832 | tf_op jit(solution)/shard_map/ppermute | solution.py:265
  98.5 3.4 %collective-permute-start.19 = (bf16[6,128,128]{2,1,0:T(8,128)(2,1)S(1)}, bf16[6,128,128]{2,1,0:T(8,128)(2,1)S(1)}, u32[]{:S(2)}, u32[]{:S(2)}) collective-permute-start(bf16[6,128,128]{2,1,0:T(8,128)(2,1)S(1)} %get-tuple-element.76), channel_id=1, source_target_pairs={{0,128},{8,136},{16,144},{24,152},{32,160},{40,168},{48,176},{56,1... | collective-permute-start | bytes 589832 | tf_op jit(solution)/shard_map/ppermute | solution.py:255
  101.9 1.8 %collective-permute-done.12 = bf16[6,128,128]{2,1,0:T(8,128)(2,1)S(1)} collective-permute-done((bf16[6,128,128]{2,1,0:T(8,128)(2,1)S(1)}, bf16[6,128,128]{2,1,0:T(8,128)(2,1)S(1)}, u32[]{:S(2)}, u32[]{:S(2)}) %collective-permute-start.12) | collective-permute-done | bytes 196640 | tf_op jit(solution)/shard_map/ppermute | solution.py:255
  103.8 1.8 %collective-permute-done.15 = bf16[6,128,128]{2,1,0:T(8,128)(2,1)S(1)} collective-permute-done((bf16[6,128,128]{2,1,0:T(8,128)(2,1)S(1)}, bf16[6,128,128]{2,1,0:T(8,128)(2,1)S(1)}, u32[]{:S(2)}, u32[]{:S(2)}) %collective-permute-start.15) | collective-permute-done | bytes 196640 | tf_op jit(solution)/shard_map/ppermute | solution.py:265
  105.6 3.2 %collective-permute-start.16 = (bf16[6,128,128]{2,1,0:T(8,128)(2,1)S(1)}, bf16[6,128,128]{2,1,0:T(8,128)(2,1)S(1)}, u32[]{:S(2)}, u32[]{:S(2)}) collective-permute-start(bf16[6,128,128]{2,1,0:T(8,128)(2,1)S(1)} %add_convert_fusion.4), channel_id=1, source_target_pairs={{1,17},{9,25},{16,0},{17,33},{24,8},{25,41},{32,16},{33,49},{40,24... | collective-permute-start | bytes 589832 | tf_op jit(solution)/shard_map/ppermute | solution.py:255
  108.8 5.1 %collective-permute-start.17 = (bf16[6,128,128]{2,1,0:T(8,128)(2,1)S(1)}, bf16[6,128,128]{2,1,0:T(8,128)(2,1)S(1)}, u32[]{:S(2)}, u32[]{:S(2)}) collective-permute-start(bf16[6,128,128]{2,1,0:T(8,128)(2,1)S(1)} %add_convert_fusion.3), channel_id=1, source_target_pairs={{0,16},{8,24},{16,32},{17,1},{24,40},{25,9},{32,48},{33,17},{40,56... | collective-permute-start | bytes 589832 | tf_op jit(solution)/shard_map/ppermute | solution.py:255
  113.9 0.1 add_convert_fusion
  114.0 1.9 %collective-permute-start.18 = (bf16[6,128,128]{2,1,0:T(8,128)(2,1)S(1)}, bf16[6,128,128]{2,1,0:T(8,128)(2,1)S(1)}, u32[]{:S(2)}, u32[]{:S(2)}) collective-permute-start(bf16[6,128,128]{2,1,0:T(8,128)(2,1)S(1)} %add_convert_fusion), channel_id=1, source_target_pairs={{0,384},{1,129},{8,392},{9,137},{16,400},{17,145},{24,408},{25,153... | collective-permute-start | bytes 589832 | tf_op jit(solution)/shard_map/ppermute | solution.py:265
  115.9 0.0 collective-permute-done.16
  115.9 2.0 %collective-permute-done.17 = bf16[6,128,128]{2,1,0:T(8,128)(2,1)S(1)} collective-permute-done((bf16[6,128,128]{2,1,0:T(8,128)(2,1)S(1)}, bf16[6,128,128]{2,1,0:T(8,128)(2,1)S(1)}, u32[]{:S(2)}, u32[]{:S(2)}) %collective-permute-start.17) | collective-permute-done | bytes 196640 | tf_op jit(solution)/shard_map/ppermute | solution.py:255
  117.9 0.1 add_convert_fusion.1
  118.0 4.2 %collective-permute-done.18.refs_3_ = bf16[6,128,128]{2,1,0:T(8,128)(2,1)S(1)} collective-permute-done((bf16[6,128,128]{2,1,0:T(8,128)(2,1)S(1)}, bf16[6,128,128]{2,1,0:T(8,128)(2,1)S(1)}, u32[]{:S(2)}, u32[]{:S(2)}) %collective-permute-start.18) | collective-permute-done | bytes 196640 | tf_op jit(solution)/shard_map/ppermute | solution.py:265
  122.2 1.9 %collective-permute-start.20 = (bf16[6,128,128]{2,1,0:T(8,128)(2,1)S(1)}, bf16[6,128,128]{2,1,0:T(8,128)(2,1)S(1)}, u32[]{:S(2)}, u32[]{:S(2)}) collective-permute-start(bf16[6,128,128]{2,1,0:T(8,128)(2,1)S(1)} %get-tuple-element.81), channel_id=1, source_target_pairs={{1,17},{9,25},{16,0},{17,33},{24,8},{25,41},{32,16},{33,49},{40,24... | collective-permute-start | bytes 589832 | tf_op jit(solution)/shard_map/ppermute | solution.py:255
  124.1 6.4 %collective-permute-start.21 = (bf16[6,128,128]{2,1,0:T(8,128)(2,1)S(1)}, bf16[6,128,128]{2,1,0:T(8,128)(2,1)S(1)}, u32[]{:S(2)}, u32[]{:S(2)}) collective-permute-start(bf16[6,128,128]{2,1,0:T(8,128)(2,1)S(1)} %get-tuple-element.82), channel_id=1, source_target_pairs={{0,16},{8,24},{16,32},{17,1},{24,40},{25,9},{32,48},{33,17},{40,56... | collective-permute-start | bytes 589832 | tf_op jit(solution)/shard_map/ppermute | solution.py:255
  130.5 3.2 %collective-permute-done.20.refs_5_ = bf16[6,128,128]{2,1,0:T(8,128)(2,1)S(1)} collective-permute-done((bf16[6,128,128]{2,1,0:T(8,128)(2,1)S(1)}, bf16[6,128,128]{2,1,0:T(8,128)(2,1)S(1)}, u32[]{:S(2)}, u32[]{:S(2)}) %collective-permute-start.20) | collective-permute-done | bytes 196640 | tf_op jit(solution)/shard_map/ppermute | solution.py:255
  133.7 3.5 %collective-permute-done.21.refs_6_ = bf16[6,128,128]{2,1,0:T(8,128)(2,1)S(1)} collective-permute-done((bf16[6,128,128]{2,1,0:T(8,128)(2,1)S(1)}, bf16[6,128,128]{2,1,0:T(8,128)(2,1)S(1)}, u32[]{:S(2)}, u32[]{:S(2)}) %collective-permute-start.21) | collective-permute-done | bytes 196640 | tf_op jit(solution)/shard_map/ppermute | solution.py:255
  137.2 0.9 terms.1
  138.2 9.2 %all_to_all.10.terms_ref = f32[8,8,128]{2,1,0:T(8,128)S(1)} all-to-all(f32[8,8,128]{2,1,0:T(8,128)S(1)} %get-tuple-element.83), channel_id=1, replica_groups=mesh['x'=4,'z'=16,'y'=4,'c'=2] {'y','c'}, dimensions={0} | all-to-all | bytes 65536 | tf_op jit(solution)/shard_map/all_to_all | solution.py:380
  147.4 0.9 final.1
  (14 shorter events, 0.1 us)
Async XLA Ops:
  0.6 75.1 %copy-start = (bf16[128,3,128]{2,0,1:T(8,128)(2,1)S(1)}, bf16[128,3,128]{2,0,1:T(8,128)(2,1)}, u32[]{:S(2)}) copy-start(bf16[128,3,128]{2,0,1:T(8,128)(2,1)} %param.10) | copy-start | bytes 294916
  2.5 9.9 %all-to-all-start = ((f32[8,8,128]{2,1,0:T(8,128)}), f32[8,8,128]{2,1,0:T(8,128)S(1)}, u32[]{:S(2)}, u32[]{:S(2)}) async-start(f32[8,8,128]{2,1,0:T(8,128)} %squares.1), calls=%async_computation | async-start | bytes 65536 | tf_op jit(solution)/shard_map/all_to_all | solution.py:340
  12.6 18.6 %collective-permute-start.3 = (bf16[6,128,128]{2,1,0:T(8,128)(2,1)S(1)}, bf16[6,128,128]{2,1,0:T(8,128)(2,1)S(1)}, u32[]{:S(2)}, u32[]{:S(2)}) collective-permute-start(bf16[6,128,128]{2,1,0:T(8,128)(2,1)S(1)} %get-tuple-element.47.refs_0_), channel_id=1, source_target_pairs={{1,17},{9,25},{16,0},{17,33},{24,8},{25,41},{32,16},{33,49},{40,24... | collective-permute-start | bytes 589832 | tf_op jit(solution)/shard_map/ppermute | solution.py:255
  17.5 17.1 %collective-permute-start.2 = (bf16[6,128,128]{2,1,0:T(8,128)(2,1)S(1)}, bf16[6,128,128]{2,1,0:T(8,128)(2,1)S(1)}, u32[]{:S(2)}, u32[]{:S(2)}) collective-permute-start(bf16[6,128,128]{2,1,0:T(8,128)(2,1)S(1)} %get-tuple-element.47.refs_0_), channel_id=1, source_target_pairs={{0,16},{8,24},{16,32},{17,1},{24,40},{25,9},{32,48},{33,17},{40,56... | collective-permute-start | bytes 589832 | tf_op jit(solution)/shard_map/ppermute | solution.py:255
  26.4 17.1 %collective-permute-start.7 = (bf16[6,128,128]{2,1,0:T(8,128)(2,1)S(1)}, bf16[6,128,128]{2,1,0:T(8,128)(2,1)S(1)}, u32[]{:S(2)}, u32[]{:S(2)}) collective-permute-start(bf16[6,128,128]{2,1,0:T(8,128)(2,1)S(1)} %get-tuple-element.47.refs_0_), channel_id=1, source_target_pairs={{1,9},{8,0},{9,17},{16,8},{17,25},{24,16},{25,33},{32,24},{33,41},... | collective-permute-start | bytes 589832 | tf_op jit(solution)/shard_map/ppermute | solution.py:255
  29.0 15.7 %collective-permute-start = (bf16[6,128,128]{2,1,0:T(8,128)(2,1)S(1)}, bf16[6,128,128]{2,1,0:T(8,128)(2,1)S(1)}, u32[]{:S(2)}, u32[]{:S(2)}) collective-permute-start(bf16[6,128,128]{2,1,0:T(8,128)(2,1)S(1)} %get-tuple-element.47.refs_0_), channel_id=1, source_target_pairs={{0,128},{1,385},{8,136},{9,393},{16,144},{17,401},{24,152},{25,409... | collective-permute-start | bytes 589832 | tf_op jit(solution)/shard_map/ppermute | solution.py:265
  31.2 17.6 %collective-permute-start.5 = (bf16[6,128,128]{2,1,0:T(8,128)(2,1)S(1)}, bf16[6,128,128]{2,1,0:T(8,128)(2,1)S(1)}, u32[]{:S(2)}, u32[]{:S(2)}) collective-permute-start(bf16[6,128,128]{2,1,0:T(8,128)(2,1)S(1)} %collective-permute-done.3.refs_4_), channel_id=1, source_target_pairs={{1,17},{9,25},{16,0},{17,33},{24,8},{25,41},{32,16},{33,49},{40,24... | collective-permute-start | bytes 589832 | tf_op jit(solution)/shard_map/ppermute | solution.py:255
  34.6 16.1 %collective-permute-start.4 = (bf16[6,128,128]{2,1,0:T(8,128)(2,1)S(1)}, bf16[6,128,128]{2,1,0:T(8,128)(2,1)S(1)}, u32[]{:S(2)}, u32[]{:S(2)}) collective-permute-start(bf16[6,128,128]{2,1,0:T(8,128)(2,1)S(1)} %collective-permute-done.2.refs_3_), channel_id=1, source_target_pairs={{0,16},{8,24},{16,32},{17,1},{24,40},{25,9},{32,48},{33,17},{40,56... | collective-permute-start | bytes 589832 | tf_op jit(solution)/shard_map/ppermute | solution.py:255
  41.5 17.4 %collective-permute-start.6 = (bf16[6,128,128]{2,1,0:T(8,128)(2,1)S(1)}, bf16[6,128,128]{2,1,0:T(8,128)(2,1)S(1)}, u32[]{:S(2)}, u32[]{:S(2)}) collective-permute-start(bf16[6,128,128]{2,1,0:T(8,128)(2,1)S(1)} %get-tuple-element.47.refs_0_), channel_id=1, source_target_pairs={{0,8},{8,16},{9,1},{16,24},{17,9},{24,32},{25,17},{32,40},{33,25},... | collective-permute-start | bytes 589832 | tf_op jit(solution)/shard_map/ppermute | solution.py:255
  43.5 15.4 %collective-permute-start.1 = (bf16[6,128,128]{2,1,0:T(8,128)(2,1)S(1)}, bf16[6,128,128]{2,1,0:T(8,128)(2,1)S(1)}, u32[]{:S(2)}, u32[]{:S(2)}) collective-permute-start(bf16[6,128,128]{2,1,0:T(8,128)(2,1)S(1)} %get-tuple-element.47.refs_0_), channel_id=1, source_target_pairs={{1,129},{9,137},{17,145},{25,153},{33,161},{41,169},{49,177},{57,1... | collective-permute-start | bytes 589832 | tf_op jit(solution)/shard_map/ppermute | solution.py:255
  44.8 14.1 %collective-permute-start.8 = (bf16[6,128,128]{2,1,0:T(8,128)(2,1)S(1)}, bf16[6,128,128]{2,1,0:T(8,128)(2,1)S(1)}, u32[]{:S(2)}, u32[]{:S(2)}) collective-permute-start(bf16[6,128,128]{2,1,0:T(8,128)(2,1)S(1)} %collective-permute-done.refs_1_), channel_id=1, source_target_pairs={{0,128},{1,385},{8,136},{9,393},{16,144},{17,401},{24,152},{25,409... | collective-permute-start | bytes 589832 | tf_op jit(solution)/shard_map/ppermute | solution.py:265
  48.8 14.9 %collective-permute-start.10 = (bf16[6,128,128]{2,1,0:T(8,128)(2,1)S(1)}, bf16[6,128,128]{2,1,0:T(8,128)(2,1)S(1)}, u32[]{:S(2)}, u32[]{:S(2)}) collective-permute-start(bf16[6,128,128]{2,1,0:T(8,128)(2,1)S(1)} %collective-permute-done.5.refs_6_), channel_id=1, source_target_pairs={{1,33},{9,41},{17,49},{25,57},{32,0},{33,65},{40,8},{41,73},{48,16... | collective-permute-start | bytes 589832 | tf_op jit(solution)/shard_map/ppermute | solution.py:255
  50.7 25.0 %collective-permute-start.9 = (bf16[6,128,128]{2,1,0:T(8,128)(2,1)S(1)}, bf16[6,128,128]{2,1,0:T(8,128)(2,1)S(1)}, u32[]{:S(2)}, u32[]{:S(2)}) collective-permute-start(bf16[6,128,128]{2,1,0:T(8,128)(2,1)S(1)} %collective-permute-done.4.refs_5_), channel_id=1, source_target_pairs={{0,32},{8,40},{16,48},{24,56},{32,64},{33,1},{40,72},{41,9},{48,80... | collective-permute-start | bytes 589832 | tf_op jit(solution)/shard_map/ppermute | solution.py:255
  77.4 21.1 %collective-permute-start.11 = (bf16[6,128,128]{2,1,0:T(8,128)(2,1)S(1)}, bf16[6,128,128]{2,1,0:T(8,128)(2,1)S(1)}, u32[]{:S(2)}, u32[]{:S(2)}) collective-permute-start(bf16[6,128,128]{2,1,0:T(8,128)(2,1)S(1)} %get-tuple-element.57), channel_id=1, source_target_pairs={{1,33},{9,41},{17,49},{25,57},{32,0},{33,65},{40,8},{41,73},{48,16... | collective-permute-start | bytes 589832 | tf_op jit(solution)/shard_map/ppermute | solution.py:255
  79.3 24.3 %collective-permute-start.12 = (bf16[6,128,128]{2,1,0:T(8,128)(2,1)S(1)}, bf16[6,128,128]{2,1,0:T(8,128)(2,1)S(1)}, u32[]{:S(2)}, u32[]{:S(2)}) collective-permute-start(bf16[6,128,128]{2,1,0:T(8,128)(2,1)S(1)} %get-tuple-element.58), channel_id=1, source_target_pairs={{0,32},{8,40},{16,48},{24,56},{32,64},{33,1},{40,72},{41,9},{48,80... | collective-permute-start | bytes 589832 | tf_op jit(solution)/shard_map/ppermute | solution.py:255
  89.2 14.6 %collective-permute-start.13 = (bf16[6,128,128]{2,1,0:T(8,128)(2,1)S(1)}, bf16[6,128,128]{2,1,0:T(8,128)(2,1)S(1)}, u32[]{:S(2)}, u32[]{:S(2)}) collective-permute-start(bf16[6,128,128]{2,1,0:T(8,128)(2,1)S(1)} %get-tuple-element.63), channel_id=1, source_target_pairs={{1,9},{8,0},{9,17},{16,8},{17,25},{24,16},{25,33},{32,24},{33,41},... | collective-permute-start | bytes 589832 | tf_op jit(solution)/shard_map/ppermute | solution.py:255
  91.1 12.7 %collective-permute-start.14 = (bf16[6,128,128]{2,1,0:T(8,128)(2,1)S(1)}, bf16[6,128,128]{2,1,0:T(8,128)(2,1)S(1)}, u32[]{:S(2)}, u32[]{:S(2)}) collective-permute-start(bf16[6,128,128]{2,1,0:T(8,128)(2,1)S(1)} %get-tuple-element.64), channel_id=1, source_target_pairs={{0,8},{8,16},{9,1},{16,24},{17,9},{24,32},{25,17},{32,40},{33,25},... | collective-permute-start | bytes 589832 | tf_op jit(solution)/shard_map/ppermute | solution.py:255
  96.6 9.1 %collective-permute-start.15 = (bf16[6,128,128]{2,1,0:T(8,128)(2,1)S(1)}, bf16[6,128,128]{2,1,0:T(8,128)(2,1)S(1)}, u32[]{:S(2)}, u32[]{:S(2)}) collective-permute-start(bf16[6,128,128]{2,1,0:T(8,128)(2,1)S(1)} %get-tuple-element.65), channel_id=1, source_target_pairs={{0,384},{1,129},{8,392},{9,137},{16,400},{17,145},{24,408},{25,153... | collective-permute-start | bytes 589832 | tf_op jit(solution)/shard_map/ppermute | solution.py:265
  98.5 19.5 %collective-permute-start.19 = (bf16[6,128,128]{2,1,0:T(8,128)(2,1)S(1)}, bf16[6,128,128]{2,1,0:T(8,128)(2,1)S(1)}, u32[]{:S(2)}, u32[]{:S(2)}) collective-permute-start(bf16[6,128,128]{2,1,0:T(8,128)(2,1)S(1)} %get-tuple-element.76), channel_id=1, source_target_pairs={{0,128},{8,136},{16,144},{24,152},{32,160},{40,168},{48,176},{56,1... | collective-permute-start | bytes 589832 | tf_op jit(solution)/shard_map/ppermute | solution.py:255
  105.6 10.3 %collective-permute-start.16 = (bf16[6,128,128]{2,1,0:T(8,128)(2,1)S(1)}, bf16[6,128,128]{2,1,0:T(8,128)(2,1)S(1)}, u32[]{:S(2)}, u32[]{:S(2)}) collective-permute-start(bf16[6,128,128]{2,1,0:T(8,128)(2,1)S(1)} %add_convert_fusion.4), channel_id=1, source_target_pairs={{1,17},{9,25},{16,0},{17,33},{24,8},{25,41},{32,16},{33,49},{40,24... | collective-permute-start | bytes 589832 | tf_op jit(solution)/shard_map/ppermute | solution.py:255
  108.8 9.1 %collective-permute-start.17 = (bf16[6,128,128]{2,1,0:T(8,128)(2,1)S(1)}, bf16[6,128,128]{2,1,0:T(8,128)(2,1)S(1)}, u32[]{:S(2)}, u32[]{:S(2)}) collective-permute-start(bf16[6,128,128]{2,1,0:T(8,128)(2,1)S(1)} %add_convert_fusion.3), channel_id=1, source_target_pairs={{0,16},{8,24},{16,32},{17,1},{24,40},{25,9},{32,48},{33,17},{40,56... | collective-permute-start | bytes 589832 | tf_op jit(solution)/shard_map/ppermute | solution.py:255
  114.0 8.2 %collective-permute-start.18 = (bf16[6,128,128]{2,1,0:T(8,128)(2,1)S(1)}, bf16[6,128,128]{2,1,0:T(8,128)(2,1)S(1)}, u32[]{:S(2)}, u32[]{:S(2)}) collective-permute-start(bf16[6,128,128]{2,1,0:T(8,128)(2,1)S(1)} %add_convert_fusion), channel_id=1, source_target_pairs={{0,384},{1,129},{8,392},{9,137},{16,400},{17,145},{24,408},{25,153... | collective-permute-start | bytes 589832 | tf_op jit(solution)/shard_map/ppermute | solution.py:265
  122.2 11.5 %collective-permute-start.20 = (bf16[6,128,128]{2,1,0:T(8,128)(2,1)S(1)}, bf16[6,128,128]{2,1,0:T(8,128)(2,1)S(1)}, u32[]{:S(2)}, u32[]{:S(2)}) collective-permute-start(bf16[6,128,128]{2,1,0:T(8,128)(2,1)S(1)} %get-tuple-element.81), channel_id=1, source_target_pairs={{1,17},{9,25},{16,0},{17,33},{24,8},{25,41},{32,16},{33,49},{40,24... | collective-permute-start | bytes 589832 | tf_op jit(solution)/shard_map/ppermute | solution.py:255
  124.1 13.1 %collective-permute-start.21 = (bf16[6,128,128]{2,1,0:T(8,128)(2,1)S(1)}, bf16[6,128,128]{2,1,0:T(8,128)(2,1)S(1)}, u32[]{:S(2)}, u32[]{:S(2)}) collective-permute-start(bf16[6,128,128]{2,1,0:T(8,128)(2,1)S(1)} %get-tuple-element.82), channel_id=1, source_target_pairs={{0,16},{8,24},{16,32},{17,1},{24,40},{25,9},{32,48},{33,17},{40,56... | collective-permute-start | bytes 589832 | tf_op jit(solution)/shard_map/ppermute | solution.py:255
